TPU v7x, 128 devices: a whole 4x4x4 slice. The times are simulated.
128 devices in a mesh: img: 16 (over z, y), tile: 8 (over x, core).
Axes of the slice: x: 4, y: 4, z: 4, core: 2. Of those that a mesh axis runs over, the one named last changes fastest.
Arguments:
- spins: float32 [16, 3, 16, 256, 256], P('img', None, None, 'tile'), may hold values from -4.5 to 4.5
- aniso: float32 [16, 256, 256], P(None, 'tile'), may hold values from 0.2 to 2
Outputs:
- path: float32 [16, 3, 16, 256, 256], P('img', None, None, 'tile')
All inputs are finite; a program needn't handle non-finite values.
Results may differ from a plain program's by a relative error of at most 0.0003.
Values sent between devices are 32-bit elements; how exact they have to be, the bound alone decides.
No kernel may reach another device: no remote copies, remote signals or barrier semaphores. Data moves between devices by JAX's collectives and lax.ppermute only.
A program may use at most 128 MiB of HBM per device.

v0:
```python
import jax
import jax.numpy as jnp
from jax import lax
from jax.sharding import Mesh
from jax.sharding import PartitionSpec as P

OUTER = 2
INNER = 3
IMG = ("img_0", "img_1")
TILE = ("tile_0", "tile_1")
IMG_TILE = ("img_0", "img_1", "tile_0", "tile_1")


exchange_coef = 1.0
cubic_coef = 0.5
spring_coef = 20.0
step_scale = 0.25
epsilon = 1e-06


def padded_2(cells, sides, width):
    for axis, dim in sides:
        count = lax.axis_size(axis)
        ends = count - 1
        head = lax.slice_in_dim(cells, 0, width, axis=dim)
        tail = lax.slice_in_dim(cells, cells.shape[dim] - width, cells.shape[dim], axis=dim)
        cells = jnp.concatenate(
            [
                lax.ppermute(tail, axis, [(i, (i + 1) % count) for i in range(ends)]),
                cells,
                lax.ppermute(head, axis, [((i + 1) % count, i) for i in range(ends)]),
            ],
            axis=dim,
        )
    return cells


def from_everyone(shard, axis):
    peers = lax.axis_size(axis)
    return lax.all_to_all(
        jnp.broadcast_to(shard[None], (peers, *shard.shape)), axis, 0, 0, tiled=True
    )


def folded_in_pairs(pieces, combine):
    while len(jax.tree.leaves(pieces)[0]) > 1:
        pieces = jax.vmap(combine)(*(pieces[side::2] for side in (0, 1)))
    return pieces[0]


def carried_in(shard, axis, combine, identity):
    peers, here = (lax.axis_size(axis), lax.axis_index(axis))
    passed = jnp.arange(peers) < here

    def kept(part, zero, own):
        part = jnp.where(
            passed.reshape(-1, *(1 for _ in own.shape)), part, jnp.asarray(zero, own.dtype)
        )
        return part

    pieces = from_everyone(shard, axis)
    return folded_in_pairs(kept(pieces, identity, shard), combine)


def over_copies(shard, axis):
    return from_everyone(shard, axis).sum(axis=0)


def over_axes(shard, axes):
    for axis in axes:
        shard = lax.psum(shard, axis)
    return shard


def laplace(field):
    widths = [(0, 0)] * (field.ndim - 4) + [(0, 0), (1, 1), (0, 0), (1, 1)]
    padded = jnp.pad(field, widths)
    centre = padded[..., 1:-1, 1:-1, 1:-1]
    beside_all = padded[..., 2:, 1:-1, 1:-1] + padded[..., :-2, 1:-1, 1:-1]
    beside_all = beside_all + padded[..., 1:-1, 2:, 1:-1] + padded[..., 1:-1, :-2, 1:-1]
    beside_all = beside_all + padded[..., 1:-1, 1:-1, 2:] + padded[..., 1:-1, 1:-1, :-2]
    return beside_all - 6.0 * centre


def axis_select():
    return (jnp.arange(3) == 2).astype(jnp.float32)[:, None, None, None]


def force_field(middle_ext, coefs):
    middle = middle_ext[..., 1:-1, :]
    square_norm = jnp.sum(middle * middle, axis=-4, keepdims=True)
    return (
        exchange_coef * laplace(middle_ext)
        + coefs * middle * axis_select()
        - cubic_coef * (square_norm - 1.0) * middle
    )


def hessian_point(middle, vector, coefs):
    square_norm = jnp.sum(middle * middle, axis=-4, keepdims=True)
    projected = jnp.sum(middle * vector, axis=-4, keepdims=True)
    return coefs * vector * axis_select() - cubic_coef * (
        (square_norm - 1.0) * vector + 2.0 * middle * projected
    )


def add_pair(earlier, later):
    return earlier + later


def body(spins, aniso):
    local_images = spins.shape[0]
    width_x = spins.shape[3]
    img_count = lax.axis_size(IMG)
    tile_count = lax.axis_size(TILE)
    images = local_images * img_count
    cell_count = float(
        images * spins.shape[1] * spins.shape[2] * width_x * tile_count * spins.shape[4]
    )
    first_image = lax.axis_index(IMG) * local_images
    image_index = first_image + jnp.arange(local_images, dtype=jnp.int32)
    segment_live = (image_index < images - 1).astype(jnp.float32)
    interior = ((image_index > 0) & (image_index < images - 1)).astype(jnp.float32)
    target = image_index.astype(jnp.float32) / (images - 1)
    rim_depth = 1
    cycle_mask = 1.0
    current = spins
    for outer_step in range(OUTER):
        repeated = current
        framed_all = padded_2(repeated, ((IMG, 0), (TILE, 3)), rim_depth)
        before_img = framed_all[:-2]
        own_framed = framed_all[1:-1]
        after_img = framed_all[2:]
        difference = (after_img - own_framed)[..., rim_depth : rim_depth + width_x, :]
        middle_seg = 0.5 * (own_framed + after_img)
        drive_own = force_field(middle_seg, aniso)
        diff_sq = jnp.sum(difference * difference, axis=(1, 2, 3, 4))
        drive_sq = jnp.sum(drive_own * drive_own, axis=(1, 2, 3, 4))
        diff_sq, drive_sq = lax.psum((diff_sq, drive_sq), TILE)
        seg_len = segment_live * jnp.sqrt(diff_sq + epsilon)
        drive_len = segment_live * jnp.sqrt(drive_sq + epsilon)
        offset = carried_in(jnp.sum(seg_len), IMG, add_pair, jnp.float32(0.0))
        path_len, drive_total = (
            over_copies(jnp.sum(seg_len), IMG),
            over_copies(jnp.sum(drive_len), IMG),
        )
        before_arc = offset + jnp.cumsum(seg_len) - seg_len
        time_step = path_len / drive_total
        spring_pull = (
            spring_coef * (before_arc / path_len - target) * (images - 1) / (2.0 * path_len)
        )
        spring_pull = spring_pull[:, None, None, None, None]
        interior_mask = interior[:, None, None, None, None]
        before_core = before_img[..., 1:-1, :]
        after_core = after_img[..., 1:-1, :]
        before_own = before_img[..., rim_depth : rim_depth + width_x, :]
        after_own = after_img[..., rim_depth : rim_depth + width_x, :]
        for inner_step in range(INNER):
            if inner_step == 0:
                own_ext = own_framed
            else:
                own_ext = padded_2(current, ((TILE, 3),), rim_depth)
            own_core = own_ext[..., 1:-1, :]
            middle_a = 0.5 * (before_img + own_ext)
            middle_b = 0.5 * (own_ext + after_img)
            res_a = (
                (own_core - before_core) / time_step - force_field(middle_a, aniso)
            ) * cycle_mask
            res_b = (
                (after_core - own_core) / time_step - force_field(middle_b, aniso)
            ) * cycle_mask
            res_sum = res_a + res_b
            adjoint_lap = laplace(padded_2(res_sum, ((TILE, 3),), 1))
            middle_a_own = middle_a[..., rim_depth : rim_depth + width_x, :]
            middle_b_own = middle_b[..., rim_depth : rim_depth + width_x, :]
            adjoint = exchange_coef * adjoint_lap
            adjoint = (
                adjoint
                + hessian_point(middle_a_own, res_a, aniso)
                + hessian_point(middle_b_own, res_b, aniso)
            )
            gradients = (
                res_a - res_b - 0.5 * time_step * adjoint + spring_pull * (after_own - before_own)
            )
            gradients = gradients * interior_mask
            grad_total = over_axes(jnp.sum(gradients * gradients), IMG_TILE)
            grad_scale = jnp.sqrt(grad_total / cell_count + epsilon)
            current = current - step_scale * gradients / grad_scale
    return current


def solution(mesh):
    split = Mesh(mesh.devices.reshape(4, 4, 4, 2), ("img_0", "img_1", "tile_0", "tile_1"))
    return jax.shard_map(
        body,
        mesh=split,
        in_specs=(P(IMG, None, None, TILE, None), P(None, TILE, None)),
        out_specs=P(IMG, None, None, TILE, None),
        check_vma=False,
    )
```

profile of v0, /device:TPU:1, one launch (start us, length us, event | category | flops | bytes accessed | tf_op | source)
XLA Modules:
  0.0 635.0 jit_solution(12374536469458918659)
XLA Ops:
  7.9 31.6 %collective-permute-done = f32[1,3,16,32,256]{4,2,3,1,0:T(8,128)S(1)} collective-permute-done((f32[1,3,16,32,256]{4,2,3,1,0:T(8,128)S(1)}, f32[1,3,16,32,256]{4,2,3,1,0:T(8,128)S(1)}, u32[]{:S(2)}, u32[]{:S(2)}) %collective-permute-start) | collective-permute-done | bytes 1572896 | tf_op jit(solution)/shard_map/ppermute | solution.py:29
  69.8 11.1 %all-reduce.19 = (f32[1]{0:T(128)}, f32[1]{0:T(128)}) all-reduce(f32[1]{0:T(128)} %bitcast.1, f32[1]{0:T(128)} %bitcast.3), channel_id=1, replica_groups=mesh['img_0'=4,'img_1'=4,'tile_0'=4,'tile_1'=2] {'tile_0','tile_1'}, use_global_device_ids=true, to_apply=%region_1.2 | all-reduce | flops 2 | bytes 16 | tf_op jit(solution)/shard_map/psum | solution.py:139
  82.7 9.1 %all-to-all-start = ((f32[16,1,1]{2,1,0:T(1,128)}), f32[16,1,1]{2,1,0:T(1,128)S(1)}, u32[]{:S(2)}, u32[]{:S(2)}) async-start(f32[16,1,1]{2,1,0:T(1,128)} %broadcast_in_dim.22), calls=%async_computation | async-start | bytes 16384 | tf_op jit(solution)/shard_map/all_to_all | solution.py:40
  110.4 8.4 %multiply_reduce_fusion.28 = (f32[16,32,256]{2,0,1:T(8,128)S(1)}, f32[1,3,16,32,256]{4,2,3,1,0:T(8,128)S(1)}, f32[16,32,256]{2,0,1:T(8,128)S(1)}, f32[1,3,16,32,256]{4,2,3,1,0:T(8,128)S(1)}) fusion(f32[1,3,16,34,256]{4,2,3,1,0:T(8,128)} %copy-done.2, f32[16,32,256]{2,0,1:T(8,128)S(1)} %get-tuple-element.128, f32[3]{0:T(128)S(1)} %compare_convert_fusion, ...), kind=kLoop, calls=%fused_computation.318 | loop fusion | flops 8388608 | bytes 19496976 | tf_op jit(solution)/shard_map/reduce_sum | solution.py:101
  138.6 7.4 %multiply_reduce_fusion.26 = (f32[]{:T(128)}, f32[1,3,16,32,256]{4,2,3,1,0:T(8,128)}, f32[1,3,16,32,256]{4,2,3,1,0:T(8,128)}) fusion(f32[]{:T(128)} %bitcast.10, f32[16,32,256]{2,0,1:T(8,128)} %broadcast_multiply_fusion.10, f32[1,3,16,34,256]{4,2,3,1,0:T(8,128)S(1)} %get-tuple-element.68, f32[1,3,16,32,256]{4,2,3,1,0:T(8,128)} %copy-done.41, ...), kind=kLoop, calls=%fused_computation.315 | loop fusion | flops 13369343 | bytes 23167004 | tf_op jit(solution)/shard_map/reduce_sum | solution.py:186
  145.9 7.5 %psum.198 = f32[]{:T(128)} all-reduce(f32[]{:T(128)} %get-tuple-element.46), channel_id=1, replica_groups=mesh['img_0'=4,'img_1'=4,'tile_0'=4,'tile_1'=2] {'img_0'}, use_global_device_ids=true, to_apply=%region_11.12 | all-reduce | flops 1 | bytes 8 | tf_op jit(solution)/shard_map/psum | solution.py:71
  153.4 7.7 %psum.199 = f32[]{:T(128)} all-reduce(f32[]{:T(128)} %psum.198), channel_id=1, replica_groups=mesh['img_0'=4,'img_1'=4,'tile_0'=4,'tile_1'=2] {'img_1'}, use_global_device_ids=true, to_apply=%region_12.13 | all-reduce | flops 1 | bytes 8 | tf_op jit(solution)/shard_map/psum | solution.py:71
  161.0 7.3 %psum.200 = f32[]{:T(128)} all-reduce(f32[]{:T(128)} %psum.199), channel_id=1, replica_groups=mesh['img_0'=4,'img_1'=4,'tile_0'=4,'tile_1'=2] {'tile_0'}, use_global_device_ids=true, to_apply=%region_13.14 | all-reduce | flops 1 | bytes 8 | tf_op jit(solution)/shard_map/psum | solution.py:71
  168.3 10.6 %psum.201 = f32[]{:T(128)} all-reduce(f32[]{:T(128)} %psum.200), channel_id=1, replica_groups=mesh['img_0'=4,'img_1'=4,'tile_0'=4,'tile_1'=2] {'tile_1'}, use_global_device_ids=true, to_apply=%region_14.15 | all-reduce | flops 1 | bytes 8 | tf_op jit(solution)/shard_map/psum | solution.py:71
  194.6 7.8 %multiply_reduce_fusion.23 = (f32[16,32,256]{2,0,1:T(8,128)}, f32[1,3,16,32,256]{4,2,3,1,0:T(8,128)}, f32[16,32,256]{2,0,1:T(8,128)}, f32[1,3,16,32,256]{4,2,3,1,0:T(8,128)}) fusion(f32[1,3,16,34,256]{4,2,3,1,0:T(8,128)S(1)} %get-tuple-element.61, f32[16,32,256]{2,0,1:T(8,128)} %get-tuple-element.124, f32[3]{0:T(128)S(1)} %compare_convert_fusion, ...), kind=kLoop, calls=%fused_computation.311 | loop fusion | flops 13107200 | bytes 23265796 | tf_op jit(solution)/shard_map/reduce_sum | solution.py:101
  227.6 7.3 %psum.203 = f32[]{:T(128)} all-reduce(f32[]{:T(128)} %psum.202), channel_id=1, replica_groups=mesh['img_0'=4,'img_1'=4,'tile_0'=4,'tile_1'=2] {'img_1'}, use_global_device_ids=true, to_apply=%region_21.22 | all-reduce | flops 1 | bytes 8 | tf_op jit(solution)/shard_map/psum | solution.py:71
  235.0 7.1 %psum.204 = f32[]{:T(128)} all-reduce(f32[]{:T(128)} %psum.203), channel_id=1, replica_groups=mesh['img_0'=4,'img_1'=4,'tile_0'=4,'tile_1'=2] {'tile_0'}, use_global_device_ids=true, to_apply=%region_22.23 | all-reduce | flops 1 | bytes 8 | tf_op jit(solution)/shard_map/psum | solution.py:71
  242.1 8.7 %psum.205 = f32[]{:T(128)} all-reduce(f32[]{:T(128)} %psum.204), channel_id=1, replica_groups=mesh['img_0'=4,'img_1'=4,'tile_0'=4,'tile_1'=2] {'tile_1'}, use_global_device_ids=true, to_apply=%region_23.24 | all-reduce | flops 1 | bytes 8 | tf_op jit(solution)/shard_map/psum | solution.py:71
  265.9 7.7 %multiply_reduce_fusion.18 = (f32[16,32,256]{2,0,1:T(8,128)}, f32[1,3,16,32,256]{4,2,3,1,0:T(8,128)}, f32[16,32,256]{2,0,1:T(8,128)}, f32[1,3,16,32,256]{4,2,3,1,0:T(8,128)}) fusion(f32[1,3,16,34,256]{4,2,3,1,0:T(8,128)S(1)} %get-tuple-element.59, f32[16,32,256]{2,0,1:T(8,128)} %get-tuple-element.120, f32[3]{0:T(128)S(1)} %compare_convert_fusion, ...), kind=kLoop, calls=%fused_computation.305 | loop fusion | flops 13107200 | bytes 23265796 | tf_op jit(solution)/shard_map/reduce_sum | solution.py:101
  291.8 7.3 %psum.206 = f32[]{:T(128)} all-reduce(f32[]{:T(128)} %get-tuple-element.34), channel_id=1, replica_groups=mesh['img_0'=4,'img_1'=4,'tile_0'=4,'tile_1'=2] {'img_0'}, use_global_device_ids=true, to_apply=%region_29.30 | all-reduce | flops 1 | bytes 8 | tf_op jit(solution)/shard_map/psum | solution.py:71
  299.1 7.7 %psum.207 = f32[]{:T(128)} all-reduce(f32[]{:T(128)} %psum.206), channel_id=1, replica_groups=mesh['img_0'=4,'img_1'=4,'tile_0'=4,'tile_1'=2] {'img_1'}, use_global_device_ids=true, to_apply=%region_30.31 | all-reduce | flops 1 | bytes 8 | tf_op jit(solution)/shard_map/psum | solution.py:71
  313.8 8.5 %psum.209 = f32[]{:T(128)} all-reduce(f32[]{:T(128)} %psum.208), channel_id=1, replica_groups=mesh['img_0'=4,'img_1'=4,'tile_0'=4,'tile_1'=2] {'tile_1'}, use_global_device_ids=true, to_apply=%region_32.33 | all-reduce | flops 1 | bytes 8 | tf_op jit(solution)/shard_map/psum | solution.py:71
  330.2 32.1 %collective-permute-done.15 = f32[1,3,16,32,256]{4,2,3,1,0:T(8,128)S(1)} collective-permute-done((f32[1,3,16,32,256]{4,2,3,1,0:T(8,128)S(1)}, f32[1,3,16,32,256]{4,2,3,1,0:T(8,128)S(1)}, u32[]{:S(2)}, u32[]{:S(2)}) %collective-permute-start.15) | collective-permute-done | bytes 1572896 | tf_op jit(solution)/shard_map/ppermute | solution.py:31
  382.0 10.6 %all-reduce.18 = (f32[1]{0:T(128)}, f32[1]{0:T(128)}) all-reduce(f32[1]{0:T(128)} %bitcast.11, f32[1]{0:T(128)} %bitcast.13), channel_id=1, replica_groups=mesh['img_0'=4,'img_1'=4,'tile_0'=4,'tile_1'=2] {'tile_0','tile_1'}, use_global_device_ids=true, to_apply=%region_34.35 | all-reduce | flops 2 | bytes 16 | tf_op jit(solution)/shard_map/psum | solution.py:139
  420.3 8.1 %multiply_reduce_fusion.12 = (f32[16,32,256]{2,0,1:T(8,128)S(1)}, f32[1,3,16,32,256]{4,2,3,1,0:T(8,128)S(1)}, f32[16,32,256]{2,0,1:T(8,128)S(1)}, f32[1,3,16,32,256]{4,2,3,1,0:T(8,128)S(1)}) fusion(f32[1,3,16,34,256]{4,2,3,1,0:T(8,128)} %copy-done, f32[16,32,256]{2,0,1:T(8,128)S(1)} %get-tuple-element.116, f32[3]{0:T(128)S(1)} %compare_convert_fusion, ...), kind=kLoop, calls=%fused_computation.297 | loop fusion | flops 8388608 | bytes 19496976 | tf_op jit(solution)/shard_map/reduce_sum | solution.py:101
  448.5 7.3 %multiply_reduce_fusion.10 = (f32[]{:T(128)}, f32[1,3,16,32,256]{4,2,3,1,0:T(8,128)}, f32[1,3,16,32,256]{4,2,3,1,0:T(8,128)}) fusion(f32[]{:T(128)} %bitcast.10, f32[16,32,256]{2,0,1:T(8,128)} %broadcast_multiply_fusion.4, f32[1,3,16,34,256]{4,2,3,1,0:T(8,128)S(1)} %get-tuple-element.64, f32[1,3,16,32,256]{4,2,3,1,0:T(8,128)} %copy-done.39, ...), kind=kLoop, calls=%fused_computation.294 | loop fusion | flops 13369343 | bytes 23167004 | tf_op jit(solution)/shard_map/reduce_sum | solution.py:186
  455.7 7.8 %psum.212 = f32[]{:T(128)} all-reduce(f32[]{:T(128)} %get-tuple-element.25), channel_id=1, replica_groups=mesh['img_0'=4,'img_1'=4,'tile_0'=4,'tile_1'=2] {'img_0'}, use_global_device_ids=true, to_apply=%region_44.45 | all-reduce | flops 1 | bytes 8 | tf_op jit(solution)/shard_map/psum | solution.py:71
  463.5 7.6 %psum.213 = f32[]{:T(128)} all-reduce(f32[]{:T(128)} %psum.212), channel_id=1, replica_groups=mesh['img_0'=4,'img_1'=4,'tile_0'=4,'tile_1'=2] {'img_1'}, use_global_device_ids=true, to_apply=%region_45.46 | all-reduce | flops 1 | bytes 8 | tf_op jit(solution)/shard_map/psum | solution.py:71
  477.8 9.8 %psum.215 = f32[]{:T(128)} all-reduce(f32[]{:T(128)} %psum.214), channel_id=1, replica_groups=mesh['img_0'=4,'img_1'=4,'tile_0'=4,'tile_1'=2] {'tile_1'}, use_global_device_ids=true, to_apply=%region_47.48 | all-reduce | flops 1 | bytes 8 | tf_op jit(solution)/shard_map/psum | solution.py:71
  502.8 7.7 %multiply_reduce_fusion.7 = (f32[16,32,256]{2,0,1:T(8,128)}, f32[1,3,16,32,256]{4,2,3,1,0:T(8,128)}, f32[16,32,256]{2,0,1:T(8,128)}, f32[1,3,16,32,256]{4,2,3,1,0:T(8,128)}) fusion(f32[1,3,16,34,256]{4,2,3,1,0:T(8,128)S(1)} %get-tuple-element.57, f32[16,32,256]{2,0,1:T(8,128)} %get-tuple-element.112, f32[3]{0:T(128)S(1)} %compare_convert_fusion, ...), kind=kLoop, calls=%fused_computation.290 | loop fusion | flops 13107200 | bytes 23265796 | tf_op jit(solution)/shard_map/reduce_sum | solution.py:101
  528.7 7.2 %psum.216 = f32[]{:T(128)} all-reduce(f32[]{:T(128)} %get-tuple-element.19), channel_id=1, replica_groups=mesh['img_0'=4,'img_1'=4,'tile_0'=4,'tile_1'=2] {'img_0'}, use_global_device_ids=true, to_apply=%region_53.54 | all-reduce | flops 1 | bytes 8 | tf_op jit(solution)/shard_map/psum | solution.py:71
  550.0 8.5 %psum.219 = f32[]{:T(128)} all-reduce(f32[]{:T(128)} %psum.218), channel_id=1, replica_groups=mesh['img_0'=4,'img_1'=4,'tile_0'=4,'tile_1'=2] {'tile_1'}, use_global_device_ids=true, to_apply=%region_56.57 | all-reduce | flops 1 | bytes 8 | tf_op jit(solution)/shard_map/psum | solution.py:71
  573.6 7.7 %multiply_reduce_fusion.2 = (f32[16,32,256]{2,0,1:T(8,128)}, f32[1,3,16,32,256]{4,2,3,1,0:T(8,128)}, f32[16,32,256]{2,0,1:T(8,128)}, f32[1,3,16,32,256]{4,2,3,1,0:T(8,128)}) fusion(f32[1,3,16,34,256]{4,2,3,1,0:T(8,128)S(1)} %get-tuple-element.55, f32[16,32,256]{2,0,1:T(8,128)} %get-tuple-element.108, f32[3]{0:T(128)S(1)} %compare_convert_fusion, ...), kind=kLoop, calls=%fused_computation.284 | loop fusion | flops 13107200 | bytes 23265796 | tf_op jit(solution)/shard_map/reduce_sum | solution.py:101
  599.4 7.7 %psum.220 = f32[]{:T(128)} all-reduce(f32[]{:T(128)} %get-tuple-element.13), channel_id=1, replica_groups=mesh['img_0'=4,'img_1'=4,'tile_0'=4,'tile_1'=2] {'img_0'}, use_global_device_ids=true, to_apply=%region_62.63 | all-reduce | flops 1 | bytes 8 | tf_op jit(solution)/shard_map/psum | solution.py:71
  607.1 7.5 %psum.221 = f32[]{:T(128)} all-reduce(f32[]{:T(128)} %psum.220), channel_id=1, replica_groups=mesh['img_0'=4,'img_1'=4,'tile_0'=4,'tile_1'=2] {'img_1'}, use_global_device_ids=true, to_apply=%region_63.64 | all-reduce | flops 1 | bytes 8 | tf_op jit(solution)/shard_map/psum | solution.py:71
  614.6 7.1 %psum.222 = f32[]{:T(128)} all-reduce(f32[]{:T(128)} %psum.221), channel_id=1, replica_groups=mesh['img_0'=4,'img_1'=4,'tile_0'=4,'tile_1'=2] {'tile_0'}, use_global_device_ids=true, to_apply=%region_64.65 | all-reduce | flops 1 | bytes 8 | tf_op jit(solution)/shard_map/psum | solution.py:71
  621.8 8.5 %psum.223 = f32[]{:T(128)} all-reduce(f32[]{:T(128)} %psum.222), channel_id=1, replica_groups=mesh['img_0'=4,'img_1'=4,'tile_0'=4,'tile_1'=2] {'tile_1'}, use_global_device_ids=true, to_apply=%region_65.66 | all-reduce | flops 1 | bytes 8 | tf_op jit(solution)/shard_map/psum | solution.py:71
  (284 shorter events, 310.5 us)
Async XLA Ops:
  2.3 37.2 %collective-permute-start = (f32[1,3,16,32,256]{4,2,3,1,0:T(8,128)S(1)}, f32[1,3,16,32,256]{4,2,3,1,0:T(8,128)S(1)}, u32[]{:S(2)}, u32[]{:S(2)}) collective-permute-start(f32[1,3,16,32,256]{4,2,3,1,0:T(8,128)S(1)} %copy.34), channel_id=1, source_target_pairs={{0,8},{8,16},{16,24},{24,32},{32,40},{40,48},{48,56},{56,64},{64,7... | collective-permute-start | bytes 4718600 | tf_op jit(solution)/shard_map/ppermute | solution.py:29
  6.6 36.8 %collective-permute-start.1 = (f32[1,3,16,32,256]{4,2,3,1,0:T(8,128)S(1)}, f32[1,3,16,32,256]{4,2,3,1,0:T(8,128)S(1)}, u32[]{:S(2)}, u32[]{:S(2)}) collective-permute-start(f32[1,3,16,32,256]{4,2,3,1,0:T(8,128)S(1)} %copy.34), channel_id=1, source_target_pairs={{8,0},{16,8},{24,16},{32,24},{40,32},{48,40},{56,48},{64,56},{72,6... | collective-permute-start | bytes 4718600 | tf_op jit(solution)/shard_map/ppermute | solution.py:31
  46.7 7.2 %collective-permute-start.2 = (f32[3,3,16,1,256]{4,2,3,1,0:T(8,128)S(1)}, f32[3,3,16,1,256]{4,2,3,1,0:T(8,128)S(1)}, u32[]{:S(2)}, u32[]{:S(2)}) collective-permute-start(f32[3,3,16,1,256]{4,2,3,1,0:T(8,128)S(1)} %get-tuple-element.73), channel_id=1, source_target_pairs={{0,1},{1,2},{2,3},{3,4},{4,5},{5,6},{6,7},{8,9},{9,10},{10,11},{11... | collective-permute-start | bytes 442376 | tf_op jit(solution)/shard_map/ppermute | solution.py:29
  51.6 6.5 %collective-permute-start.3 = (f32[3,3,16,1,256]{4,2,3,1,0:T(8,128)S(1)}, f32[3,3,16,1,256]{4,2,3,1,0:T(8,128)S(1)}, u32[]{:S(2)}, u32[]{:S(2)}) collective-permute-start(f32[3,3,16,1,256]{4,2,3,1,0:T(8,128)S(1)} %get-tuple-element.74), channel_id=1, source_target_pairs={{1,0},{2,1},{3,2},{4,3},{5,4},{6,5},{7,6},{9,8},{10,9},{11,10},{12... | collective-permute-start | bytes 442376 | tf_op jit(solution)/shard_map/ppermute | solution.py:31
  82.7 15.4 %all-to-all-start = ((f32[16,1,1]{2,1,0:T(1,128)}), f32[16,1,1]{2,1,0:T(1,128)S(1)}, u32[]{:S(2)}, u32[]{:S(2)}) async-start(f32[16,1,1]{2,1,0:T(1,128)} %broadcast_in_dim.22), calls=%async_computation | async-start | bytes 16384 | tf_op jit(solution)/shard_map/all_to_all | solution.py:40
  98.8 9.6 %all-to-all-start.1 = ((f32[16,1,1]{2,1,0:T(1,128)}), f32[16,1,1]{2,1,0:T(1,128)S(1)}, u32[]{:S(2)}, u32[]{:S(2)}) async-start(f32[16,1,1]{2,1,0:T(1,128)} %broadcast_in_dim.24), calls=%async_computation.1 | async-start | bytes 16384 | tf_op jit(solution)/shard_map/all_to_all | solution.py:40
  122.3 12.1 %collective-permute-start.4 = (f32[1,3,16,1,256]{4,2,3,1,0:T(8,128)S(1)}, f32[1,3,16,1,256]{4,2,3,1,0:T(8,128)S(1)}, u32[]{:S(2)}, u32[]{:S(2)}) collective-permute-start(f32[1,3,16,1,256]{4,2,3,1,0:T(8,128)S(1)} %get-tuple-element.103), channel_id=1, source_target_pairs={{0,1},{1,2},{2,3},{3,4},{4,5},{5,6},{6,7},{8,9},{9,10},{10,11},{11... | collective-permute-start | bytes 147464 | tf_op jit(solution)/shard_map/ppermute | solution.py:29
  128.7 5.7 collective-permute-start.5
  182.5 4.3 collective-permute-start.6
  184.5 5.4 collective-permute-start.7
  205.8 4.4 collective-permute-start.8
  207.7 5.4 collective-permute-start.9
  253.7 4.3 collective-permute-start.10
  255.7 5.4 collective-permute-start.11
  277.0 4.4 collective-permute-start.12
  278.9 5.4 collective-permute-start.13
  324.8 37.5 %collective-permute-start.15 = (f32[1,3,16,32,256]{4,2,3,1,0:T(8,128)S(1)}, f32[1,3,16,32,256]{4,2,3,1,0:T(8,128)S(1)}, u32[]{:S(2)}, u32[]{:S(2)}) collective-permute-start(f32[1,3,16,32,256]{4,2,3,1,0:T(8,128)S(1)} %divide_subtract_fusion.4), channel_id=1, source_target_pairs={{8,0},{16,8},{24,16},{32,24},{40,32},{48,40},{56,48},{64,56},{72,6... | collective-permute-start | bytes 4718600 | tf_op jit(solution)/shard_map/ppermute | solution.py:31
  326.1 37.1 %collective-permute-start.14 = (f32[1,3,16,32,256]{4,2,3,1,0:T(8,128)S(1)}, f32[1,3,16,32,256]{4,2,3,1,0:T(8,128)S(1)}, u32[]{:S(2)}, u32[]{:S(2)}) collective-permute-start(f32[1,3,16,32,256]{4,2,3,1,0:T(8,128)S(1)} %divide_subtract_fusion.4), channel_id=1, source_target_pairs={{0,8},{8,16},{16,24},{24,32},{32,40},{40,48},{48,56},{56,64},{64,7... | collective-permute-start | bytes 4718600 | tf_op jit(solution)/shard_map/ppermute | solution.py:29
  363.2 5.2 collective-permute-start.16
  366.3 6.5 %collective-permute-start.17 = (f32[3,3,16,1,256]{4,2,3,1,0:T(8,128)S(1)}, f32[3,3,16,1,256]{4,2,3,1,0:T(8,128)S(1)}, u32[]{:S(2)}, u32[]{:S(2)}) collective-permute-start(f32[3,3,16,1,256]{4,2,3,1,0:T(8,128)S(1)} %get-tuple-element.72), channel_id=1, source_target_pairs={{1,0},{2,1},{3,2},{4,3},{5,4},{6,5},{7,6},{9,8},{10,9},{11,10},{12... | collective-permute-start | bytes 442376 | tf_op jit(solution)/shard_map/ppermute | solution.py:31
  394.6 13.3 %all-to-all-start.2 = ((f32[16,1,1]{2,1,0:T(1,128)}), f32[16,1,1]{2,1,0:T(1,128)S(1)}, u32[]{:S(2)}, u32[]{:S(2)}) async-start(f32[16,1,1]{2,1,0:T(1,128)} %broadcast_in_dim.27), calls=%async_computation.2 | async-start | bytes 16384 | tf_op jit(solution)/shard_map/all_to_all | solution.py:40
  408.5 9.8 %all-to-all-start.3 = ((f32[16,1,1]{2,1,0:T(1,128)}), f32[16,1,1]{2,1,0:T(1,128)S(1)}, u32[]{:S(2)}, u32[]{:S(2)}) async-start(f32[16,1,1]{2,1,0:T(1,128)} %broadcast_in_dim.29), calls=%async_computation.3 | async-start | bytes 16384 | tf_op jit(solution)/shard_map/all_to_all | solution.py:40
  432.0 12.3 %collective-permute-start.18 = (f32[1,3,16,1,256]{4,2,3,1,0:T(8,128)S(1)}, f32[1,3,16,1,256]{4,2,3,1,0:T(8,128)S(1)}, u32[]{:S(2)}, u32[]{:S(2)}) collective-permute-start(f32[1,3,16,1,256]{4,2,3,1,0:T(8,128)S(1)} %get-tuple-element.91), channel_id=1, source_target_pairs={{0,1},{1,2},{2,3},{3,4},{4,5},{5,6},{6,7},{8,9},{9,10},{10,11},{11... | collective-permute-start | bytes 147464 | tf_op jit(solution)/shard_map/ppermute | solution.py:29
  438.5 5.9 collective-permute-start.19
  490.6 4.3 collective-permute-start.20
  492.6 5.4 collective-permute-start.21
  513.9 4.6 collective-permute-start.22
  515.8 5.4 collective-permute-start.23
  561.5 4.3 collective-permute-start.24
  563.4 5.4 collective-permute-start.25
  584.6 4.4 collective-permute-start.26
  586.6 5.4 collective-permute-start.27
  (50 other events, 384.3 us)
where the time goes:
time: 644 us; the launch traced here: 635 us
  blocking collectives  208 us (32%)
  other arithmetic  169 us (26%)
  waiting for transfers between devices  121 us (19%)
  starting transfers between devices  98.1 us (15%)
  local copies, waits for them, and re-layouts  22.4 us (3%)
  between operations  16.4 us (3%)
    psum x24, blocking collectives, over_axes(): shard = lax.psum(shard, axis)  186 us
    ppermute x14, waiting for transfers between devices, padded_2(): lax.ppermute(head, axis, [((i + 1) % count, i) for i in range(ends)])  65.9 us
    reduce_sum x6, other arithmetic, hessian_point(): projected = jnp.sum(middle * vector, axis=-4, keepdims=True)  47.5 us
    ppermute x14, starting transfers between devices, padded_2(): lax.ppermute(tail, axis, [(i, (i + 1) % count) for i in range(ends)])  44.6 us
    reduce_sum x6, other arithmetic, body(): grad_total = over_axes(jnp.sum(gradients * gradients), IMG_TILE)  33.5 us
    ppermute x14, waiting for transfers between devices, padded_2(): lax.ppermute(tail, axis, [(i, (i + 1) % count) for i in range(ends)])  32.7 us
    ppermute x14, starting transfers between devices, padded_2(): lax.ppermute(head, axis, [((i + 1) % count, i) for i in range(ends)])  30.5 us
    all_to_all x4, starting transfers between devices, from_everyone(): lax.all_to_all(jnp.broadcast_to(shard[None], (peers, *shard.shape)), axis...  23 us
  transfers between devices with their start and end apart: 32, of which 19 were waited for; matrix products, arithmetic and copies ran while one was open for 1% of the time, Pallas kernels for 0%

commit v1 on v0

--- a/solution.py
+++ b/solution.py
@@ -35,41 +35,11 @@
     return cells
 
 
-def from_everyone(shard, axis):
-    peers = lax.axis_size(axis)
+def from_everyone(values):
+    peers = lax.axis_size(IMG_TILE)
     return lax.all_to_all(
-        jnp.broadcast_to(shard[None], (peers, *shard.shape)), axis, 0, 0, tiled=True
+        jnp.broadcast_to(values[None], (peers, *values.shape)), IMG_TILE, 0, 0, tiled=True
     )
-
-
-def folded_in_pairs(pieces, combine):
-    while len(jax.tree.leaves(pieces)[0]) > 1:
-        pieces = jax.vmap(combine)(*(pieces[side::2] for side in (0, 1)))
-    return pieces[0]
-
-
-def carried_in(shard, axis, combine, identity):
-    peers, here = (lax.axis_size(axis), lax.axis_index(axis))
-    passed = jnp.arange(peers) < here
-
-    def kept(part, zero, own):
-        part = jnp.where(
-            passed.reshape(-1, *(1 for _ in own.shape)), part, jnp.asarray(zero, own.dtype)
-        )
-        return part
-
-    pieces = from_everyone(shard, axis)
-    return folded_in_pairs(kept(pieces, identity, shard), combine)
-
-
-def over_copies(shard, axis):
-    return from_everyone(shard, axis).sum(axis=0)
-
-
-def over_axes(shard, axes):
-    for axis in axes:
-        shard = lax.psum(shard, axis)
-    return shard
 
 
 def laplace(field):
@@ -104,10 +74,6 @@
     )
 
 
-def add_pair(earlier, later):
-    return earlier + later
-
-
 def body(spins, aniso):
     local_images = spins.shape[0]
     width_x = spins.shape[3]
@@ -119,7 +85,6 @@
     )
     first_image = lax.axis_index(IMG) * local_images
     image_index = first_image + jnp.arange(local_images, dtype=jnp.int32)
-    segment_live = (image_index < images - 1).astype(jnp.float32)
     interior = ((image_index > 0) & (image_index < images - 1)).astype(jnp.float32)
     target = image_index.astype(jnp.float32) / (images - 1)
     rim_depth = 1
@@ -136,15 +101,16 @@
         drive_own = force_field(middle_seg, aniso)
         diff_sq = jnp.sum(difference * difference, axis=(1, 2, 3, 4))
         drive_sq = jnp.sum(drive_own * drive_own, axis=(1, 2, 3, 4))
-        diff_sq, drive_sq = lax.psum((diff_sq, drive_sq), TILE)
-        seg_len = segment_live * jnp.sqrt(diff_sq + epsilon)
-        drive_len = segment_live * jnp.sqrt(drive_sq + epsilon)
-        offset = carried_in(jnp.sum(seg_len), IMG, add_pair, jnp.float32(0.0))
-        path_len, drive_total = (
-            over_copies(jnp.sum(seg_len), IMG),
-            over_copies(jnp.sum(drive_len), IMG),
+        shares = from_everyone(jnp.concatenate([diff_sq, drive_sq]))
+        shares = shares.reshape(img_count, tile_count, 2, local_images).sum(axis=1)
+        shares = jnp.moveaxis(shares, 1, 0).reshape(2, images)
+        every_image = jnp.arange(images)
+        lengths = jnp.sqrt(shares + epsilon) * (every_image < images - 1)
+        seg_len = lengths[0]
+        path_len, drive_total = jnp.sum(seg_len), jnp.sum(lengths[1])
+        before_arc = jnp.sum(
+            jnp.where(every_image[None, :] < image_index[:, None], seg_len[None, :], 0.0), axis=1
         )
-        before_arc = offset + jnp.cumsum(seg_len) - seg_len
         time_step = path_len / drive_total
         spring_pull = (
             spring_coef * (before_arc / path_len - target) * (images - 1) / (2.0 * path_len)
@@ -183,7 +149,7 @@
                 res_a - res_b - 0.5 * time_step * adjoint + spring_pull * (after_own - before_own)
             )
             gradients = gradients * interior_mask
-            grad_total = over_axes(jnp.sum(gradients * gradients), IMG_TILE)
+            grad_total = jnp.sum(from_everyone(jnp.sum(gradients * gradients)[None]))
             grad_scale = jnp.sqrt(grad_total / cell_count + epsilon)
             current = current - step_scale * gradients / grad_scale
     return current

time: 644 us -> 513 us (0.80)
  blocking collectives: 208 us -> 85.2 us
  starting transfers between devices: 98.1 us -> 89.8 us
    psum x26 -> x0, blocking collectives: 208 us -> none  [the longest x24 186 us: over_axes(): shard = lax.psum(shard, axis)]
    all_to_all x0 -> x6, blocking collectives: none -> 85.2 us  [from_everyone(): lax.all_to_all(jnp.broadcast_to(values[None], (peers, *values.shape)), IM...]
    all_to_all x4 -> x2, waiting for transfers between devices: 22.6 us -> 17.4 us  [from_everyone(): lax.all_to_all(jnp.broadcast_to(values[None], (peers, *values.shape)), IM...]
    all_to_all x4 -> x2, starting transfers between devices: 23 us -> 19.3 us  [from_everyone(): lax.all_to_all(jnp.broadcast_to(values[None], (peers, *values.shape)), IM...]
    reduce_sum x10 -> x16, other arithmetic: 36.2 us -> 39.4 us  [the longest x12 37.9 us: body(): grad_total = jnp.sum(from_everyone(jnp.sum(gradients * gradients)[None]))]
    unnamed x104 -> x110, local copies, waits for them, and re-layouts: 15.3 us -> 16.1 us
  transfers between devices with their start and end apart: 32 -> 30, of which waited for: 19 -> 18; matrix products, arithmetic and copies ran while one was open for 1% -> 1% of each run, Pallas kernels for 0% -> 0%
where the time goes in v1:
time: 513 us; the launch traced here: 504 us
  other arithmetic  175 us (34%)
  waiting for transfers between devices  119 us (23%)
  starting transfers between devices  89.8 us (18%)
  blocking collectives  85.2 us (17%)
  local copies, waits for them, and re-layouts  23.4 us (5%)
  between operations  12.4 us (2%)
    all_to_all x6, blocking collectives, from_everyone(): lax.all_to_all(jnp.broadcast_to(values[None], (peers, *values.shape)), IM...  85.2 us
    ppermute x14, waiting for transfers between devices, padded_2(): lax.ppermute(head, axis, [((i + 1) % count, i) for i in range(ends)])  68.8 us
    reduce_sum x6, other arithmetic, hessian_point(): projected = jnp.sum(middle * vector, axis=-4, keepdims=True)  47.5 us
    ppermute x14, starting transfers between devices, padded_2(): lax.ppermute(tail, axis, [(i, (i + 1) % count) for i in range(ends)])  42 us
    reduce_sum x12, other arithmetic, body(): grad_total = jnp.sum(from_everyone(jnp.sum(gradients * gradients)[None]))  37.9 us
    ppermute x14, waiting for transfers between devices, padded_2(): lax.ppermute(tail, axis, [(i, (i + 1) % count) for i in range(ends)])  32.5 us
    ppermute x14, starting transfers between devices, padded_2(): lax.ppermute(head, axis, [((i + 1) % count, i) for i in range(ends)])  28.4 us
    concatenate x8, other arithmetic, padded_2(): jnp.concatenate([lax.ppermute(tail, axis, [(i, (i + 1) % count) for i in...  22.7 us
  transfers between devices with their start and end apart: 30, of which 18 were waited for; matrix products, arithmetic and copies ran while one was open for 1% of the time, Pallas kernels for 0%

profile of v1, /device:TPU:1, one launch (start us, length us, event | category | flops | bytes accessed | tf_op | source)
XLA Modules:
  0.0 504.2 jit_solution(11426127931433338985)
XLA Ops:
  2.3 4.3 collective-permute-start
  7.9 31.6 %collective-permute-done = f32[1,3,16,32,256]{4,2,3,1,0:T(8,128)S(1)} collective-permute-done((f32[1,3,16,32,256]{4,2,3,1,0:T(8,128)S(1)}, f32[1,3,16,32,256]{4,2,3,1,0:T(8,128)S(1)}, u32[]{:S(2)}, u32[]{:S(2)}) %collective-permute-start) | collective-permute-done | bytes 1572896 | tf_op jit(solution)/shard_map/ppermute | solution.py:29
  46.7 4.9 collective-permute-start.2
  53.9 4.2 collective-permute-done.3
  70.9 11.2 %all-to-all-start = ((f32[128,1,2]{2,1,0:T(1,128)}), f32[128,1,2]{2,1,0:T(1,128)S(1)}, u32[]{:S(2)}, u32[]{:S(2)}) async-start(f32[128,1,2]{2,1,0:T(1,128)} %broadcast_in_dim.21), calls=%async_computation | async-start | bytes 131072 | tf_op jit(solution)/shard_map/all_to_all | solution.py:40
  83.0 8.7 %all-to-all-done = f32[128,1,2]{2,1,0:T(1,128)S(1)} async-done(((f32[128,1,2]{2,1,0:T(1,128)}), f32[128,1,2]{2,1,0:T(1,128)S(1)}, u32[]{:S(2)}, u32[]{:S(2)}) %all-to-all-start) | async-done | bytes 1056 | tf_op jit(solution)/shard_map/all_to_all | solution.py:40
  93.8 8.4 %multiply_reduce_fusion.28 = (f32[16,32,256]{2,0,1:T(8,128)S(1)}, f32[1,3,16,32,256]{4,2,3,1,0:T(8,128)S(1)}, f32[16,32,256]{2,0,1:T(8,128)S(1)}, f32[1,3,16,32,256]{4,2,3,1,0:T(8,128)S(1)}) fusion(f32[1,3,16,34,256]{4,2,3,1,0:T(8,128)} %copy-done.2, f32[16,32,256]{2,0,1:T(8,128)S(1)} %get-tuple-element.126, f32[3]{0:T(128)S(1)} %compare_convert_fusion.1, ...), kind=kLoop, calls=%fused_computation.318 | loop fusion | flops 8388608 | bytes 19496976 | tf_op jit(solution)/shard_map/reduce_sum | solution.py:71
  113.4 4.1 select_maximum_fusion.10
  117.5 7.3 %multiply_reduce_fusion.26 = (f32[]{:T(128)}, f32[1,3,16,32,256]{4,2,3,1,0:T(8,128)}, f32[1,3,16,32,256]{4,2,3,1,0:T(8,128)}) fusion(f32[]{:T(128)S(6)} %convert_element_type.120, f32[16,32,256]{2,0,1:T(8,128)} %broadcast_multiply_fusion.10, f32[1,3,16,34,256]{4,2,3,1,0:T(8,128)S(1)} %get-tuple-element.66, f32[1,3,16,32,256]{4,2,3,1,0:T(8,128)} %copy-done.41, ...), kind=kLoop, calls=%fused_computation.315 | loop fusion | flops 13369343 | bytes 23167004 | tf_op jit(solution)/shard_map/reduce_sum | solution.py:152
  125.4 14.5 %all_to_all.48 = f32[128,1,1]{2,1,0:T(1,128)S(1)} all-to-all(f32[128,1,1]{2,1,0:T(1,128)S(1)} %broadcast_in_dim.23), channel_id=1, replica_groups=mesh['img_0'=4,'img_1'=4,'tile_0'=4,'tile_1'=2] {'img_0','img_1','tile_0..., dimensions={0} | all-to-all | bytes 1024 | tf_op jit(solution)/shard_map/all_to_all | solution.py:40
  157.2 7.8 %multiply_reduce_fusion.23 = (f32[16,32,256]{2,0,1:T(8,128)}, f32[1,3,16,32,256]{4,2,3,1,0:T(8,128)}, f32[16,32,256]{2,0,1:T(8,128)}, f32[1,3,16,32,256]{4,2,3,1,0:T(8,128)}) fusion(f32[1,3,16,34,256]{4,2,3,1,0:T(8,128)S(1)} %get-tuple-element.59, f32[16,32,256]{2,0,1:T(8,128)} %get-tuple-element.122, f32[3]{0:T(128)S(1)} %compare_convert_fusion.1, ...), kind=kLoop, calls=%fused_computation.311 | loop fusion | flops 13107200 | bytes 23265796 | tf_op jit(solution)/shard_map/reduce_sum | solution.py:71
  178.4 4.7 multiply_reduce_fusion.21
  183.8 14.2 %all_to_all.49 = f32[128,1,1]{2,1,0:T(1,128)S(1)} all-to-all(f32[128,1,1]{2,1,0:T(1,128)S(1)} %broadcast_in_dim.24), channel_id=1, replica_groups=mesh['img_0'=4,'img_1'=4,'tile_0'=4,'tile_1'=2] {'img_0','img_1','tile_0..., dimensions={0} | all-to-all | bytes 1024 | tf_op jit(solution)/shard_map/all_to_all | solution.py:40
  214.6 7.7 %multiply_reduce_fusion.18 = (f32[16,32,256]{2,0,1:T(8,128)}, f32[1,3,16,32,256]{4,2,3,1,0:T(8,128)}, f32[16,32,256]{2,0,1:T(8,128)}, f32[1,3,16,32,256]{4,2,3,1,0:T(8,128)}) fusion(f32[1,3,16,34,256]{4,2,3,1,0:T(8,128)S(1)} %get-tuple-element.57, f32[16,32,256]{2,0,1:T(8,128)} %get-tuple-element.118, f32[3]{0:T(128)S(1)} %compare_convert_fusion.1, ...), kind=kLoop, calls=%fused_computation.305 | loop fusion | flops 13107200 | bytes 23265796 | tf_op jit(solution)/shard_map/reduce_sum | solution.py:71
  235.8 4.7 multiply_reduce_fusion.16
  241.2 14.2 %all_to_all.50 = f32[128,1,1]{2,1,0:T(1,128)S(1)} all-to-all(f32[128,1,1]{2,1,0:T(1,128)S(1)} %broadcast_in_dim.25), channel_id=1, replica_groups=mesh['img_0'=4,'img_1'=4,'tile_0'=4,'tile_1'=2] {'img_0','img_1','tile_0..., dimensions={0} | all-to-all | bytes 1024 | tf_op jit(solution)/shard_map/all_to_all | solution.py:40
  259.9 4.1 collective-permute-start.14
  264.0 31.7 %collective-permute-done.15 = f32[1,3,16,32,256]{4,2,3,1,0:T(8,128)S(1)} collective-permute-done((f32[1,3,16,32,256]{4,2,3,1,0:T(8,128)S(1)}, f32[1,3,16,32,256]{4,2,3,1,0:T(8,128)S(1)}, u32[]{:S(2)}, u32[]{:S(2)}) %collective-permute-start.15) | collective-permute-done | bytes 1572896 | tf_op jit(solution)/shard_map/ppermute | solution.py:31
  296.5 4.1 collective-permute-start.16
  302.7 4.4 collective-permute-done.17
  318.3 8.1 %all-to-all-start.4 = ((f32[128,1,2]{2,1,0:T(1,128)}), f32[128,1,2]{2,1,0:T(1,128)S(1)}, u32[]{:S(2)}, u32[]{:S(2)}) async-start(f32[128,1,2]{2,1,0:T(1,128)} %broadcast_in_dim.26), calls=%async_computation.4 | async-start | bytes 131072 | tf_op jit(solution)/shard_map/all_to_all | solution.py:40
  327.4 8.7 %all-to-all-done.4 = f32[128,1,2]{2,1,0:T(1,128)S(1)} async-done(((f32[128,1,2]{2,1,0:T(1,128)}), f32[128,1,2]{2,1,0:T(1,128)S(1)}, u32[]{:S(2)}, u32[]{:S(2)}) %all-to-all-start.4) | async-done | bytes 1056 | tf_op jit(solution)/shard_map/all_to_all | solution.py:40
  338.2 8.1 %multiply_reduce_fusion.12 = (f32[16,32,256]{2,0,1:T(8,128)S(1)}, f32[1,3,16,32,256]{4,2,3,1,0:T(8,128)S(1)}, f32[16,32,256]{2,0,1:T(8,128)S(1)}, f32[1,3,16,32,256]{4,2,3,1,0:T(8,128)S(1)}) fusion(f32[1,3,16,34,256]{4,2,3,1,0:T(8,128)} %copy-done, f32[16,32,256]{2,0,1:T(8,128)S(1)} %get-tuple-element.114, f32[3]{0:T(128)S(1)} %compare_convert_fusion.1, ...), kind=kLoop, calls=%fused_computation.297 | loop fusion | flops 8388608 | bytes 19496976 | tf_op jit(solution)/shard_map/reduce_sum | solution.py:71
  357.4 4.3 select_maximum_fusion.4
  361.8 7.2 %multiply_reduce_fusion.10 = (f32[]{:T(128)}, f32[1,3,16,32,256]{4,2,3,1,0:T(8,128)}, f32[1,3,16,32,256]{4,2,3,1,0:T(8,128)}) fusion(f32[]{:T(128)S(6)} %convert_element_type.120, f32[16,32,256]{2,0,1:T(8,128)} %broadcast_multiply_fusion.4, f32[1,3,16,34,256]{4,2,3,1,0:T(8,128)S(1)} %get-tuple-element.62, f32[1,3,16,32,256]{4,2,3,1,0:T(8,128)} %copy-done.39, ...), kind=kLoop, calls=%fused_computation.294 | loop fusion | flops 13369343 | bytes 23167004 | tf_op jit(solution)/shard_map/reduce_sum | solution.py:152
  369.6 14.2 %all_to_all.51 = f32[128,1,1]{2,1,0:T(1,128)S(1)} all-to-all(f32[128,1,1]{2,1,0:T(1,128)S(1)} %broadcast_in_dim.27), channel_id=1, replica_groups=mesh['img_0'=4,'img_1'=4,'tile_0'=4,'tile_1'=2] {'img_0','img_1','tile_0..., dimensions={0} | all-to-all | bytes 1024 | tf_op jit(solution)/shard_map/all_to_all | solution.py:40
  400.4 7.7 %multiply_reduce_fusion.7 = (f32[16,32,256]{2,0,1:T(8,128)}, f32[1,3,16,32,256]{4,2,3,1,0:T(8,128)}, f32[16,32,256]{2,0,1:T(8,128)}, f32[1,3,16,32,256]{4,2,3,1,0:T(8,128)}) fusion(f32[1,3,16,34,256]{4,2,3,1,0:T(8,128)S(1)} %get-tuple-element.55, f32[16,32,256]{2,0,1:T(8,128)} %get-tuple-element.110, f32[3]{0:T(128)S(1)} %compare_convert_fusion.1, ...), kind=kLoop, calls=%fused_computation.290 | loop fusion | flops 13107200 | bytes 23265796 | tf_op jit(solution)/shard_map/reduce_sum | solution.py:71
  421.6 4.7 multiply_reduce_fusion.5
  426.9 14.2 %all_to_all.52 = f32[128,1,1]{2,1,0:T(1,128)S(1)} all-to-all(f32[128,1,1]{2,1,0:T(1,128)S(1)} %broadcast_in_dim.28), channel_id=1, replica_groups=mesh['img_0'=4,'img_1'=4,'tile_0'=4,'tile_1'=2] {'img_0','img_1','tile_0..., dimensions={0} | all-to-all | bytes 1024 | tf_op jit(solution)/shard_map/all_to_all | solution.py:40
  457.8 7.7 %multiply_reduce_fusion.2 = (f32[16,32,256]{2,0,1:T(8,128)}, f32[1,3,16,32,256]{4,2,3,1,0:T(8,128)}, f32[16,32,256]{2,0,1:T(8,128)}, f32[1,3,16,32,256]{4,2,3,1,0:T(8,128)}) fusion(f32[1,3,16,34,256]{4,2,3,1,0:T(8,128)S(1)} %get-tuple-element.53, f32[16,32,256]{2,0,1:T(8,128)} %get-tuple-element.106, f32[3]{0:T(128)S(1)} %compare_convert_fusion.1, ...), kind=kLoop, calls=%fused_computation.284 | loop fusion | flops 13107200 | bytes 23265796 | tf_op jit(solution)/shard_map/reduce_sum | solution.py:71
  478.9 4.7 multiply_reduce_fusion
  484.3 14.2 %all_to_all.53 = f32[128,1,1]{2,1,0:T(1,128)S(1)} all-to-all(f32[128,1,1]{2,1,0:T(1,128)S(1)} %broadcast_in_dim.29), channel_id=1, replica_groups=mesh['img_0'=4,'img_1'=4,'tile_0'=4,'tile_1'=2] {'img_0','img_1','tile_0..., dimensions={0} | all-to-all | bytes 1024 | tf_op jit(solution)/shard_map/all_to_all | solution.py:40
  (261 shorter events, 191.5 us)
Async XLA Ops:
  2.3 37.4 %copy-start.23 = (f32[1,3,16,32,256]{4,3,2,1,0:T(8,128)S(1)}, f32[1,3,16,32,256]{4,3,2,1,0:T(8,128)}, u32[]{:S(2)}) copy-start(f32[1,3,16,32,256]{4,3,2,1,0:T(8,128)} %param.2) | copy-start | bytes 4718596
  2.3 37.2 %collective-permute-start = (f32[1,3,16,32,256]{4,2,3,1,0:T(8,128)S(1)}, f32[1,3,16,32,256]{4,2,3,1,0:T(8,128)S(1)}, u32[]{:S(2)}, u32[]{:S(2)}) collective-permute-start(f32[1,3,16,32,256]{4,2,3,1,0:T(8,128)S(1)} %copy.38), channel_id=1, source_target_pairs={{0,8},{8,16},{16,24},{24,32},{32,40},{40,48},{48,56},{56,64},{64,7... | collective-permute-start | bytes 4718600 | tf_op jit(solution)/shard_map/ppermute | solution.py:29
  6.6 36.8 %collective-permute-start.1 = (f32[1,3,16,32,256]{4,2,3,1,0:T(8,128)S(1)}, f32[1,3,16,32,256]{4,2,3,1,0:T(8,128)S(1)}, u32[]{:S(2)}, u32[]{:S(2)}) collective-permute-start(f32[1,3,16,32,256]{4,2,3,1,0:T(8,128)S(1)} %copy.38), channel_id=1, source_target_pairs={{8,0},{16,8},{24,16},{32,24},{40,32},{48,40},{56,48},{64,56},{72,6... | collective-permute-start | bytes 4718600 | tf_op jit(solution)/shard_map/ppermute | solution.py:31
  46.7 7.2 %collective-permute-start.2 = (f32[3,3,16,1,256]{4,2,3,1,0:T(8,128)S(1)}, f32[3,3,16,1,256]{4,2,3,1,0:T(8,128)S(1)}, u32[]{:S(2)}, u32[]{:S(2)}) collective-permute-start(f32[3,3,16,1,256]{4,2,3,1,0:T(8,128)S(1)} %get-tuple-element.71), channel_id=1, source_target_pairs={{0,1},{1,2},{2,3},{3,4},{4,5},{5,6},{6,7},{8,9},{9,10},{10,11},{11... | collective-permute-start | bytes 442376 | tf_op jit(solution)/shard_map/ppermute | solution.py:29
  51.6 6.5 %collective-permute-start.3 = (f32[3,3,16,1,256]{4,2,3,1,0:T(8,128)S(1)}, f32[3,3,16,1,256]{4,2,3,1,0:T(8,128)S(1)}, u32[]{:S(2)}, u32[]{:S(2)}) collective-permute-start(f32[3,3,16,1,256]{4,2,3,1,0:T(8,128)S(1)} %get-tuple-element.72), channel_id=1, source_target_pairs={{1,0},{2,1},{3,2},{4,3},{5,4},{6,5},{7,6},{9,8},{10,9},{11,10},{12... | collective-permute-start | bytes 442376 | tf_op jit(solution)/shard_map/ppermute | solution.py:31
  70.9 20.8 %all-to-all-start = ((f32[128,1,2]{2,1,0:T(1,128)}), f32[128,1,2]{2,1,0:T(1,128)S(1)}, u32[]{:S(2)}, u32[]{:S(2)}) async-start(f32[128,1,2]{2,1,0:T(1,128)} %broadcast_in_dim.21), calls=%async_computation | async-start | bytes 131072 | tf_op jit(solution)/shard_map/all_to_all | solution.py:40
  105.1 8.0 %collective-permute-start.4 = (f32[1,3,16,1,256]{4,2,3,1,0:T(8,128)S(1)}, f32[1,3,16,1,256]{4,2,3,1,0:T(8,128)S(1)}, u32[]{:S(2)}, u32[]{:S(2)}) collective-permute-start(f32[1,3,16,1,256]{4,2,3,1,0:T(8,128)S(1)} %get-tuple-element.101), channel_id=1, source_target_pairs={{0,1},{1,2},{2,3},{3,4},{4,5},{5,6},{6,7},{8,9},{9,10},{10,11},{11... | collective-permute-start | bytes 147464 | tf_op jit(solution)/shard_map/ppermute | solution.py:29
  107.9 5.4 %collective-permute-start.5 = (f32[1,3,16,1,256]{4,2,3,1,0:T(8,128)S(1)}, f32[1,3,16,1,256]{4,2,3,1,0:T(8,128)S(1)}, u32[]{:S(2)}, u32[]{:S(2)}) collective-permute-start(f32[1,3,16,1,256]{4,2,3,1,0:T(8,128)S(1)} %get-tuple-element.102), channel_id=1, source_target_pairs={{1,0},{2,1},{3,2},{4,3},{5,4},{6,5},{7,6},{9,8},{10,9},{11,10},{12... | collective-permute-start | bytes 147464 | tf_op jit(solution)/shard_map/ppermute | solution.py:31
  144.2 4.8 collective-permute-start.6
  147.1 5.4 %collective-permute-start.7 = (f32[1,3,16,1,256]{4,2,3,1,0:T(8,128)S(1)}, f32[1,3,16,1,256]{4,2,3,1,0:T(8,128)S(1)}, u32[]{:S(2)}, u32[]{:S(2)}) collective-permute-start(f32[1,3,16,1,256]{4,2,3,1,0:T(8,128)S(1)} %get-tuple-element.100), channel_id=1, source_target_pairs={{1,0},{2,1},{3,2},{4,3},{5,4},{6,5},{7,6},{9,8},{10,9},{11,10},{12... | collective-permute-start | bytes 147464 | tf_op jit(solution)/shard_map/ppermute | solution.py:31
  168.4 4.4 collective-permute-start.8
  170.3 5.4 %collective-permute-start.9 = (f32[1,3,16,1,256]{4,2,3,1,0:T(8,128)S(1)}, f32[1,3,16,1,256]{4,2,3,1,0:T(8,128)S(1)}, u32[]{:S(2)}, u32[]{:S(2)}) collective-permute-start(f32[1,3,16,1,256]{4,2,3,1,0:T(8,128)S(1)} %get-tuple-element.98), channel_id=1, source_target_pairs={{1,0},{2,1},{3,2},{4,3},{5,4},{6,5},{7,6},{9,8},{10,9},{11,10},{12... | collective-permute-start | bytes 147464 | tf_op jit(solution)/shard_map/ppermute | solution.py:31
  201.6 4.8 collective-permute-start.10
  204.5 5.4 %collective-permute-start.11 = (f32[1,3,16,1,256]{4,2,3,1,0:T(8,128)S(1)}, f32[1,3,16,1,256]{4,2,3,1,0:T(8,128)S(1)}, u32[]{:S(2)}, u32[]{:S(2)}) collective-permute-start(f32[1,3,16,1,256]{4,2,3,1,0:T(8,128)S(1)} %get-tuple-element.96), channel_id=1, source_target_pairs={{1,0},{2,1},{3,2},{4,3},{5,4},{6,5},{7,6},{9,8},{10,9},{11,10},{12... | collective-permute-start | bytes 147464 | tf_op jit(solution)/shard_map/ppermute | solution.py:31
  225.8 4.4 collective-permute-start.12
  227.7 5.4 %collective-permute-start.13 = (f32[1,3,16,1,256]{4,2,3,1,0:T(8,128)S(1)}, f32[1,3,16,1,256]{4,2,3,1,0:T(8,128)S(1)}, u32[]{:S(2)}, u32[]{:S(2)}) collective-permute-start(f32[1,3,16,1,256]{4,2,3,1,0:T(8,128)S(1)} %get-tuple-element.94), channel_id=1, source_target_pairs={{1,0},{2,1},{3,2},{4,3},{5,4},{6,5},{7,6},{9,8},{10,9},{11,10},{12... | collective-permute-start | bytes 147464 | tf_op jit(solution)/shard_map/ppermute | solution.py:31
  258.6 48.5 %copy-start.11 = (f32[1,3,16,32,256]{4,2,3,1,0:T(8,128)}, f32[1,3,16,32,256]{4,2,3,1,0:T(8,128)S(1)}, u32[]{:S(2)}) copy-start(f32[1,3,16,32,256]{4,2,3,1,0:T(8,128)S(1)} %divide_subtract_fusion.4) | copy-start | bytes 4718596
  258.6 37.1 %collective-permute-start.15 = (f32[1,3,16,32,256]{4,2,3,1,0:T(8,128)S(1)}, f32[1,3,16,32,256]{4,2,3,1,0:T(8,128)S(1)}, u32[]{:S(2)}, u32[]{:S(2)}) collective-permute-start(f32[1,3,16,32,256]{4,2,3,1,0:T(8,128)S(1)} %divide_subtract_fusion.4), channel_id=1, source_target_pairs={{8,0},{16,8},{24,16},{32,24},{40,32},{48,40},{56,48},{64,56},{72,6... | collective-permute-start | bytes 4718600 | tf_op jit(solution)/shard_map/ppermute | solution.py:31
  259.9 36.6 %collective-permute-start.14 = (f32[1,3,16,32,256]{4,2,3,1,0:T(8,128)S(1)}, f32[1,3,16,32,256]{4,2,3,1,0:T(8,128)S(1)}, u32[]{:S(2)}, u32[]{:S(2)}) collective-permute-start(f32[1,3,16,32,256]{4,2,3,1,0:T(8,128)S(1)} %divide_subtract_fusion.4), channel_id=1, source_target_pairs={{0,8},{8,16},{16,24},{24,32},{32,40},{40,48},{48,56},{56,64},{64,7... | collective-permute-start | bytes 4718600 | tf_op jit(solution)/shard_map/ppermute | solution.py:29
  296.5 6.2 %collective-permute-start.16 = (f32[3,3,16,1,256]{4,2,3,1,0:T(8,128)S(1)}, f32[3,3,16,1,256]{4,2,3,1,0:T(8,128)S(1)}, u32[]{:S(2)}, u32[]{:S(2)}) collective-permute-start(f32[3,3,16,1,256]{4,2,3,1,0:T(8,128)S(1)} %get-tuple-element.69), channel_id=1, source_target_pairs={{0,1},{1,2},{2,3},{3,4},{4,5},{5,6},{6,7},{8,9},{9,10},{10,11},{11... | collective-permute-start | bytes 442376 | tf_op jit(solution)/shard_map/ppermute | solution.py:29
  300.6 6.5 %collective-permute-start.17 = (f32[3,3,16,1,256]{4,2,3,1,0:T(8,128)S(1)}, f32[3,3,16,1,256]{4,2,3,1,0:T(8,128)S(1)}, u32[]{:S(2)}, u32[]{:S(2)}) collective-permute-start(f32[3,3,16,1,256]{4,2,3,1,0:T(8,128)S(1)} %get-tuple-element.70), channel_id=1, source_target_pairs={{1,0},{2,1},{3,2},{4,3},{5,4},{6,5},{7,6},{9,8},{10,9},{11,10},{12... | collective-permute-start | bytes 442376 | tf_op jit(solution)/shard_map/ppermute | solution.py:31
  318.3 17.8 %all-to-all-start.4 = ((f32[128,1,2]{2,1,0:T(1,128)}), f32[128,1,2]{2,1,0:T(1,128)S(1)}, u32[]{:S(2)}, u32[]{:S(2)}) async-start(f32[128,1,2]{2,1,0:T(1,128)} %broadcast_in_dim.26), calls=%async_computation.4 | async-start | bytes 131072 | tf_op jit(solution)/shard_map/all_to_all | solution.py:40
  349.2 7.5 %collective-permute-start.18 = (f32[1,3,16,1,256]{4,2,3,1,0:T(8,128)S(1)}, f32[1,3,16,1,256]{4,2,3,1,0:T(8,128)S(1)}, u32[]{:S(2)}, u32[]{:S(2)}) collective-permute-start(f32[1,3,16,1,256]{4,2,3,1,0:T(8,128)S(1)} %get-tuple-element.89), channel_id=1, source_target_pairs={{0,1},{1,2},{2,3},{3,4},{4,5},{5,6},{6,7},{8,9},{9,10},{10,11},{11... | collective-permute-start | bytes 147464 | tf_op jit(solution)/shard_map/ppermute | solution.py:29
  352.0 5.4 %collective-permute-start.19 = (f32[1,3,16,1,256]{4,2,3,1,0:T(8,128)S(1)}, f32[1,3,16,1,256]{4,2,3,1,0:T(8,128)S(1)}, u32[]{:S(2)}, u32[]{:S(2)}) collective-permute-start(f32[1,3,16,1,256]{4,2,3,1,0:T(8,128)S(1)} %get-tuple-element.90), channel_id=1, source_target_pairs={{1,0},{2,1},{3,2},{4,3},{5,4},{6,5},{7,6},{9,8},{10,9},{11,10},{12... | collective-permute-start | bytes 147464 | tf_op jit(solution)/shard_map/ppermute | solution.py:31
  387.4 5.0 collective-permute-start.20
  390.3 5.4 %collective-permute-start.21 = (f32[1,3,16,1,256]{4,2,3,1,0:T(8,128)S(1)}, f32[1,3,16,1,256]{4,2,3,1,0:T(8,128)S(1)}, u32[]{:S(2)}, u32[]{:S(2)}) collective-permute-start(f32[1,3,16,1,256]{4,2,3,1,0:T(8,128)S(1)} %get-tuple-element.88), channel_id=1, source_target_pairs={{1,0},{2,1},{3,2},{4,3},{5,4},{6,5},{7,6},{9,8},{10,9},{11,10},{12... | collective-permute-start | bytes 147464 | tf_op jit(solution)/shard_map/ppermute | solution.py:31
  411.5 4.4 collective-permute-start.22
  413.5 5.4 %collective-permute-start.23 = (f32[1,3,16,1,256]{4,2,3,1,0:T(8,128)S(1)}, f32[1,3,16,1,256]{4,2,3,1,0:T(8,128)S(1)}, u32[]{:S(2)}, u32[]{:S(2)}) collective-permute-start(f32[1,3,16,1,256]{4,2,3,1,0:T(8,128)S(1)} %get-tuple-element.86), channel_id=1, source_target_pairs={{1,0},{2,1},{3,2},{4,3},{5,4},{6,5},{7,6},{9,8},{10,9},{11,10},{12... | collective-permute-start | bytes 147464 | tf_op jit(solution)/shard_map/ppermute | solution.py:31
  444.8 4.8 collective-permute-start.24
  447.6 5.4 %collective-permute-start.25 = (f32[1,3,16,1,256]{4,2,3,1,0:T(8,128)S(1)}, f32[1,3,16,1,256]{4,2,3,1,0:T(8,128)S(1)}, u32[]{:S(2)}, u32[]{:S(2)}) collective-permute-start(f32[1,3,16,1,256]{4,2,3,1,0:T(8,128)S(1)} %get-tuple-element.84), channel_id=1, source_target_pairs={{1,0},{2,1},{3,2},{4,3},{5,4},{6,5},{7,6},{9,8},{10,9},{11,10},{12... | collective-permute-start | bytes 147464 | tf_op jit(solution)/shard_map/ppermute | solution.py:31
  468.8 4.7 collective-permute-start.26
  470.8 5.4 %collective-permute-start.27 = (f32[1,3,16,1,256]{4,2,3,1,0:T(8,128)S(1)}, f32[1,3,16,1,256]{4,2,3,1,0:T(8,128)S(1)}, u32[]{:S(2)}, u32[]{:S(2)}) collective-permute-start(f32[1,3,16,1,256]{4,2,3,1,0:T(8,128)S(1)} %get-tuple-element.82), channel_id=1, source_target_pairs={{1,0},{2,1},{3,2},{4,3},{5,4},{6,5},{7,6},{9,8},{10,9},{11,10},{12... | collective-permute-start | bytes 147464 | tf_op jit(solution)/shard_map/ppermute | solution.py:31
  (50 other events, 290.2 us)

commit v2 on v1

v2 whole, which is shorter than its diff:
```python
import jax
import jax.numpy as jnp
from jax import lax
from jax.experimental import pallas as pl
from jax.experimental.pallas import tpu as pltpu
from jax.sharding import Mesh
from jax.sharding import PartitionSpec as P

OUTER = 2
INNER = 3
IMG = ("img_0", "img_1")
TILE = ("tile_0", "tile_1")
IMG_TILE = ("img_0", "img_1", "tile_0", "tile_1")

spring_coef = 20.0
step_scale = 0.25
epsilon = 1e-06

HALO = 2 * INNER
PRODUCTS = 12
VMEM_LIMIT = 48 * 1024 * 1024


def shifted(cells, axis, total):
    where = lax.broadcasted_iota(jnp.int32, cells.shape, axis)
    size = cells.shape[axis]
    total = total + jnp.where(where == 0, 0.0, pltpu.roll(cells, 1, axis))
    return total + jnp.where(where == size - 1, 0.0, pltpu.roll(cells, size - 1, axis))


def laplace(cells, beside):
    return [
        shifted(cell, 1, shifted(cell, 0, total - 6.0 * cell))
        for cell, total in zip(cells, beside)
    ]


def dot(left, right):
    return left[0] * right[0] + left[1] * right[1] + left[2] * right[2]


def row(ref, at):
    return [ref[comp, at] for comp in range(3)]


def put(ref, at, cells):
    for comp in range(3):
        ref[comp, at] = cells[comp]


def plus(left, right):
    return [one + other for one, other in zip(left, right)]


def scaled(factors, cells):
    return [factor * cell for factor, cell in zip(factors, cells)]


def stiffness(square, coefs):
    plain = 0.5 - 0.125 * square
    return [plain, plain, plain + coefs]


def folded(cells):
    cells = cells[:8] + cells[8:]
    return cells[:, :128] + cells[:, 128:]


def loop(low, high, body, carry=0):
    return lax.fori_loop(low, high, body, carry)


def clear_outside(tile, last_tile, refs, own):
    rows = refs[0].shape[1]

    @pl.when(tile == 0)
    def _():
        for ref in refs:
            ref[:, 0:HALO] = jnp.zeros((3, HALO) + ref.shape[2:], jnp.float32)

    @pl.when(tile == last_tile)
    def _():
        for ref in refs:
            ref[:, HALO + own :] = jnp.zeros((3, rows - HALO - own) + ref.shape[2:], jnp.float32)


def drives(phi_ref, a_ref, b_ref, coef_ref, fa_ref, fb_ref, low, high):
    def body(at, carry):
        phi, a, b = row(phi_ref, at), row(a_ref, at), row(b_ref, at)
        m, n = plus(phi, a), plus(phi, b)
        side = plus(row(phi_ref, at - 1), row(phi_ref, at + 1))
        side_m = plus(side, plus(row(a_ref, at - 1), row(a_ref, at + 1)))
        side_n = plus(side, plus(row(b_ref, at - 1), row(b_ref, at + 1)))
        coefs = coef_ref[at]
        put(fa_ref, at, plus(laplace(m, side_m), scaled(stiffness(dot(m, m), coefs), m)))
        put(fb_ref, at, plus(laplace(n, side_n), scaled(stiffness(dot(n, n), coefs), n)))
        return carry

    loop(low, high, body)


def parts(phi, a, b, coefs, fa_ref, fb_ref, at):
    m, n = plus(phi, a), plus(phi, b)
    square_m, square_n = dot(m, m), dot(n, n)
    square_phi = dot(phi, phi)
    fa, fb = row(fa_ref, at), row(fb_ref, at)
    side = plus(row(fa_ref, at - 1), row(fa_ref, at + 1))
    side = plus(side, plus(row(fb_ref, at - 1), row(fb_ref, at + 1)))
    adjoint = laplace(plus(fa, fb), side)
    stiff_m, stiff_n = stiffness(square_m, coefs), stiffness(square_n, coefs)
    turn_m, turn_n = 0.25 * dot(m, fa), 0.25 * dot(n, fb)
    rise_m, rise_n = square_phi - dot(a, a), dot(b, b) - square_phi
    return m, n, square_m - square_n, fa, fb, adjoint, stiff_m, stiff_n, turn_m, turn_n, rise_m, rise_n


def first_kernel(
    place_ref, own_edge, own_mid, a_edge, a_mid, b_edge, b_mid, up_ref, down_ref, coef_ref,
    phi_ref, a_ref, b_ref, q_ref, r_ref, sums_ref, fa_ref, fb_ref, acc_ref
):
    own = own_edge.shape[1] + own_mid.shape[1]
    rows = own + 2 * HALO
    last_tile = place_ref[2] - 1
    tile = place_ref[1]
    for which, (ref, edge, mid) in enumerate(
        ((a_ref, a_edge, a_mid), (phi_ref, own_edge, own_mid), (b_ref, b_edge, b_mid))
    ):
        ref[:, 0:HALO] = up_ref[which]
        ref[:, HALO : 2 * HALO] = edge[:, 0:HALO]
        ref[:, 2 * HALO : own] = mid[...]
        ref[:, own : own + HALO] = edge[:, HALO:]
        ref[:, own + HALO :] = down_ref[which]
    drives(phi_ref, a_ref, b_ref, coef_ref, fa_ref, fb_ref, 1, rows - 1)
    clear_outside(tile, last_tile, (fa_ref, fb_ref), own)
    acc_ref[...] = jnp.zeros_like(acc_ref)

    def fields(at):
        phi, a, b = row(phi_ref, at), row(a_ref, at), row(b_ref, at)
        coefs = coef_ref[at]
        m, n, gap, fa, fb, adjoint, stiff_m, stiff_n, turn_m, turn_n, rise_m, rise_n = parts(
            phi, a, b, coefs, fa_ref, fb_ref, at
        )
        gap, rise_m, rise_n = 0.125 * gap, 0.125 * rise_m, 0.125 * rise_n
        flat, bent = [], []
        for c in range(3):
            flat.append(phi[c] * gap + m[c] * rise_m + n[c] * rise_n)
            bent.append(
                0.25
                * (
                    adjoint[c]
                    + (stiff_m[c] * fa[c] + stiff_n[c] * fb[c])
                    - (m[c] * turn_m + n[c] * turn_n)
                )
            )
        put(q_ref, at, flat)
        put(r_ref, at, bent)
        return phi, a, b, fb, flat, bent

    def rim(at, carry):
        fields(at)
        return carry

    def inside(at, carry):
        phi, a, b, fb, flat, bent = fields(at)
        ahead = [one - other for one, other in zip(b, phi)]
        pull = [one - other for one, other in zip(b, a)]
        curve = [2.0 * one - (two + other) for one, two, other in zip(phi, a, b)]
        pairs = (
            (curve, curve), (curve, flat), (curve, bent), (curve, pull),
            (flat, flat), (flat, bent), (flat, pull),
            (bent, bent), (bent, pull), (pull, pull),
            (ahead, ahead), (fb, fb),
        )
        for which, (left, right) in enumerate(pairs):
            acc_ref[which] += folded(dot(left, right))
        return carry

    loop(2, HALO, rim)
    loop(HALO, HALO + own, inside)
    loop(HALO + own, rows - 2, rim)
    clear_outside(tile, last_tile, (q_ref, r_ref), own)
    lane = lax.broadcasted_iota(jnp.int32, (1, 128), 1)
    sums = jnp.zeros((1, 128), jnp.float32)
    for which in range(PRODUCTS):
        sums = jnp.where(lane == which, jnp.sum(acc_ref[which]), sums)
    sums_ref[...] = jnp.broadcast_to(sums, sums_ref.shape)


def path_scalars(place_ref, all_ref, tiles, cells):
    devices = all_ref.shape[0]
    images = devices // tiles
    table = jnp.sum(all_ref[...].reshape(images, tiles, 128), axis=1)
    lane = lax.broadcasted_iota(jnp.int32, (images, 128), 1)
    image = lax.broadcasted_iota(jnp.int32, (images, 128), 0)
    one = image[:, :1]

    def column(which):
        return jnp.sum(jnp.where(lane == which, table, 0.0), axis=1, keepdims=True)

    live = one < images - 1
    seg = jnp.where(live, jnp.sqrt(column(10) + epsilon), 0.0)
    drv = jnp.where(live, jnp.sqrt(0.25 * column(11) + epsilon), 0.0)
    path_len = jnp.sum(seg, axis=0, keepdims=True)
    tau = path_len / jnp.sum(drv, axis=0, keepdims=True)
    before = jnp.sum(jnp.where(image < lane, seg, 0.0), axis=0, keepdims=True)
    before = jnp.sum(jnp.where(image == lane, before, 0.0), axis=1, keepdims=True)
    target = one.astype(jnp.float32) / (images - 1)
    pull = spring_coef * (before / path_len - target) * (images - 1) / (2.0 * path_len)
    inv = 1.0 / tau
    norm = inv * (inv * column(0) + 2.0 * (column(1) + tau * column(2) + pull * column(3)))
    norm += column(4) + 2.0 * (tau * column(5) + pull * column(6))
    norm += tau * (tau * column(7) + 2.0 * pull * column(8)) + pull * pull * column(9)
    inner = (one > 0) & (one < images - 1)
    total = jnp.sum(jnp.where(inner, norm, 0.0), axis=0, keepdims=True)
    step = step_scale / jnp.sqrt(total / cells + epsilon)
    mine = jnp.sum(jnp.where(one == place_ref[0], pull, 0.0), axis=0, keepdims=True)
    return tau[0, 0], mine[0, 0], step[0, 0]


def gradients(phi_ref, a_ref, b_ref, coef_ref, fa_ref, fb_ref, g_ref, acc_ref, tau, pull, out):
    inv = 1.0 / tau
    turned = 0.25 * tau

    def grad(at):
        phi, a, b = row(phi_ref, at), row(a_ref, at), row(b_ref, at)
        m, n, gap, fa, fb, adjoint, stiff_m, stiff_n, turn_m, turn_n, rise_m, rise_n = parts(
            phi, a, b, coef_ref[at], fa_ref, fb_ref, at
        )
        gap = 0.125 * gap + 2.0 * inv
        lean_m = 0.125 * rise_m - turned * turn_m
        lean_n = 0.125 * rise_n - turned * turn_n
        return [
            phi[c] * gap
            + (m[c] * lean_m + n[c] * lean_n)
            + turned * (adjoint[c] + (stiff_m[c] * fa[c] + stiff_n[c] * fb[c]))
            + ((pull - inv) * b[c] - (pull + inv) * a[c])
            for c in range(3)
        ]

    def rim(at, carry):
        put(g_ref, at - out, grad(at))
        return carry

    def inside(at, carry):
        cells = grad(at)
        put(g_ref, at - out, cells)
        acc_ref[...] += folded(dot(cells, cells))
        return carry

    return rim, inside


def interior(place_ref):
    return jnp.where((place_ref[0] > 0) & (place_ref[0] < place_ref[3] - 1), 1.0, 0.0)


def second_kernel(
    tiles, cells, place_ref, all_ref, p_ref, a_ref, b_ref, q_ref, r_ref, coef_ref,
    phi_ref, g_ref, scal_ref, sums_ref, fa_ref, fb_ref, acc_ref
):
    rows = p_ref.shape[1]
    own = rows - 2 * HALO
    tile, last_tile = place_ref[1], place_ref[2] - 1
    tau, pull, step = path_scalars(place_ref, all_ref, tiles, cells)
    live = interior(place_ref)
    step = step * live
    inv = 1.0 / tau
    scal_ref[0] = tau
    scal_ref[1] = pull
    keep, from_a, from_b = 1.0 - 2.0 * step * inv, step * (inv + pull), step * (inv - pull)
    bend = step * tau

    def update(at, carry):
        p, a, b, q, r = (row(ref, at) for ref in (p_ref, a_ref, b_ref, q_ref, r_ref))
        put(
            phi_ref,
            at,
            [
                (keep * p[c] + from_a * a[c]) + (from_b * b[c] - step * q[c]) - bend * r[c]
                for c in range(3)
            ],
        )
        return carry

    loop(2, rows - 2, update)
    drives(phi_ref, a_ref, b_ref, coef_ref, fa_ref, fb_ref, 3, rows - 3)
    clear_outside(tile, last_tile, (fa_ref, fb_ref), own)
    acc_ref[...] = jnp.zeros_like(acc_ref)
    rim, inside = gradients(
        phi_ref, a_ref, b_ref, coef_ref, fa_ref, fb_ref, g_ref, acc_ref, tau, pull, 0
    )
    loop(4, HALO, rim)
    loop(HALO, HALO + own, inside)
    loop(HALO + own, rows - 4, rim)
    clear_outside(tile, last_tile, (g_ref,), own)
    sums = jnp.sum(acc_ref[...], axis=0, keepdims=True) * live
    sums_ref[...] = jnp.broadcast_to(sums, sums_ref.shape)


def step_of(all_ref, cells):
    return step_scale / jnp.sqrt(jnp.sum(all_ref[...]) / cells + epsilon)


def third_kernel(
    cells, place_ref, scal_ref, all_ref, p_ref, h_ref, a_ref, b_ref, coef_ref,
    phi_ref, g_ref, sums_ref, fa_ref, fb_ref, acc_ref
):
    rows = p_ref.shape[1]
    own = rows - 2 * HALO
    tile, last_tile = place_ref[1], place_ref[2] - 1
    live = interior(place_ref)
    tau, pull = scal_ref[0], scal_ref[1]
    step = step_of(all_ref, cells) * live

    def update(at, carry):
        p, h = row(p_ref, at), row(h_ref, at)
        put(phi_ref, at, [p[c] - step * h[c] for c in range(3)])
        return carry

    loop(4, rows - 4, update)
    drives(phi_ref, a_ref, b_ref, coef_ref, fa_ref, fb_ref, 5, rows - 5)
    clear_outside(tile, last_tile, (fa_ref, fb_ref), own)
    acc_ref[...] = jnp.zeros_like(acc_ref)
    _, inside = gradients(
        phi_ref, a_ref, b_ref, coef_ref, fa_ref, fb_ref, g_ref, acc_ref, tau, pull, HALO
    )
    loop(HALO, HALO + own, inside)
    sums = jnp.sum(acc_ref[...], axis=0, keepdims=True) * live
    sums_ref[...] = jnp.broadcast_to(sums, sums_ref.shape)


def last_kernel(cells, place_ref, all_ref, p_ref, g_ref, edge_ref, mid_ref):
    own = g_ref.shape[1]
    step = step_of(all_ref, cells) * interior(place_ref)

    def moved(at):
        p, g = row(p_ref, at + HALO), row(g_ref, at)
        return [p[c] - step * g[c] for c in range(3)]

    def top(at, carry):
        put(edge_ref, at, moved(at))
        return carry

    def middle(at, carry):
        put(mid_ref, at - HALO, moved(at))
        return carry

    def bottom(at, carry):
        put(edge_ref, at - (own - 2 * HALO), moved(at))
        return carry

    loop(0, HALO, top)
    loop(HALO, own - HALO, middle)
    loop(own - HALO, own, bottom)


def f32(*shape):
    return jax.ShapeDtypeStruct(shape, jnp.float32)


def call(kernel, operands, outs, scratch, scalars=1, small_out=()):
    smem = pl.BlockSpec(memory_space=pltpu.SMEM)
    vmem = pl.BlockSpec(memory_space=pltpu.VMEM)
    return pl.pallas_call(
        kernel,
        out_shape=outs,
        in_specs=[smem if i < scalars else vmem for i in range(len(operands))],
        out_specs=[smem if i in small_out else vmem for i in range(len(outs))],
        scratch_shapes=[pltpu.VMEM(shape, jnp.float32) for shape in scratch],
        compiler_params=pltpu.CompilerParams(vmem_limit_bytes=VMEM_LIMIT),
    )(*operands)


def beside(cells, axis, forward):
    count = lax.axis_size(axis)
    pairs = [(i, i + 1) if forward else (i + 1, i) for i in range(count - 1)]
    return lax.ppermute(cells, axis, pairs)


def from_everyone(rows):
    return lax.all_to_all(rows, IMG_TILE, 0, 0, tiled=True)


def body(spins, aniso):
    _, comps, depth, own, width = spins.shape
    images, tiles = lax.axis_size(IMG), lax.axis_size(TILE)
    devices = images * tiles
    cells = float(images * comps * depth * own * tiles * width)
    rows = own + 2 * HALO
    place = jnp.stack(
        [lax.axis_index(IMG), lax.axis_index(TILE), jnp.int32(tiles), jnp.int32(images)]
    ).astype(jnp.int32)
    start = jnp.swapaxes(spins[0], 1, 2)
    coefs = jnp.swapaxes(aniso, 0, 1)
    coefs = jnp.concatenate(
        [beside(coefs[own - HALO :], TILE, True), coefs, beside(coefs[:HALO], TILE, False)]
    )
    edge = jnp.concatenate([start[:, :HALO], start[:, own - HALO :]], axis=1)
    mid = start[:, HALO : own - HALO]
    ext = (3, rows, depth, width)
    whole = f32(*ext)
    table = f32(devices, 128)
    for _ in range(OUTER):
        a_edge, b_edge = beside(edge, IMG, True), beside(edge, IMG, False)
        trio = jnp.stack([a_edge, edge, b_edge])
        up = beside(trio[:, :, HALO:], TILE, True)
        down = beside(trio[:, :, :HALO], TILE, False)
        a_mid, b_mid = beside(mid, IMG, True), beside(mid, IMG, False)
        phi, a, b, q, r, sums = call(
            first_kernel,
            [place, edge, mid, a_edge, a_mid, b_edge, b_mid, up, down, coefs],
            [whole, whole, whole, whole, whole, table],
            [ext, ext, (PRODUCTS, 8, 128)],
        )
        phi, g, scal, sums = call(
            lambda *refs: second_kernel(tiles, cells, *refs),
            [place, from_everyone(sums), phi, a, b, q, r, coefs],
            [whole, whole, f32(2), table],
            [ext, ext, (8, 128)],
            small_out=(2,),
        )
        phi, g, sums = call(
            lambda *refs: third_kernel(cells, *refs),
            [place, scal, from_everyone(sums), phi, g, a, b, coefs],
            [whole, f32(3, own, depth, width), table],
            [ext, ext, (8, 128)],
            scalars=2,
        )
        edge, mid = call(
            lambda *refs: last_kernel(cells, *refs),
            [place, from_everyone(sums), phi, g],
            [f32(3, 2 * HALO, depth, width), f32(3, own - 2 * HALO, depth, width)],
            [],
        )
    final = jnp.concatenate([edge[:, :HALO], mid, edge[:, HALO:]], axis=1)
    return jnp.swapaxes(final, 1, 2)[None]


def solution(mesh):
    split = Mesh(mesh.devices.reshape(4, 4, 4, 2), IMG_TILE)
    return jax.shard_map(
        body,
        mesh=split,
        in_specs=(P(IMG, None, None, TILE, None), P(None, TILE, None)),
        out_specs=P(IMG, None, None, TILE, None),
        check_vma=False,
    )
```

time: 513 us -> 281 us (0.55); the launches traced: 504 us -> 280 us
  other arithmetic: 175 us -> 0.61 us
  Pallas kernels: 0 us -> 88.7 us
  waiting for transfers between devices: 119 us -> 37.1 us
  starting transfers between devices: 89.8 us -> 43.2 us
  between operations: 12.4 us -> 0.3 us
  blocking collectives: 85.2 us -> 96.7 us
  local copies, waits for them, and re-layouts: 23.4 us -> 13.6 us
    reduce_sum x37 -> x0, other arithmetic: 97 us -> none  [the longest x6 47.5 us: hessian_point(): projected = jnp.sum(middle * vector, axis=-4, keepdims=True)]
    pallas_call x0 -> x8, Pallas kernels: none -> 88.7 us  [call(): pl.pallas_call(kernel, out_shape=outs, in_specs=[smem if i < scalars else...]
    ppermute x28 -> x14, waiting for transfers between devices: 101 us -> 37.1 us  [beside(): return lax.ppermute(cells, axis, pairs)]
    ppermute x28 -> x14, starting transfers between devices: 70.4 us -> 43.2 us  [beside(): return lax.ppermute(cells, axis, pairs)]
    concatenate x10 -> x1, other arithmetic: 25.4 us -> 0.05 us  [body(): jnp.concatenate([beside(coefs[own - HALO:], TILE, True), coefs, beside(co...]
    sub x18 -> x0, other arithmetic: 24.3 us -> none  [the longest x6 13.3 us: body(): current = current - step_scale * gradients / grad_scale]
    all_to_all x2 -> x0, starting transfers between devices: 19.3 us -> none  [from_everyone(): lax.all_to_all(jnp.broadcast_to(values[None], (peers, *values.shape)), IM...]
    mul x20 -> x0, other arithmetic: 18 us -> none  [the longest x6 11.8 us: body(): middle_a = 0.5 * (before_img + own_ext)]
  transfers between devices with their start and end apart: 30 -> 14, of which waited for: 18 -> 8; matrix products, arithmetic and copies ran while one was open for 1% -> 1% of each run, Pallas kernels for 0% -> 0%
where the time goes in v2:
time: 281 us; the launch traced here: 280 us
  blocking collectives  96.7 us (34%)
  Pallas kernels  88.7 us (32%)
  starting transfers between devices  43.2 us (15%)
  waiting for transfers between devices  37.1 us (13%)
  local copies, waits for them, and re-layouts  13.6 us (5%)
    all_to_all x6, blocking collectives, from_everyone(): return lax.all_to_all(rows, IMG_TILE, 0, 0, tiled=True)  96.7 us
    pallas_call x8, Pallas kernels, call(): pl.pallas_call(kernel, out_shape=outs, in_specs=[smem if i < scalars else...  88.7 us
    ppermute x14, starting transfers between devices, beside(): return lax.ppermute(cells, axis, pairs)  43.2 us
    ppermute x14, waiting for transfers between devices, beside(): return lax.ppermute(cells, axis, pairs)  37.1 us
    unnamed x16, local copies, waits for them, and re-layouts  9.16 us
  transfers between devices with their start and end apart: 14, of which 8 were waited for; matrix products, arithmetic and copies ran while one was open for 1% of the time, Pallas kernels for 0%

profile of v2, /device:TPU:1, one launch (start us, length us, event | category | flops | bytes accessed | tf_op | source)
XLA Modules:
  0.0 280.2 jit_solution(18227232223330118710)
XLA Ops:
  0.0 2.3 copy.17
  3.8 4.7 %collective-permute-start = (f32[3,12,16,256]{3,2,1,0:T(8,128)S(1)}, f32[3,12,16,256]{3,2,1,0:T(8,128)S(1)}, u32[]{:S(2)}, u32[]{:S(2)}) collective-permute-start(f32[3,12,16,256]{3,2,1,0:T(8,128)S(1)} %get-tuple-element.74.own_edge), channel_id=1, source_target_pairs={{0,8},{8,16},{16,24},{24,32},{32,40},{40,48},{48,56},{56,64},{64,7... | collective-permute-start | bytes 1769480 | tf_op jit(solution)/shard_map/ppermute | solution.py:376
  9.8 4.9 %collective-permute-start.1 = (f32[3,20,16,256]{3,2,1,0:T(8,128)S(1)}, f32[3,20,16,256]{3,2,1,0:T(8,128)}, u32[]{:S(2)}, u32[]{:S(2)}) collective-permute-start(f32[3,20,16,256]{3,2,1,0:T(8,128)S(1)} %slice.46.own_mid), channel_id=1, source_target_pairs={{0,8},{8,16},{16,24},{24,32},{32,40},{40,48},{48,56},{56,64},{64,7... | collective-permute-start | bytes 2949128 | tf_op jit(solution)/shard_map/ppermute | solution.py:376
  14.8 4.4 %collective-permute-done.2.b_edge = f32[3,12,16,256]{3,2,1,0:T(8,128)S(1)} collective-permute-done((f32[3,12,16,256]{3,2,1,0:T(8,128)S(1)}, f32[3,12,16,256]{3,2,1,0:T(8,128)S(1)}, u32[]{:S(2)}, u32[]{:S(2)}) %collective-permute-start.2) | collective-permute-done | bytes 589856 | tf_op jit(solution)/shard_map/ppermute | solution.py:376
  21.5 5.4 %collective-permute-start.5 = (f32[3,3,6,16,256]{4,3,2,1,0:T(8,128)}, f32[3,3,6,16,256]{4,3,2,1,0:T(8,128)}, u32[]{:S(2)}, u32[]{:S(2)}) collective-permute-start(f32[3,3,6,16,256]{4,3,2,1,0:T(8,128)} %get-tuple-element.67), channel_id=1, source_target_pairs={{1,0},{2,1},{3,2},{4,3},{5,4},{6,5},{7,6},{9,8},{10,9},{11,10},{12... | collective-permute-start | bytes 2654216 | tf_op jit(solution)/shard_map/ppermute | solution.py:376
  26.9 3.1 %collective-permute-start.4 = (f32[3,3,6,16,256]{4,3,2,1,0:T(8,128)}, f32[3,3,6,16,256]{4,3,2,1,0:T(8,128)}, u32[]{:S(2)}, u32[]{:S(2)}) collective-permute-start(f32[3,3,6,16,256]{4,3,2,1,0:T(8,128)} %get-tuple-element.68), channel_id=1, source_target_pairs={{0,1},{1,2},{2,3},{3,4},{4,5},{5,6},{6,7},{8,9},{9,10},{10,11},{11... | collective-permute-start | bytes 2654216 | tf_op jit(solution)/shard_map/ppermute | solution.py:376
  31.0 2.4 collective-permute-start.6
  33.4 7.9 %collective-permute-done.6 = f32[6,16,256]{2,1,0:T(8,128)S(1)} collective-permute-done((f32[6,16,256]{2,1,0:T(8,128)}, f32[6,16,256]{2,1,0:T(8,128)S(1)}, u32[]{:S(2)}, u32[]{:S(2)}) %collective-permute-start.6) | collective-permute-done | bytes 98336 | tf_op jit(solution)/shard_map/ppermute | solution.py:376
  41.4 1.9 collective-permute-start.7
  43.4 4.6 %collective-permute-done.7 = f32[6,16,256]{2,1,0:T(8,128)S(1)} collective-permute-done((f32[6,16,256]{2,1,0:T(8,128)S(1)}, f32[6,16,256]{2,1,0:T(8,128)S(1)}, u32[]{:S(2)}, u32[]{:S(2)}) %collective-permute-start.7) | collective-permute-done | bytes 98336 | tf_op jit(solution)/shard_map/ppermute | solution.py:376
  48.0 17.1 %shard_map.28 = (f32[3,44,16,256]{3,2,1,0:T(8,128)}, f32[3,44,16,256]{3,2,1,0:T(8,128)}, f32[3,44,16,256]{3,2,1,0:T(8,128)}, f32[3,44,16,256]{3,2,1,0:T(8,128)},...) custom-call(s32[4]{0:T(128)S(1)} %pad_add_fusion.place_ref.refs_0_, ...), custom_call_target="tpu_custom_call" | custom-call | tf_op jit(solution)/shard_map/pallas_call | solution.py:363
  65.1 22.0 %all_to_all.66 = f32[128,1,128]{2,1,0:T(1,128)S(1)} all-to-all(f32[128,1,128]{2,1,0:T(1,128)S(1)} %bitcast.56), channel_id=1, replica_groups=mesh['img_0'=4,'img_1'=4,'tile_0'=4,'tile_1'=2] {'img_0','img_1','tile_0..., dimensions={0} | all-to-all | bytes 131072 | tf_op jit(solution)/shard_map/all_to_all | solution.py:380
  87.1 14.6 %shard_map.29 = (f32[3,44,16,256]{3,2,1,0:T(8,128)S(1)}, f32[3,44,16,256]{3,2,1,0:T(8,128)S(1)}, f32[2]{0:T(128)S(1)}, f32[128,128]{1,0:T(8,128)S(1)}) custom-call(s32[4]{0:T(128)S(1)} %pad_add_fusion.place_ref.refs_0_, f32[128,128]{1,0:T(8,128)S(1)} %bitcast.52, f32[3,44,16,256]{3,2,1,0:T(8,128)} %get-tuple-element.36.refs_2_, ...), custom_call_target="tpu_custom_call" | custom-call | tf_op jit(solution)/shard_map/pallas_call | solution.py:363
  101.7 1.4 copy-done.2
  103.1 1.4 copy-done.3
  104.5 13.9 %all_to_all.67 = f32[128,1,128]{2,1,0:T(1,128)S(1)} all-to-all(f32[128,1,128]{2,1,0:T(1,128)S(1)} %bitcast.60), channel_id=1, replica_groups=mesh['img_0'=4,'img_1'=4,'tile_0'=4,'tile_1'=2] {'img_0','img_1','tile_0..., dimensions={0} | all-to-all | bytes 131072 | tf_op jit(solution)/shard_map/all_to_all | solution.py:380
  118.4 11.9 %shard_map.30 = (f32[3,44,16,256]{3,2,1,0:T(8,128)S(1)}, f32[3,32,16,256]{3,2,1,0:T(8,128)S(1)}, f32[128,128]{1,0:T(8,128)S(1)}) custom-call(s32[4]{0:T(128)S(1)} %pad_add_fusion.place_ref.refs_0_, f32[2]{0:T(128)S(1)} %get-tuple-element.41.refs_1_, f32[128,128]{1,0:T(8,128)S(1)} %bitcast.51, f32[3,44,16,256]{3,2,1,0:T(8,128)} %copy-done.2, ...), custom_call_target="tpu_custom_call" | custom-call | tf_op jit(solution)/shard_map/pallas_call | solution.py:363
  130.3 13.9 %all_to_all.68 = f32[128,1,128]{2,1,0:T(1,128)S(1)} all-to-all(f32[128,1,128]{2,1,0:T(1,128)S(1)} %bitcast.59), channel_id=1, replica_groups=mesh['img_0'=4,'img_1'=4,'tile_0'=4,'tile_1'=2] {'img_0','img_1','tile_0..., dimensions={0} | all-to-all | bytes 131072 | tf_op jit(solution)/shard_map/all_to_all | solution.py:380
  146.6 4.0 %collective-permute-start.8 = (f32[3,12,16,256]{3,2,1,0:T(8,128)S(1)}, f32[3,12,16,256]{3,2,1,0:T(8,128)S(1)}, u32[]{:S(2)}, u32[]{:S(2)}) collective-permute-start(f32[3,12,16,256]{3,2,1,0:T(8,128)S(1)} %get-tuple-element.48.own_edge), channel_id=1, source_target_pairs={{0,8},{8,16},{16,24},{24,32},{32,40},{40,48},{48,56},{56,64},{64,7... | collective-permute-start | bytes 1769480 | tf_op jit(solution)/shard_map/ppermute | solution.py:376
  151.9 4.0 %collective-permute-start.9 = (f32[3,20,16,256]{3,2,1,0:T(8,128)S(1)}, f32[3,20,16,256]{3,2,1,0:T(8,128)S(1)}, u32[]{:S(2)}, u32[]{:S(2)}) collective-permute-start(f32[3,20,16,256]{3,2,1,0:T(8,128)S(1)} %get-tuple-element.49.own_mid), channel_id=1, source_target_pairs={{0,8},{8,16},{16,24},{24,32},{32,40},{40,48},{48,56},{56,64},{64,7... | collective-permute-start | bytes 2949128 | tf_op jit(solution)/shard_map/ppermute | solution.py:376
  156.0 5.3 %collective-permute-done.10.b_edge = f32[3,12,16,256]{3,2,1,0:T(8,128)S(1)} collective-permute-done((f32[3,12,16,256]{3,2,1,0:T(8,128)S(1)}, f32[3,12,16,256]{3,2,1,0:T(8,128)S(1)}, u32[]{:S(2)}, u32[]{:S(2)}) %collective-permute-start.10) | collective-permute-done | bytes 589856 | tf_op jit(solution)/shard_map/ppermute | solution.py:376
  162.4 5.4 %collective-permute-start.13 = (f32[3,3,6,16,256]{4,3,2,1,0:T(8,128)S(1)}, f32[3,3,6,16,256]{4,3,2,1,0:T(8,128)S(1)}, u32[]{:S(2)}, u32[]{:S(2)}) collective-permute-start(f32[3,3,6,16,256]{4,3,2,1,0:T(8,128)S(1)} %get-tuple-element.65), channel_id=1, source_target_pairs={{1,0},{2,1},{3,2},{4,3},{5,4},{6,5},{7,6},{9,8},{10,9},{11,10},{12... | collective-permute-start | bytes 2654216 | tf_op jit(solution)/shard_map/ppermute | solution.py:376
  167.9 2.1 collective-permute-start.12
  170.0 12.3 %collective-permute-done.11.b_mid = f32[3,20,16,256]{3,2,1,0:T(8,128)S(1)} collective-permute-done((f32[3,20,16,256]{3,2,1,0:T(8,128)S(1)}, f32[3,20,16,256]{3,2,1,0:T(8,128)S(1)}, u32[]{:S(2)}, u32[]{:S(2)}) %collective-permute-start.11) | collective-permute-done | bytes 983072 | tf_op jit(solution)/shard_map/ppermute | solution.py:376
  184.1 16.5 %shard_map.32 = (f32[3,44,16,256]{3,2,1,0:T(8,128)}, f32[3,44,16,256]{3,2,1,0:T(8,128)}, f32[3,44,16,256]{3,2,1,0:T(8,128)}, f32[3,44,16,256]{3,2,1,0:T(8,128)},...) custom-call(s32[4]{0:T(128)S(1)} %pad_add_fusion.place_ref.refs_0_, ...), custom_call_target="tpu_custom_call" | custom-call | tf_op jit(solution)/shard_map/pallas_call | solution.py:363
  200.7 19.1 %all_to_all.69 = f32[128,1,128]{2,1,0:T(1,128)S(1)} all-to-all(f32[128,1,128]{2,1,0:T(1,128)S(1)} %bitcast.57), channel_id=1, replica_groups=mesh['img_0'=4,'img_1'=4,'tile_0'=4,'tile_1'=2] {'img_0','img_1','tile_0..., dimensions={0} | all-to-all | bytes 131072 | tf_op jit(solution)/shard_map/all_to_all | solution.py:380
  219.7 14.6 %shard_map.33 = (f32[3,44,16,256]{3,2,1,0:T(8,128)S(1)}, f32[3,44,16,256]{3,2,1,0:T(8,128)S(1)}, f32[2]{0:T(128)S(1)}, f32[128,128]{1,0:T(8,128)S(1)}) custom-call(s32[4]{0:T(128)S(1)} %pad_add_fusion.place_ref.refs_0_, f32[128,128]{1,0:T(8,128)S(1)} %bitcast.53, f32[3,44,16,256]{3,2,1,0:T(8,128)} %get-tuple-element.51.refs_2_, ...), custom_call_target="tpu_custom_call" | custom-call | tf_op jit(solution)/shard_map/pallas_call | solution.py:363
  235.7 1.4 copy-done.1
  237.1 13.9 %all_to_all.70 = f32[128,1,128]{2,1,0:T(1,128)S(1)} all-to-all(f32[128,1,128]{2,1,0:T(1,128)S(1)} %bitcast.61), channel_id=1, replica_groups=mesh['img_0'=4,'img_1'=4,'tile_0'=4,'tile_1'=2] {'img_0','img_1','tile_0..., dimensions={0} | all-to-all | bytes 131072 | tf_op jit(solution)/shard_map/all_to_all | solution.py:380
  251.0 11.9 %shard_map.34 = (f32[3,44,16,256]{3,2,1,0:T(8,128)S(1)}, f32[3,32,16,256]{3,2,1,0:T(8,128)S(1)}, f32[128,128]{1,0:T(8,128)S(1)}) custom-call(s32[4]{0:T(128)S(1)} %pad_add_fusion.place_ref.refs_0_, f32[2]{0:T(128)S(1)} %get-tuple-element.56.refs_1_, f32[128,128]{1,0:T(8,128)S(1)} %bitcast.50, f32[3,44,16,256]{3,2,1,0:T(8,128)} %copy-done, ...), custom_call_target="tpu_custom_call" | custom-call | tf_op jit(solution)/shard_map/pallas_call | solution.py:363
  263.0 13.9 %all_to_all.71 = f32[128,1,128]{2,1,0:T(1,128)S(1)} all-to-all(f32[128,1,128]{2,1,0:T(1,128)S(1)} %bitcast.58), channel_id=1, replica_groups=mesh['img_0'=4,'img_1'=4,'tile_0'=4,'tile_1'=2] {'img_0','img_1','tile_0..., dimensions={0} | all-to-all | bytes 131072 | tf_op jit(solution)/shard_map/all_to_all | solution.py:380
  278.1 2.1 copy.14
  (39 shorter events, 15.5 us)
Async XLA Ops:
  2.5 16.7 %collective-permute-start.2 = (f32[3,12,16,256]{3,2,1,0:T(8,128)S(1)}, f32[3,12,16,256]{3,2,1,0:T(8,128)S(1)}, u32[]{:S(2)}, u32[]{:S(2)}) collective-permute-start(f32[3,12,16,256]{3,2,1,0:T(8,128)S(1)} %get-tuple-element.74.own_edge), channel_id=1, source_target_pairs={{8,0},{16,8},{24,16},{32,24},{40,32},{48,40},{56,48},{64,56},{72,6... | collective-permute-start | bytes 1769480 | tf_op jit(solution)/shard_map/ppermute | solution.py:376
  3.8 16.2 %collective-permute-start = (f32[3,12,16,256]{3,2,1,0:T(8,128)S(1)}, f32[3,12,16,256]{3,2,1,0:T(8,128)S(1)}, u32[]{:S(2)}, u32[]{:S(2)}) collective-permute-start(f32[3,12,16,256]{3,2,1,0:T(8,128)S(1)} %get-tuple-element.74.own_edge), channel_id=1, source_target_pairs={{0,8},{8,16},{16,24},{24,32},{32,40},{40,48},{48,56},{56,64},{64,7... | collective-permute-start | bytes 1769480 | tf_op jit(solution)/shard_map/ppermute | solution.py:376
  8.5 39.4 %collective-permute-start.3 = (f32[3,20,16,256]{3,2,1,0:T(8,128)S(1)}, f32[3,20,16,256]{3,2,1,0:T(8,128)}, u32[]{:S(2)}, u32[]{:S(2)}) collective-permute-start(f32[3,20,16,256]{3,2,1,0:T(8,128)S(1)} %slice.46.own_mid), channel_id=1, source_target_pairs={{8,0},{16,8},{24,16},{32,24},{40,32},{48,40},{56,48},{64,56},{72,6... | collective-permute-start | bytes 2949128 | tf_op jit(solution)/shard_map/ppermute | solution.py:376
  9.8 38.2 %collective-permute-start.1 = (f32[3,20,16,256]{3,2,1,0:T(8,128)S(1)}, f32[3,20,16,256]{3,2,1,0:T(8,128)}, u32[]{:S(2)}, u32[]{:S(2)}) collective-permute-start(f32[3,20,16,256]{3,2,1,0:T(8,128)S(1)} %slice.46.own_mid), channel_id=1, source_target_pairs={{0,8},{8,16},{16,24},{24,32},{32,40},{40,48},{48,56},{56,64},{64,7... | collective-permute-start | bytes 2949128 | tf_op jit(solution)/shard_map/ppermute | solution.py:376
  20.1 9.9 %copy-start.6 = (f32[16,32,256]{2,1,0:T(8,128)S(1)}, f32[16,32,256]{2,1,0:T(8,128)}, u32[]{:S(2)}) copy-start(f32[16,32,256]{2,1,0:T(8,128)} %param.3) | copy-start | bytes 1572868
  21.5 26.5 %collective-permute-start.5 = (f32[3,3,6,16,256]{4,3,2,1,0:T(8,128)}, f32[3,3,6,16,256]{4,3,2,1,0:T(8,128)}, u32[]{:S(2)}, u32[]{:S(2)}) collective-permute-start(f32[3,3,6,16,256]{4,3,2,1,0:T(8,128)} %get-tuple-element.67), channel_id=1, source_target_pairs={{1,0},{2,1},{3,2},{4,3},{5,4},{6,5},{7,6},{9,8},{10,9},{11,10},{12... | collective-permute-start | bytes 2654216 | tf_op jit(solution)/shard_map/ppermute | solution.py:376
  26.9 21.1 %collective-permute-start.4 = (f32[3,3,6,16,256]{4,3,2,1,0:T(8,128)}, f32[3,3,6,16,256]{4,3,2,1,0:T(8,128)}, u32[]{:S(2)}, u32[]{:S(2)}) collective-permute-start(f32[3,3,6,16,256]{4,3,2,1,0:T(8,128)} %get-tuple-element.68), channel_id=1, source_target_pairs={{0,1},{1,2},{2,3},{3,4},{4,5},{5,6},{6,7},{8,9},{9,10},{10,11},{11... | collective-permute-start | bytes 2654216 | tf_op jit(solution)/shard_map/ppermute | solution.py:376
  31.0 10.3 %collective-permute-start.6 = (f32[6,16,256]{2,1,0:T(8,128)}, f32[6,16,256]{2,1,0:T(8,128)S(1)}, u32[]{:S(2)}, u32[]{:S(2)}) collective-permute-start(f32[6,16,256]{2,1,0:T(8,128)} %get-tuple-element.75), channel_id=1, source_target_pairs={{0,1},{1,2},{2,3},{3,4},{4,5},{5,6},{6,7},{8,9},{9,10},{10,11},{11... | collective-permute-start | bytes 294920 | tf_op jit(solution)/shard_map/ppermute | solution.py:376
  41.4 6.6 %collective-permute-start.7 = (f32[6,16,256]{2,1,0:T(8,128)S(1)}, f32[6,16,256]{2,1,0:T(8,128)S(1)}, u32[]{:S(2)}, u32[]{:S(2)}) collective-permute-start(f32[6,16,256]{2,1,0:T(8,128)S(1)} %get-tuple-element.76), channel_id=1, source_target_pairs={{1,0},{2,1},{3,2},{4,3},{5,4},{6,5},{7,6},{9,8},{10,9},{11,10},{12... | collective-permute-start | bytes 294920 | tf_op jit(solution)/shard_map/ppermute | solution.py:376
  101.7 1.4 copy-start.2
  103.1 1.4 copy-start.3
  145.3 16.0 %collective-permute-start.10 = (f32[3,12,16,256]{3,2,1,0:T(8,128)S(1)}, f32[3,12,16,256]{3,2,1,0:T(8,128)S(1)}, u32[]{:S(2)}, u32[]{:S(2)}) collective-permute-start(f32[3,12,16,256]{3,2,1,0:T(8,128)S(1)} %get-tuple-element.48.own_edge), channel_id=1, source_target_pairs={{8,0},{16,8},{24,16},{32,24},{40,32},{48,40},{56,48},{64,56},{72,6... | collective-permute-start | bytes 1769480 | tf_op jit(solution)/shard_map/ppermute | solution.py:376
  146.6 15.6 %collective-permute-start.8 = (f32[3,12,16,256]{3,2,1,0:T(8,128)S(1)}, f32[3,12,16,256]{3,2,1,0:T(8,128)S(1)}, u32[]{:S(2)}, u32[]{:S(2)}) collective-permute-start(f32[3,12,16,256]{3,2,1,0:T(8,128)S(1)} %get-tuple-element.48.own_edge), channel_id=1, source_target_pairs={{0,8},{8,16},{16,24},{24,32},{32,40},{40,48},{48,56},{56,64},{64,7... | collective-permute-start | bytes 1769480 | tf_op jit(solution)/shard_map/ppermute | solution.py:376
  150.6 31.7 %collective-permute-start.11 = (f32[3,20,16,256]{3,2,1,0:T(8,128)S(1)}, f32[3,20,16,256]{3,2,1,0:T(8,128)S(1)}, u32[]{:S(2)}, u32[]{:S(2)}) collective-permute-start(f32[3,20,16,256]{3,2,1,0:T(8,128)S(1)} %get-tuple-element.49.own_mid), channel_id=1, source_target_pairs={{8,0},{16,8},{24,16},{32,24},{40,32},{48,40},{56,48},{64,56},{72,6... | collective-permute-start | bytes 2949128 | tf_op jit(solution)/shard_map/ppermute | solution.py:376
  151.9 31.3 %collective-permute-start.9 = (f32[3,20,16,256]{3,2,1,0:T(8,128)S(1)}, f32[3,20,16,256]{3,2,1,0:T(8,128)S(1)}, u32[]{:S(2)}, u32[]{:S(2)}) collective-permute-start(f32[3,20,16,256]{3,2,1,0:T(8,128)S(1)} %get-tuple-element.49.own_mid), channel_id=1, source_target_pairs={{0,8},{8,16},{16,24},{24,32},{32,40},{40,48},{48,56},{56,64},{64,7... | collective-permute-start | bytes 2949128 | tf_op jit(solution)/shard_map/ppermute | solution.py:376
  162.4 20.8 %collective-permute-start.13 = (f32[3,3,6,16,256]{4,3,2,1,0:T(8,128)S(1)}, f32[3,3,6,16,256]{4,3,2,1,0:T(8,128)S(1)}, u32[]{:S(2)}, u32[]{:S(2)}) collective-permute-start(f32[3,3,6,16,256]{4,3,2,1,0:T(8,128)S(1)} %get-tuple-element.65), channel_id=1, source_target_pairs={{1,0},{2,1},{3,2},{4,3},{5,4},{6,5},{7,6},{9,8},{10,9},{11,10},{12... | collective-permute-start | bytes 2654216 | tf_op jit(solution)/shard_map/ppermute | solution.py:376
  167.9 15.3 %collective-permute-start.12 = (f32[3,3,6,16,256]{4,3,2,1,0:T(8,128)S(1)}, f32[3,3,6,16,256]{4,3,2,1,0:T(8,128)S(1)}, u32[]{:S(2)}, u32[]{:S(2)}) collective-permute-start(f32[3,3,6,16,256]{4,3,2,1,0:T(8,128)S(1)} %get-tuple-element.66), channel_id=1, source_target_pairs={{0,1},{1,2},{2,3},{3,4},{4,5},{5,6},{6,7},{8,9},{9,10},{10,11},{11... | collective-permute-start | bytes 2654216 | tf_op jit(solution)/shard_map/ppermute | solution.py:376
  182.3 0.9 copy-start.4
  183.2 0.9 copy-start.5
  234.3 1.4 copy-start
  235.7 1.4 copy-start.1

commit v3 on v2

v3 whole, which is shorter than its diff:
```python
import jax
import jax.numpy as jnp
from jax import lax
from jax.experimental import pallas as pl
from jax.experimental.pallas import tpu as pltpu
from jax.sharding import Mesh
from jax.sharding import PartitionSpec as P

OUTER = 2
INNER = 3
IMG = ("img_0", "img_1")
TILE = ("tile_0", "tile_1")
IMG_TILE = ("img_0", "img_1", "tile_0", "tile_1")

spring_coef = 20.0
step_scale = 0.25
epsilon = 1e-06

HALO = 2 * INNER
PRODUCTS = 11
SUBLANES = 2
LANES = 2
TILES = range(SUBLANES * LANES)
VMEM_LIMIT = 24 * 1024 * 1024


def tile_of(ref, comp, at, place):
    z, y = divmod(place, LANES)
    return ref[comp, at, z * 8 : z * 8 + 8, y * 128 : y * 128 + 128]


def put(ref, comp, at, place, cells):
    z, y = divmod(place, LANES)
    ref[comp, at, z * 8 : z * 8 + 8, y * 128 : y * 128 + 128] = cells


def flat_of(ref, at, place):
    z, y = divmod(place, LANES)
    return ref[at, z * 8 : z * 8 + 8, y * 128 : y * 128 + 128]


def put_flat(ref, at, place, cells):
    z, y = divmod(place, LANES)
    ref[at, z * 8 : z * 8 + 8, y * 128 : y * 128 + 128] = cells


def vector(ref, at, place):
    return [tile_of(ref, comp, at, place) for comp in range(3)]


def around(line, axis):
    size = line[0].shape[axis]
    where = lax.broadcasted_iota(jnp.int32, line[0].shape, axis)
    first, last = where == 0, where == size - 1
    later = [pltpu.roll(cells, 1, axis) for cells in line]
    earlier = [pltpu.roll(cells, size - 1, axis) for cells in line]
    later, earlier = [0.0, *later], [*earlier, 0.0]
    return [
        jnp.where(first, later[i], later[i + 1]) + jnp.where(last, earlier[i + 1], earlier[i])
        for i in range(len(line))
    ]


def laplace(ref, comp, at):
    cells = [tile_of(ref, comp, at, place) for place in TILES]
    total = [
        (tile_of(ref, comp, at - 1, place) + tile_of(ref, comp, at + 1, place)) - 6.0 * cells[place]
        for place in TILES
    ]
    for z in range(SUBLANES):
        picked = range(z * LANES, z * LANES + LANES)
        for place, side in zip(picked, around([cells[i] for i in picked], 1)):
            total[place] = total[place] + side
    for y in range(LANES):
        picked = range(y, SUBLANES * LANES, LANES)
        for place, side in zip(picked, around([cells[i] for i in picked], 0)):
            total[place] = total[place] + side
    return cells, total


def dot(left, right):
    return left[0] * right[0] + left[1] * right[1] + left[2] * right[2]


def stiffness(square, coefs):
    plain = 0.5 - 0.125 * square
    return [plain, plain, plain + coefs]


def loop(low, high, body, carry=0):
    return lax.fori_loop(low, high, body, carry, unroll=4)


def clear_outside(tile, last_tile, refs, own):
    rows = refs[0].shape[1]

    @pl.when(tile == 0)
    def _():
        for ref in refs:
            ref[:, 0:HALO] = jnp.zeros((3, HALO) + ref.shape[2:], jnp.float32)

    @pl.when(tile == last_tile)
    def _():
        for ref in refs:
            ref[:, HALO + own :] = jnp.zeros((3, rows - HALO - own) + ref.shape[2:], jnp.float32)


def drives(m_ref, n_ref, coef_ref, fa_ref, fb_ref, fs_ref, sm_ref, sn_ref, low, high):
    def body(at, carry):
        for which, (ref, out, squares) in enumerate(
            ((m_ref, fa_ref, sm_ref), (n_ref, fb_ref, sn_ref))
        ):
            stiff = []
            for place in TILES:
                cells = vector(ref, at, place)
                square = dot(cells, cells)
                put_flat(squares, at, place, square)
                stiff.append(stiffness(square, flat_of(coef_ref, at, place)))
            for comp in range(3):
                cells, bent = laplace(ref, comp, at)
                for place in TILES:
                    drive = bent[place] + stiff[place][comp] * cells[place]
                    put(out, comp, at, place, drive)
                    if which:
                        drive = drive + tile_of(fa_ref, comp, at, place)
                        put(fs_ref, comp, at, place, drive)
        return carry

    loop(low, high, body)


def assemble(phi_ref, m_ref, n_ref, own, at, to, pieces):
    own_ref, a_ref, b_ref = pieces
    for comp in range(3):
        for place in TILES:
            phi = tile_of(own_ref, comp, at, place)
            put(phi_ref, comp, to, place, phi)
            put(m_ref, comp, to, place, phi + tile_of(a_ref, comp, at, place))
            put(n_ref, comp, to, place, phi + tile_of(b_ref, comp, at, place))


def first_kernel(
    place_ref, own_edge, own_mid, a_edge, a_mid, b_edge, b_mid, up_ref, down_ref, coef_ref,
    phi_ref, m_ref, n_ref, q_ref, r_ref, sums_ref, fa_ref, fb_ref, fs_ref, sm_ref, sn_ref
):
    own = own_edge.shape[1] + own_mid.shape[1]
    rows = own + 2 * HALO
    tile, last_tile = place_ref[1], place_ref[2] - 1
    edges, mids = (own_edge, a_edge, b_edge), (own_mid, a_mid, b_mid)
    ups, downs = ([ref.at[which] for which in (1, 0, 2)] for ref in (up_ref, down_ref))
    for pieces, low, high, shift in (
        (ups, 0, HALO, 0),
        (edges, 0, HALO, HALO),
        (mids, 0, own - 2 * HALO, 2 * HALO),
        (edges, HALO, 2 * HALO, own - HALO),
        (downs, 0, HALO, own + HALO),
    ):

        def join(at, carry, pieces=pieces, shift=shift):
            assemble(phi_ref, m_ref, n_ref, own, at, at + shift, pieces)
            return carry

        loop(low, high, join)
    drives(m_ref, n_ref, coef_ref, fa_ref, fb_ref, fs_ref, sm_ref, sn_ref, 1, rows - 1)
    clear_outside(tile, last_tile, (fa_ref, fb_ref, fs_ref), own)

    def fields(at, sums):
        adjoint = [laplace(fs_ref, comp, at)[1] for comp in range(3)]
        for place in TILES:
            phi, m, n = (vector(ref, at, place) for ref in (phi_ref, m_ref, n_ref))
            fa, fb = vector(fa_ref, at, place), vector(fb_ref, at, place)
            square_m, square_n = flat_of(sm_ref, at, place), flat_of(sn_ref, at, place)
            coefs = flat_of(coef_ref, at, place)
            stiff_m, stiff_n = stiffness(square_m, coefs), stiffness(square_n, coefs)
            turn_m, turn_n = 0.25 * dot(m, fa), 0.25 * dot(n, fb)
            gap = 0.125 * (square_m - square_n)
            rise_m = 0.25 * dot(m, phi) - 0.125 * square_m
            rise_n = 0.125 * square_n - 0.25 * dot(n, phi)
            flat, bent = [], []
            for c in range(3):
                flat.append(phi[c] * gap + m[c] * rise_m + n[c] * rise_n)
                bent.append(
                    0.25
                    * (
                        adjoint[c][place]
                        + (stiff_m[c] * fa[c] + stiff_n[c] * fb[c])
                        - (m[c] * turn_m + n[c] * turn_n)
                    )
                )
                put(q_ref, c, at, place, flat[c])
                put(r_ref, c, at, place, bent[c])
            if sums:
                behind = [2.0 * one - other for one, other in zip(phi, m)]
                ahead = [other - 2.0 * one for one, other in zip(phi, n)]
                pairs = (
                    (behind, behind), (behind, ahead), (ahead, ahead),
                    (flat, behind), (flat, ahead), (bent, behind), (bent, ahead),
                    (flat, flat), (flat, bent), (bent, bent), (fb, fb),
                )
                sums = [total + dot(left, right) for total, (left, right) in zip(sums, pairs)]
        return sums

    def rim(at, carry):
        fields(at, None)
        return carry

    loop(2, HALO, rim)
    sums = loop(HALO, HALO + own, fields, [jnp.zeros((8, 128), jnp.float32)] * PRODUCTS)
    loop(HALO + own, rows - 2, rim)
    clear_outside(tile, last_tile, (q_ref, r_ref), own)
    lane = lax.broadcasted_iota(jnp.int32, (1, 128), 1)
    result = jnp.zeros((1, 128), jnp.float32)
    for which in range(PRODUCTS):
        result = jnp.where(lane == which, jnp.sum(sums[which]), result)
    sums_ref[...] = jnp.broadcast_to(result, sums_ref.shape)


def path_scalars(place_ref, all_ref, tiles, cells):
    devices = all_ref.shape[0]
    images = devices // tiles
    table = jnp.sum(all_ref[...].reshape(images, tiles, 128), axis=1)
    lane = lax.broadcasted_iota(jnp.int32, (images, 128), 1)
    image = lax.broadcasted_iota(jnp.int32, (images, 128), 0)
    one = image[:, :1]

    def column(which):
        return jnp.sum(jnp.where(lane == which, table, 0.0), axis=1, keepdims=True)

    live = one < images - 1
    seg = jnp.where(live, jnp.sqrt(column(2) + epsilon), 0.0)
    drv = jnp.where(live, jnp.sqrt(0.25 * column(10) + epsilon), 0.0)
    path_len = jnp.sum(seg, axis=0, keepdims=True)
    tau = path_len / jnp.sum(drv, axis=0, keepdims=True)
    before = jnp.sum(jnp.where(image < lane, seg, 0.0), axis=0, keepdims=True)
    before = jnp.sum(jnp.where(image == lane, before, 0.0), axis=1, keepdims=True)
    target = one.astype(jnp.float32) / (images - 1)
    pull = spring_coef * (before / path_len - target) * (images - 1) / (2.0 * path_len)
    inv = 1.0 / tau
    near, far = inv + pull, pull - inv
    norm = near * near * column(0) + far * far * column(2) + 2.0 * near * far * column(1)
    norm += 2.0 * (near * column(3) + far * column(4))
    norm += 2.0 * tau * (near * column(5) + far * column(6))
    norm += column(7) + tau * (2.0 * column(8) + tau * column(9))
    inner = (one > 0) & (one < images - 1)
    total = jnp.sum(jnp.where(inner, norm, 0.0), axis=0, keepdims=True)
    step = step_scale / jnp.sqrt(total / cells + epsilon)
    mine = jnp.sum(jnp.where(one == place_ref[0], pull, 0.0), axis=0, keepdims=True)
    return tau[0, 0], mine[0, 0], step[0, 0]


def gradients(
    phi_ref, m_ref, n_ref, coef_ref, fa_ref, fb_ref, fs_ref, sm_ref, sn_ref, g_ref, tau, pull, out
):
    inv = 1.0 / tau
    turned = 0.25 * tau

    def grad(at, total):
        adjoint = [laplace(fs_ref, comp, at)[1] for comp in range(3)]
        for place in TILES:
            phi, m, n = (vector(ref, at, place) for ref in (phi_ref, m_ref, n_ref))
            fa, fb = vector(fa_ref, at, place), vector(fb_ref, at, place)
            square_m, square_n = flat_of(sm_ref, at, place), flat_of(sn_ref, at, place)
            coefs = flat_of(coef_ref, at, place)
            stiff_m, stiff_n = stiffness(square_m, coefs), stiffness(square_n, coefs)
            gap = 0.125 * (square_m - square_n) + 4.0 * inv
            lean_m = (
                0.25 * (dot(m, phi) - turned * dot(m, fa)) - 0.125 * square_m - (pull + inv)
            )
            lean_n = (
                0.125 * square_n - 0.25 * (dot(n, phi) + turned * dot(n, fb)) + (pull - inv)
            )
            cells = [
                phi[c] * gap
                + (m[c] * lean_m + n[c] * lean_n)
                + turned * (adjoint[c][place] + (stiff_m[c] * fa[c] + stiff_n[c] * fb[c]))
                for c in range(3)
            ]
            for c in range(3):
                put(g_ref, c, at - out, place, cells[c])
            total = total + dot(cells, cells)
        return total

    def rim(at, carry):
        grad(at, 0.0)
        return carry

    return rim, grad


def interior(place_ref):
    return jnp.where((place_ref[0] > 0) & (place_ref[0] < place_ref[3] - 1), 1.0, 0.0)


def second_kernel(
    tiles, cells, place_ref, all_ref, p_ref, m0_ref, n0_ref, q_ref, r_ref, coef_ref,
    phi_ref, m_ref, n_ref, g_ref, scal_ref, sums_ref, fa_ref, fb_ref, fs_ref, sm_ref, sn_ref
):
    rows = p_ref.shape[1]
    own = rows - 2 * HALO
    tile, last_tile = place_ref[1], place_ref[2] - 1
    tau, pull, step = path_scalars(place_ref, all_ref, tiles, cells)
    live = interior(place_ref)
    step = step * live
    inv = 1.0 / tau
    scal_ref[0] = tau
    scal_ref[1] = pull
    from_p, from_m, from_n = -4.0 * step * inv, step * (inv + pull), step * (inv - pull)
    bend = step * tau

    def update(at, carry):
        for comp in range(3):
            for place in TILES:
                p, m, n, q, r = (
                    tile_of(ref, comp, at, place) for ref in (p_ref, m0_ref, n0_ref, q_ref, r_ref)
                )
                move = (from_p * p + from_m * m) + (from_n * n - step * q) - bend * r
                put(phi_ref, comp, at, place, p + move)
                put(m_ref, comp, at, place, m + move)
                put(n_ref, comp, at, place, n + move)
        return carry

    loop(2, rows - 2, update)
    drives(m_ref, n_ref, coef_ref, fa_ref, fb_ref, fs_ref, sm_ref, sn_ref, 3, rows - 3)
    clear_outside(tile, last_tile, (fa_ref, fb_ref, fs_ref), own)
    rim, inside = gradients(
        phi_ref, m_ref, n_ref, coef_ref, fa_ref, fb_ref, fs_ref, sm_ref, sn_ref, g_ref, tau, pull, 0
    )
    loop(4, HALO, rim)
    total = loop(HALO, HALO + own, inside, jnp.zeros((8, 128), jnp.float32))
    loop(HALO + own, rows - 4, rim)
    clear_outside(tile, last_tile, (g_ref,), own)
    sums = jnp.sum(total, axis=0, keepdims=True) * live
    sums_ref[...] = jnp.broadcast_to(sums, sums_ref.shape)


def step_of(all_ref, cells):
    return step_scale / jnp.sqrt(jnp.sum(all_ref[...]) / cells + epsilon)


def third_kernel(
    cells, place_ref, scal_ref, all_ref, p_ref, m0_ref, n0_ref, h_ref, coef_ref,
    phi_ref, g_ref, sums_ref, m_ref, n_ref, fa_ref, fb_ref, fs_ref, sm_ref, sn_ref
):
    rows = p_ref.shape[1]
    own = rows - 2 * HALO
    tile, last_tile = place_ref[1], place_ref[2] - 1
    live = interior(place_ref)
    tau, pull = scal_ref[0], scal_ref[1]
    step = step_of(all_ref, cells) * live

    def update(at, carry):
        for comp in range(3):
            for place in TILES:
                move = step * tile_of(h_ref, comp, at, place)
                for old, new in ((p_ref, phi_ref), (m0_ref, m_ref), (n0_ref, n_ref)):
                    put(new, comp, at, place, tile_of(old, comp, at, place) - move)
        return carry

    loop(4, rows - 4, update)
    drives(m_ref, n_ref, coef_ref, fa_ref, fb_ref, fs_ref, sm_ref, sn_ref, 5, rows - 5)
    clear_outside(tile, last_tile, (fa_ref, fb_ref, fs_ref), own)
    _, inside = gradients(
        phi_ref, m_ref, n_ref, coef_ref, fa_ref, fb_ref, fs_ref, sm_ref, sn_ref, g_ref, tau, pull,
        HALO,
    )
    total = loop(HALO, HALO + own, inside, jnp.zeros((8, 128), jnp.float32))
    sums = jnp.sum(total, axis=0, keepdims=True) * live
    sums_ref[...] = jnp.broadcast_to(sums, sums_ref.shape)


def last_kernel(cells, place_ref, all_ref, p_ref, g_ref, edge_ref, mid_ref):
    own = g_ref.shape[1]
    step = step_of(all_ref, cells) * interior(place_ref)
    for ref, low, high, shift in (
        (edge_ref, 0, HALO, 0),
        (mid_ref, HALO, own - HALO, HALO),
        (edge_ref, own - HALO, own, own - 2 * HALO),
    ):

        def move(at, carry, ref=ref, shift=shift):
            for comp in range(3):
                for place in TILES:
                    old = tile_of(p_ref, comp, at + HALO, place)
                    put(ref, comp, at - shift, place, old - step * tile_of(g_ref, comp, at, place))
            return carry

        loop(low, high, move)


def f32(*shape):
    return jax.ShapeDtypeStruct(shape, jnp.float32)


def call(kernel, operands, outs, scratch, scalars=1, small_out=()):
    smem = pl.BlockSpec(memory_space=pltpu.SMEM)
    vmem = pl.BlockSpec(memory_space=pltpu.VMEM)
    return pl.pallas_call(
        kernel,
        out_shape=outs,
        in_specs=[smem if i < scalars else vmem for i in range(len(operands))],
        out_specs=[smem if i in small_out else vmem for i in range(len(outs))],
        scratch_shapes=[pltpu.VMEM(shape, jnp.float32) for shape in scratch],
        compiler_params=pltpu.CompilerParams(vmem_limit_bytes=VMEM_LIMIT),
    )(*operands)


def beside(cells, axis, forward):
    count = lax.axis_size(axis)
    pairs = [(i, i + 1) if forward else (i + 1, i) for i in range(count - 1)]
    return lax.ppermute(cells, axis, pairs)


def from_everyone(rows):
    return lax.all_to_all(rows, IMG_TILE, 0, 0, tiled=True)


def body(spins, aniso):
    _, comps, depth, own, width = spins.shape
    images, tiles = lax.axis_size(IMG), lax.axis_size(TILE)
    devices = images * tiles
    cells = float(images * comps * depth * own * tiles * width)
    rows = own + 2 * HALO
    place = jnp.stack(
        [lax.axis_index(IMG), lax.axis_index(TILE), jnp.int32(tiles), jnp.int32(images)]
    ).astype(jnp.int32)
    start = jnp.swapaxes(spins[0], 1, 2)
    coefs = jnp.swapaxes(aniso, 0, 1)
    coefs = jnp.concatenate(
        [beside(coefs[own - HALO :], TILE, True), coefs, beside(coefs[:HALO], TILE, False)]
    )
    edge = jnp.concatenate([start[:, :HALO], start[:, own - HALO :]], axis=1)
    mid = start[:, HALO : own - HALO]
    ext = (3, rows, depth, width)
    whole = f32(*ext)
    table = f32(devices, 128)
    scratch = [ext, ext, ext, ext[1:], ext[1:]]
    for _ in range(OUTER):
        a_edge, b_edge = beside(edge, IMG, True), beside(edge, IMG, False)
        trio = jnp.stack([a_edge, edge, b_edge])
        up = beside(trio[:, :, HALO:], TILE, True)
        down = beside(trio[:, :, :HALO], TILE, False)
        a_mid, b_mid = beside(mid, IMG, True), beside(mid, IMG, False)
        phi, m, n, q, r, sums = call(
            first_kernel,
            [place, edge, mid, a_edge, a_mid, b_edge, b_mid, up, down, coefs],
            [whole, whole, whole, whole, whole, table],
            scratch,
        )
        phi, m, n, g, scal, sums = call(
            lambda *refs: second_kernel(tiles, cells, *refs),
            [place, from_everyone(sums), phi, m, n, q, r, coefs],
            [whole, whole, whole, whole, f32(2), table],
            scratch,
            small_out=(4,),
        )
        phi, g, sums = call(
            lambda *refs: third_kernel(cells, *refs),
            [place, scal, from_everyone(sums), phi, m, n, g, coefs],
            [whole, f32(3, own, depth, width), table],
            [ext, ext, *scratch],
            scalars=2,
        )
        edge, mid = call(
            lambda *refs: last_kernel(cells, *refs),
            [place, from_everyone(sums), phi, g],
            [f32(3, 2 * HALO, depth, width), f32(3, own - 2 * HALO, depth, width)],
            [],
        )
    final = jnp.concatenate([edge[:, :HALO], mid, edge[:, HALO:]], axis=1)
    return jnp.swapaxes(final, 1, 2)[None]


def solution(mesh):
    split = Mesh(mesh.devices.reshape(4, 4, 4, 2), IMG_TILE)
    return jax.shard_map(
        body,
        mesh=split,
        in_specs=(P(IMG, None, None, TILE, None), P(None, TILE, None)),
        out_specs=P(IMG, None, None, TILE, None),
        check_vma=False,
    )
```

time: 281 us -> 234 us (0.83)
  Pallas kernels: 88.7 us -> 48.2 us
  local copies, waits for them, and re-layouts: 13.6 us -> 7.07 us
    pallas_call x8, Pallas kernels: 88.7 us -> 48.2 us  [call(): pl.pallas_call(kernel, out_shape=outs, in_specs=[smem if i < scalars else...]
    unnamed x16 -> x4, local copies, waits for them, and re-layouts: 9.16 us -> 2.64 us
where the time goes in v3:
time: 234 us; the launch traced here: 233 us
  blocking collectives  96.8 us (41%)
  Pallas kernels  48.2 us (21%)
  starting transfers between devices  43.2 us (18%)
  waiting for transfers between devices  37.1 us (16%)
  local copies, waits for them, and re-layouts  7.07 us (3%)
    all_to_all x6, blocking collectives, from_everyone(): return lax.all_to_all(rows, IMG_TILE, 0, 0, tiled=True)  96.8 us
    pallas_call x8, Pallas kernels, call(): pl.pallas_call(kernel, out_shape=outs, in_specs=[smem if i < scalars else...  48.2 us
    ppermute x14, starting transfers between devices, beside(): return lax.ppermute(cells, axis, pairs)  43.2 us
    ppermute x14, waiting for transfers between devices, beside(): return lax.ppermute(cells, axis, pairs)  37.1 us
  transfers between devices with their start and end apart: 14, of which 8 were waited for; matrix products, arithmetic and copies ran while one was open for 1% of the time, Pallas kernels for 0%

profile of v3, /device:TPU:1, one launch (start us, length us, event | category | flops | bytes accessed | tf_op | source)
XLA Modules:
  0.0 233.3 jit_solution(6291058371099422328)
XLA Ops:
  0.0 2.3 copy.17
  2.5 1.3 collective-permute-start.2
  3.8 4.7 %collective-permute-start = (f32[3,12,16,256]{3,2,1,0:T(8,128)S(1)}, f32[3,12,16,256]{3,2,1,0:T(8,128)S(1)}, u32[]{:S(2)}, u32[]{:S(2)}) collective-permute-start(f32[3,12,16,256]{3,2,1,0:T(8,128)S(1)} %get-tuple-element.82.own_edge), channel_id=1, source_target_pairs={{0,8},{8,16},{16,24},{24,32},{32,40},{40,48},{48,56},{56,64},{64,7... | collective-permute-start | bytes 1769480 | tf_op jit(solution)/shard_map/ppermute | solution.py:410
  9.8 5.0 %collective-permute-start.1 = (f32[3,20,16,256]{3,2,1,0:T(8,128)S(1)}, f32[3,20,16,256]{3,2,1,0:T(8,128)}, u32[]{:S(2)}, u32[]{:S(2)}) collective-permute-start(f32[3,20,16,256]{3,2,1,0:T(8,128)S(1)} %slice.46.own_mid), channel_id=1, source_target_pairs={{0,8},{8,16},{16,24},{24,32},{32,40},{40,48},{48,56},{56,64},{64,7... | collective-permute-start | bytes 2949128 | tf_op jit(solution)/shard_map/ppermute | solution.py:410
  14.8 4.3 %collective-permute-done.2.b_edge = f32[3,12,16,256]{3,2,1,0:T(8,128)S(1)} collective-permute-done((f32[3,12,16,256]{3,2,1,0:T(8,128)S(1)}, f32[3,12,16,256]{3,2,1,0:T(8,128)S(1)}, u32[]{:S(2)}, u32[]{:S(2)}) %collective-permute-start.2) | collective-permute-done | bytes 589856 | tf_op jit(solution)/shard_map/ppermute | solution.py:410
  20.2 1.4 fusion.2
  21.5 5.4 %collective-permute-start.5 = (f32[3,3,6,16,256]{4,3,2,1,0:T(8,128)}, f32[3,3,6,16,256]{4,3,2,1,0:T(8,128)}, u32[]{:S(2)}, u32[]{:S(2)}) collective-permute-start(f32[3,3,6,16,256]{4,3,2,1,0:T(8,128)} %get-tuple-element.75), channel_id=1, source_target_pairs={{1,0},{2,1},{3,2},{4,3},{5,4},{6,5},{7,6},{9,8},{10,9},{11,10},{12... | collective-permute-start | bytes 2654216 | tf_op jit(solution)/shard_map/ppermute | solution.py:410
  26.9 3.1 %collective-permute-start.4 = (f32[3,3,6,16,256]{4,3,2,1,0:T(8,128)}, f32[3,3,6,16,256]{4,3,2,1,0:T(8,128)}, u32[]{:S(2)}, u32[]{:S(2)}) collective-permute-start(f32[3,3,6,16,256]{4,3,2,1,0:T(8,128)} %get-tuple-element.76), channel_id=1, source_target_pairs={{0,1},{1,2},{2,3},{3,4},{4,5},{5,6},{6,7},{8,9},{9,10},{10,11},{11... | collective-permute-start | bytes 2654216 | tf_op jit(solution)/shard_map/ppermute | solution.py:410
  31.0 2.4 %collective-permute-start.6 = (f32[6,16,256]{2,1,0:T(8,128)}, f32[6,16,256]{2,1,0:T(8,128)S(1)}, u32[]{:S(2)}, u32[]{:S(2)}) collective-permute-start(f32[6,16,256]{2,1,0:T(8,128)} %get-tuple-element.83), channel_id=1, source_target_pairs={{0,1},{1,2},{2,3},{3,4},{4,5},{5,6},{6,7},{8,9},{9,10},{10,11},{11... | collective-permute-start | bytes 294920 | tf_op jit(solution)/shard_map/ppermute | solution.py:410
  33.4 7.9 %collective-permute-done.6 = f32[6,16,256]{2,1,0:T(8,128)S(1)} collective-permute-done((f32[6,16,256]{2,1,0:T(8,128)}, f32[6,16,256]{2,1,0:T(8,128)S(1)}, u32[]{:S(2)}, u32[]{:S(2)}) %collective-permute-start.6) | collective-permute-done | bytes 98336 | tf_op jit(solution)/shard_map/ppermute | solution.py:410
  41.4 1.9 collective-permute-start.7
  43.3 4.6 %collective-permute-done.7 = f32[6,16,256]{2,1,0:T(8,128)S(1)} collective-permute-done((f32[6,16,256]{2,1,0:T(8,128)S(1)}, f32[6,16,256]{2,1,0:T(8,128)S(1)}, u32[]{:S(2)}, u32[]{:S(2)}) %collective-permute-start.7) | collective-permute-done | bytes 98336 | tf_op jit(solution)/shard_map/ppermute | solution.py:410
  48.0 10.1 %shard_map.28 = (f32[3,44,16,256]{3,2,1,0:T(8,128)S(1)}, f32[3,44,16,256]{3,2,1,0:T(8,128)S(1)}, f32[3,44,16,256]{3,2,1,0:T(8,128)S(1)}, f32[3,44,16,256]{3,2,1,...) custom-call(s32[4]{0:T(128)S(1)} %pad_add_fusion.place_ref.refs_0_, ...), custom_call_target="tpu_custom_call" | custom-call | tf_op jit(solution)/shard_map/pallas_call | solution.py:397
  58.1 22.0 %all_to_all.66 = f32[128,1,128]{2,1,0:T(1,128)S(1)} all-to-all(f32[128,1,128]{2,1,0:T(1,128)S(1)} %bitcast.56), channel_id=1, replica_groups=mesh['img_0'=4,'img_1'=4,'tile_0'=4,'tile_1'=2] {'img_0','img_1','tile_0..., dimensions={0} | all-to-all | bytes 131072 | tf_op jit(solution)/shard_map/all_to_all | solution.py:414
  80.1 7.9 %shard_map.29 = (f32[3,44,16,256]{3,2,1,0:T(8,128)S(1)}, f32[3,44,16,256]{3,2,1,0:T(8,128)S(1)}, f32[3,44,16,256]{3,2,1,0:T(8,128)S(1)}, f32[3,44,16,256]{3,2,1,...) custom-call(s32[4]{0:T(128)S(1)} %pad_add_fusion.place_ref.refs_0_, f32[128,128]{1,0:T(8,128)S(1)} %bitcast.50, ...), custom_call_target="tpu_custom_call" | custom-call | tf_op jit(solution)/shard_map/pallas_call | solution.py:397
  88.0 13.9 %all_to_all.67 = f32[128,1,128]{2,1,0:T(1,128)S(1)} all-to-all(f32[128,1,128]{2,1,0:T(1,128)S(1)} %bitcast.58), channel_id=1, replica_groups=mesh['img_0'=4,'img_1'=4,'tile_0'=4,'tile_1'=2] {'img_0','img_1','tile_0..., dimensions={0} | all-to-all | bytes 131072 | tf_op jit(solution)/shard_map/all_to_all | solution.py:414
  101.9 6.0 %shard_map.30 = (f32[3,44,16,256]{3,2,1,0:T(8,128)S(1)}, f32[3,32,16,256]{3,2,1,0:T(8,128)S(1)}, f32[128,128]{1,0:T(8,128)S(1)}) custom-call(s32[4]{0:T(128)S(1)} %pad_add_fusion.place_ref.refs_0_, f32[2]{0:T(128)S(1)} %get-tuple-element.45.refs_1_, f32[128,128]{1,0:T(8,128)S(1)} %bitcast.53, f32[3,44,16,256]{3,2,1,0:T(8,128)S(1)} %get-tuple-element.47.refs_3_, ...), custom_call_target="tpu_custom_call" | custom-call | tf_op jit(solution)/shard_map/pallas_call | solution.py:397
  107.9 13.9 %all_to_all.68 = f32[128,1,128]{2,1,0:T(1,128)S(1)} all-to-all(f32[128,1,128]{2,1,0:T(1,128)S(1)} %bitcast.61), channel_id=1, replica_groups=mesh['img_0'=4,'img_1'=4,'tile_0'=4,'tile_1'=2] {'img_0','img_1','tile_0..., dimensions={0} | all-to-all | bytes 131072 | tf_op jit(solution)/shard_map/all_to_all | solution.py:414
  122.7 1.3 collective-permute-start.10
  124.0 4.0 %collective-permute-start.8 = (f32[3,12,16,256]{3,2,1,0:T(8,128)S(1)}, f32[3,12,16,256]{3,2,1,0:T(8,128)S(1)}, u32[]{:S(2)}, u32[]{:S(2)}) collective-permute-start(f32[3,12,16,256]{3,2,1,0:T(8,128)S(1)} %get-tuple-element.54.own_edge), channel_id=1, source_target_pairs={{0,8},{8,16},{16,24},{24,32},{32,40},{40,48},{48,56},{56,64},{64,7... | collective-permute-start | bytes 1769480 | tf_op jit(solution)/shard_map/ppermute | solution.py:410
  129.3 4.0 %collective-permute-start.9 = (f32[3,20,16,256]{3,2,1,0:T(8,128)S(1)}, f32[3,20,16,256]{3,2,1,0:T(8,128)S(1)}, u32[]{:S(2)}, u32[]{:S(2)}) collective-permute-start(f32[3,20,16,256]{3,2,1,0:T(8,128)S(1)} %get-tuple-element.55.own_mid), channel_id=1, source_target_pairs={{0,8},{8,16},{16,24},{24,32},{32,40},{40,48},{48,56},{56,64},{64,7... | collective-permute-start | bytes 2949128 | tf_op jit(solution)/shard_map/ppermute | solution.py:410
  133.4 5.3 %collective-permute-done.10.b_edge = f32[3,12,16,256]{3,2,1,0:T(8,128)S(1)} collective-permute-done((f32[3,12,16,256]{3,2,1,0:T(8,128)S(1)}, f32[3,12,16,256]{3,2,1,0:T(8,128)S(1)}, u32[]{:S(2)}, u32[]{:S(2)}) %collective-permute-start.10) | collective-permute-done | bytes 589856 | tf_op jit(solution)/shard_map/ppermute | solution.py:410
  139.9 5.4 %collective-permute-start.13 = (f32[3,3,6,16,256]{4,3,2,1,0:T(8,128)S(1)}, f32[3,3,6,16,256]{4,3,2,1,0:T(8,128)S(1)}, u32[]{:S(2)}, u32[]{:S(2)}) collective-permute-start(f32[3,3,6,16,256]{4,3,2,1,0:T(8,128)S(1)} %get-tuple-element.73), channel_id=1, source_target_pairs={{1,0},{2,1},{3,2},{4,3},{5,4},{6,5},{7,6},{9,8},{10,9},{11,10},{12... | collective-permute-start | bytes 2654216 | tf_op jit(solution)/shard_map/ppermute | solution.py:410
  145.4 2.1 collective-permute-start.12
  147.5 12.3 %collective-permute-done.11.b_mid = f32[3,20,16,256]{3,2,1,0:T(8,128)S(1)} collective-permute-done((f32[3,20,16,256]{3,2,1,0:T(8,128)S(1)}, f32[3,20,16,256]{3,2,1,0:T(8,128)S(1)}, u32[]{:S(2)}, u32[]{:S(2)}) %collective-permute-start.11) | collective-permute-done | bytes 983072 | tf_op jit(solution)/shard_map/ppermute | solution.py:410
  160.7 8.7 %shard_map.32 = (f32[3,44,16,256]{3,2,1,0:T(8,128)S(1)}, f32[3,44,16,256]{3,2,1,0:T(8,128)S(1)}, f32[3,44,16,256]{3,2,1,0:T(8,128)S(1)}, f32[3,44,16,256]{3,2,1,...) custom-call(s32[4]{0:T(128)S(1)} %pad_add_fusion.place_ref.refs_0_, ...), custom_call_target="tpu_custom_call" | custom-call | tf_op jit(solution)/shard_map/pallas_call | solution.py:397
  169.4 19.1 %all_to_all.69 = f32[128,1,128]{2,1,0:T(1,128)S(1)} all-to-all(f32[128,1,128]{2,1,0:T(1,128)S(1)} %bitcast.57), channel_id=1, replica_groups=mesh['img_0'=4,'img_1'=4,'tile_0'=4,'tile_1'=2] {'img_0','img_1','tile_0..., dimensions={0} | all-to-all | bytes 131072 | tf_op jit(solution)/shard_map/all_to_all | solution.py:414
  188.5 7.8 %shard_map.33 = (f32[3,44,16,256]{3,2,1,0:T(8,128)S(1)}, f32[3,44,16,256]{3,2,1,0:T(8,128)S(1)}, f32[3,44,16,256]{3,2,1,0:T(8,128)S(1)}, f32[3,44,16,256]{3,2,1,...) custom-call(s32[4]{0:T(128)S(1)} %pad_add_fusion.place_ref.refs_0_, f32[128,128]{1,0:T(8,128)S(1)} %bitcast.51, ...), custom_call_target="tpu_custom_call" | custom-call | tf_op jit(solution)/shard_map/pallas_call | solution.py:397
  196.2 13.9 %all_to_all.70 = f32[128,1,128]{2,1,0:T(1,128)S(1)} all-to-all(f32[128,1,128]{2,1,0:T(1,128)S(1)} %bitcast.59), channel_id=1, replica_groups=mesh['img_0'=4,'img_1'=4,'tile_0'=4,'tile_1'=2] {'img_0','img_1','tile_0..., dimensions={0} | all-to-all | bytes 131072 | tf_op jit(solution)/shard_map/all_to_all | solution.py:414
  210.2 6.0 %shard_map.34 = (f32[3,44,16,256]{3,2,1,0:T(8,128)S(1)}, f32[3,32,16,256]{3,2,1,0:T(8,128)S(1)}, f32[128,128]{1,0:T(8,128)S(1)}) custom-call(s32[4]{0:T(128)S(1)} %pad_add_fusion.place_ref.refs_0_, f32[2]{0:T(128)S(1)} %get-tuple-element.62.refs_1_, f32[128,128]{1,0:T(8,128)S(1)} %bitcast.52, f32[3,44,16,256]{3,2,1,0:T(8,128)S(1)} %get-tuple-element.64.refs_3_, ...), custom_call_target="tpu_custom_call" | custom-call | tf_op jit(solution)/shard_map/pallas_call | solution.py:397
  216.1 13.9 %all_to_all.71 = f32[128,1,128]{2,1,0:T(1,128)S(1)} all-to-all(f32[128,1,128]{2,1,0:T(1,128)S(1)} %bitcast.60), channel_id=1, replica_groups=mesh['img_0'=4,'img_1'=4,'tile_0'=4,'tile_1'=2] {'img_0','img_1','tile_0..., dimensions={0} | all-to-all | bytes 131072 | tf_op jit(solution)/shard_map/all_to_all | solution.py:414
  231.2 2.1 copy.14
  (27 shorter events, 9.0 us)
Async XLA Ops:
  2.5 16.7 %collective-permute-start.2 = (f32[3,12,16,256]{3,2,1,0:T(8,128)S(1)}, f32[3,12,16,256]{3,2,1,0:T(8,128)S(1)}, u32[]{:S(2)}, u32[]{:S(2)}) collective-permute-start(f32[3,12,16,256]{3,2,1,0:T(8,128)S(1)} %get-tuple-element.82.own_edge), channel_id=1, source_target_pairs={{8,0},{16,8},{24,16},{32,24},{40,32},{48,40},{56,48},{64,56},{72,6... | collective-permute-start | bytes 1769480 | tf_op jit(solution)/shard_map/ppermute | solution.py:410
  3.8 16.2 %collective-permute-start = (f32[3,12,16,256]{3,2,1,0:T(8,128)S(1)}, f32[3,12,16,256]{3,2,1,0:T(8,128)S(1)}, u32[]{:S(2)}, u32[]{:S(2)}) collective-permute-start(f32[3,12,16,256]{3,2,1,0:T(8,128)S(1)} %get-tuple-element.82.own_edge), channel_id=1, source_target_pairs={{0,8},{8,16},{16,24},{24,32},{32,40},{40,48},{48,56},{56,64},{64,7... | collective-permute-start | bytes 1769480 | tf_op jit(solution)/shard_map/ppermute | solution.py:410
  8.5 39.4 %collective-permute-start.3 = (f32[3,20,16,256]{3,2,1,0:T(8,128)S(1)}, f32[3,20,16,256]{3,2,1,0:T(8,128)}, u32[]{:S(2)}, u32[]{:S(2)}) collective-permute-start(f32[3,20,16,256]{3,2,1,0:T(8,128)S(1)} %slice.46.own_mid), channel_id=1, source_target_pairs={{8,0},{16,8},{24,16},{32,24},{40,32},{48,40},{56,48},{64,56},{72,6... | collective-permute-start | bytes 2949128 | tf_op jit(solution)/shard_map/ppermute | solution.py:410
  9.8 38.1 %collective-permute-start.1 = (f32[3,20,16,256]{3,2,1,0:T(8,128)S(1)}, f32[3,20,16,256]{3,2,1,0:T(8,128)}, u32[]{:S(2)}, u32[]{:S(2)}) collective-permute-start(f32[3,20,16,256]{3,2,1,0:T(8,128)S(1)} %slice.46.own_mid), channel_id=1, source_target_pairs={{0,8},{8,16},{16,24},{24,32},{32,40},{40,48},{48,56},{56,64},{64,7... | collective-permute-start | bytes 2949128 | tf_op jit(solution)/shard_map/ppermute | solution.py:410
  20.1 9.9 %copy-start = (f32[16,32,256]{2,1,0:T(8,128)S(1)}, f32[16,32,256]{2,1,0:T(8,128)}, u32[]{:S(2)}) copy-start(f32[16,32,256]{2,1,0:T(8,128)} %param.3) | copy-start | bytes 1572868
  21.5 26.5 %collective-permute-start.5 = (f32[3,3,6,16,256]{4,3,2,1,0:T(8,128)}, f32[3,3,6,16,256]{4,3,2,1,0:T(8,128)}, u32[]{:S(2)}, u32[]{:S(2)}) collective-permute-start(f32[3,3,6,16,256]{4,3,2,1,0:T(8,128)} %get-tuple-element.75), channel_id=1, source_target_pairs={{1,0},{2,1},{3,2},{4,3},{5,4},{6,5},{7,6},{9,8},{10,9},{11,10},{12... | collective-permute-start | bytes 2654216 | tf_op jit(solution)/shard_map/ppermute | solution.py:410
  26.9 21.1 %collective-permute-start.4 = (f32[3,3,6,16,256]{4,3,2,1,0:T(8,128)}, f32[3,3,6,16,256]{4,3,2,1,0:T(8,128)}, u32[]{:S(2)}, u32[]{:S(2)}) collective-permute-start(f32[3,3,6,16,256]{4,3,2,1,0:T(8,128)} %get-tuple-element.76), channel_id=1, source_target_pairs={{0,1},{1,2},{2,3},{3,4},{4,5},{5,6},{6,7},{8,9},{9,10},{10,11},{11... | collective-permute-start | bytes 2654216 | tf_op jit(solution)/shard_map/ppermute | solution.py:410
  31.0 10.3 %collective-permute-start.6 = (f32[6,16,256]{2,1,0:T(8,128)}, f32[6,16,256]{2,1,0:T(8,128)S(1)}, u32[]{:S(2)}, u32[]{:S(2)}) collective-permute-start(f32[6,16,256]{2,1,0:T(8,128)} %get-tuple-element.83), channel_id=1, source_target_pairs={{0,1},{1,2},{2,3},{3,4},{4,5},{5,6},{6,7},{8,9},{9,10},{10,11},{11... | collective-permute-start | bytes 294920 | tf_op jit(solution)/shard_map/ppermute | solution.py:410
  41.4 6.6 %collective-permute-start.7 = (f32[6,16,256]{2,1,0:T(8,128)S(1)}, f32[6,16,256]{2,1,0:T(8,128)S(1)}, u32[]{:S(2)}, u32[]{:S(2)}) collective-permute-start(f32[6,16,256]{2,1,0:T(8,128)S(1)} %get-tuple-element.84), channel_id=1, source_target_pairs={{1,0},{2,1},{3,2},{4,3},{5,4},{6,5},{7,6},{9,8},{10,9},{11,10},{12... | collective-permute-start | bytes 294920 | tf_op jit(solution)/shard_map/ppermute | solution.py:410
  122.7 16.0 %collective-permute-start.10 = (f32[3,12,16,256]{3,2,1,0:T(8,128)S(1)}, f32[3,12,16,256]{3,2,1,0:T(8,128)S(1)}, u32[]{:S(2)}, u32[]{:S(2)}) collective-permute-start(f32[3,12,16,256]{3,2,1,0:T(8,128)S(1)} %get-tuple-element.54.own_edge), channel_id=1, source_target_pairs={{8,0},{16,8},{24,16},{32,24},{40,32},{48,40},{56,48},{64,56},{72,6... | collective-permute-start | bytes 1769480 | tf_op jit(solution)/shard_map/ppermute | solution.py:410
  124.0 15.6 %collective-permute-start.8 = (f32[3,12,16,256]{3,2,1,0:T(8,128)S(1)}, f32[3,12,16,256]{3,2,1,0:T(8,128)S(1)}, u32[]{:S(2)}, u32[]{:S(2)}) collective-permute-start(f32[3,12,16,256]{3,2,1,0:T(8,128)S(1)} %get-tuple-element.54.own_edge), channel_id=1, source_target_pairs={{0,8},{8,16},{16,24},{24,32},{32,40},{40,48},{48,56},{56,64},{64,7... | collective-permute-start | bytes 1769480 | tf_op jit(solution)/shard_map/ppermute | solution.py:410
  128.1 31.7 %collective-permute-start.11 = (f32[3,20,16,256]{3,2,1,0:T(8,128)S(1)}, f32[3,20,16,256]{3,2,1,0:T(8,128)S(1)}, u32[]{:S(2)}, u32[]{:S(2)}) collective-permute-start(f32[3,20,16,256]{3,2,1,0:T(8,128)S(1)} %get-tuple-element.55.own_mid), channel_id=1, source_target_pairs={{8,0},{16,8},{24,16},{32,24},{40,32},{48,40},{56,48},{64,56},{72,6... | collective-permute-start | bytes 2949128 | tf_op jit(solution)/shard_map/ppermute | solution.py:410
  129.3 31.3 %collective-permute-start.9 = (f32[3,20,16,256]{3,2,1,0:T(8,128)S(1)}, f32[3,20,16,256]{3,2,1,0:T(8,128)S(1)}, u32[]{:S(2)}, u32[]{:S(2)}) collective-permute-start(f32[3,20,16,256]{3,2,1,0:T(8,128)S(1)} %get-tuple-element.55.own_mid), channel_id=1, source_target_pairs={{0,8},{8,16},{16,24},{24,32},{32,40},{40,48},{48,56},{56,64},{64,7... | collective-permute-start | bytes 2949128 | tf_op jit(solution)/shard_map/ppermute | solution.py:410
  139.9 20.7 %collective-permute-start.13 = (f32[3,3,6,16,256]{4,3,2,1,0:T(8,128)S(1)}, f32[3,3,6,16,256]{4,3,2,1,0:T(8,128)S(1)}, u32[]{:S(2)}, u32[]{:S(2)}) collective-permute-start(f32[3,3,6,16,256]{4,3,2,1,0:T(8,128)S(1)} %get-tuple-element.73), channel_id=1, source_target_pairs={{1,0},{2,1},{3,2},{4,3},{5,4},{6,5},{7,6},{9,8},{10,9},{11,10},{12... | collective-permute-start | bytes 2654216 | tf_op jit(solution)/shard_map/ppermute | solution.py:410
  145.4 15.3 %collective-permute-start.12 = (f32[3,3,6,16,256]{4,3,2,1,0:T(8,128)S(1)}, f32[3,3,6,16,256]{4,3,2,1,0:T(8,128)S(1)}, u32[]{:S(2)}, u32[]{:S(2)}) collective-permute-start(f32[3,3,6,16,256]{4,3,2,1,0:T(8,128)S(1)} %get-tuple-element.74), channel_id=1, source_target_pairs={{0,1},{1,2},{2,3},{3,4},{4,5},{5,6},{6,7},{8,9},{9,10},{10,11},{11... | collective-permute-start | bytes 2654216 | tf_op jit(solution)/shard_map/ppermute | solution.py:410

commit v4 on v3

--- a/solution.py
+++ b/solution.py
@@ -105,64 +105,34 @@
             ref[:, HALO + own :] = jnp.zeros((3, rows - HALO - own) + ref.shape[2:], jnp.float32)
 
 
-def drives(m_ref, n_ref, coef_ref, fa_ref, fb_ref, fs_ref, sm_ref, sn_ref, low, high):
-    def body(at, carry):
-        for which, (ref, out, squares) in enumerate(
-            ((m_ref, fa_ref, sm_ref), (n_ref, fb_ref, sn_ref))
+def block(phi_ref, m_ref, n_ref, lm_ref, ln_ref, q_ref, r_ref, coef_ref, offset, scratch, cuts, clear, sums):
+    fa_ref, fb_ref, fs_ref, sm_ref, sn_ref = scratch
+    rows = phi_ref.shape[1]
+
+    def drive(at, carry):
+        for ref, lap_ref, out, squares, before in (
+            (m_ref, lm_ref, fa_ref, sm_ref, None),
+            (n_ref, ln_ref, fb_ref, sn_ref, (fa_ref, fs_ref)),
         ):
             stiff = []
             for place in TILES:
                 cells = vector(ref, at, place)
                 square = dot(cells, cells)
                 put_flat(squares, at, place, square)
-                stiff.append(stiffness(square, flat_of(coef_ref, at, place)))
+                stiff.append(stiffness(square, flat_of(coef_ref, at + offset, place)))
             for comp in range(3):
                 cells, bent = laplace(ref, comp, at)
                 for place in TILES:
-                    drive = bent[place] + stiff[place][comp] * cells[place]
-                    put(out, comp, at, place, drive)
-                    if which:
-                        drive = drive + tile_of(fa_ref, comp, at, place)
-                        put(fs_ref, comp, at, place, drive)
+                    put(lap_ref, comp, at, place, bent[place])
+                    total = bent[place] + stiff[place][comp] * cells[place]
+                    put(out, comp, at, place, total)
+                    if before is not None:
+                        total = total + tile_of(fa_ref, comp, at, place)
+                        put(fs_ref, comp, at, place, total)
         return carry
 
-    loop(low, high, body)
-
-
-def assemble(phi_ref, m_ref, n_ref, own, at, to, pieces):
-    own_ref, a_ref, b_ref = pieces
-    for comp in range(3):
-        for place in TILES:
-            phi = tile_of(own_ref, comp, at, place)
-            put(phi_ref, comp, to, place, phi)
-            put(m_ref, comp, to, place, phi + tile_of(a_ref, comp, at, place))
-            put(n_ref, comp, to, place, phi + tile_of(b_ref, comp, at, place))
-
-
-def first_kernel(
-    place_ref, own_edge, own_mid, a_edge, a_mid, b_edge, b_mid, up_ref, down_ref, coef_ref,
-    phi_ref, m_ref, n_ref, q_ref, r_ref, sums_ref, fa_ref, fb_ref, fs_ref, sm_ref, sn_ref
-):
-    own = own_edge.shape[1] + own_mid.shape[1]
-    rows = own + 2 * HALO
-    tile, last_tile = place_ref[1], place_ref[2] - 1
-    edges, mids = (own_edge, a_edge, b_edge), (own_mid, a_mid, b_mid)
-    ups, downs = ([ref.at[which] for which in (1, 0, 2)] for ref in (up_ref, down_ref))
-    for pieces, low, high, shift in (
-        (ups, 0, HALO, 0),
-        (edges, 0, HALO, HALO),
-        (mids, 0, own - 2 * HALO, 2 * HALO),
-        (edges, HALO, 2 * HALO, own - HALO),
-        (downs, 0, HALO, own + HALO),
-    ):
-
-        def join(at, carry, pieces=pieces, shift=shift):
-            assemble(phi_ref, m_ref, n_ref, own, at, at + shift, pieces)
-            return carry
-
-        loop(low, high, join)
-    drives(m_ref, n_ref, coef_ref, fa_ref, fb_ref, fs_ref, sm_ref, sn_ref, 1, rows - 1)
-    clear_outside(tile, last_tile, (fa_ref, fb_ref, fs_ref), own)
+    loop(1, rows - 1, drive)
+    clear((fa_ref, fb_ref, fs_ref))
 
     def fields(at, sums):
         adjoint = [laplace(fs_ref, comp, at)[1] for comp in range(3)]
@@ -170,7 +140,7 @@
             phi, m, n = (vector(ref, at, place) for ref in (phi_ref, m_ref, n_ref))
             fa, fb = vector(fa_ref, at, place), vector(fb_ref, at, place)
             square_m, square_n = flat_of(sm_ref, at, place), flat_of(sn_ref, at, place)
-            coefs = flat_of(coef_ref, at, place)
+            coefs = flat_of(coef_ref, at + offset, place)
             stiff_m, stiff_n = stiffness(square_m, coefs), stiffness(square_n, coefs)
             turn_m, turn_n = 0.25 * dot(m, fa), 0.25 * dot(n, fb)
             gap = 0.125 * (square_m - square_n)
@@ -204,10 +174,82 @@
         fields(at, None)
         return carry
 
-    loop(2, HALO, rim)
-    sums = loop(HALO, HALO + own, fields, [jnp.zeros((8, 128), jnp.float32)] * PRODUCTS)
-    loop(HALO + own, rows - 2, rim)
-    clear_outside(tile, last_tile, (q_ref, r_ref), own)
+    loop(2, cuts[0], rim)
+    sums = loop(cuts[0], cuts[1], fields, sums)
+    loop(cuts[1], rows - 2, rim)
+    clear((q_ref, r_ref))
+    return sums
+
+
+def join(pieces, outs, low, high, shift):
+    own_ref, a_ref, b_ref = pieces
+    phi_ref, m_ref, n_ref = outs
+
+    def one(at, carry):
+        for comp in range(3):
+            for place in TILES:
+                phi = tile_of(own_ref, comp, at, place)
+                put(phi_ref, comp, at + shift, place, phi)
+                put(m_ref, comp, at + shift, place, phi + tile_of(a_ref, comp, at, place))
+                put(n_ref, comp, at + shift, place, phi + tile_of(b_ref, comp, at, place))
+        return carry
+
+    loop(low, high, one)
+
+
+def ends_kernel(
+    place_ref, own_edge, a_edge, b_edge, up_ref, down_ref, coef_ref,
+    phi_ref, m_ref, n_ref, lm_ref, ln_ref, q_ref, r_ref, sums_ref,
+    fa_ref, fb_ref, fs_ref, sm_ref, sn_ref
+):
+    tile, last_tile = place_ref[1], place_ref[2] - 1
+    span = 2 * HALO
+    fields = (phi_ref, m_ref, n_ref, lm_ref, ln_ref, q_ref, r_ref)
+    scratch = (fa_ref, fb_ref, fs_ref, sm_ref, sn_ref)
+    halos = [[ref.at[3 * which : 3 * which + 3] for which in (1, 0, 2)] for ref in (up_ref, down_ref)]
+    edges = (own_edge, a_edge, b_edge)
+    sums = [jnp.zeros((8, 128), jnp.float32)] * PRODUCTS
+    for top in (True, False):
+        first = 0 if top else span
+        here = [ref.at[:, first : first + span] for ref in fields]
+        join(halos[0 if top else 1], here[:3], 0, HALO, 0 if top else HALO)
+        if top:
+            join(edges, here[:3], 0, HALO, HALO)
+        else:
+            join(edges, here[:3], HALO, span, -HALO)
+
+        def clear(refs, top=top):
+            outside = slice(0, HALO) if top else slice(HALO, span)
+
+            @pl.when(tile == (0 if top else last_tile))
+            def _():
+                for ref in refs:
+                    ref[:, outside] = jnp.zeros((3, HALO) + ref.shape[2:], jnp.float32)
+
+        cuts = (HALO, span - 2) if top else (2, HALO)
+        offset = 0 if top else coef_ref.shape[0] - span
+        sums = block(*here, coef_ref, offset, scratch, cuts, clear, sums)
+    for which in range(PRODUCTS):
+        sums_ref[which] = sums[which]
+
+
+def middle_kernel(
+    place_ref, own_mid, a_mid, b_mid, phi_end, m_end, n_end, part_ref, coef_ref,
+    phi_ref, m_ref, n_ref, lm_ref, ln_ref, q_ref, r_ref, sums_ref,
+    fa_ref, fb_ref, fs_ref, sm_ref, sn_ref
+):
+    span = 2 * HALO
+    rows = phi_ref.shape[1]
+    outs = (phi_ref, m_ref, n_ref)
+    for end, ref in zip((phi_end, m_end, n_end), outs):
+        ref[:, 0:4] = end[:, span - 4 : span]
+        ref[:, rows - 4 :] = end[:, span : span + 4]
+    join((own_mid, a_mid, b_mid), outs, 0, rows - 8, 4)
+    sums = block(
+        *outs, lm_ref, ln_ref, q_ref, r_ref, coef_ref, span - 4,
+        (fa_ref, fb_ref, fs_ref, sm_ref, sn_ref), (2, rows - 2), lambda refs: None,
+        [part_ref[which] for which in range(PRODUCTS)],
+    )
     lane = lax.broadcasted_iota(jnp.int32, (1, 128), 1)
     result = jnp.zeros((1, 128), jnp.float32)
     for which in range(PRODUCTS):
@@ -291,12 +333,55 @@
     return jnp.where((place_ref[0] > 0) & (place_ref[0] < place_ref[3] - 1), 1.0, 0.0)
 
 
-def second_kernel(
-    tiles, cells, place_ref, all_ref, p_ref, m0_ref, n0_ref, q_ref, r_ref, coef_ref,
-    phi_ref, m_ref, n_ref, g_ref, scal_ref, sums_ref, fa_ref, fb_ref, fs_ref, sm_ref, sn_ref
+def advance(
+    step_ref, scale, old, old_shift, new, coef_ref, scratch, low, high, keep
 ):
-    rows = p_ref.shape[1]
+    p_ref, m0_ref, n0_ref, lm0_ref, ln0_ref = old
+    phi_ref, m_ref, n_ref, lm_ref, ln_ref = new
+    fa_ref, fb_ref, fs_ref, sm_ref, sn_ref = scratch
+
+    def body(at, carry):
+        was = at + old_shift
+        moves, bends = [], []
+        for comp in range(3):
+            cells, bent = laplace(step_ref, comp, at)
+            if scale is not None:
+                cells, bent = [scale * cell for cell in cells], [scale * cell for cell in bent]
+            moves.append(cells)
+            bends.append(bent)
+            for place in TILES:
+                put(phi_ref, comp, at, place, tile_of(p_ref, comp, was, place) + cells[place])
+        for ref, lap_old, out, lap_new, drive_ref, squares, last in (
+            (m0_ref, lm0_ref, m_ref, lm_ref, fa_ref, sm_ref, False),
+            (n0_ref, ln0_ref, n_ref, ln_ref, fb_ref, sn_ref, True),
+        ):
+            for place in TILES:
+                cells = [tile_of(ref, comp, was, place) + moves[comp][place] for comp in range(3)]
+                square = dot(cells, cells)
+                put_flat(squares, at, place, square)
+                stiff = stiffness(square, flat_of(coef_ref, at, place))
+                for comp in range(3):
+                    put(out, comp, at, place, cells[comp])
+                    bent = tile_of(lap_old, comp, was, place) + bends[comp][place]
+                    if keep:
+                        put(lap_new, comp, at, place, bent)
+                    total = bent + stiff[comp] * cells[comp]
+                    put(drive_ref, comp, at, place, total)
+                    if last:
+                        total = total + tile_of(fa_ref, comp, at, place)
+                        put(fs_ref, comp, at, place, total)
+        return carry
+
+    loop(low, high, body)
+
+
+def second_kernel(tiles, cells, place_ref, all_ref, *refs):
+    ends, mids, refs = refs[:7], refs[7:14], refs[14:]
+    coef_ref, phi_ref, m_ref, n_ref, lm_ref, ln_ref, g_ref, scal_ref, sums_ref, d_ref = refs[:10]
+    scratch = refs[10:]
+    rows = phi_ref.shape[1]
     own = rows - 2 * HALO
+    span = 2 * HALO
     tile, last_tile = place_ref[1], place_ref[2] - 1
     tau, pull, step = path_scalars(place_ref, all_ref, tiles, cells)
     live = interior(place_ref)
@@ -306,21 +391,30 @@
     scal_ref[1] = pull
     from_p, from_m, from_n = -4.0 * step * inv, step * (inv + pull), step * (inv - pull)
     bend = step * tau
-
-    def update(at, carry):
-        for comp in range(3):
-            for place in TILES:
-                p, m, n, q, r = (
-                    tile_of(ref, comp, at, place) for ref in (p_ref, m0_ref, n0_ref, q_ref, r_ref)
-                )
-                move = (from_p * p + from_m * m) + (from_n * n - step * q) - bend * r
-                put(phi_ref, comp, at, place, p + move)
-                put(m_ref, comp, at, place, m + move)
-                put(n_ref, comp, at, place, n + move)
-        return carry
-
-    loop(2, rows - 2, update)
-    drives(m_ref, n_ref, coef_ref, fa_ref, fb_ref, fs_ref, sm_ref, sn_ref, 3, rows - 3)
+    regions = (
+        (ends, 2, span - 2, 0),
+        (mids, span - 2, rows - span + 2, 4 - span),
+        (ends, rows - span + 2, rows - 2, 2 * span - rows),
+    )
+    for here, low, high, shift in regions:
+
+        def direction(at, carry, here=here, shift=shift):
+            was = at + shift
+            for comp in range(3):
+                for place in TILES:
+                    p, m, n, q, r = (
+                        tile_of(here[i], comp, was, place) for i in (0, 1, 2, 5, 6)
+                    )
+                    move = (from_p * p + from_m * m) + (from_n * n - step * q) - bend * r
+                    put(d_ref, comp, at, place, move)
+            return carry
+
+        loop(low, high, direction)
+    new = (phi_ref, m_ref, n_ref, lm_ref, ln_ref)
+    for here, low, high, shift in regions:
+        low, high = max(low, 3), min(high, rows - 3)
+        advance(d_ref, None, here[:5], shift, new, coef_ref, scratch, low, high, True)
+    fa_ref, fb_ref, fs_ref, sm_ref, sn_ref = scratch
     clear_outside(tile, last_tile, (fa_ref, fb_ref, fs_ref), own)
     rim, inside = gradients(
         phi_ref, m_ref, n_ref, coef_ref, fa_ref, fb_ref, fs_ref, sm_ref, sn_ref, g_ref, tau, pull, 0
@@ -338,7 +432,7 @@
 
 
 def third_kernel(
-    cells, place_ref, scal_ref, all_ref, p_ref, m0_ref, n0_ref, h_ref, coef_ref,
+    cells, place_ref, scal_ref, all_ref, p_ref, m0_ref, n0_ref, lm0_ref, ln0_ref, h_ref, coef_ref,
     phi_ref, g_ref, sums_ref, m_ref, n_ref, fa_ref, fb_ref, fs_ref, sm_ref, sn_ref
 ):
     rows = p_ref.shape[1]
@@ -347,17 +441,11 @@
     live = interior(place_ref)
     tau, pull = scal_ref[0], scal_ref[1]
     step = step_of(all_ref, cells) * live
-
-    def update(at, carry):
-        for comp in range(3):
-            for place in TILES:
-                move = step * tile_of(h_ref, comp, at, place)
-                for old, new in ((p_ref, phi_ref), (m0_ref, m_ref), (n0_ref, n_ref)):
-                    put(new, comp, at, place, tile_of(old, comp, at, place) - move)
-        return carry
-
-    loop(4, rows - 4, update)
-    drives(m_ref, n_ref, coef_ref, fa_ref, fb_ref, fs_ref, sm_ref, sn_ref, 5, rows - 5)
+    advance(
+        h_ref, -step, (p_ref, m0_ref, n0_ref, lm0_ref, ln0_ref), 0,
+        (phi_ref, m_ref, n_ref, None, None), coef_ref,
+        (fa_ref, fb_ref, fs_ref, sm_ref, sn_ref), HALO - 1, HALO + own + 1, False,
+    )
     clear_outside(tile, last_tile, (fa_ref, fb_ref, fs_ref), own)
     _, inside = gradients(
         phi_ref, m_ref, n_ref, coef_ref, fa_ref, fb_ref, fs_ref, sm_ref, sn_ref, g_ref, tau, pull,
@@ -425,39 +513,53 @@
     ).astype(jnp.int32)
     start = jnp.swapaxes(spins[0], 1, 2)
     coefs = jnp.swapaxes(aniso, 0, 1)
-    coefs = jnp.concatenate(
-        [beside(coefs[own - HALO :], TILE, True), coefs, beside(coefs[:HALO], TILE, False)]
-    )
     edge = jnp.concatenate([start[:, :HALO], start[:, own - HALO :]], axis=1)
     mid = start[:, HALO : own - HALO]
     ext = (3, rows, depth, width)
+    ends, middle = (3, 4 * HALO, depth, width), (3, own - 4, depth, width)
     whole = f32(*ext)
     table = f32(devices, 128)
-    scratch = [ext, ext, ext, ext[1:], ext[1:]]
+    coef_ext = None
+
+    def scratch(count):
+        return [(3, count, depth, width)] * 3 + [(count, depth, width)] * 2
+
     for _ in range(OUTER):
         a_edge, b_edge = beside(edge, IMG, True), beside(edge, IMG, False)
-        trio = jnp.stack([a_edge, edge, b_edge])
-        up = beside(trio[:, :, HALO:], TILE, True)
-        down = beside(trio[:, :, :HALO], TILE, False)
         a_mid, b_mid = beside(mid, IMG, True), beside(mid, IMG, False)
-        phi, m, n, q, r, sums = call(
-            first_kernel,
-            [place, edge, mid, a_edge, a_mid, b_edge, b_mid, up, down, coefs],
-            [whole, whole, whole, whole, whole, table],
-            scratch,
+        heads = [cells_[:, :HALO] for cells_ in (a_edge, edge, b_edge)]
+        tails = [cells_[:, HALO:] for cells_ in (a_edge, edge, b_edge)]
+        if coef_ext is None:
+            heads.append(coefs[None, :HALO])
+            tails.append(coefs[None, own - HALO :])
+        up = beside(jnp.concatenate(tails), TILE, True)
+        down = beside(jnp.concatenate(heads), TILE, False)
+        if coef_ext is None:
+            coef_ext = jnp.concatenate([up[9], coefs, down[9]])
+        *far, part = call(
+            ends_kernel,
+            [place, edge, a_edge, b_edge, up, down, coef_ext],
+            [f32(*ends)] * 7 + [f32(PRODUCTS, 8, 128)],
+            scratch(2 * HALO),
         )
-        phi, m, n, g, scal, sums = call(
+        *near, sums = call(
+            middle_kernel,
+            [place, mid, a_mid, b_mid, *far[:3], part, coef_ext],
+            [f32(*middle)] * 7 + [table],
+            scratch(own - 4),
+        )
+        phi, m, n, lm, ln, g, scal, sums = call(
             lambda *refs: second_kernel(tiles, cells, *refs),
-            [place, from_everyone(sums), phi, m, n, q, r, coefs],
-            [whole, whole, whole, whole, f32(2), table],
-            scratch,
-            small_out=(4,),
+            [place, from_everyone(sums), *far, *near, coef_ext],
+            [whole] * 6 + [f32(2), table],
+            [ext, *scratch(rows)],
+            small_out=(6,),
         )
         phi, g, sums = call(
             lambda *refs: third_kernel(cells, *refs),
-            [place, scal, from_everyone(sums), phi, m, n, g, coefs],
+            [place, scal, from_everyone(sums), phi, m, n, lm, ln, g, coef_ext],
             [whole, f32(3, own, depth, width), table],
-            [ext, ext, *scratch],
+            [ext, ext, *scratch(rows)],
             scalars=2,
         )
         edge, mid = call(

time: 234 us -> 243 us (1.038)
  waiting for transfers between devices: 37.1 us -> 42.6 us
  starting transfers between devices: 43.2 us -> 38.5 us
  local copies, waits for them, and re-layouts: 7.07 us -> 10.1 us
    ppermute x14 -> x12, waiting for transfers between devices: 37.1 us -> 42.6 us  [beside(): return lax.ppermute(cells, axis, pairs)]
    ppermute x14 -> x12, starting transfers between devices: 43.2 us -> 38.5 us  [beside(): return lax.ppermute(cells, axis, pairs)]
    unnamed x4 -> x8, local copies, waits for them, and re-layouts: 2.64 us -> 5.86 us
    pallas_call x8 -> x10, Pallas kernels: 48.2 us -> 49.4 us  [call(): pl.pallas_call(kernel, out_shape=outs, in_specs=[smem if i < scalars else...]
  transfers between devices with their start and end apart: 14 -> 12, of which waited for: 8 -> 10; matrix products, arithmetic and copies ran while one was open for 1% -> 2% of each run, Pallas kernels for 0% -> 4%
where the time goes in v4:
time: 243 us; the launch traced here: 242 us
  blocking collectives  98.6 us (41%)
  Pallas kernels  49.4 us (20%)
  waiting for transfers between devices  42.6 us (18%)
  starting transfers between devices  38.5 us (16%)
  local copies, waits for them, and re-layouts  10.1 us (4%)
  other arithmetic  2.55 us (1%)
    all_to_all x6, blocking collectives, from_everyone(): return lax.all_to_all(rows, IMG_TILE, 0, 0, tiled=True)  98.6 us
    pallas_call x10, Pallas kernels, call(): pl.pallas_call(kernel, out_shape=outs, in_specs=[smem if i < scalars else...  49.4 us
    ppermute x12, waiting for transfers between devices, beside(): return lax.ppermute(cells, axis, pairs)  42.6 us
    ppermute x12, starting transfers between devices, beside(): return lax.ppermute(cells, axis, pairs)  38.5 us
    unnamed x8, local copies, waits for them, and re-layouts  5.86 us
  transfers between devices with their start and end apart: 12, of which 10 were waited for; matrix products, arithmetic and copies ran while one was open for 2% of the time, Pallas kernels for 4%

profile of v4, /device:TPU:1, one launch (start us, length us, event | category | flops | bytes accessed | tf_op | source)
XLA Modules:
  0.0 242.1 jit_solution(6049711409369672019)
XLA Ops:
  0.0 2.3 copy.17
  3.9 4.7 %collective-permute-start.2 = (f32[3,12,16,256]{3,2,1,0:T(8,128)S(1)}, f32[3,12,16,256]{3,2,1,0:T(8,128)S(1)}, u32[]{:S(2)}, u32[]{:S(2)}) collective-permute-start(f32[3,12,16,256]{3,2,1,0:T(8,128)S(1)} %pad_maximum_fusion.5.own_edge), channel_id=1, source_target_pairs={{0,8},{8,16},{16,24},{24,32},{32,40},{40,48},{48,56},{56,64},{64,7... | collective-permute-start | bytes 1769480 | tf_op jit(solution)/shard_map/ppermute | solution.py:498
  8.9 10.3 %collective-permute-done.3.b_edge = f32[3,12,16,256]{3,2,1,0:T(8,128)S(1)} collective-permute-done((f32[3,12,16,256]{3,2,1,0:T(8,128)S(1)}, f32[3,12,16,256]{3,2,1,0:T(8,128)S(1)}, u32[]{:S(2)}, u32[]{:S(2)}) %collective-permute-start.3) | collective-permute-done | bytes 589856 | tf_op jit(solution)/shard_map/ppermute | solution.py:498
  21.2 5.1 %collective-permute-start.4 = (f32[10,6,16,256]{3,2,1,0:T(8,128)}, f32[10,6,16,256]{3,2,1,0:T(8,128)}, u32[]{:S(2)}, u32[]{:S(2)}) collective-permute-start(f32[10,6,16,256]{3,2,1,0:T(8,128)} %pad_maximum_fusion), channel_id=1, source_target_pairs={{0,1},{1,2},{2,3},{3,4},{4,5},{5,6},{6,7},{8,9},{9,10},{10,11},{11... | collective-permute-start | bytes 2949128 | tf_op jit(solution)/shard_map/ppermute | solution.py:498
  27.4 1.9 collective-permute-start.5
  30.7 5.7 %collective-permute-start = (f32[3,20,16,256]{3,2,1,0:T(8,128)S(1)}, f32[3,20,16,256]{3,2,1,0:T(8,128)}, u32[]{:S(2)}, u32[]{:S(2)}) collective-permute-start(f32[3,20,16,256]{3,2,1,0:T(8,128)S(1)} %slice.76.own_mid), channel_id=1, source_target_pairs={{0,8},{8,16},{16,24},{24,32},{32,40},{40,48},{48,56},{56,64},{64,7... | collective-permute-start | bytes 2949128 | tf_op jit(solution)/shard_map/ppermute | solution.py:498
  38.6 4.8 %collective-permute-done.5.down_ref = f32[10,6,16,256]{3,2,1,0:T(8,128)} collective-permute-done((f32[10,6,16,256]{3,2,1,0:T(8,128)}, f32[10,6,16,256]{3,2,1,0:T(8,128)}, u32[]{:S(2)}, u32[]{:S(2)}) %collective-permute-start.5) | collective-permute-done | bytes 983072 | tf_op jit(solution)/shard_map/ppermute | solution.py:498
  44.4 4.9 %shard_map.28 = (f32[3,24,16,256]{3,2,1,0:T(8,128)S(1)}, f32[3,24,16,256]{3,2,1,0:T(8,128)S(1)}, f32[3,24,16,256]{3,2,1,0:T(8,128)S(1)}, f32[3,24,16,256]{3,2,1,...) custom-call(s32[4]{0:T(128)S(1)} %pad_add_fusion.place_ref.refs_0_, ...), custom_call_target="tpu_custom_call" | custom-call | tf_op jit(solution)/shard_map/pallas_call | solution.py:485
  49.2 5.0 %collective-permute-done.1.b_mid = f32[3,20,16,256]{3,2,1,0:T(8,128)} collective-permute-done((f32[3,20,16,256]{3,2,1,0:T(8,128)S(1)}, f32[3,20,16,256]{3,2,1,0:T(8,128)}, u32[]{:S(2)}, u32[]{:S(2)}) %collective-permute-start.1) | collective-permute-done | bytes 983072 | tf_op jit(solution)/shard_map/ppermute | solution.py:498
  54.3 1.7 collective-permute-done.a_mid
  55.9 6.7 %shard_map.29 = (f32[3,28,16,256]{3,2,1,0:T(8,128)S(1)}, f32[3,28,16,256]{3,2,1,0:T(8,128)S(1)}, f32[3,28,16,256]{3,2,1,0:T(8,128)S(1)}, f32[3,28,16,256]{3,2,1,...) custom-call(s32[4]{0:T(128)S(1)} %pad_add_fusion.place_ref.refs_0_, ...), custom_call_target="tpu_custom_call" | custom-call | tf_op jit(solution)/shard_map/pallas_call | solution.py:485
  62.6 25.6 %all_to_all.66 = f32[128,1,128]{2,1,0:T(1,128)S(1)} all-to-all(f32[128,1,128]{2,1,0:T(1,128)S(1)} %bitcast.54), channel_id=1, replica_groups=mesh['img_0'=4,'img_1'=4,'tile_0'=4,'tile_1'=2] {'img_0','img_1','tile_0..., dimensions={0} | all-to-all | bytes 131072 | tf_op jit(solution)/shard_map/all_to_all | solution.py:502
  88.2 7.9 %shard_map.30 = (f32[3,44,16,256]{3,2,1,0:T(8,128)S(1)}, f32[3,44,16,256]{3,2,1,0:T(8,128)S(1)}, f32[3,44,16,256]{3,2,1,0:T(8,128)S(1)}, f32[3,44,16,256]{3,2,1,...) custom-call(s32[4]{0:T(128)S(1)} %pad_add_fusion.place_ref.refs_0_, ...), custom_call_target="tpu_custom_call" | custom-call | tf_op jit(solution)/shard_map/pallas_call | solution.py:485
  96.1 13.9 %all_to_all.67 = f32[128,1,128]{2,1,0:T(1,128)S(1)} all-to-all(f32[128,1,128]{2,1,0:T(1,128)S(1)} %bitcast.52), channel_id=1, replica_groups=mesh['img_0'=4,'img_1'=4,'tile_0'=4,'tile_1'=2] {'img_0','img_1','tile_0..., dimensions={0} | all-to-all | bytes 131072 | tf_op jit(solution)/shard_map/all_to_all | solution.py:502
  110.0 1.6 copy-done.1
  111.7 5.2 %shard_map.31 = (f32[3,44,16,256]{3,2,1,0:T(8,128)S(1)}, f32[3,32,16,256]{3,2,1,0:T(8,128)S(1)}, f32[128,128]{1,0:T(8,128)S(1)}) custom-call(s32[4]{0:T(128)S(1)} %pad_add_fusion.place_ref.refs_0_, f32[2]{0:T(128)S(1)} %get-tuple-element.79.refs_1_, f32[128,128]{1,0:T(8,128)S(1)} %bitcast.49, f32[3,44,16,256]{3,2,1,0:T(8,128)S(1)} %get-tuple-element.81.refs_3_, ...), custom_call_target="tpu_custom_call" | custom-call | tf_op jit(solution)/shard_map/pallas_call | solution.py:485
  116.8 13.9 %all_to_all.68 = f32[128,1,128]{2,1,0:T(1,128)S(1)} all-to-all(f32[128,1,128]{2,1,0:T(1,128)S(1)} %bitcast.57), channel_id=1, replica_groups=mesh['img_0'=4,'img_1'=4,'tile_0'=4,'tile_1'=2] {'img_0','img_1','tile_0..., dimensions={0} | all-to-all | bytes 131072 | tf_op jit(solution)/shard_map/all_to_all | solution.py:502
  133.0 4.0 %collective-permute-start.8 = (f32[3,12,16,256]{3,2,1,0:T(8,128)S(1)}, f32[3,12,16,256]{3,2,1,0:T(8,128)S(1)}, u32[]{:S(2)}, u32[]{:S(2)}) collective-permute-start(f32[3,12,16,256]{3,2,1,0:T(8,128)S(1)} %get-tuple-element.91.own_edge), channel_id=1, source_target_pairs={{0,8},{8,16},{16,24},{24,32},{32,40},{40,48},{48,56},{56,64},{64,7... | collective-permute-start | bytes 1769480 | tf_op jit(solution)/shard_map/ppermute | solution.py:498
  138.3 4.0 %collective-permute-start.6 = (f32[3,20,16,256]{3,2,1,0:T(8,128)S(1)}, f32[3,20,16,256]{3,2,1,0:T(8,128)S(1)}, u32[]{:S(2)}, u32[]{:S(2)}) collective-permute-start(f32[3,20,16,256]{3,2,1,0:T(8,128)S(1)} %get-tuple-element.90.own_mid), channel_id=1, source_target_pairs={{0,8},{8,16},{16,24},{24,32},{32,40},{40,48},{48,56},{56,64},{64,7... | collective-permute-start | bytes 2949128 | tf_op jit(solution)/shard_map/ppermute | solution.py:498
  142.5 5.3 %collective-permute-done.9.b_edge = f32[3,12,16,256]{3,2,1,0:T(8,128)S(1)} collective-permute-done((f32[3,12,16,256]{3,2,1,0:T(8,128)S(1)}, f32[3,12,16,256]{3,2,1,0:T(8,128)S(1)}, u32[]{:S(2)}, u32[]{:S(2)}) %collective-permute-start.9) | collective-permute-done | bytes 589856 | tf_op jit(solution)/shard_map/ppermute | solution.py:498
  148.7 5.8 %collective-permute-start.10 = (f32[9,6,16,256]{3,2,1,0:T(8,128)S(1)}, f32[9,6,16,256]{3,2,1,0:T(8,128)S(1)}, u32[]{:S(2)}, u32[]{:S(2)}) collective-permute-start(f32[9,6,16,256]{3,2,1,0:T(8,128)S(1)} %pad_maximum_fusion.2), channel_id=1, source_target_pairs={{0,1},{1,2},{2,3},{3,4},{4,5},{5,6},{6,7},{8,9},{9,10},{10,11},{11... | collective-permute-start | bytes 2654216 | tf_op jit(solution)/shard_map/ppermute | solution.py:498
  154.5 1.9 collective-permute-start.11
  156.5 7.8 %collective-permute-done.10.up_ref = f32[9,6,16,256]{3,2,1,0:T(8,128)S(1)} collective-permute-done((f32[9,6,16,256]{3,2,1,0:T(8,128)S(1)}, f32[9,6,16,256]{3,2,1,0:T(8,128)S(1)}, u32[]{:S(2)}, u32[]{:S(2)}) %collective-permute-start.10) | collective-permute-done | bytes 884768 | tf_op jit(solution)/shard_map/ppermute | solution.py:498
  164.3 4.9 %collective-permute-done.11.down_ref = f32[9,6,16,256]{3,2,1,0:T(8,128)S(1)} collective-permute-done((f32[9,6,16,256]{3,2,1,0:T(8,128)S(1)}, f32[9,6,16,256]{3,2,1,0:T(8,128)S(1)}, u32[]{:S(2)}, u32[]{:S(2)}) %collective-permute-start.11) | collective-permute-done | bytes 884768 | tf_op jit(solution)/shard_map/ppermute | solution.py:498
  169.2 3.9 %shard_map.33 = (f32[3,24,16,256]{3,2,1,0:T(8,128)S(1)}, f32[3,24,16,256]{3,2,1,0:T(8,128)S(1)}, f32[3,24,16,256]{3,2,1,0:T(8,128)S(1)}, f32[3,24,16,256]{3,2,1,...) custom-call(s32[4]{0:T(128)S(1)} %pad_add_fusion.place_ref.refs_0_, ...), custom_call_target="tpu_custom_call" | custom-call | tf_op jit(solution)/shard_map/pallas_call | solution.py:485
  173.1 5.7 %shard_map.34 = (f32[3,28,16,256]{3,2,1,0:T(8,128)S(1)}, f32[3,28,16,256]{3,2,1,0:T(8,128)S(1)}, f32[3,28,16,256]{3,2,1,0:T(8,128)S(1)}, f32[3,28,16,256]{3,2,1,...) custom-call(s32[4]{0:T(128)S(1)} %pad_add_fusion.place_ref.refs_0_, ...), custom_call_target="tpu_custom_call" | custom-call | tf_op jit(solution)/shard_map/pallas_call | solution.py:485
  178.9 17.4 %all_to_all.69 = f32[128,1,128]{2,1,0:T(1,128)S(1)} all-to-all(f32[128,1,128]{2,1,0:T(1,128)S(1)} %bitcast.55), channel_id=1, replica_groups=mesh['img_0'=4,'img_1'=4,'tile_0'=4,'tile_1'=2] {'img_0','img_1','tile_0..., dimensions={0} | all-to-all | bytes 131072 | tf_op jit(solution)/shard_map/all_to_all | solution.py:502
  196.3 7.9 %shard_map.35 = (f32[3,44,16,256]{3,2,1,0:T(8,128)S(1)}, f32[3,44,16,256]{3,2,1,0:T(8,128)S(1)}, f32[3,44,16,256]{3,2,1,0:T(8,128)S(1)}, f32[3,44,16,256]{3,2,1,...) custom-call(s32[4]{0:T(128)S(1)} %pad_add_fusion.place_ref.refs_0_, ...), custom_call_target="tpu_custom_call" | custom-call | tf_op jit(solution)/shard_map/pallas_call | solution.py:485
  204.2 13.9 %all_to_all.70 = f32[128,1,128]{2,1,0:T(1,128)S(1)} all-to-all(f32[128,1,128]{2,1,0:T(1,128)S(1)} %bitcast.53), channel_id=1, replica_groups=mesh['img_0'=4,'img_1'=4,'tile_0'=4,'tile_1'=2] {'img_0','img_1','tile_0..., dimensions={0} | all-to-all | bytes 131072 | tf_op jit(solution)/shard_map/all_to_all | solution.py:502
  219.7 5.2 %shard_map.36 = (f32[3,44,16,256]{3,2,1,0:T(8,128)S(1)}, f32[3,32,16,256]{3,2,1,0:T(8,128)S(1)}, f32[128,128]{1,0:T(8,128)S(1)}) custom-call(s32[4]{0:T(128)S(1)} %pad_add_fusion.place_ref.refs_0_, f32[2]{0:T(128)S(1)} %get-tuple-element.108.refs_1_, f32[128,128]{1,0:T(8,128)S(1)} %bitcast.48, f32[3,44,16,256]{3,2,1,0:T(8,128)S(1)} %get-tuple-element.110.refs_3_, ...), custom_call_target="tpu_custom_call" | custom-call | tf_op jit(solution)/shard_map/pallas_call | solution.py:485
  224.9 13.9 %all_to_all.71 = f32[128,1,128]{2,1,0:T(1,128)S(1)} all-to-all(f32[128,1,128]{2,1,0:T(1,128)S(1)} %bitcast.56), channel_id=1, replica_groups=mesh['img_0'=4,'img_1'=4,'tile_0'=4,'tile_1'=2] {'img_0','img_1','tile_0..., dimensions={0} | all-to-all | bytes 131072 | tf_op jit(solution)/shard_map/all_to_all | solution.py:502
  240.0 2.1 copy.14
  (36 shorter events, 16.7 us)
Async XLA Ops:
  2.3 6.3 %copy-start.2 = (f32[16,32,256]{2,1,0:T(8,128)S(1)}, f32[16,32,256]{2,1,0:T(8,128)}, u32[]{:S(2)}) copy-start(f32[16,32,256]{2,1,0:T(8,128)} %param.3) | copy-start | bytes 1572868
  2.4 16.8 %collective-permute-start.3 = (f32[3,12,16,256]{3,2,1,0:T(8,128)S(1)}, f32[3,12,16,256]{3,2,1,0:T(8,128)S(1)}, u32[]{:S(2)}, u32[]{:S(2)}) collective-permute-start(f32[3,12,16,256]{3,2,1,0:T(8,128)S(1)} %pad_maximum_fusion.5.own_edge), channel_id=1, source_target_pairs={{8,0},{16,8},{24,16},{32,24},{40,32},{48,40},{56,48},{64,56},{72,6... | collective-permute-start | bytes 1769480 | tf_op jit(solution)/shard_map/ppermute | solution.py:498
  3.9 16.2 %collective-permute-start.2 = (f32[3,12,16,256]{3,2,1,0:T(8,128)S(1)}, f32[3,12,16,256]{3,2,1,0:T(8,128)S(1)}, u32[]{:S(2)}, u32[]{:S(2)}) collective-permute-start(f32[3,12,16,256]{3,2,1,0:T(8,128)S(1)} %pad_maximum_fusion.5.own_edge), channel_id=1, source_target_pairs={{0,8},{8,16},{16,24},{24,32},{32,40},{40,48},{48,56},{56,64},{64,7... | collective-permute-start | bytes 1769480 | tf_op jit(solution)/shard_map/ppermute | solution.py:498
  21.2 16.4 %collective-permute-start.4 = (f32[10,6,16,256]{3,2,1,0:T(8,128)}, f32[10,6,16,256]{3,2,1,0:T(8,128)}, u32[]{:S(2)}, u32[]{:S(2)}) collective-permute-start(f32[10,6,16,256]{3,2,1,0:T(8,128)} %pad_maximum_fusion), channel_id=1, source_target_pairs={{0,1},{1,2},{2,3},{3,4},{4,5},{5,6},{6,7},{8,9},{9,10},{10,11},{11... | collective-permute-start | bytes 2949128 | tf_op jit(solution)/shard_map/ppermute | solution.py:498
  27.4 16.0 %collective-permute-start.5 = (f32[10,6,16,256]{3,2,1,0:T(8,128)}, f32[10,6,16,256]{3,2,1,0:T(8,128)}, u32[]{:S(2)}, u32[]{:S(2)}) collective-permute-start(f32[10,6,16,256]{3,2,1,0:T(8,128)} %pad_maximum_fusion.1), channel_id=1, source_target_pairs={{1,0},{2,1},{3,2},{4,3},{5,4},{6,5},{7,6},{9,8},{10,9},{11,10},{12... | collective-permute-start | bytes 2949128 | tf_op jit(solution)/shard_map/ppermute | solution.py:498
  29.4 24.9 %collective-permute-start.1 = (f32[3,20,16,256]{3,2,1,0:T(8,128)S(1)}, f32[3,20,16,256]{3,2,1,0:T(8,128)}, u32[]{:S(2)}, u32[]{:S(2)}) collective-permute-start(f32[3,20,16,256]{3,2,1,0:T(8,128)S(1)} %slice.76.own_mid), channel_id=1, source_target_pairs={{8,0},{16,8},{24,16},{32,24},{40,32},{48,40},{56,48},{64,56},{72,6... | collective-permute-start | bytes 2949128 | tf_op jit(solution)/shard_map/ppermute | solution.py:498
  30.7 25.2 %collective-permute-start = (f32[3,20,16,256]{3,2,1,0:T(8,128)S(1)}, f32[3,20,16,256]{3,2,1,0:T(8,128)}, u32[]{:S(2)}, u32[]{:S(2)}) collective-permute-start(f32[3,20,16,256]{3,2,1,0:T(8,128)S(1)} %slice.76.own_mid), channel_id=1, source_target_pairs={{0,8},{8,16},{16,24},{24,32},{32,40},{40,48},{48,56},{56,64},{64,7... | collective-permute-start | bytes 2949128 | tf_op jit(solution)/shard_map/ppermute | solution.py:498
  110.0 1.6 copy-start.1
  131.7 16.0 %collective-permute-start.9 = (f32[3,12,16,256]{3,2,1,0:T(8,128)S(1)}, f32[3,12,16,256]{3,2,1,0:T(8,128)S(1)}, u32[]{:S(2)}, u32[]{:S(2)}) collective-permute-start(f32[3,12,16,256]{3,2,1,0:T(8,128)S(1)} %get-tuple-element.91.own_edge), channel_id=1, source_target_pairs={{8,0},{16,8},{24,16},{32,24},{40,32},{48,40},{56,48},{64,56},{72,6... | collective-permute-start | bytes 1769480 | tf_op jit(solution)/shard_map/ppermute | solution.py:498
  133.0 15.6 %collective-permute-start.8 = (f32[3,12,16,256]{3,2,1,0:T(8,128)S(1)}, f32[3,12,16,256]{3,2,1,0:T(8,128)S(1)}, u32[]{:S(2)}, u32[]{:S(2)}) collective-permute-start(f32[3,12,16,256]{3,2,1,0:T(8,128)S(1)} %get-tuple-element.91.own_edge), channel_id=1, source_target_pairs={{0,8},{8,16},{16,24},{24,32},{32,40},{40,48},{48,56},{56,64},{64,7... | collective-permute-start | bytes 1769480 | tf_op jit(solution)/shard_map/ppermute | solution.py:498
  137.0 36.1 %collective-permute-start.7 = (f32[3,20,16,256]{3,2,1,0:T(8,128)S(1)}, f32[3,20,16,256]{3,2,1,0:T(8,128)S(1)}, u32[]{:S(2)}, u32[]{:S(2)}) collective-permute-start(f32[3,20,16,256]{3,2,1,0:T(8,128)S(1)} %get-tuple-element.90.own_mid), channel_id=1, source_target_pairs={{8,0},{16,8},{24,16},{32,24},{40,32},{48,40},{56,48},{64,56},{72,6... | collective-permute-start | bytes 2949128 | tf_op jit(solution)/shard_map/ppermute | solution.py:498
  138.3 34.8 %collective-permute-start.6 = (f32[3,20,16,256]{3,2,1,0:T(8,128)S(1)}, f32[3,20,16,256]{3,2,1,0:T(8,128)S(1)}, u32[]{:S(2)}, u32[]{:S(2)}) collective-permute-start(f32[3,20,16,256]{3,2,1,0:T(8,128)S(1)} %get-tuple-element.90.own_mid), channel_id=1, source_target_pairs={{0,8},{8,16},{16,24},{24,32},{32,40},{40,48},{48,56},{56,64},{64,7... | collective-permute-start | bytes 2949128 | tf_op jit(solution)/shard_map/ppermute | solution.py:498
  148.7 15.6 %collective-permute-start.10 = (f32[9,6,16,256]{3,2,1,0:T(8,128)S(1)}, f32[9,6,16,256]{3,2,1,0:T(8,128)S(1)}, u32[]{:S(2)}, u32[]{:S(2)}) collective-permute-start(f32[9,6,16,256]{3,2,1,0:T(8,128)S(1)} %pad_maximum_fusion.2), channel_id=1, source_target_pairs={{0,1},{1,2},{2,3},{3,4},{4,5},{5,6},{6,7},{8,9},{9,10},{10,11},{11... | collective-permute-start | bytes 2654216 | tf_op jit(solution)/shard_map/ppermute | solution.py:498
  154.5 14.7 %collective-permute-start.11 = (f32[9,6,16,256]{3,2,1,0:T(8,128)S(1)}, f32[9,6,16,256]{3,2,1,0:T(8,128)S(1)}, u32[]{:S(2)}, u32[]{:S(2)}) collective-permute-start(f32[9,6,16,256]{3,2,1,0:T(8,128)S(1)} %pad_maximum_fusion.3), channel_id=1, source_target_pairs={{1,0},{2,1},{3,2},{4,3},{5,4},{6,5},{7,6},{9,8},{10,9},{11,10},{12... | collective-permute-start | bytes 2654216 | tf_op jit(solution)/shard_map/ppermute | solution.py:498
  218.1 1.6 copy-start

commit v5 on v4

--- a/solution.py
+++ b/solution.py
@@ -21,7 +21,7 @@
 SUBLANES = 2
 LANES = 2
 TILES = range(SUBLANES * LANES)
-VMEM_LIMIT = 24 * 1024 * 1024
+VMEM_LIMIT = 16 * 1024 * 1024
 
 
 def tile_of(ref, comp, at, place):
@@ -197,6 +197,17 @@
     loop(low, high, one)
 
 
+def first_ends_kernel(
+    place_ref, own_edge, a_edge, b_edge, up_ref, down_ref, coef_up, coef_ref, coef_down, *refs
+):
+    own = coef_ref.shape[0]
+    coef_out, refs = refs[8], refs[:8] + refs[9:]
+    coef_out[0:HALO] = coef_up[...]
+    coef_out[HALO : HALO + own] = coef_ref[...]
+    coef_out[HALO + own :] = coef_down[...]
+    ends_kernel(place_ref, own_edge, a_edge, b_edge, up_ref, down_ref, coef_out, *refs)
+
+
 def ends_kernel(
     place_ref, own_edge, a_edge, b_edge, up_ref, down_ref, coef_ref,
     phi_ref, m_ref, n_ref, lm_ref, ln_ref, q_ref, r_ref, sums_ref,
@@ -530,18 +541,28 @@
         heads = [cells_[:, :HALO] for cells_ in (a_edge, edge, b_edge)]
         tails = [cells_[:, HALO:] for cells_ in (a_edge, edge, b_edge)]
         if coef_ext is None:
-            heads.append(coefs[None, :HALO])
-            tails.append(coefs[None, own - HALO :])
+            coef_up = beside(coefs[own - HALO :], TILE, True)
+            coef_down = beside(coefs[:HALO], TILE, False)
+            heads, tails, coef_up, coef_down = lax.optimization_barrier(
+                (heads, tails, coef_up, coef_down)
+            )
         up = beside(jnp.concatenate(tails), TILE, True)
         down = beside(jnp.concatenate(heads), TILE, False)
+        shapes = [f32(*ends)] * 7 + [f32(PRODUCTS, 8, 128)]
         if coef_ext is None:
-            coef_ext = jnp.concatenate([up[9], coefs, down[9]])
-        *far, part = call(
-            ends_kernel,
-            [place, edge, a_edge, b_edge, up, down, coef_ext],
-            [f32(*ends)] * 7 + [f32(PRODUCTS, 8, 128)],
-            scratch(2 * HALO),
-        )
+            *far, part, coef_ext = call(
+                first_ends_kernel,
+                [place, edge, a_edge, b_edge, up, down, coef_up, coefs, coef_down],
+                [*shapes, f32(*ext[1:])],
+                scratch(2 * HALO),
+            )
+        else:
+            *far, part = call(
+                ends_kernel,
+                [place, edge, a_edge, b_edge, up, down, coef_ext],
+                shapes,
+                scratch(2 * HALO),
+            )
         *near, sums = call(
             middle_kernel,
             [place, mid, a_mid, b_mid, *far[:3], part, coef_ext],

time: 243 us -> 229 us (0.942)
  waiting for transfers between devices: 42.6 us -> 30.7 us
  starting transfers between devices: 38.5 us -> 46.7 us
  local copies, waits for them, and re-layouts: 10.1 us -> 5.09 us
  blocking collectives: 98.6 us -> 95.6 us
    ppermute x12 -> x14, waiting for transfers between devices: 42.6 us -> 30.7 us  [beside(): return lax.ppermute(cells, axis, pairs)]
    ppermute x12 -> x14, starting transfers between devices: 38.5 us -> 46.7 us  [beside(): return lax.ppermute(cells, axis, pairs)]
    unnamed x8 -> x4, local copies, waits for them, and re-layouts: 5.86 us -> 2.64 us
    all_to_all x6, blocking collectives: 98.6 us -> 95.6 us  [from_everyone(): return lax.all_to_all(rows, IMG_TILE, 0, 0, tiled=True)]
  transfers between devices with their start and end apart: 12 -> 14, of which waited for: 10 -> 8; matrix products, arithmetic and copies ran while one was open for 2% -> 1% of each run, Pallas kernels for 4% -> 4%
where the time goes in v5:
time: 229 us
  blocking collectives  95.6 us (42%)
  Pallas kernels  47.7 us (21%)
  starting transfers between devices  46.7 us (20%)
  waiting for transfers between devices  30.7 us (13%)
  local copies, waits for them, and re-layouts  5.09 us (2%)
  other arithmetic  2.38 us (1%)
    all_to_all x6, blocking collectives, from_everyone(): return lax.all_to_all(rows, IMG_TILE, 0, 0, tiled=True)  95.6 us
    pallas_call x10, Pallas kernels, call(): pl.pallas_call(kernel, out_shape=outs, in_specs=[smem if i < scalars else...  47.7 us
    ppermute x14, starting transfers between devices, beside(): return lax.ppermute(cells, axis, pairs)  46.7 us
    ppermute x14, waiting for transfers between devices, beside(): return lax.ppermute(cells, axis, pairs)  30.7 us
  transfers between devices with their start and end apart: 14, of which 8 were waited for; matrix products, arithmetic and copies ran while one was open for 1% of the time, Pallas kernels for 4%

profile of v5, /device:TPU:1, one launch (start us, length us, event | category | flops | bytes accessed | tf_op | source)
XLA Modules:
  0.0 228.5 jit_solution(7108219883432621128)
XLA Ops:
  0.0 2.3 %copy.17 = f32[1,3,16,32,256]{4,2,3,1,0:T(8,128)S(1)} copy(f32[1,3,16,32,256]{4,3,2,1,0:T(8,128)} %param.2) | data formatting | bytes 3145728 | tf_op args[0]
  3.9 4.7 %collective-permute-start.2 = (f32[3,12,16,256]{3,2,1,0:T(8,128)S(1)}, f32[3,12,16,256]{3,2,1,0:T(8,128)S(1)}, u32[]{:S(2)}, u32[]{:S(2)}) collective-permute-start(f32[3,12,16,256]{3,2,1,0:T(8,128)S(1)} %pad_maximum_fusion.4.own_edge), channel_id=1, source_target_pairs={{0,8},{8,16},{16,24},{24,32},{32,40},{40,48},{48,56},{56,64},{64,7... | collective-permute-start | bytes 1769480 | tf_op jit(solution)/shard_map/ppermute | solution.py:509
  9.9 5.0 %collective-permute-start = (f32[3,20,16,256]{3,2,1,0:T(8,128)S(1)}, f32[3,20,16,256]{3,2,1,0:T(8,128)}, u32[]{:S(2)}, u32[]{:S(2)}) collective-permute-start(f32[3,20,16,256]{3,2,1,0:T(8,128)S(1)} %slice.68.own_mid), channel_id=1, source_target_pairs={{0,8},{8,16},{16,24},{24,32},{32,40},{40,48},{48,56},{56,64},{64,7... | collective-permute-start | bytes 2949128 | tf_op jit(solution)/shard_map/ppermute | solution.py:509
  15.3 3.8 %collective-permute-start.5 = (f32[6,16,256]{2,1,0:T(8,128)S(1)}, f32[6,16,256]{2,1,0:T(8,128)S(1)}, u32[]{:S(2)}, u32[]{:S(2)}) collective-permute-start(f32[6,16,256]{2,1,0:T(8,128)S(1)} %get-tuple-element.153), channel_id=1, source_target_pairs={{1,0},{2,1},{3,2},{4,3},{5,4},{6,5},{7,6},{9,8},{10,9},{11,10},{12... | collective-permute-start | bytes 294920 | tf_op jit(solution)/shard_map/ppermute | solution.py:509
  19.2 5.9 %collective-permute-start.4 = (f32[6,16,256]{2,1,0:T(8,128)S(1)}, f32[6,16,256]{2,1,0:T(8,128)S(1)}, u32[]{:S(2)}, u32[]{:S(2)}) collective-permute-start(f32[6,16,256]{2,1,0:T(8,128)S(1)} %get-tuple-element.154), channel_id=1, source_target_pairs={{0,1},{1,2},{2,3},{3,4},{4,5},{5,6},{6,7},{8,9},{9,10},{10,11},{11... | collective-permute-start | bytes 294920 | tf_op jit(solution)/shard_map/ppermute | solution.py:509
  25.3 1.5 collective-permute-done.4.coef_up
  27.8 1.9 collective-permute-start.7
  30.7 4.3 %collective-permute-start.6 = (f32[9,6,16,256]{3,2,1,0:T(8,128)}, f32[9,6,16,256]{3,2,1,0:T(8,128)}, u32[]{:S(2)}, u32[]{:S(2)}) collective-permute-start(f32[9,6,16,256]{3,2,1,0:T(8,128)} %pad_maximum_fusion), channel_id=1, source_target_pairs={{0,1},{1,2},{2,3},{3,4},{4,5},{5,6},{6,7},{8,9},{9,10},{10,11},{11... | collective-permute-start | bytes 2654216 | tf_op jit(solution)/shard_map/ppermute | solution.py:509
  35.1 8.0 %collective-permute-done.7.down_ref = f32[9,6,16,256]{3,2,1,0:T(8,128)} collective-permute-done((f32[9,6,16,256]{3,2,1,0:T(8,128)}, f32[9,6,16,256]{3,2,1,0:T(8,128)}, u32[]{:S(2)}, u32[]{:S(2)}) %collective-permute-start.7) | collective-permute-done | bytes 884768 | tf_op jit(solution)/shard_map/ppermute | solution.py:509
  43.2 2.2 collective-permute-done.6.up_ref
  45.3 4.9 %shard_map.28 = (f32[3,24,16,256]{3,2,1,0:T(8,128)S(1)}, f32[3,24,16,256]{3,2,1,0:T(8,128)S(1)}, f32[3,24,16,256]{3,2,1,0:T(8,128)S(1)}, f32[3,24,16,256]{3,2,1,...) custom-call(s32[4]{0:T(128)S(1)} %pad_add_fusion.place_ref.refs_0_, ...), custom_call_target="tpu_custom_call" | custom-call | tf_op jit(solution)/shard_map/pallas_call | solution.py:496
  50.2 6.7 %shard_map.29 = (f32[3,28,16,256]{3,2,1,0:T(8,128)S(1)}, f32[3,28,16,256]{3,2,1,0:T(8,128)S(1)}, f32[3,28,16,256]{3,2,1,0:T(8,128)S(1)}, f32[3,28,16,256]{3,2,1,...) custom-call(s32[4]{0:T(128)S(1)} %pad_add_fusion.place_ref.refs_0_, ...), custom_call_target="tpu_custom_call" | custom-call | tf_op jit(solution)/shard_map/pallas_call | solution.py:496
  57.0 22.6 %all_to_all.66 = f32[128,1,128]{2,1,0:T(1,128)S(1)} all-to-all(f32[128,1,128]{2,1,0:T(1,128)S(1)} %bitcast.48), channel_id=1, replica_groups=mesh['img_0'=4,'img_1'=4,'tile_0'=4,'tile_1'=2] {'img_0','img_1','tile_0..., dimensions={0} | all-to-all | bytes 131072 | tf_op jit(solution)/shard_map/all_to_all | solution.py:513
  79.5 7.1 %shard_map.30 = (f32[3,44,16,256]{3,2,1,0:T(8,128)S(1)}, f32[3,44,16,256]{3,2,1,0:T(8,128)S(1)}, f32[3,44,16,256]{3,2,1,0:T(8,128)S(1)}, f32[3,44,16,256]{3,2,1,...) custom-call(s32[4]{0:T(128)S(1)} %pad_add_fusion.place_ref.refs_0_, ...), custom_call_target="tpu_custom_call" | custom-call | tf_op jit(solution)/shard_map/pallas_call | solution.py:496
  86.6 13.9 %all_to_all.67 = f32[128,1,128]{2,1,0:T(1,128)S(1)} all-to-all(f32[128,1,128]{2,1,0:T(1,128)S(1)} %bitcast.46), channel_id=1, replica_groups=mesh['img_0'=4,'img_1'=4,'tile_0'=4,'tile_1'=2] {'img_0','img_1','tile_0..., dimensions={0} | all-to-all | bytes 131072 | tf_op jit(solution)/shard_map/all_to_all | solution.py:513
  100.6 5.2 %shard_map.31 = (f32[3,44,16,256]{3,2,1,0:T(8,128)S(1)}, f32[3,32,16,256]{3,2,1,0:T(8,128)S(1)}, f32[128,128]{1,0:T(8,128)S(1)}) custom-call(s32[4]{0:T(128)S(1)} %pad_add_fusion.place_ref.refs_0_, f32[2]{0:T(128)S(1)} %get-tuple-element.97.refs_1_, f32[128,128]{1,0:T(8,128)S(1)} %bitcast.43, f32[3,44,16,256]{3,2,1,0:T(8,128)S(1)} %get-tuple-element.99.refs_3_, ...), custom_call_target="tpu_custom_call" | custom-call | tf_op jit(solution)/shard_map/pallas_call | solution.py:496
  105.7 13.9 %all_to_all.68 = f32[128,1,128]{2,1,0:T(1,128)S(1)} all-to-all(f32[128,1,128]{2,1,0:T(1,128)S(1)} %bitcast.51), channel_id=1, replica_groups=mesh['img_0'=4,'img_1'=4,'tile_0'=4,'tile_1'=2] {'img_0','img_1','tile_0..., dimensions={0} | all-to-all | bytes 131072 | tf_op jit(solution)/shard_map/all_to_all | solution.py:513
  121.9 4.0 %collective-permute-start.10 = (f32[3,12,16,256]{3,2,1,0:T(8,128)S(1)}, f32[3,12,16,256]{3,2,1,0:T(8,128)S(1)}, u32[]{:S(2)}, u32[]{:S(2)}) collective-permute-start(f32[3,12,16,256]{3,2,1,0:T(8,128)S(1)} %get-tuple-element.109.own_edge), channel_id=1, source_target_pairs={{0,8},{8,16},{16,24},{24,32},{32,40},{40,48},{48,56},{56,64},{64,7... | collective-permute-start | bytes 1769480 | tf_op jit(solution)/shard_map/ppermute | solution.py:509
  127.2 4.0 %collective-permute-start.8 = (f32[3,20,16,256]{3,2,1,0:T(8,128)S(1)}, f32[3,20,16,256]{3,2,1,0:T(8,128)S(1)}, u32[]{:S(2)}, u32[]{:S(2)}) collective-permute-start(f32[3,20,16,256]{3,2,1,0:T(8,128)S(1)} %get-tuple-element.108.own_mid), channel_id=1, source_target_pairs={{0,8},{8,16},{16,24},{24,32},{32,40},{40,48},{48,56},{56,64},{64,7... | collective-permute-start | bytes 2949128 | tf_op jit(solution)/shard_map/ppermute | solution.py:509
  131.3 5.3 %collective-permute-done.11.b_edge = f32[3,12,16,256]{3,2,1,0:T(8,128)S(1)} collective-permute-done((f32[3,12,16,256]{3,2,1,0:T(8,128)S(1)}, f32[3,12,16,256]{3,2,1,0:T(8,128)S(1)}, u32[]{:S(2)}, u32[]{:S(2)}) %collective-permute-start.11) | collective-permute-done | bytes 589856 | tf_op jit(solution)/shard_map/ppermute | solution.py:509
  137.6 5.8 %collective-permute-start.12 = (f32[9,6,16,256]{3,2,1,0:T(8,128)S(1)}, f32[9,6,16,256]{3,2,1,0:T(8,128)S(1)}, u32[]{:S(2)}, u32[]{:S(2)}) collective-permute-start(f32[9,6,16,256]{3,2,1,0:T(8,128)S(1)} %pad_maximum_fusion.2), channel_id=1, source_target_pairs={{0,1},{1,2},{2,3},{3,4},{4,5},{5,6},{6,7},{8,9},{9,10},{10,11},{11... | collective-permute-start | bytes 2654216 | tf_op jit(solution)/shard_map/ppermute | solution.py:509
  143.4 1.9 collective-permute-start.13
  145.4 7.8 %collective-permute-done.12.up_ref = f32[9,6,16,256]{3,2,1,0:T(8,128)S(1)} collective-permute-done((f32[9,6,16,256]{3,2,1,0:T(8,128)S(1)}, f32[9,6,16,256]{3,2,1,0:T(8,128)S(1)}, u32[]{:S(2)}, u32[]{:S(2)}) %collective-permute-start.12) | collective-permute-done | bytes 884768 | tf_op jit(solution)/shard_map/ppermute | solution.py:509
  153.2 4.9 %collective-permute-done.13.down_ref = f32[9,6,16,256]{3,2,1,0:T(8,128)S(1)} collective-permute-done((f32[9,6,16,256]{3,2,1,0:T(8,128)S(1)}, f32[9,6,16,256]{3,2,1,0:T(8,128)S(1)}, u32[]{:S(2)}, u32[]{:S(2)}) %collective-permute-start.13) | collective-permute-done | bytes 884768 | tf_op jit(solution)/shard_map/ppermute | solution.py:509
  158.1 3.9 %shard_map.33 = (f32[3,24,16,256]{3,2,1,0:T(8,128)S(1)}, f32[3,24,16,256]{3,2,1,0:T(8,128)S(1)}, f32[3,24,16,256]{3,2,1,0:T(8,128)S(1)}, f32[3,24,16,256]{3,2,1,...) custom-call(s32[4]{0:T(128)S(1)} %pad_add_fusion.place_ref.refs_0_, ...), custom_call_target="tpu_custom_call" | custom-call | tf_op jit(solution)/shard_map/pallas_call | solution.py:496
  162.0 5.7 %shard_map.34 = (f32[3,28,16,256]{3,2,1,0:T(8,128)S(1)}, f32[3,28,16,256]{3,2,1,0:T(8,128)S(1)}, f32[3,28,16,256]{3,2,1,0:T(8,128)S(1)}, f32[3,28,16,256]{3,2,1,...) custom-call(s32[4]{0:T(128)S(1)} %pad_add_fusion.place_ref.refs_0_, ...), custom_call_target="tpu_custom_call" | custom-call | tf_op jit(solution)/shard_map/pallas_call | solution.py:496
  167.8 17.4 %all_to_all.69 = f32[128,1,128]{2,1,0:T(1,128)S(1)} all-to-all(f32[128,1,128]{2,1,0:T(1,128)S(1)} %bitcast.49), channel_id=1, replica_groups=mesh['img_0'=4,'img_1'=4,'tile_0'=4,'tile_1'=2] {'img_0','img_1','tile_0..., dimensions={0} | all-to-all | bytes 131072 | tf_op jit(solution)/shard_map/all_to_all | solution.py:513
  185.2 7.1 %shard_map.35 = (f32[3,44,16,256]{3,2,1,0:T(8,128)S(1)}, f32[3,44,16,256]{3,2,1,0:T(8,128)S(1)}, f32[3,44,16,256]{3,2,1,0:T(8,128)S(1)}, f32[3,44,16,256]{3,2,1,...) custom-call(s32[4]{0:T(128)S(1)} %pad_add_fusion.place_ref.refs_0_, ...), custom_call_target="tpu_custom_call" | custom-call | tf_op jit(solution)/shard_map/pallas_call | solution.py:496
  192.3 13.9 %all_to_all.70 = f32[128,1,128]{2,1,0:T(1,128)S(1)} all-to-all(f32[128,1,128]{2,1,0:T(1,128)S(1)} %bitcast.47), channel_id=1, replica_groups=mesh['img_0'=4,'img_1'=4,'tile_0'=4,'tile_1'=2] {'img_0','img_1','tile_0..., dimensions={0} | all-to-all | bytes 131072 | tf_op jit(solution)/shard_map/all_to_all | solution.py:513
  206.2 5.2 %shard_map.36 = (f32[3,44,16,256]{3,2,1,0:T(8,128)S(1)}, f32[3,32,16,256]{3,2,1,0:T(8,128)S(1)}, f32[128,128]{1,0:T(8,128)S(1)}) custom-call(s32[4]{0:T(128)S(1)} %pad_add_fusion.place_ref.refs_0_, f32[2]{0:T(128)S(1)} %get-tuple-element.126.refs_1_, f32[128,128]{1,0:T(8,128)S(1)} %bitcast.42, f32[3,44,16,256]{3,2,1,0:T(8,128)S(1)} %get-tuple-element.128.refs_3_, ...), custom_call_target="tpu_custom_call" | custom-call | tf_op jit(solution)/shard_map/pallas_call | solution.py:496
  211.4 13.9 %all_to_all.71 = f32[128,1,128]{2,1,0:T(1,128)S(1)} all-to-all(f32[128,1,128]{2,1,0:T(1,128)S(1)} %bitcast.50), channel_id=1, replica_groups=mesh['img_0'=4,'img_1'=4,'tile_0'=4,'tile_1'=2] {'img_0','img_1','tile_0..., dimensions={0} | all-to-all | bytes 131072 | tf_op jit(solution)/shard_map/all_to_all | solution.py:513
  226.5 2.1 copy.14
  (33 shorter events, 11.3 us)
Async XLA Ops:
  2.4 12.5 %copy-start = (f32[16,32,256]{2,1,0:T(8,128)S(1)}, f32[16,32,256]{2,1,0:T(8,128)}, u32[]{:S(2)}) copy-start(f32[16,32,256]{2,1,0:T(8,128)} %param.3) | copy-start | bytes 1572868
  2.4 16.8 %collective-permute-start.3 = (f32[3,12,16,256]{3,2,1,0:T(8,128)S(1)}, f32[3,12,16,256]{3,2,1,0:T(8,128)S(1)}, u32[]{:S(2)}, u32[]{:S(2)}) collective-permute-start(f32[3,12,16,256]{3,2,1,0:T(8,128)S(1)} %pad_maximum_fusion.4.own_edge), channel_id=1, source_target_pairs={{8,0},{16,8},{24,16},{32,24},{40,32},{48,40},{56,48},{64,56},{72,6... | collective-permute-start | bytes 1769480 | tf_op jit(solution)/shard_map/ppermute | solution.py:509
  3.9 21.4 %collective-permute-start.2 = (f32[3,12,16,256]{3,2,1,0:T(8,128)S(1)}, f32[3,12,16,256]{3,2,1,0:T(8,128)S(1)}, u32[]{:S(2)}, u32[]{:S(2)}) collective-permute-start(f32[3,12,16,256]{3,2,1,0:T(8,128)S(1)} %pad_maximum_fusion.4.own_edge), channel_id=1, source_target_pairs={{0,8},{8,16},{16,24},{24,32},{32,40},{40,48},{48,56},{56,64},{64,7... | collective-permute-start | bytes 1769480 | tf_op jit(solution)/shard_map/ppermute | solution.py:509
  8.7 41.6 %collective-permute-start.1 = (f32[3,20,16,256]{3,2,1,0:T(8,128)S(1)}, f32[3,20,16,256]{3,2,1,0:T(8,128)}, u32[]{:S(2)}, u32[]{:S(2)}) collective-permute-start(f32[3,20,16,256]{3,2,1,0:T(8,128)S(1)} %slice.68.own_mid), channel_id=1, source_target_pairs={{8,0},{16,8},{24,16},{32,24},{40,32},{48,40},{56,48},{64,56},{72,6... | collective-permute-start | bytes 2949128 | tf_op jit(solution)/shard_map/ppermute | solution.py:509
  9.9 40.3 %collective-permute-start = (f32[3,20,16,256]{3,2,1,0:T(8,128)S(1)}, f32[3,20,16,256]{3,2,1,0:T(8,128)}, u32[]{:S(2)}, u32[]{:S(2)}) collective-permute-start(f32[3,20,16,256]{3,2,1,0:T(8,128)S(1)} %slice.68.own_mid), channel_id=1, source_target_pairs={{0,8},{8,16},{16,24},{24,32},{32,40},{40,48},{48,56},{56,64},{64,7... | collective-permute-start | bytes 2949128 | tf_op jit(solution)/shard_map/ppermute | solution.py:509
  15.3 10.1 %collective-permute-start.5 = (f32[6,16,256]{2,1,0:T(8,128)S(1)}, f32[6,16,256]{2,1,0:T(8,128)S(1)}, u32[]{:S(2)}, u32[]{:S(2)}) collective-permute-start(f32[6,16,256]{2,1,0:T(8,128)S(1)} %get-tuple-element.153), channel_id=1, source_target_pairs={{1,0},{2,1},{3,2},{4,3},{5,4},{6,5},{7,6},{9,8},{10,9},{11,10},{12... | collective-permute-start | bytes 294920 | tf_op jit(solution)/shard_map/ppermute | solution.py:509
  19.2 7.6 %collective-permute-start.4 = (f32[6,16,256]{2,1,0:T(8,128)S(1)}, f32[6,16,256]{2,1,0:T(8,128)S(1)}, u32[]{:S(2)}, u32[]{:S(2)}) collective-permute-start(f32[6,16,256]{2,1,0:T(8,128)S(1)} %get-tuple-element.154), channel_id=1, source_target_pairs={{0,1},{1,2},{2,3},{3,4},{4,5},{5,6},{6,7},{8,9},{9,10},{10,11},{11... | collective-permute-start | bytes 294920 | tf_op jit(solution)/shard_map/ppermute | solution.py:509
  27.8 15.3 %collective-permute-start.7 = (f32[9,6,16,256]{3,2,1,0:T(8,128)}, f32[9,6,16,256]{3,2,1,0:T(8,128)}, u32[]{:S(2)}, u32[]{:S(2)}) collective-permute-start(f32[9,6,16,256]{3,2,1,0:T(8,128)} %pad_maximum_fusion.1), channel_id=1, source_target_pairs={{1,0},{2,1},{3,2},{4,3},{5,4},{6,5},{7,6},{9,8},{10,9},{11,10},{12... | collective-permute-start | bytes 2654216 | tf_op jit(solution)/shard_map/ppermute | solution.py:509
  30.7 14.6 %collective-permute-start.6 = (f32[9,6,16,256]{3,2,1,0:T(8,128)}, f32[9,6,16,256]{3,2,1,0:T(8,128)}, u32[]{:S(2)}, u32[]{:S(2)}) collective-permute-start(f32[9,6,16,256]{3,2,1,0:T(8,128)} %pad_maximum_fusion), channel_id=1, source_target_pairs={{0,1},{1,2},{2,3},{3,4},{4,5},{5,6},{6,7},{8,9},{9,10},{10,11},{11... | collective-permute-start | bytes 2654216 | tf_op jit(solution)/shard_map/ppermute | solution.py:509
  120.6 16.0 %collective-permute-start.11 = (f32[3,12,16,256]{3,2,1,0:T(8,128)S(1)}, f32[3,12,16,256]{3,2,1,0:T(8,128)S(1)}, u32[]{:S(2)}, u32[]{:S(2)}) collective-permute-start(f32[3,12,16,256]{3,2,1,0:T(8,128)S(1)} %get-tuple-element.109.own_edge), channel_id=1, source_target_pairs={{8,0},{16,8},{24,16},{32,24},{40,32},{48,40},{56,48},{64,56},{72,6... | collective-permute-start | bytes 1769480 | tf_op jit(solution)/shard_map/ppermute | solution.py:509
  121.9 15.6 %collective-permute-start.10 = (f32[3,12,16,256]{3,2,1,0:T(8,128)S(1)}, f32[3,12,16,256]{3,2,1,0:T(8,128)S(1)}, u32[]{:S(2)}, u32[]{:S(2)}) collective-permute-start(f32[3,12,16,256]{3,2,1,0:T(8,128)S(1)} %get-tuple-element.109.own_edge), channel_id=1, source_target_pairs={{0,8},{8,16},{16,24},{24,32},{32,40},{40,48},{48,56},{56,64},{64,7... | collective-permute-start | bytes 1769480 | tf_op jit(solution)/shard_map/ppermute | solution.py:509
  125.9 36.1 %collective-permute-start.9 = (f32[3,20,16,256]{3,2,1,0:T(8,128)S(1)}, f32[3,20,16,256]{3,2,1,0:T(8,128)S(1)}, u32[]{:S(2)}, u32[]{:S(2)}) collective-permute-start(f32[3,20,16,256]{3,2,1,0:T(8,128)S(1)} %get-tuple-element.108.own_mid), channel_id=1, source_target_pairs={{8,0},{16,8},{24,16},{32,24},{40,32},{48,40},{56,48},{64,56},{72,6... | collective-permute-start | bytes 2949128 | tf_op jit(solution)/shard_map/ppermute | solution.py:509
  127.2 34.8 %collective-permute-start.8 = (f32[3,20,16,256]{3,2,1,0:T(8,128)S(1)}, f32[3,20,16,256]{3,2,1,0:T(8,128)S(1)}, u32[]{:S(2)}, u32[]{:S(2)}) collective-permute-start(f32[3,20,16,256]{3,2,1,0:T(8,128)S(1)} %get-tuple-element.108.own_mid), channel_id=1, source_target_pairs={{0,8},{8,16},{16,24},{24,32},{32,40},{40,48},{48,56},{56,64},{64,7... | collective-permute-start | bytes 2949128 | tf_op jit(solution)/shard_map/ppermute | solution.py:509
  137.6 15.6 %collective-permute-start.12 = (f32[9,6,16,256]{3,2,1,0:T(8,128)S(1)}, f32[9,6,16,256]{3,2,1,0:T(8,128)S(1)}, u32[]{:S(2)}, u32[]{:S(2)}) collective-permute-start(f32[9,6,16,256]{3,2,1,0:T(8,128)S(1)} %pad_maximum_fusion.2), channel_id=1, source_target_pairs={{0,1},{1,2},{2,3},{3,4},{4,5},{5,6},{6,7},{8,9},{9,10},{10,11},{11... | collective-permute-start | bytes 2654216 | tf_op jit(solution)/shard_map/ppermute | solution.py:509
  143.4 14.7 %collective-permute-start.13 = (f32[9,6,16,256]{3,2,1,0:T(8,128)S(1)}, f32[9,6,16,256]{3,2,1,0:T(8,128)S(1)}, u32[]{:S(2)}, u32[]{:S(2)}) collective-permute-start(f32[9,6,16,256]{3,2,1,0:T(8,128)S(1)} %pad_maximum_fusion.3), channel_id=1, source_target_pairs={{1,0},{2,1},{3,2},{4,3},{5,4},{6,5},{7,6},{9,8},{10,9},{11,10},{12... | collective-permute-start | bytes 2654216 | tf_op jit(solution)/shard_map/ppermute | solution.py:509

commit v6 on v5

--- a/solution.py
+++ b/solution.py
@@ -526,6 +526,9 @@
     coefs = jnp.swapaxes(aniso, 0, 1)
     edge = jnp.concatenate([start[:, :HALO], start[:, own - HALO :]], axis=1)
     mid = start[:, HALO : own - HALO]
+    coef_up = beside(coefs[own - HALO :], TILE, True)
+    coef_down = beside(coefs[:HALO], TILE, False)
+    edge, mid, coef_up, coef_down = lax.optimization_barrier((edge, mid, coef_up, coef_down))
     ext = (3, rows, depth, width)
     ends, middle = (3, 4 * HALO, depth, width), (3, own - 4, depth, width)
     whole = f32(*ext)
@@ -540,12 +543,6 @@
         a_mid, b_mid = beside(mid, IMG, True), beside(mid, IMG, False)
         heads = [cells_[:, :HALO] for cells_ in (a_edge, edge, b_edge)]
         tails = [cells_[:, HALO:] for cells_ in (a_edge, edge, b_edge)]
-        if coef_ext is None:
-            coef_up = beside(coefs[own - HALO :], TILE, True)
-            coef_down = beside(coefs[:HALO], TILE, False)
-            heads, tails, coef_up, coef_down = lax.optimization_barrier(
-                (heads, tails, coef_up, coef_down)
-            )
         up = beside(jnp.concatenate(tails), TILE, True)
         down = beside(jnp.concatenate(heads), TILE, False)
         shapes = [f32(*ends)] * 7 + [f32(PRODUCTS, 8, 128)]

time: 229 us -> 234 us (1.022)
  waiting for transfers between devices: 30.7 us -> 38.1 us
  starting transfers between devices: 46.7 us -> 42.9 us
    ppermute x14, waiting for transfers between devices: 30.7 us -> 38.1 us  [beside(): return lax.ppermute(cells, axis, pairs)]
    ppermute x14, starting transfers between devices: 46.7 us -> 42.9 us  [beside(): return lax.ppermute(cells, axis, pairs)]
  transfers between devices with their start and end apart: 14 -> 14, of which waited for: 8 -> 8; matrix products, arithmetic and copies ran while one was open for 1% -> 2% of each run, Pallas kernels for 4% -> 4%
where the time goes in v6:
time: 234 us; the launch traced here: 233 us
  blocking collectives  95.4 us (41%)
  Pallas kernels  47.7 us (20%)
  starting transfers between devices  42.9 us (18%)
  waiting for transfers between devices  38.1 us (16%)
  local copies, waits for them, and re-layouts  6.17 us (3%)
  other arithmetic  2.36 us (1%)
    all_to_all x6, blocking collectives, from_everyone(): return lax.all_to_all(rows, IMG_TILE, 0, 0, tiled=True)  95.4 us
    pallas_call x10, Pallas kernels, call(): pl.pallas_call(kernel, out_shape=outs, in_specs=[smem if i < scalars else...  47.7 us
    ppermute x14, starting transfers between devices, beside(): return lax.ppermute(cells, axis, pairs)  42.9 us
    ppermute x14, waiting for transfers between devices, beside(): return lax.ppermute(cells, axis, pairs)  38.1 us
  transfers between devices with their start and end apart: 14, of which 8 were waited for; matrix products, arithmetic and copies ran while one was open for 2% of the time, Pallas kernels for 4%

profile of v6, /device:TPU:1, one launch (start us, length us, event | category | flops | bytes accessed | tf_op | source)
XLA Modules:
  0.0 233.0 jit_solution(13394997017619600582)
XLA Ops:
  1.4 3.3 %collective-permute-start.1 = (f32[6,16,256]{2,1,0:T(8,128)S(1)}, f32[6,16,256]{2,1,0:T(8,128)S(1)}, u32[]{:S(2)}, u32[]{:S(2)}) collective-permute-start(f32[6,16,256]{2,1,0:T(8,128)S(1)} %get-tuple-element.147), channel_id=1, source_target_pairs={{1,0},{2,1},{3,2},{4,3},{5,4},{6,5},{7,6},{9,8},{10,9},{11,10},{12... | collective-permute-start | bytes 294920 | tf_op jit(solution)/shard_map/ppermute | solution.py:509
  4.7 3.1 %collective-permute-start = (f32[6,16,256]{2,1,0:T(8,128)S(1)}, f32[6,16,256]{2,1,0:T(8,128)S(1)}, u32[]{:S(2)}, u32[]{:S(2)}) collective-permute-start(f32[6,16,256]{2,1,0:T(8,128)S(1)} %get-tuple-element.148), channel_id=1, source_target_pairs={{0,1},{1,2},{2,3},{3,4},{4,5},{5,6},{6,7},{8,9},{9,10},{10,11},{11... | collective-permute-start | bytes 294920 | tf_op jit(solution)/shard_map/ppermute | solution.py:509
  7.8 2.3 copy.17
  11.6 4.0 %collective-permute-start.4 = (f32[3,12,16,256]{3,2,1,0:T(8,128)S(1)}, f32[3,12,16,256]{3,2,1,0:T(8,128)S(1)}, u32[]{:S(2)}, u32[]{:S(2)}) collective-permute-start(f32[3,12,16,256]{3,2,1,0:T(8,128)S(1)} %pad_maximum_fusion.4.own_edge), channel_id=1, source_target_pairs={{0,8},{8,16},{16,24},{24,32},{32,40},{40,48},{48,56},{56,64},{64,7... | collective-permute-start | bytes 1769480 | tf_op jit(solution)/shard_map/ppermute | solution.py:509
  17.0 5.0 %collective-permute-start.2 = (f32[3,20,16,256]{3,2,1,0:T(8,128)S(1)}, f32[3,20,16,256]{3,2,1,0:T(8,128)}, u32[]{:S(2)}, u32[]{:S(2)}) collective-permute-start(f32[3,20,16,256]{3,2,1,0:T(8,128)S(1)} %slice.78.own_mid), channel_id=1, source_target_pairs={{0,8},{8,16},{16,24},{24,32},{32,40},{40,48},{48,56},{56,64},{64,7... | collective-permute-start | bytes 2949128 | tf_op jit(solution)/shard_map/ppermute | solution.py:509
  22.0 5.7 %collective-permute-done.5.b_edge = f32[3,12,16,256]{3,2,1,0:T(8,128)S(1)} collective-permute-done((f32[3,12,16,256]{3,2,1,0:T(8,128)S(1)}, f32[3,12,16,256]{3,2,1,0:T(8,128)S(1)}, u32[]{:S(2)}, u32[]{:S(2)}) %collective-permute-start.5) | collective-permute-done | bytes 589856 | tf_op jit(solution)/shard_map/ppermute | solution.py:509
  29.8 4.6 %collective-permute-start.6 = (f32[9,6,16,256]{3,2,1,0:T(8,128)}, f32[9,6,16,256]{3,2,1,0:T(8,128)}, u32[]{:S(2)}, u32[]{:S(2)}) collective-permute-start(f32[9,6,16,256]{3,2,1,0:T(8,128)} %pad_maximum_fusion), channel_id=1, source_target_pairs={{0,1},{1,2},{2,3},{3,4},{4,5},{5,6},{6,7},{8,9},{9,10},{10,11},{11... | collective-permute-start | bytes 2654216 | tf_op jit(solution)/shard_map/ppermute | solution.py:509
  35.4 1.9 collective-permute-start.7
  37.4 7.3 %collective-permute-done.6.up_ref = f32[9,6,16,256]{3,2,1,0:T(8,128)} collective-permute-done((f32[9,6,16,256]{3,2,1,0:T(8,128)}, f32[9,6,16,256]{3,2,1,0:T(8,128)}, u32[]{:S(2)}, u32[]{:S(2)}) %collective-permute-start.6) | collective-permute-done | bytes 884768 | tf_op jit(solution)/shard_map/ppermute | solution.py:509
  44.7 5.4 %collective-permute-done.7.down_ref = f32[9,6,16,256]{3,2,1,0:T(8,128)} collective-permute-done((f32[9,6,16,256]{3,2,1,0:T(8,128)}, f32[9,6,16,256]{3,2,1,0:T(8,128)}, u32[]{:S(2)}, u32[]{:S(2)}) %collective-permute-start.7) | collective-permute-done | bytes 884768 | tf_op jit(solution)/shard_map/ppermute | solution.py:509
  50.0 4.9 %shard_map.28 = (f32[3,24,16,256]{3,2,1,0:T(8,128)S(1)}, f32[3,24,16,256]{3,2,1,0:T(8,128)S(1)}, f32[3,24,16,256]{3,2,1,0:T(8,128)S(1)}, f32[3,24,16,256]{3,2,1,...) custom-call(s32[4]{0:T(128)S(1)} %pad_add_fusion.place_ref.refs_0_, ...), custom_call_target="tpu_custom_call" | custom-call | tf_op jit(solution)/shard_map/pallas_call | solution.py:496
  54.9 6.7 %shard_map.29 = (f32[3,28,16,256]{3,2,1,0:T(8,128)S(1)}, f32[3,28,16,256]{3,2,1,0:T(8,128)S(1)}, f32[3,28,16,256]{3,2,1,0:T(8,128)S(1)}, f32[3,28,16,256]{3,2,1,...) custom-call(s32[4]{0:T(128)S(1)} %pad_add_fusion.place_ref.refs_0_, ...), custom_call_target="tpu_custom_call" | custom-call | tf_op jit(solution)/shard_map/pallas_call | solution.py:496
  61.7 22.3 %all_to_all.66 = f32[128,1,128]{2,1,0:T(1,128)S(1)} all-to-all(f32[128,1,128]{2,1,0:T(1,128)S(1)} %bitcast.48), channel_id=1, replica_groups=mesh['img_0'=4,'img_1'=4,'tile_0'=4,'tile_1'=2] {'img_0','img_1','tile_0..., dimensions={0} | all-to-all | bytes 131072 | tf_op jit(solution)/shard_map/all_to_all | solution.py:513
  84.0 7.1 %shard_map.30 = (f32[3,44,16,256]{3,2,1,0:T(8,128)S(1)}, f32[3,44,16,256]{3,2,1,0:T(8,128)S(1)}, f32[3,44,16,256]{3,2,1,0:T(8,128)S(1)}, f32[3,44,16,256]{3,2,1,...) custom-call(s32[4]{0:T(128)S(1)} %pad_add_fusion.place_ref.refs_0_, ...), custom_call_target="tpu_custom_call" | custom-call | tf_op jit(solution)/shard_map/pallas_call | solution.py:496
  91.1 13.9 %all_to_all.67 = f32[128,1,128]{2,1,0:T(1,128)S(1)} all-to-all(f32[128,1,128]{2,1,0:T(1,128)S(1)} %bitcast.46), channel_id=1, replica_groups=mesh['img_0'=4,'img_1'=4,'tile_0'=4,'tile_1'=2] {'img_0','img_1','tile_0..., dimensions={0} | all-to-all | bytes 131072 | tf_op jit(solution)/shard_map/all_to_all | solution.py:513
  105.0 5.2 %shard_map.31 = (f32[3,44,16,256]{3,2,1,0:T(8,128)S(1)}, f32[3,32,16,256]{3,2,1,0:T(8,128)S(1)}, f32[128,128]{1,0:T(8,128)S(1)}) custom-call(s32[4]{0:T(128)S(1)} %pad_add_fusion.place_ref.refs_0_, f32[2]{0:T(128)S(1)} %get-tuple-element.89.refs_1_, f32[128,128]{1,0:T(8,128)S(1)} %bitcast.43, f32[3,44,16,256]{3,2,1,0:T(8,128)S(1)} %get-tuple-element.91.refs_3_, ...), custom_call_target="tpu_custom_call" | custom-call | tf_op jit(solution)/shard_map/pallas_call | solution.py:496
  110.2 13.9 %all_to_all.68 = f32[128,1,128]{2,1,0:T(1,128)S(1)} all-to-all(f32[128,1,128]{2,1,0:T(1,128)S(1)} %bitcast.51), channel_id=1, replica_groups=mesh['img_0'=4,'img_1'=4,'tile_0'=4,'tile_1'=2] {'img_0','img_1','tile_0..., dimensions={0} | all-to-all | bytes 131072 | tf_op jit(solution)/shard_map/all_to_all | solution.py:513
  126.4 4.0 %collective-permute-start.10 = (f32[3,12,16,256]{3,2,1,0:T(8,128)S(1)}, f32[3,12,16,256]{3,2,1,0:T(8,128)S(1)}, u32[]{:S(2)}, u32[]{:S(2)}) collective-permute-start(f32[3,12,16,256]{3,2,1,0:T(8,128)S(1)} %get-tuple-element.101.own_edge), channel_id=1, source_target_pairs={{0,8},{8,16},{16,24},{24,32},{32,40},{40,48},{48,56},{56,64},{64,7... | collective-permute-start | bytes 1769480 | tf_op jit(solution)/shard_map/ppermute | solution.py:509
  131.7 4.0 %collective-permute-start.8 = (f32[3,20,16,256]{3,2,1,0:T(8,128)S(1)}, f32[3,20,16,256]{3,2,1,0:T(8,128)S(1)}, u32[]{:S(2)}, u32[]{:S(2)}) collective-permute-start(f32[3,20,16,256]{3,2,1,0:T(8,128)S(1)} %get-tuple-element.100.own_mid), channel_id=1, source_target_pairs={{0,8},{8,16},{16,24},{24,32},{32,40},{40,48},{48,56},{56,64},{64,7... | collective-permute-start | bytes 2949128 | tf_op jit(solution)/shard_map/ppermute | solution.py:509
  135.8 5.3 %collective-permute-done.11.b_edge = f32[3,12,16,256]{3,2,1,0:T(8,128)S(1)} collective-permute-done((f32[3,12,16,256]{3,2,1,0:T(8,128)S(1)}, f32[3,12,16,256]{3,2,1,0:T(8,128)S(1)}, u32[]{:S(2)}, u32[]{:S(2)}) %collective-permute-start.11) | collective-permute-done | bytes 589856 | tf_op jit(solution)/shard_map/ppermute | solution.py:509
  142.0 5.8 %collective-permute-start.12 = (f32[9,6,16,256]{3,2,1,0:T(8,128)S(1)}, f32[9,6,16,256]{3,2,1,0:T(8,128)S(1)}, u32[]{:S(2)}, u32[]{:S(2)}) collective-permute-start(f32[9,6,16,256]{3,2,1,0:T(8,128)S(1)} %pad_maximum_fusion.2), channel_id=1, source_target_pairs={{0,1},{1,2},{2,3},{3,4},{4,5},{5,6},{6,7},{8,9},{9,10},{10,11},{11... | collective-permute-start | bytes 2654216 | tf_op jit(solution)/shard_map/ppermute | solution.py:509
  147.9 1.9 collective-permute-start.13
  149.8 7.8 %collective-permute-done.12.up_ref = f32[9,6,16,256]{3,2,1,0:T(8,128)S(1)} collective-permute-done((f32[9,6,16,256]{3,2,1,0:T(8,128)S(1)}, f32[9,6,16,256]{3,2,1,0:T(8,128)S(1)}, u32[]{:S(2)}, u32[]{:S(2)}) %collective-permute-start.12) | collective-permute-done | bytes 884768 | tf_op jit(solution)/shard_map/ppermute | solution.py:509
  157.6 4.9 %collective-permute-done.13.down_ref = f32[9,6,16,256]{3,2,1,0:T(8,128)S(1)} collective-permute-done((f32[9,6,16,256]{3,2,1,0:T(8,128)S(1)}, f32[9,6,16,256]{3,2,1,0:T(8,128)S(1)}, u32[]{:S(2)}, u32[]{:S(2)}) %collective-permute-start.13) | collective-permute-done | bytes 884768 | tf_op jit(solution)/shard_map/ppermute | solution.py:509
  162.5 3.9 %shard_map.33 = (f32[3,24,16,256]{3,2,1,0:T(8,128)S(1)}, f32[3,24,16,256]{3,2,1,0:T(8,128)S(1)}, f32[3,24,16,256]{3,2,1,0:T(8,128)S(1)}, f32[3,24,16,256]{3,2,1,...) custom-call(s32[4]{0:T(128)S(1)} %pad_add_fusion.place_ref.refs_0_, ...), custom_call_target="tpu_custom_call" | custom-call | tf_op jit(solution)/shard_map/pallas_call | solution.py:496
  166.5 5.7 %shard_map.34 = (f32[3,28,16,256]{3,2,1,0:T(8,128)S(1)}, f32[3,28,16,256]{3,2,1,0:T(8,128)S(1)}, f32[3,28,16,256]{3,2,1,0:T(8,128)S(1)}, f32[3,28,16,256]{3,2,1,...) custom-call(s32[4]{0:T(128)S(1)} %pad_add_fusion.place_ref.refs_0_, ...), custom_call_target="tpu_custom_call" | custom-call | tf_op jit(solution)/shard_map/pallas_call | solution.py:496
  172.2 17.4 %all_to_all.69 = f32[128,1,128]{2,1,0:T(1,128)S(1)} all-to-all(f32[128,1,128]{2,1,0:T(1,128)S(1)} %bitcast.49), channel_id=1, replica_groups=mesh['img_0'=4,'img_1'=4,'tile_0'=4,'tile_1'=2] {'img_0','img_1','tile_0..., dimensions={0} | all-to-all | bytes 131072 | tf_op jit(solution)/shard_map/all_to_all | solution.py:513
  189.6 7.1 %shard_map.35 = (f32[3,44,16,256]{3,2,1,0:T(8,128)S(1)}, f32[3,44,16,256]{3,2,1,0:T(8,128)S(1)}, f32[3,44,16,256]{3,2,1,0:T(8,128)S(1)}, f32[3,44,16,256]{3,2,1,...) custom-call(s32[4]{0:T(128)S(1)} %pad_add_fusion.place_ref.refs_0_, ...), custom_call_target="tpu_custom_call" | custom-call | tf_op jit(solution)/shard_map/pallas_call | solution.py:496
  196.8 13.9 %all_to_all.70 = f32[128,1,128]{2,1,0:T(1,128)S(1)} all-to-all(f32[128,1,128]{2,1,0:T(1,128)S(1)} %bitcast.47), channel_id=1, replica_groups=mesh['img_0'=4,'img_1'=4,'tile_0'=4,'tile_1'=2] {'img_0','img_1','tile_0..., dimensions={0} | all-to-all | bytes 131072 | tf_op jit(solution)/shard_map/all_to_all | solution.py:513
  210.7 5.2 %shard_map.36 = (f32[3,44,16,256]{3,2,1,0:T(8,128)S(1)}, f32[3,32,16,256]{3,2,1,0:T(8,128)S(1)}, f32[128,128]{1,0:T(8,128)S(1)}) custom-call(s32[4]{0:T(128)S(1)} %pad_add_fusion.place_ref.refs_0_, f32[2]{0:T(128)S(1)} %get-tuple-element.118.refs_1_, f32[128,128]{1,0:T(8,128)S(1)} %bitcast.42, f32[3,44,16,256]{3,2,1,0:T(8,128)S(1)} %get-tuple-element.120.refs_3_, ...), custom_call_target="tpu_custom_call" | custom-call | tf_op jit(solution)/shard_map/pallas_call | solution.py:496
  215.9 13.9 %all_to_all.71 = f32[128,1,128]{2,1,0:T(1,128)S(1)} all-to-all(f32[128,1,128]{2,1,0:T(1,128)S(1)} %bitcast.50), channel_id=1, replica_groups=mesh['img_0'=4,'img_1'=4,'tile_0'=4,'tile_1'=2] {'img_0','img_1','tile_0..., dimensions={0} | all-to-all | bytes 131072 | tf_op jit(solution)/shard_map/all_to_all | solution.py:513
  230.9 2.1 copy.14
  (32 shorter events, 13.0 us)
Async XLA Ops:
  1.4 9.0 %collective-permute-start.1 = (f32[6,16,256]{2,1,0:T(8,128)S(1)}, f32[6,16,256]{2,1,0:T(8,128)S(1)}, u32[]{:S(2)}, u32[]{:S(2)}) collective-permute-start(f32[6,16,256]{2,1,0:T(8,128)S(1)} %get-tuple-element.147), channel_id=1, source_target_pairs={{1,0},{2,1},{3,2},{4,3},{5,4},{6,5},{7,6},{9,8},{10,9},{11,10},{12... | collective-permute-start | bytes 294920 | tf_op jit(solution)/shard_map/ppermute | solution.py:509
  4.7 5.6 %collective-permute-start = (f32[6,16,256]{2,1,0:T(8,128)S(1)}, f32[6,16,256]{2,1,0:T(8,128)S(1)}, u32[]{:S(2)}, u32[]{:S(2)}) collective-permute-start(f32[6,16,256]{2,1,0:T(8,128)S(1)} %get-tuple-element.148), channel_id=1, source_target_pairs={{0,1},{1,2},{2,3},{3,4},{4,5},{5,6},{6,7},{8,9},{9,10},{10,11},{11... | collective-permute-start | bytes 294920 | tf_op jit(solution)/shard_map/ppermute | solution.py:509
  10.3 17.3 %collective-permute-start.5 = (f32[3,12,16,256]{3,2,1,0:T(8,128)S(1)}, f32[3,12,16,256]{3,2,1,0:T(8,128)S(1)}, u32[]{:S(2)}, u32[]{:S(2)}) collective-permute-start(f32[3,12,16,256]{3,2,1,0:T(8,128)S(1)} %pad_maximum_fusion.4.own_edge), channel_id=1, source_target_pairs={{8,0},{16,8},{24,16},{32,24},{40,32},{48,40},{56,48},{64,56},{72,6... | collective-permute-start | bytes 1769480 | tf_op jit(solution)/shard_map/ppermute | solution.py:509
  11.6 17.1 %collective-permute-start.4 = (f32[3,12,16,256]{3,2,1,0:T(8,128)S(1)}, f32[3,12,16,256]{3,2,1,0:T(8,128)S(1)}, u32[]{:S(2)}, u32[]{:S(2)}) collective-permute-start(f32[3,12,16,256]{3,2,1,0:T(8,128)S(1)} %pad_maximum_fusion.4.own_edge), channel_id=1, source_target_pairs={{0,8},{8,16},{16,24},{24,32},{32,40},{40,48},{48,56},{56,64},{64,7... | collective-permute-start | bytes 1769480 | tf_op jit(solution)/shard_map/ppermute | solution.py:509
  15.7 39.2 %collective-permute-start.3 = (f32[3,20,16,256]{3,2,1,0:T(8,128)S(1)}, f32[3,20,16,256]{3,2,1,0:T(8,128)}, u32[]{:S(2)}, u32[]{:S(2)}) collective-permute-start(f32[3,20,16,256]{3,2,1,0:T(8,128)S(1)} %slice.78.own_mid), channel_id=1, source_target_pairs={{8,0},{16,8},{24,16},{32,24},{40,32},{48,40},{56,48},{64,56},{72,6... | collective-permute-start | bytes 2949128 | tf_op jit(solution)/shard_map/ppermute | solution.py:509
  17.0 37.9 %collective-permute-start.2 = (f32[3,20,16,256]{3,2,1,0:T(8,128)S(1)}, f32[3,20,16,256]{3,2,1,0:T(8,128)}, u32[]{:S(2)}, u32[]{:S(2)}) collective-permute-start(f32[3,20,16,256]{3,2,1,0:T(8,128)S(1)} %slice.78.own_mid), channel_id=1, source_target_pairs={{0,8},{8,16},{16,24},{24,32},{32,40},{40,48},{48,56},{56,64},{64,7... | collective-permute-start | bytes 2949128 | tf_op jit(solution)/shard_map/ppermute | solution.py:509
  29.8 14.9 %collective-permute-start.6 = (f32[9,6,16,256]{3,2,1,0:T(8,128)}, f32[9,6,16,256]{3,2,1,0:T(8,128)}, u32[]{:S(2)}, u32[]{:S(2)}) collective-permute-start(f32[9,6,16,256]{3,2,1,0:T(8,128)} %pad_maximum_fusion), channel_id=1, source_target_pairs={{0,1},{1,2},{2,3},{3,4},{4,5},{5,6},{6,7},{8,9},{9,10},{10,11},{11... | collective-permute-start | bytes 2654216 | tf_op jit(solution)/shard_map/ppermute | solution.py:509
  35.4 14.7 %collective-permute-start.7 = (f32[9,6,16,256]{3,2,1,0:T(8,128)}, f32[9,6,16,256]{3,2,1,0:T(8,128)}, u32[]{:S(2)}, u32[]{:S(2)}) collective-permute-start(f32[9,6,16,256]{3,2,1,0:T(8,128)} %pad_maximum_fusion.1), channel_id=1, source_target_pairs={{1,0},{2,1},{3,2},{4,3},{5,4},{6,5},{7,6},{9,8},{10,9},{11,10},{12... | collective-permute-start | bytes 2654216 | tf_op jit(solution)/shard_map/ppermute | solution.py:509
  125.1 16.0 %collective-permute-start.11 = (f32[3,12,16,256]{3,2,1,0:T(8,128)S(1)}, f32[3,12,16,256]{3,2,1,0:T(8,128)S(1)}, u32[]{:S(2)}, u32[]{:S(2)}) collective-permute-start(f32[3,12,16,256]{3,2,1,0:T(8,128)S(1)} %get-tuple-element.101.own_edge), channel_id=1, source_target_pairs={{8,0},{16,8},{24,16},{32,24},{40,32},{48,40},{56,48},{64,56},{72,6... | collective-permute-start | bytes 1769480 | tf_op jit(solution)/shard_map/ppermute | solution.py:509
  126.4 15.6 %collective-permute-start.10 = (f32[3,12,16,256]{3,2,1,0:T(8,128)S(1)}, f32[3,12,16,256]{3,2,1,0:T(8,128)S(1)}, u32[]{:S(2)}, u32[]{:S(2)}) collective-permute-start(f32[3,12,16,256]{3,2,1,0:T(8,128)S(1)} %get-tuple-element.101.own_edge), channel_id=1, source_target_pairs={{0,8},{8,16},{16,24},{24,32},{32,40},{40,48},{48,56},{56,64},{64,7... | collective-permute-start | bytes 1769480 | tf_op jit(solution)/shard_map/ppermute | solution.py:509
  130.4 36.1 %collective-permute-start.9 = (f32[3,20,16,256]{3,2,1,0:T(8,128)S(1)}, f32[3,20,16,256]{3,2,1,0:T(8,128)S(1)}, u32[]{:S(2)}, u32[]{:S(2)}) collective-permute-start(f32[3,20,16,256]{3,2,1,0:T(8,128)S(1)} %get-tuple-element.100.own_mid), channel_id=1, source_target_pairs={{8,0},{16,8},{24,16},{32,24},{40,32},{48,40},{56,48},{64,56},{72,6... | collective-permute-start | bytes 2949128 | tf_op jit(solution)/shard_map/ppermute | solution.py:509
  131.7 34.8 %collective-permute-start.8 = (f32[3,20,16,256]{3,2,1,0:T(8,128)S(1)}, f32[3,20,16,256]{3,2,1,0:T(8,128)S(1)}, u32[]{:S(2)}, u32[]{:S(2)}) collective-permute-start(f32[3,20,16,256]{3,2,1,0:T(8,128)S(1)} %get-tuple-element.100.own_mid), channel_id=1, source_target_pairs={{0,8},{8,16},{16,24},{24,32},{32,40},{40,48},{48,56},{56,64},{64,7... | collective-permute-start | bytes 2949128 | tf_op jit(solution)/shard_map/ppermute | solution.py:509
  142.0 15.6 %collective-permute-start.12 = (f32[9,6,16,256]{3,2,1,0:T(8,128)S(1)}, f32[9,6,16,256]{3,2,1,0:T(8,128)S(1)}, u32[]{:S(2)}, u32[]{:S(2)}) collective-permute-start(f32[9,6,16,256]{3,2,1,0:T(8,128)S(1)} %pad_maximum_fusion.2), channel_id=1, source_target_pairs={{0,1},{1,2},{2,3},{3,4},{4,5},{5,6},{6,7},{8,9},{9,10},{10,11},{11... | collective-permute-start | bytes 2654216 | tf_op jit(solution)/shard_map/ppermute | solution.py:509
  147.9 14.7 %collective-permute-start.13 = (f32[9,6,16,256]{3,2,1,0:T(8,128)S(1)}, f32[9,6,16,256]{3,2,1,0:T(8,128)S(1)}, u32[]{:S(2)}, u32[]{:S(2)}) collective-permute-start(f32[9,6,16,256]{3,2,1,0:T(8,128)S(1)} %pad_maximum_fusion.3), channel_id=1, source_target_pairs={{1,0},{2,1},{3,2},{4,3},{5,4},{6,5},{7,6},{9,8},{10,9},{11,10},{12... | collective-permute-start | bytes 2654216 | tf_op jit(solution)/shard_map/ppermute | solution.py:509

commit v7 on v6

--- a/solution.py
+++ b/solution.py
@@ -198,18 +198,20 @@
 
 
 def first_ends_kernel(
-    place_ref, own_edge, a_edge, b_edge, up_ref, down_ref, coef_up, coef_ref, coef_down, *refs
+    place_ref, own_edge, a_edge, b_edge, up_own, down_own, up_ref, down_ref, coef_ref, *refs
 ):
     own = coef_ref.shape[0]
     coef_out, refs = refs[8], refs[:8] + refs[9:]
-    coef_out[0:HALO] = coef_up[...]
+    coef_out[0:HALO] = up_own[3]
     coef_out[HALO : HALO + own] = coef_ref[...]
-    coef_out[HALO + own :] = coef_down[...]
-    ends_kernel(place_ref, own_edge, a_edge, b_edge, up_ref, down_ref, coef_out, *refs)
+    coef_out[HALO + own :] = down_own[3]
+    ends_kernel(
+        place_ref, own_edge, a_edge, b_edge, up_own, down_own, up_ref, down_ref, coef_out, *refs
+    )
 
 
 def ends_kernel(
-    place_ref, own_edge, a_edge, b_edge, up_ref, down_ref, coef_ref,
+    place_ref, own_edge, a_edge, b_edge, up_own, down_own, up_ref, down_ref, coef_ref,
     phi_ref, m_ref, n_ref, lm_ref, ln_ref, q_ref, r_ref, sums_ref,
     fa_ref, fb_ref, fs_ref, sm_ref, sn_ref
 ):
@@ -217,7 +219,10 @@
     span = 2 * HALO
     fields = (phi_ref, m_ref, n_ref, lm_ref, ln_ref, q_ref, r_ref)
     scratch = (fa_ref, fb_ref, fs_ref, sm_ref, sn_ref)
-    halos = [[ref.at[3 * which : 3 * which + 3] for which in (1, 0, 2)] for ref in (up_ref, down_ref)]
+    halos = [
+        (first, ref.at[0:3], ref.at[3:6])
+        for first, ref in ((up_own, up_ref), (down_own, down_ref))
+    ]
     edges = (own_edge, a_edge, b_edge)
     sums = [jnp.zeros((8, 128), jnp.float32)] * PRODUCTS
     for top in (True, False):
@@ -526,9 +531,6 @@
     coefs = jnp.swapaxes(aniso, 0, 1)
     edge = jnp.concatenate([start[:, :HALO], start[:, own - HALO :]], axis=1)
     mid = start[:, HALO : own - HALO]
-    coef_up = beside(coefs[own - HALO :], TILE, True)
-    coef_down = beside(coefs[:HALO], TILE, False)
-    edge, mid, coef_up, coef_down = lax.optimization_barrier((edge, mid, coef_up, coef_down))
     ext = (3, rows, depth, width)
     ends, middle = (3, 4 * HALO, depth, width), (3, own - 4, depth, width)
     whole = f32(*ext)
@@ -541,22 +543,26 @@
     for _ in range(OUTER):
         a_edge, b_edge = beside(edge, IMG, True), beside(edge, IMG, False)
         a_mid, b_mid = beside(mid, IMG, True), beside(mid, IMG, False)
-        heads = [cells_[:, :HALO] for cells_ in (a_edge, edge, b_edge)]
-        tails = [cells_[:, HALO:] for cells_ in (a_edge, edge, b_edge)]
-        up = beside(jnp.concatenate(tails), TILE, True)
-        down = beside(jnp.concatenate(heads), TILE, False)
+        bottom, top = edge[:, HALO:], edge[:, :HALO]
+        if coef_ext is None:
+            bottom = jnp.concatenate([bottom, coefs[None, own - HALO :]])
+            top = jnp.concatenate([top, coefs[None, :HALO]])
+        up_own, down_own = beside(bottom, TILE, True), beside(top, TILE, False)
+        a_edge, b_edge, up_own, down_own = lax.optimization_barrier((a_edge, b_edge, up_own, down_own))
+        up = beside(jnp.concatenate([a_edge[:, HALO:], b_edge[:, HALO:]]), TILE, True)
+        down = beside(jnp.concatenate([a_edge[:, :HALO], b_edge[:, :HALO]]), TILE, False)
         shapes = [f32(*ends)] * 7 + [f32(PRODUCTS, 8, 128)]
         if coef_ext is None:
             *far, part, coef_ext = call(
                 first_ends_kernel,
-                [place, edge, a_edge, b_edge, up, down, coef_up, coefs, coef_down],
+                [place, edge, a_edge, b_edge, up_own, down_own, up, down, coefs],
                 [*shapes, f32(*ext[1:])],
                 scratch(2 * HALO),
             )
         else:
             *far, part = call(
                 ends_kernel,
-                [place, edge, a_edge, b_edge, up, down, coef_ext],
+                [place, edge, a_edge, b_edge, up_own, down_own, up, down, coef_ext],
                 shapes,
                 scratch(2 * HALO),
             )

time: 234 us -> 224 us (0.957)
  waiting for transfers between devices: 38.1 us -> 23.2 us
  starting transfers between devices: 42.9 us -> 46.2 us
    ppermute x14 -> x16, waiting for transfers between devices: 38.1 us -> 23.2 us  [beside(): return lax.ppermute(cells, axis, pairs)]
    ppermute x14 -> x16, starting transfers between devices: 42.9 us -> 46.2 us  [beside(): return lax.ppermute(cells, axis, pairs)]
  transfers between devices with their start and end apart: 14 -> 16, of which waited for: 8 -> 8; matrix products, arithmetic and copies ran while one was open for 2% -> 1% of each run, Pallas kernels for 4% -> 4%
where the time goes in v7:
time: 224 us; the launch traced here: 223 us
  blocking collectives  96.1 us (43%)
  Pallas kernels  47.6 us (21%)
  starting transfers between devices  46.2 us (21%)
  waiting for transfers between devices  23.2 us (10%)
  local copies, waits for them, and re-layouts  7.15 us (3%)
    all_to_all x6, blocking collectives, from_everyone(): return lax.all_to_all(rows, IMG_TILE, 0, 0, tiled=True)  96.1 us
    pallas_call x10, Pallas kernels, call(): pl.pallas_call(kernel, out_shape=outs, in_specs=[smem if i < scalars else...  47.6 us
    ppermute x16, starting transfers between devices, beside(): return lax.ppermute(cells, axis, pairs)  46.2 us
    ppermute x16, waiting for transfers between devices, beside(): return lax.ppermute(cells, axis, pairs)  23.2 us
    unnamed x12, local copies, waits for them, and re-layouts  4.63 us
  transfers between devices with their start and end apart: 16, of which 8 were waited for; matrix products, arithmetic and copies ran while one was open for 1% of the time, Pallas kernels for 4%

profile of v7, /device:TPU:1, one launch (start us, length us, event | category | flops | bytes accessed | tf_op | source)
XLA Modules:
  0.0 222.8 jit_solution(9726489426910852298)
XLA Ops:
  0.0 2.3 %copy.17 = f32[1,3,16,32,256]{4,2,3,1,0:T(8,128)S(1)} copy(f32[1,3,16,32,256]{4,3,2,1,0:T(8,128)} %param.2) | data formatting | bytes 3145728 | tf_op args[0]
  3.9 4.7 %collective-permute-start.2 = (f32[3,12,16,256]{3,2,1,0:T(8,128)S(1)}, f32[3,12,16,256]{3,2,1,0:T(8,128)S(1)}, u32[]{:S(2)}, u32[]{:S(2)}) collective-permute-start(f32[3,12,16,256]{3,2,1,0:T(8,128)S(1)} %pad_maximum_fusion.own_edge), channel_id=1, source_target_pairs={{0,8},{8,16},{16,24},{24,32},{32,40},{40,48},{48,56},{56,64},{64,7... | collective-permute-start | bytes 1769480 | tf_op jit(solution)/shard_map/ppermute | solution.py:514
  9.0 4.4 %collective-permute-start.4 = (f32[4,6,16,256]{3,2,1,0:T(8,128)S(1)}, f32[4,6,16,256]{3,2,1,0:T(8,128)S(1)}, u32[]{:S(2)}, u32[]{:S(2)}) collective-permute-start(f32[4,6,16,256]{3,2,1,0:T(8,128)S(1)} %pad_maximum_fusion.5), channel_id=1, source_target_pairs={{0,1},{1,2},{2,3},{3,4},{4,5},{5,6},{6,7},{8,9},{9,10},{10,11},{11... | collective-permute-start | bytes 1179656 | tf_op jit(solution)/shard_map/ppermute | solution.py:514
  13.4 1.9 collective-permute-start.5
  18.1 4.1 %collective-permute-start = (f32[3,20,16,256]{3,2,1,0:T(8,128)S(1)}, f32[3,20,16,256]{3,2,1,0:T(8,128)}, u32[]{:S(2)}, u32[]{:S(2)}) collective-permute-start(f32[3,20,16,256]{3,2,1,0:T(8,128)S(1)} %slice.68.own_mid), channel_id=1, source_target_pairs={{0,8},{8,16},{16,24},{24,32},{32,40},{40,48},{48,56},{56,64},{64,7... | collective-permute-start | bytes 2949128 | tf_op jit(solution)/shard_map/ppermute | solution.py:514
  23.9 3.9 %collective-permute-start.6 = (f32[6,6,16,256]{3,2,1,0:T(8,128)}, f32[6,6,16,256]{3,2,1,0:T(8,128)}, u32[]{:S(2)}, u32[]{:S(2)}) collective-permute-start(f32[6,6,16,256]{3,2,1,0:T(8,128)} %pad_maximum_fusion.1), channel_id=1, source_target_pairs={{0,1},{1,2},{2,3},{3,4},{4,5},{5,6},{6,7},{8,9},{9,10},{10,11},{11... | collective-permute-start | bytes 1769480 | tf_op jit(solution)/shard_map/ppermute | solution.py:514
  28.7 1.9 collective-permute-start.7
  30.7 4.2 %collective-permute-done.6.up_ref = f32[6,6,16,256]{3,2,1,0:T(8,128)} collective-permute-done((f32[6,6,16,256]{3,2,1,0:T(8,128)}, f32[6,6,16,256]{3,2,1,0:T(8,128)}, u32[]{:S(2)}, u32[]{:S(2)}) %collective-permute-start.6) | collective-permute-done | bytes 589856 | tf_op jit(solution)/shard_map/ppermute | solution.py:514
  35.0 5.6 %collective-permute-done.7.down_ref = f32[6,6,16,256]{3,2,1,0:T(8,128)} collective-permute-done((f32[6,6,16,256]{3,2,1,0:T(8,128)}, f32[6,6,16,256]{3,2,1,0:T(8,128)}, u32[]{:S(2)}, u32[]{:S(2)}) %collective-permute-start.7) | collective-permute-done | bytes 589856 | tf_op jit(solution)/shard_map/ppermute | solution.py:514
  42.5 4.7 %shard_map.28 = (f32[3,24,16,256]{3,2,1,0:T(8,128)S(1)}, f32[3,24,16,256]{3,2,1,0:T(8,128)S(1)}, f32[3,24,16,256]{3,2,1,0:T(8,128)S(1)}, f32[3,24,16,256]{3,2,1,...) custom-call(s32[4]{0:T(128)S(1)} %pad_add_fusion.place_ref.refs_0_, ...), custom_call_target="tpu_custom_call" | custom-call | tf_op jit(solution)/shard_map/pallas_call | solution.py:501
  47.2 6.7 %shard_map.29 = (f32[3,28,16,256]{3,2,1,0:T(8,128)S(1)}, f32[3,28,16,256]{3,2,1,0:T(8,128)S(1)}, f32[3,28,16,256]{3,2,1,0:T(8,128)S(1)}, f32[3,28,16,256]{3,2,1,...) custom-call(s32[4]{0:T(128)S(1)} %pad_add_fusion.place_ref.refs_0_, ...), custom_call_target="tpu_custom_call" | custom-call | tf_op jit(solution)/shard_map/pallas_call | solution.py:501
  54.0 21.2 %all_to_all.66 = f32[128,1,128]{2,1,0:T(1,128)S(1)} all-to-all(f32[128,1,128]{2,1,0:T(1,128)S(1)} %bitcast.52), channel_id=1, replica_groups=mesh['img_0'=4,'img_1'=4,'tile_0'=4,'tile_1'=2] {'img_0','img_1','tile_0..., dimensions={0} | all-to-all | bytes 131072 | tf_op jit(solution)/shard_map/all_to_all | solution.py:518
  75.2 7.1 %shard_map.30 = (f32[3,44,16,256]{3,2,1,0:T(8,128)S(1)}, f32[3,44,16,256]{3,2,1,0:T(8,128)S(1)}, f32[3,44,16,256]{3,2,1,0:T(8,128)S(1)}, f32[3,44,16,256]{3,2,1,...) custom-call(s32[4]{0:T(128)S(1)} %pad_add_fusion.place_ref.refs_0_, ...), custom_call_target="tpu_custom_call" | custom-call | tf_op jit(solution)/shard_map/pallas_call | solution.py:501
  82.3 13.9 %all_to_all.67 = f32[128,1,128]{2,1,0:T(1,128)S(1)} all-to-all(f32[128,1,128]{2,1,0:T(1,128)S(1)} %bitcast.50), channel_id=1, replica_groups=mesh['img_0'=4,'img_1'=4,'tile_0'=4,'tile_1'=2] {'img_0','img_1','tile_0..., dimensions={0} | all-to-all | bytes 131072 | tf_op jit(solution)/shard_map/all_to_all | solution.py:518
  96.2 5.2 %shard_map.31 = (f32[3,44,16,256]{3,2,1,0:T(8,128)S(1)}, f32[3,32,16,256]{3,2,1,0:T(8,128)S(1)}, f32[128,128]{1,0:T(8,128)S(1)}) custom-call(s32[4]{0:T(128)S(1)} %pad_add_fusion.place_ref.refs_0_, f32[2]{0:T(128)S(1)} %get-tuple-element.93.refs_1_, f32[128,128]{1,0:T(8,128)S(1)} %bitcast.47, f32[3,44,16,256]{3,2,1,0:T(8,128)S(1)} %get-tuple-element.95.refs_3_, ...), custom_call_target="tpu_custom_call" | custom-call | tf_op jit(solution)/shard_map/pallas_call | solution.py:501
  101.4 13.9 %all_to_all.68 = f32[128,1,128]{2,1,0:T(1,128)S(1)} all-to-all(f32[128,1,128]{2,1,0:T(1,128)S(1)} %bitcast.55), channel_id=1, replica_groups=mesh['img_0'=4,'img_1'=4,'tile_0'=4,'tile_1'=2] {'img_0','img_1','tile_0..., dimensions={0} | all-to-all | bytes 131072 | tf_op jit(solution)/shard_map/all_to_all | solution.py:518
  117.5 4.0 %collective-permute-start.10 = (f32[3,12,16,256]{3,2,1,0:T(8,128)S(1)}, f32[3,12,16,256]{3,2,1,0:T(8,128)S(1)}, u32[]{:S(2)}, u32[]{:S(2)}) collective-permute-start(f32[3,12,16,256]{3,2,1,0:T(8,128)S(1)} %get-tuple-element.105.own_edge), channel_id=1, source_target_pairs={{0,8},{8,16},{16,24},{24,32},{32,40},{40,48},{48,56},{56,64},{64,7... | collective-permute-start | bytes 1769480 | tf_op jit(solution)/shard_map/ppermute | solution.py:514
  121.6 3.2 %collective-permute-start.13 = (f32[3,6,16,256]{3,2,1,0:T(8,128)S(1)}, f32[3,6,16,256]{3,2,1,0:T(8,128)S(1)}, u32[]{:S(2)}, u32[]{:S(2)}) collective-permute-start(f32[3,6,16,256]{3,2,1,0:T(8,128)S(1)} %get-tuple-element.147), channel_id=1, source_target_pairs={{1,0},{2,1},{3,2},{4,3},{5,4},{6,5},{7,6},{9,8},{10,9},{11,10},{12... | collective-permute-start | bytes 884744 | tf_op jit(solution)/shard_map/ppermute | solution.py:514
  124.8 2.3 %collective-permute-start.12 = (f32[3,6,16,256]{3,2,1,0:T(8,128)S(1)}, f32[3,6,16,256]{3,2,1,0:T(8,128)S(1)}, u32[]{:S(2)}, u32[]{:S(2)}) collective-permute-start(f32[3,6,16,256]{3,2,1,0:T(8,128)S(1)} %get-tuple-element.148), channel_id=1, source_target_pairs={{0,1},{1,2},{2,3},{3,4},{4,5},{5,6},{6,7},{8,9},{9,10},{10,11},{11... | collective-permute-start | bytes 884744 | tf_op jit(solution)/shard_map/ppermute | solution.py:514
  130.0 2.8 %collective-permute-start.8 = (f32[3,20,16,256]{3,2,1,0:T(8,128)S(1)}, f32[3,20,16,256]{3,2,1,0:T(8,128)S(1)}, u32[]{:S(2)}, u32[]{:S(2)}) collective-permute-start(f32[3,20,16,256]{3,2,1,0:T(8,128)S(1)} %get-tuple-element.104.own_mid), channel_id=1, source_target_pairs={{0,8},{8,16},{16,24},{24,32},{32,40},{40,48},{48,56},{56,64},{64,7... | collective-permute-start | bytes 2949128 | tf_op jit(solution)/shard_map/ppermute | solution.py:514
  133.3 5.6 %collective-permute-start.14 = (f32[6,6,16,256]{3,2,1,0:T(8,128)S(1)}, f32[6,6,16,256]{3,2,1,0:T(8,128)S(1)}, u32[]{:S(2)}, u32[]{:S(2)}) collective-permute-start(f32[6,6,16,256]{3,2,1,0:T(8,128)S(1)} %pad_maximum_fusion.3), channel_id=1, source_target_pairs={{0,1},{1,2},{2,3},{3,4},{4,5},{5,6},{6,7},{8,9},{9,10},{10,11},{11... | collective-permute-start | bytes 1769480 | tf_op jit(solution)/shard_map/ppermute | solution.py:514
  138.9 1.9 collective-permute-start.15
  140.9 4.8 %collective-permute-done.14.up_ref = f32[6,6,16,256]{3,2,1,0:T(8,128)S(1)} collective-permute-done((f32[6,6,16,256]{3,2,1,0:T(8,128)S(1)}, f32[6,6,16,256]{3,2,1,0:T(8,128)S(1)}, u32[]{:S(2)}, u32[]{:S(2)}) %collective-permute-start.14) | collective-permute-done | bytes 589856 | tf_op jit(solution)/shard_map/ppermute | solution.py:514
  145.7 4.7 %collective-permute-done.15.down_ref = f32[6,6,16,256]{3,2,1,0:T(8,128)S(1)} collective-permute-done((f32[6,6,16,256]{3,2,1,0:T(8,128)S(1)}, f32[6,6,16,256]{3,2,1,0:T(8,128)S(1)}, u32[]{:S(2)}, u32[]{:S(2)}) %collective-permute-start.15) | collective-permute-done | bytes 589856 | tf_op jit(solution)/shard_map/ppermute | solution.py:514
  150.4 3.9 %shard_map.33 = (f32[3,24,16,256]{3,2,1,0:T(8,128)S(1)}, f32[3,24,16,256]{3,2,1,0:T(8,128)S(1)}, f32[3,24,16,256]{3,2,1,0:T(8,128)S(1)}, f32[3,24,16,256]{3,2,1,...) custom-call(s32[4]{0:T(128)S(1)} %pad_add_fusion.place_ref.refs_0_, ...), custom_call_target="tpu_custom_call" | custom-call | tf_op jit(solution)/shard_map/pallas_call | solution.py:501
  154.4 5.7 %shard_map.34 = (f32[3,28,16,256]{3,2,1,0:T(8,128)S(1)}, f32[3,28,16,256]{3,2,1,0:T(8,128)S(1)}, f32[3,28,16,256]{3,2,1,0:T(8,128)S(1)}, f32[3,28,16,256]{3,2,1,...) custom-call(s32[4]{0:T(128)S(1)} %pad_add_fusion.place_ref.refs_0_, ...), custom_call_target="tpu_custom_call" | custom-call | tf_op jit(solution)/shard_map/pallas_call | solution.py:501
  160.1 19.3 %all_to_all.69 = f32[128,1,128]{2,1,0:T(1,128)S(1)} all-to-all(f32[128,1,128]{2,1,0:T(1,128)S(1)} %bitcast.53), channel_id=1, replica_groups=mesh['img_0'=4,'img_1'=4,'tile_0'=4,'tile_1'=2] {'img_0','img_1','tile_0..., dimensions={0} | all-to-all | bytes 131072 | tf_op jit(solution)/shard_map/all_to_all | solution.py:518
  179.4 7.1 %shard_map.35 = (f32[3,44,16,256]{3,2,1,0:T(8,128)S(1)}, f32[3,44,16,256]{3,2,1,0:T(8,128)S(1)}, f32[3,44,16,256]{3,2,1,0:T(8,128)S(1)}, f32[3,44,16,256]{3,2,1,...) custom-call(s32[4]{0:T(128)S(1)} %pad_add_fusion.place_ref.refs_0_, ...), custom_call_target="tpu_custom_call" | custom-call | tf_op jit(solution)/shard_map/pallas_call | solution.py:501
  186.5 13.9 %all_to_all.70 = f32[128,1,128]{2,1,0:T(1,128)S(1)} all-to-all(f32[128,1,128]{2,1,0:T(1,128)S(1)} %bitcast.51), channel_id=1, replica_groups=mesh['img_0'=4,'img_1'=4,'tile_0'=4,'tile_1'=2] {'img_0','img_1','tile_0..., dimensions={0} | all-to-all | bytes 131072 | tf_op jit(solution)/shard_map/all_to_all | solution.py:518
  200.5 5.2 %shard_map.36 = (f32[3,44,16,256]{3,2,1,0:T(8,128)S(1)}, f32[3,32,16,256]{3,2,1,0:T(8,128)S(1)}, f32[128,128]{1,0:T(8,128)S(1)}) custom-call(s32[4]{0:T(128)S(1)} %pad_add_fusion.place_ref.refs_0_, f32[2]{0:T(128)S(1)} %get-tuple-element.126.refs_1_, f32[128,128]{1,0:T(8,128)S(1)} %bitcast.46, f32[3,44,16,256]{3,2,1,0:T(8,128)S(1)} %get-tuple-element.128.refs_3_, ...), custom_call_target="tpu_custom_call" | custom-call | tf_op jit(solution)/shard_map/pallas_call | solution.py:501
  205.6 13.9 %all_to_all.71 = f32[128,1,128]{2,1,0:T(1,128)S(1)} all-to-all(f32[128,1,128]{2,1,0:T(1,128)S(1)} %bitcast.54), channel_id=1, replica_groups=mesh['img_0'=4,'img_1'=4,'tile_0'=4,'tile_1'=2] {'img_0','img_1','tile_0..., dimensions={0} | all-to-all | bytes 131072 | tf_op jit(solution)/shard_map/all_to_all | solution.py:518
  220.7 2.1 copy.14
  (46 shorter events, 16.0 us)
Async XLA Ops:
  2.3 6.2 %copy-start.4 = (f32[16,32,256]{2,1,0:T(8,128)S(1)}, f32[16,32,256]{2,1,0:T(8,128)}, u32[]{:S(2)}) copy-start(f32[16,32,256]{2,1,0:T(8,128)} %param.3) | copy-start | bytes 1572868
  2.4 20.5 %collective-permute-start.3 = (f32[3,12,16,256]{3,2,1,0:T(8,128)S(1)}, f32[3,12,16,256]{3,2,1,0:T(8,128)S(1)}, u32[]{:S(2)}, u32[]{:S(2)}) collective-permute-start(f32[3,12,16,256]{3,2,1,0:T(8,128)S(1)} %pad_maximum_fusion.own_edge), channel_id=1, source_target_pairs={{8,0},{16,8},{24,16},{32,24},{40,32},{48,40},{56,48},{64,56},{72,6... | collective-permute-start | bytes 1769480 | tf_op jit(solution)/shard_map/ppermute | solution.py:514
  3.9 19.0 %collective-permute-start.2 = (f32[3,12,16,256]{3,2,1,0:T(8,128)S(1)}, f32[3,12,16,256]{3,2,1,0:T(8,128)S(1)}, u32[]{:S(2)}, u32[]{:S(2)}) collective-permute-start(f32[3,12,16,256]{3,2,1,0:T(8,128)S(1)} %pad_maximum_fusion.own_edge), channel_id=1, source_target_pairs={{0,8},{8,16},{16,24},{24,32},{32,40},{40,48},{48,56},{56,64},{64,7... | collective-permute-start | bytes 1769480 | tf_op jit(solution)/shard_map/ppermute | solution.py:514
  9.0 9.1 %collective-permute-start.4 = (f32[4,6,16,256]{3,2,1,0:T(8,128)S(1)}, f32[4,6,16,256]{3,2,1,0:T(8,128)S(1)}, u32[]{:S(2)}, u32[]{:S(2)}) collective-permute-start(f32[4,6,16,256]{3,2,1,0:T(8,128)S(1)} %pad_maximum_fusion.5), channel_id=1, source_target_pairs={{0,1},{1,2},{2,3},{3,4},{4,5},{5,6},{6,7},{8,9},{9,10},{10,11},{11... | collective-permute-start | bytes 1179656 | tf_op jit(solution)/shard_map/ppermute | solution.py:514
  13.4 9.5 %collective-permute-start.5 = (f32[4,6,16,256]{3,2,1,0:T(8,128)S(1)}, f32[4,6,16,256]{3,2,1,0:T(8,128)S(1)}, u32[]{:S(2)}, u32[]{:S(2)}) collective-permute-start(f32[4,6,16,256]{3,2,1,0:T(8,128)S(1)} %pad_maximum_fusion.6), channel_id=1, source_target_pairs={{1,0},{2,1},{3,2},{4,3},{5,4},{6,5},{7,6},{9,8},{10,9},{11,10},{12... | collective-permute-start | bytes 1179656 | tf_op jit(solution)/shard_map/ppermute | solution.py:514
  15.4 31.8 %collective-permute-start.1 = (f32[3,20,16,256]{3,2,1,0:T(8,128)S(1)}, f32[3,20,16,256]{3,2,1,0:T(8,128)}, u32[]{:S(2)}, u32[]{:S(2)}) collective-permute-start(f32[3,20,16,256]{3,2,1,0:T(8,128)S(1)} %slice.68.own_mid), channel_id=1, source_target_pairs={{8,0},{16,8},{24,16},{32,24},{40,32},{48,40},{56,48},{64,56},{72,6... | collective-permute-start | bytes 2949128 | tf_op jit(solution)/shard_map/ppermute | solution.py:514
  18.1 5.9 %copy-start = (f32[4,6,16,256]{3,2,1,0:T(8,128)}, f32[4,6,16,256]{3,2,1,0:T(8,128)S(1)}, u32[]{:S(2)}) copy-start(f32[4,6,16,256]{3,2,1,0:T(8,128)S(1)} %collective-permute-done.4.up_own) | copy-start | bytes 1179652
  18.1 29.2 %collective-permute-start = (f32[3,20,16,256]{3,2,1,0:T(8,128)S(1)}, f32[3,20,16,256]{3,2,1,0:T(8,128)}, u32[]{:S(2)}, u32[]{:S(2)}) collective-permute-start(f32[3,20,16,256]{3,2,1,0:T(8,128)S(1)} %slice.68.own_mid), channel_id=1, source_target_pairs={{0,8},{8,16},{16,24},{24,32},{32,40},{40,48},{48,56},{56,64},{64,7... | collective-permute-start | bytes 2949128 | tf_op jit(solution)/shard_map/ppermute | solution.py:514
  22.9 1.0 copy-start.2
  23.9 11.1 %collective-permute-start.6 = (f32[6,6,16,256]{3,2,1,0:T(8,128)}, f32[6,6,16,256]{3,2,1,0:T(8,128)}, u32[]{:S(2)}, u32[]{:S(2)}) collective-permute-start(f32[6,6,16,256]{3,2,1,0:T(8,128)} %pad_maximum_fusion.1), channel_id=1, source_target_pairs={{0,1},{1,2},{2,3},{3,4},{4,5},{5,6},{6,7},{8,9},{9,10},{10,11},{11... | collective-permute-start | bytes 1769480 | tf_op jit(solution)/shard_map/ppermute | solution.py:514
  28.7 11.8 %collective-permute-start.7 = (f32[6,6,16,256]{3,2,1,0:T(8,128)}, f32[6,6,16,256]{3,2,1,0:T(8,128)}, u32[]{:S(2)}, u32[]{:S(2)}) collective-permute-start(f32[6,6,16,256]{3,2,1,0:T(8,128)} %pad_maximum_fusion.2), channel_id=1, source_target_pairs={{1,0},{2,1},{3,2},{4,3},{5,4},{6,5},{7,6},{9,8},{10,9},{11,10},{12... | collective-permute-start | bytes 1769480 | tf_op jit(solution)/shard_map/ppermute | solution.py:514
  40.5 1.0 copy-start.1
  41.5 1.0 copy-start.3
  116.2 16.5 %collective-permute-start.11 = (f32[3,12,16,256]{3,2,1,0:T(8,128)S(1)}, f32[3,12,16,256]{3,2,1,0:T(8,128)S(1)}, u32[]{:S(2)}, u32[]{:S(2)}) collective-permute-start(f32[3,12,16,256]{3,2,1,0:T(8,128)S(1)} %get-tuple-element.105.own_edge), channel_id=1, source_target_pairs={{8,0},{16,8},{24,16},{32,24},{40,32},{48,40},{56,48},{64,56},{72,6... | collective-permute-start | bytes 1769480 | tf_op jit(solution)/shard_map/ppermute | solution.py:514
  117.5 15.6 %collective-permute-start.10 = (f32[3,12,16,256]{3,2,1,0:T(8,128)S(1)}, f32[3,12,16,256]{3,2,1,0:T(8,128)S(1)}, u32[]{:S(2)}, u32[]{:S(2)}) collective-permute-start(f32[3,12,16,256]{3,2,1,0:T(8,128)S(1)} %get-tuple-element.105.own_edge), channel_id=1, source_target_pairs={{0,8},{8,16},{16,24},{24,32},{32,40},{40,48},{48,56},{56,64},{64,7... | collective-permute-start | bytes 1769480 | tf_op jit(solution)/shard_map/ppermute | solution.py:514
  121.6 8.3 %collective-permute-start.13 = (f32[3,6,16,256]{3,2,1,0:T(8,128)S(1)}, f32[3,6,16,256]{3,2,1,0:T(8,128)S(1)}, u32[]{:S(2)}, u32[]{:S(2)}) collective-permute-start(f32[3,6,16,256]{3,2,1,0:T(8,128)S(1)} %get-tuple-element.147), channel_id=1, source_target_pairs={{1,0},{2,1},{3,2},{4,3},{5,4},{6,5},{7,6},{9,8},{10,9},{11,10},{12... | collective-permute-start | bytes 884744 | tf_op jit(solution)/shard_map/ppermute | solution.py:514
  124.8 7.9 %collective-permute-start.12 = (f32[3,6,16,256]{3,2,1,0:T(8,128)S(1)}, f32[3,6,16,256]{3,2,1,0:T(8,128)S(1)}, u32[]{:S(2)}, u32[]{:S(2)}) collective-permute-start(f32[3,6,16,256]{3,2,1,0:T(8,128)S(1)} %get-tuple-element.148), channel_id=1, source_target_pairs={{0,1},{1,2},{2,3},{3,4},{4,5},{5,6},{6,7},{8,9},{9,10},{10,11},{11... | collective-permute-start | bytes 884744 | tf_op jit(solution)/shard_map/ppermute | solution.py:514
  127.2 27.2 %collective-permute-start.9 = (f32[3,20,16,256]{3,2,1,0:T(8,128)S(1)}, f32[3,20,16,256]{3,2,1,0:T(8,128)S(1)}, u32[]{:S(2)}, u32[]{:S(2)}) collective-permute-start(f32[3,20,16,256]{3,2,1,0:T(8,128)S(1)} %get-tuple-element.104.own_mid), channel_id=1, source_target_pairs={{8,0},{16,8},{24,16},{32,24},{40,32},{48,40},{56,48},{64,56},{72,6... | collective-permute-start | bytes 2949128 | tf_op jit(solution)/shard_map/ppermute | solution.py:514
  130.0 24.4 %collective-permute-start.8 = (f32[3,20,16,256]{3,2,1,0:T(8,128)S(1)}, f32[3,20,16,256]{3,2,1,0:T(8,128)S(1)}, u32[]{:S(2)}, u32[]{:S(2)}) collective-permute-start(f32[3,20,16,256]{3,2,1,0:T(8,128)S(1)} %get-tuple-element.104.own_mid), channel_id=1, source_target_pairs={{0,8},{8,16},{16,24},{24,32},{32,40},{40,48},{48,56},{56,64},{64,7... | collective-permute-start | bytes 2949128 | tf_op jit(solution)/shard_map/ppermute | solution.py:514
  133.3 12.4 %collective-permute-start.14 = (f32[6,6,16,256]{3,2,1,0:T(8,128)S(1)}, f32[6,6,16,256]{3,2,1,0:T(8,128)S(1)}, u32[]{:S(2)}, u32[]{:S(2)}) collective-permute-start(f32[6,6,16,256]{3,2,1,0:T(8,128)S(1)} %pad_maximum_fusion.3), channel_id=1, source_target_pairs={{0,1},{1,2},{2,3},{3,4},{4,5},{5,6},{6,7},{8,9},{9,10},{10,11},{11... | collective-permute-start | bytes 1769480 | tf_op jit(solution)/shard_map/ppermute | solution.py:514
  138.9 11.5 %collective-permute-start.15 = (f32[6,6,16,256]{3,2,1,0:T(8,128)S(1)}, f32[6,6,16,256]{3,2,1,0:T(8,128)S(1)}, u32[]{:S(2)}, u32[]{:S(2)}) collective-permute-start(f32[6,6,16,256]{3,2,1,0:T(8,128)S(1)} %pad_maximum_fusion.4), channel_id=1, source_target_pairs={{1,0},{2,1},{3,2},{4,3},{5,4},{6,5},{7,6},{9,8},{10,9},{11,10},{12... | collective-permute-start | bytes 1769480 | tf_op jit(solution)/shard_map/ppermute | solution.py:514

commit v8 on v7

--- a/solution.py
+++ b/solution.py
@@ -198,7 +198,7 @@
 
 
 def first_ends_kernel(
-    place_ref, own_edge, a_edge, b_edge, up_own, down_own, up_ref, down_ref, coef_ref, *refs
+    where, own_edge, a_edge, b_edge, up_own, down_own, up_ref, down_ref, coef_ref, *refs
 ):
     own = coef_ref.shape[0]
     coef_out, refs = refs[8], refs[:8] + refs[9:]
@@ -206,16 +206,16 @@
     coef_out[HALO : HALO + own] = coef_ref[...]
     coef_out[HALO + own :] = down_own[3]
     ends_kernel(
-        place_ref, own_edge, a_edge, b_edge, up_own, down_own, up_ref, down_ref, coef_out, *refs
+        where, own_edge, a_edge, b_edge, up_own, down_own, up_ref, down_ref, coef_out, *refs
     )
 
 
 def ends_kernel(
-    place_ref, own_edge, a_edge, b_edge, up_own, down_own, up_ref, down_ref, coef_ref,
+    where, own_edge, a_edge, b_edge, up_own, down_own, up_ref, down_ref, coef_ref,
     phi_ref, m_ref, n_ref, lm_ref, ln_ref, q_ref, r_ref, sums_ref,
     fa_ref, fb_ref, fs_ref, sm_ref, sn_ref
 ):
-    tile, last_tile = place_ref[1], place_ref[2] - 1
+    tile, last_tile = where[1], where[2] - 1
     span = 2 * HALO
     fields = (phi_ref, m_ref, n_ref, lm_ref, ln_ref, q_ref, r_ref)
     scratch = (fa_ref, fb_ref, fs_ref, sm_ref, sn_ref)
@@ -250,7 +250,7 @@
 
 
 def middle_kernel(
-    place_ref, own_mid, a_mid, b_mid, phi_end, m_end, n_end, part_ref, coef_ref,
+    where, own_mid, a_mid, b_mid, phi_end, m_end, n_end, part_ref, coef_ref,
     phi_ref, m_ref, n_ref, lm_ref, ln_ref, q_ref, r_ref, sums_ref,
     fa_ref, fb_ref, fs_ref, sm_ref, sn_ref
 ):
@@ -273,7 +273,7 @@
     sums_ref[...] = jnp.broadcast_to(result, sums_ref.shape)
 
 
-def path_scalars(place_ref, all_ref, tiles, cells):
+def path_scalars(where, all_ref, tiles, cells):
     devices = all_ref.shape[0]
     images = devices // tiles
     table = jnp.sum(all_ref[...].reshape(images, tiles, 128), axis=1)
@@ -302,7 +302,7 @@
     inner = (one > 0) & (one < images - 1)
     total = jnp.sum(jnp.where(inner, norm, 0.0), axis=0, keepdims=True)
     step = step_scale / jnp.sqrt(total / cells + epsilon)
-    mine = jnp.sum(jnp.where(one == place_ref[0], pull, 0.0), axis=0, keepdims=True)
+    mine = jnp.sum(jnp.where(one == where[0], pull, 0.0), axis=0, keepdims=True)
     return tau[0, 0], mine[0, 0], step[0, 0]
 
 
@@ -345,8 +345,8 @@
     return rim, grad
 
 
-def interior(place_ref):
-    return jnp.where((place_ref[0] > 0) & (place_ref[0] < place_ref[3] - 1), 1.0, 0.0)
+def interior(where):
+    return jnp.where((where[0] > 0) & (where[0] < where[3] - 1), 1.0, 0.0)
 
 
 def advance(
@@ -391,16 +391,16 @@
     loop(low, high, body)
 
 
-def second_kernel(tiles, cells, place_ref, all_ref, *refs):
+def second_kernel(tiles, cells, where, all_ref, *refs):
     ends, mids, refs = refs[:7], refs[7:14], refs[14:]
     coef_ref, phi_ref, m_ref, n_ref, lm_ref, ln_ref, g_ref, scal_ref, sums_ref, d_ref = refs[:10]
     scratch = refs[10:]
     rows = phi_ref.shape[1]
     own = rows - 2 * HALO
     span = 2 * HALO
-    tile, last_tile = place_ref[1], place_ref[2] - 1
-    tau, pull, step = path_scalars(place_ref, all_ref, tiles, cells)
-    live = interior(place_ref)
+    tile, last_tile = where[1], where[2] - 1
+    tau, pull, step = path_scalars(where, all_ref, tiles, cells)
+    live = interior(where)
     step = step * live
     inv = 1.0 / tau
     scal_ref[0] = tau
@@ -448,13 +448,13 @@
 
 
 def third_kernel(
-    cells, place_ref, scal_ref, all_ref, p_ref, m0_ref, n0_ref, lm0_ref, ln0_ref, h_ref, coef_ref,
+    cells, where, scal_ref, all_ref, p_ref, m0_ref, n0_ref, lm0_ref, ln0_ref, h_ref, coef_ref,
     phi_ref, g_ref, sums_ref, m_ref, n_ref, fa_ref, fb_ref, fs_ref, sm_ref, sn_ref
 ):
     rows = p_ref.shape[1]
     own = rows - 2 * HALO
-    tile, last_tile = place_ref[1], place_ref[2] - 1
-    live = interior(place_ref)
+    tile, last_tile = where[1], where[2] - 1
+    live = interior(where)
     tau, pull = scal_ref[0], scal_ref[1]
     step = step_of(all_ref, cells) * live
     advance(
@@ -472,9 +472,9 @@
     sums_ref[...] = jnp.broadcast_to(sums, sums_ref.shape)
 
 
-def last_kernel(cells, place_ref, all_ref, p_ref, g_ref, edge_ref, mid_ref):
+def last_kernel(cells, where, all_ref, p_ref, g_ref, edge_ref, mid_ref):
     own = g_ref.shape[1]
-    step = step_of(all_ref, cells) * interior(place_ref)
+    step = step_of(all_ref, cells) * interior(where)
     for ref, low, high, shift in (
         (edge_ref, 0, HALO, 0),
         (mid_ref, HALO, own - HALO, HALO),
@@ -495,11 +495,21 @@
     return jax.ShapeDtypeStruct(shape, jnp.float32)
 
 
-def call(kernel, operands, outs, scratch, scalars=1, small_out=()):
+def position():
+    found = []
+    for axes in (IMG, TILE):
+        index = 0
+        for axis in axes:
+            index = index * lax.axis_size(axis) + lax.axis_index(axis)
+        found.append(index)
+    return (*found, lax.axis_size(TILE), lax.axis_size(IMG))
+
+
+def call(kernel, operands, outs, scratch, scalars=0, small_out=()):
     smem = pl.BlockSpec(memory_space=pltpu.SMEM)
     vmem = pl.BlockSpec(memory_space=pltpu.VMEM)
     return pl.pallas_call(
-        kernel,
+        lambda *refs: kernel(position(), *refs),
         out_shape=outs,
         in_specs=[smem if i < scalars else vmem for i in range(len(operands))],
         out_specs=[smem if i in small_out else vmem for i in range(len(outs))],
@@ -524,9 +534,6 @@
     devices = images * tiles
     cells = float(images * comps * depth * own * tiles * width)
     rows = own + 2 * HALO
-    place = jnp.stack(
-        [lax.axis_index(IMG), lax.axis_index(TILE), jnp.int32(tiles), jnp.int32(images)]
-    ).astype(jnp.int32)
     start = jnp.swapaxes(spins[0], 1, 2)
     coefs = jnp.swapaxes(aniso, 0, 1)
     edge = jnp.concatenate([start[:, :HALO], start[:, own - HALO :]], axis=1)
@@ -555,40 +562,40 @@
         if coef_ext is None:
             *far, part, coef_ext = call(
                 first_ends_kernel,
-                [place, edge, a_edge, b_edge, up_own, down_own, up, down, coefs],
+                [edge, a_edge, b_edge, up_own, down_own, up, down, coefs],
                 [*shapes, f32(*ext[1:])],
                 scratch(2 * HALO),
             )
         else:
             *far, part = call(
                 ends_kernel,
-                [place, edge, a_edge, b_edge, up_own, down_own, up, down, coef_ext],
+                [edge, a_edge, b_edge, up_own, down_own, up, down, coef_ext],
                 shapes,
                 scratch(2 * HALO),
             )
         *near, sums = call(
             middle_kernel,
-            [place, mid, a_mid, b_mid, *far[:3], part, coef_ext],
+            [mid, a_mid, b_mid, *far[:3], part, coef_ext],
             [f32(*middle)] * 7 + [table],
             scratch(own - 4),
         )
         phi, m, n, lm, ln, g, scal, sums = call(
             lambda *refs: second_kernel(tiles, cells, *refs),
-            [place, from_everyone(sums), *far, *near, coef_ext],
+            [from_everyone(sums), *far, *near, coef_ext],
             [whole] * 6 + [f32(2), table],
             [ext, *scratch(rows)],
             small_out=(6,),
         )
         phi, g, sums = call(
             lambda *refs: third_kernel(cells, *refs),
-            [place, scal, from_everyone(sums), phi, m, n, lm, ln, g, coef_ext],
+            [scal, from_everyone(sums), phi, m, n, lm, ln, g, coef_ext],
             [whole, f32(3, own, depth, width), table],
             [ext, ext, *scratch(rows)],
-            scalars=2,
+            scalars=1,
         )
         edge, mid = call(
             lambda *refs: last_kernel(cells, *refs),
-            [place, from_everyone(sums), phi, g],
+            [from_everyone(sums), phi, g],
             [f32(3, 2 * HALO, depth, width), f32(3, own - 2 * HALO, depth, width)],
             [],
         )

time: 224 us -> 217 us (0.969)
  Pallas kernels: 47.6 us -> 40.8 us
  blocking collectives: 96.1 us -> 99 us
  waiting for transfers between devices: 23.2 us -> 25.9 us
    pallas_call x10, Pallas kernels: 47.6 us -> 40.8 us  [call(): pl.pallas_call(lambda *refs: kernel(position(), *refs), out_shape=outs, i...]
    all_to_all x6, blocking collectives: 96.1 us -> 99 us  [from_everyone(): return lax.all_to_all(rows, IMG_TILE, 0, 0, tiled=True)]
    ppermute x16, waiting for transfers between devices: 23.2 us -> 25.9 us  [beside(): return lax.ppermute(cells, axis, pairs)]
    unnamed x12 -> x4, local copies, waits for them, and re-layouts: 4.63 us -> 2.64 us
  transfers between devices with their start and end apart: 16 -> 16, of which waited for: 8 -> 10; matrix products, arithmetic and copies ran while one was open for 1% -> 0% of each run, Pallas kernels for 4% -> 3%
where the time goes in v8:
time: 217 us; the launch traced here: 216 us
  blocking collectives  99 us (46%)
  starting transfers between devices  44.6 us (21%)
  Pallas kernels  40.8 us (19%)
  waiting for transfers between devices  25.9 us (12%)
  local copies, waits for them, and re-layouts  5.11 us (2%)
    all_to_all x6, blocking collectives, from_everyone(): return lax.all_to_all(rows, IMG_TILE, 0, 0, tiled=True)  99 us
    ppermute x16, starting transfers between devices, beside(): return lax.ppermute(cells, axis, pairs)  44.6 us
    pallas_call x10, Pallas kernels, call(): pl.pallas_call(lambda *refs: kernel(position(), *refs), out_shape=outs, i...  40.8 us
    ppermute x16, waiting for transfers between devices, beside(): return lax.ppermute(cells, axis, pairs)  25.9 us
  transfers between devices with their start and end apart: 16, of which 10 were waited for; matrix products, arithmetic and copies ran while one was open for 0% of the time, Pallas kernels for 3%

profile of v8, /device:TPU:1, one launch (start us, length us, event | category | flops | bytes accessed | tf_op | source)
XLA Modules:
  0.0 216.1 jit_solution(49828270972863816)
XLA Ops:
  0.0 2.3 %copy.17 = f32[1,3,16,32,256]{4,2,3,1,0:T(8,128)S(1)} copy(f32[1,3,16,32,256]{4,3,2,1,0:T(8,128)} %param.2) | data formatting | bytes 3145728 | tf_op args[0]
  3.9 4.7 %collective-permute-start.2 = (f32[3,12,16,256]{3,2,1,0:T(8,128)S(1)}, f32[3,12,16,256]{3,2,1,0:T(8,128)S(1)}, u32[]{:S(2)}, u32[]{:S(2)}) collective-permute-start(f32[3,12,16,256]{3,2,1,0:T(8,128)S(1)} %pad_maximum_fusion.refs_0_), channel_id=1, source_target_pairs={{0,8},{8,16},{16,24},{24,32},{32,40},{40,48},{48,56},{56,64},{64,7... | collective-permute-start | bytes 1769480 | tf_op jit(solution)/shard_map/ppermute | solution.py:524
  9.0 4.4 %collective-permute-start.4 = (f32[4,6,16,256]{3,2,1,0:T(8,128)S(1)}, f32[4,6,16,256]{3,2,1,0:T(8,128)S(1)}, u32[]{:S(2)}, u32[]{:S(2)}) collective-permute-start(f32[4,6,16,256]{3,2,1,0:T(8,128)S(1)} %pad_maximum_fusion.5), channel_id=1, source_target_pairs={{0,1},{1,2},{2,3},{3,4},{4,5},{5,6},{6,7},{8,9},{9,10},{10,11},{11... | collective-permute-start | bytes 1179656 | tf_op jit(solution)/shard_map/ppermute | solution.py:524
  13.4 1.9 collective-permute-start.5
  18.1 3.2 %collective-permute-start = (f32[3,20,16,256]{3,2,1,0:T(8,128)S(1)}, f32[3,20,16,256]{3,2,1,0:T(8,128)S(1)}, u32[]{:S(2)}, u32[]{:S(2)}) collective-permute-start(f32[3,20,16,256]{3,2,1,0:T(8,128)S(1)} %slice.68.refs_0_), channel_id=1, source_target_pairs={{0,8},{8,16},{16,24},{24,32},{32,40},{40,48},{48,56},{56,64},{64,7... | collective-permute-start | bytes 2949128 | tf_op jit(solution)/shard_map/ppermute | solution.py:524
  22.9 3.2 %collective-permute-start.6 = (f32[6,6,16,256]{3,2,1,0:T(8,128)S(1)}, f32[6,6,16,256]{3,2,1,0:T(8,128)S(1)}, u32[]{:S(2)}, u32[]{:S(2)}) collective-permute-start(f32[6,6,16,256]{3,2,1,0:T(8,128)S(1)} %pad_maximum_fusion.1), channel_id=1, source_target_pairs={{0,1},{1,2},{2,3},{3,4},{4,5},{5,6},{6,7},{8,9},{9,10},{10,11},{11... | collective-permute-start | bytes 1769480 | tf_op jit(solution)/shard_map/ppermute | solution.py:524
  26.2 1.9 collective-permute-start.7
  28.1 4.8 %collective-permute-done.6.refs_5_ = f32[6,6,16,256]{3,2,1,0:T(8,128)S(1)} collective-permute-done((f32[6,6,16,256]{3,2,1,0:T(8,128)S(1)}, f32[6,6,16,256]{3,2,1,0:T(8,128)S(1)}, u32[]{:S(2)}, u32[]{:S(2)}) %collective-permute-start.6) | collective-permute-done | bytes 589856 | tf_op jit(solution)/shard_map/ppermute | solution.py:524
  33.0 4.7 %collective-permute-done.7.refs_6_ = f32[6,6,16,256]{3,2,1,0:T(8,128)S(1)} collective-permute-done((f32[6,6,16,256]{3,2,1,0:T(8,128)S(1)}, f32[6,6,16,256]{3,2,1,0:T(8,128)S(1)}, u32[]{:S(2)}, u32[]{:S(2)}) %collective-permute-start.7) | collective-permute-done | bytes 589856 | tf_op jit(solution)/shard_map/ppermute | solution.py:524
  37.7 3.4 %shard_map.28 = (f32[3,24,16,256]{3,2,1,0:T(8,128)S(1)}, f32[3,24,16,256]{3,2,1,0:T(8,128)S(1)}, f32[3,24,16,256]{3,2,1,0:T(8,128)S(1)}, f32[3,24,16,256]{3,2,1,...) custom-call(f32[3,12,16,256]{3,2,1,0:T(8,128)S(1)} %pad_maximum_fusi, ...), custom_call_target="tpu_custom_call" | custom-call | tf_op jit(solution)/shard_map/pallas_call | solution.py:511
  42.8 5.1 %shard_map.29 = (f32[3,28,16,256]{3,2,1,0:T(8,128)S(1)}, f32[3,28,16,256]{3,2,1,0:T(8,128)S(1)}, f32[3,28,16,256]{3,2,1,0:T(8,128)S(1)}, f32[3,28,16,256]{3,2,1,...) custom-call(f32[3,20,16,256]{3,2,1,0:T(8,128)S(1)} %slice.68.refs_0_, ...), custom_call_target="tpu_custom_call" | custom-call | tf_op jit(solution)/shard_map/pallas_call | solution.py:511
  47.9 23.8 %all_to_all.66 = f32[128,1,128]{2,1,0:T(1,128)S(1)} all-to-all(f32[128,1,128]{2,1,0:T(1,128)S(1)} %bitcast.50), channel_id=1, replica_groups=mesh['img_0'=4,'img_1'=4,'tile_0'=4,'tile_1'=2] {'img_0','img_1','tile_0..., dimensions={0} | all-to-all | bytes 131072 | tf_op jit(solution)/shard_map/all_to_all | solution.py:528
  71.7 6.4 %shard_map.30 = (f32[3,44,16,256]{3,2,1,0:T(8,128)S(1)}, f32[3,44,16,256]{3,2,1,0:T(8,128)S(1)}, f32[3,44,16,256]{3,2,1,0:T(8,128)S(1)}, f32[3,44,16,256]{3,2,1,...) custom-call(f32[128,128]{1,0:T(8,128)S(1)} %bitcast.42, ...), custom_call_target="tpu_custom_call" | custom-call | tf_op jit(solution)/shard_map/pallas_call | solution.py:511
  78.2 13.9 %all_to_all.67 = f32[128,1,128]{2,1,0:T(1,128)S(1)} all-to-all(f32[128,1,128]{2,1,0:T(1,128)S(1)} %bitcast.48), channel_id=1, replica_groups=mesh['img_0'=4,'img_1'=4,'tile_0'=4,'tile_1'=2] {'img_0','img_1','tile_0..., dimensions={0} | all-to-all | bytes 131072 | tf_op jit(solution)/shard_map/all_to_all | solution.py:528
  92.1 5.0 %shard_map.31 = (f32[3,44,16,256]{3,2,1,0:T(8,128)S(1)}, f32[3,32,16,256]{3,2,1,0:T(8,128)S(1)}, f32[128,128]{1,0:T(8,128)S(1)}) custom-call(f32[2]{0:T(128)S(1)} %get-tuple-element.93.refs_0_, f32[128,128]{1,0:T(8,128)S(1)} %bitcast.45, f32[3,44,16,256]{3,2,1,0:T(8,128)S(1)} %get-tuple-element.95.refs_2_, f32[3,44,16,256]{3,2,1,0:T(8,128)S(1)} %get-tuple-element.96.refs_3_, ...), custom_call_target="tpu_custom_call" | custom-call | tf_op jit(solution)/shard_map/pallas_call | solution.py:511
  97.1 13.9 %all_to_all.68 = f32[128,1,128]{2,1,0:T(1,128)S(1)} all-to-all(f32[128,1,128]{2,1,0:T(1,128)S(1)} %bitcast.53), channel_id=1, replica_groups=mesh['img_0'=4,'img_1'=4,'tile_0'=4,'tile_1'=2] {'img_0','img_1','tile_0..., dimensions={0} | all-to-all | bytes 131072 | tf_op jit(solution)/shard_map/all_to_all | solution.py:528
  112.7 4.0 %collective-permute-start.10 = (f32[3,12,16,256]{3,2,1,0:T(8,128)S(1)}, f32[3,12,16,256]{3,2,1,0:T(8,128)S(1)}, u32[]{:S(2)}, u32[]{:S(2)}) collective-permute-start(f32[3,12,16,256]{3,2,1,0:T(8,128)S(1)} %get-tuple-element.105.refs_0_), channel_id=1, source_target_pairs={{0,8},{8,16},{16,24},{24,32},{32,40},{40,48},{48,56},{56,64},{64,7... | collective-permute-start | bytes 1769480 | tf_op jit(solution)/shard_map/ppermute | solution.py:524
  116.8 3.2 %collective-permute-start.13 = (f32[3,6,16,256]{3,2,1,0:T(8,128)S(1)}, f32[3,6,16,256]{3,2,1,0:T(8,128)S(1)}, u32[]{:S(2)}, u32[]{:S(2)}) collective-permute-start(f32[3,6,16,256]{3,2,1,0:T(8,128)S(1)} %get-tuple-element.147), channel_id=1, source_target_pairs={{1,0},{2,1},{3,2},{4,3},{5,4},{6,5},{7,6},{9,8},{10,9},{11,10},{12... | collective-permute-start | bytes 884744 | tf_op jit(solution)/shard_map/ppermute | solution.py:524
  120.0 2.3 %collective-permute-start.12 = (f32[3,6,16,256]{3,2,1,0:T(8,128)S(1)}, f32[3,6,16,256]{3,2,1,0:T(8,128)S(1)}, u32[]{:S(2)}, u32[]{:S(2)}) collective-permute-start(f32[3,6,16,256]{3,2,1,0:T(8,128)S(1)} %get-tuple-element.148), channel_id=1, source_target_pairs={{0,1},{1,2},{2,3},{3,4},{4,5},{5,6},{6,7},{8,9},{9,10},{10,11},{11... | collective-permute-start | bytes 884744 | tf_op jit(solution)/shard_map/ppermute | solution.py:524
  125.1 2.8 %collective-permute-start.8 = (f32[3,20,16,256]{3,2,1,0:T(8,128)S(1)}, f32[3,20,16,256]{3,2,1,0:T(8,128)S(1)}, u32[]{:S(2)}, u32[]{:S(2)}) collective-permute-start(f32[3,20,16,256]{3,2,1,0:T(8,128)S(1)} %get-tuple-element.104.refs_0_), channel_id=1, source_target_pairs={{0,8},{8,16},{16,24},{24,32},{32,40},{40,48},{48,56},{56,64},{64,7... | collective-permute-start | bytes 2949128 | tf_op jit(solution)/shard_map/ppermute | solution.py:524
  128.4 5.5 %collective-permute-start.14 = (f32[6,6,16,256]{3,2,1,0:T(8,128)S(1)}, f32[6,6,16,256]{3,2,1,0:T(8,128)S(1)}, u32[]{:S(2)}, u32[]{:S(2)}) collective-permute-start(f32[6,6,16,256]{3,2,1,0:T(8,128)S(1)} %pad_maximum_fusion.3), channel_id=1, source_target_pairs={{0,1},{1,2},{2,3},{3,4},{4,5},{5,6},{6,7},{8,9},{9,10},{10,11},{11... | collective-permute-start | bytes 1769480 | tf_op jit(solution)/shard_map/ppermute | solution.py:524
  133.9 1.9 collective-permute-start.15
  135.9 4.8 %collective-permute-done.14.refs_5_ = f32[6,6,16,256]{3,2,1,0:T(8,128)S(1)} collective-permute-done((f32[6,6,16,256]{3,2,1,0:T(8,128)S(1)}, f32[6,6,16,256]{3,2,1,0:T(8,128)S(1)}, u32[]{:S(2)}, u32[]{:S(2)}) %collective-permute-start.14) | collective-permute-done | bytes 589856 | tf_op jit(solution)/shard_map/ppermute | solution.py:524
  140.7 4.7 %collective-permute-done.15.refs_6_ = f32[6,6,16,256]{3,2,1,0:T(8,128)S(1)} collective-permute-done((f32[6,6,16,256]{3,2,1,0:T(8,128)S(1)}, f32[6,6,16,256]{3,2,1,0:T(8,128)S(1)}, u32[]{:S(2)}, u32[]{:S(2)}) %collective-permute-start.15) | collective-permute-done | bytes 589856 | tf_op jit(solution)/shard_map/ppermute | solution.py:524
  145.4 3.4 %shard_map.33 = (f32[3,24,16,256]{3,2,1,0:T(8,128)S(1)}, f32[3,24,16,256]{3,2,1,0:T(8,128)S(1)}, f32[3,24,16,256]{3,2,1,0:T(8,128)S(1)}, f32[3,24,16,256]{3,2,1,...) custom-call(f32[3,12,16,256]{3,2,1,0:T(8,128)S(1)} %get-tuple-elemen, ...), custom_call_target="tpu_custom_call" | custom-call | tf_op jit(solution)/shard_map/pallas_call | solution.py:511
  149.5 5.1 %shard_map.34 = (f32[3,28,16,256]{3,2,1,0:T(8,128)S(1)}, f32[3,28,16,256]{3,2,1,0:T(8,128)S(1)}, f32[3,28,16,256]{3,2,1,0:T(8,128)S(1)}, f32[3,28,16,256]{3,2,1,...) custom-call(f32[3,20,16,256]{3,2,1,0:T(8,128)S(1)} %get-tuple-elemen, ...), custom_call_target="tpu_custom_call" | custom-call | tf_op jit(solution)/shard_map/pallas_call | solution.py:511
  154.6 19.5 %all_to_all.69 = f32[128,1,128]{2,1,0:T(1,128)S(1)} all-to-all(f32[128,1,128]{2,1,0:T(1,128)S(1)} %bitcast.51), channel_id=1, replica_groups=mesh['img_0'=4,'img_1'=4,'tile_0'=4,'tile_1'=2] {'img_0','img_1','tile_0..., dimensions={0} | all-to-all | bytes 131072 | tf_op jit(solution)/shard_map/all_to_all | solution.py:528
  174.2 6.5 %shard_map.35 = (f32[3,44,16,256]{3,2,1,0:T(8,128)S(1)}, f32[3,44,16,256]{3,2,1,0:T(8,128)S(1)}, f32[3,44,16,256]{3,2,1,0:T(8,128)S(1)}, f32[3,44,16,256]{3,2,1,...) custom-call(f32[128,128]{1,0:T(8,128)S(1)} %bitcast.43, ...), custom_call_target="tpu_custom_call" | custom-call | tf_op jit(solution)/shard_map/pallas_call | solution.py:511
  180.7 13.9 %all_to_all.70 = f32[128,1,128]{2,1,0:T(1,128)S(1)} all-to-all(f32[128,1,128]{2,1,0:T(1,128)S(1)} %bitcast.49), channel_id=1, replica_groups=mesh['img_0'=4,'img_1'=4,'tile_0'=4,'tile_1'=2] {'img_0','img_1','tile_0..., dimensions={0} | all-to-all | bytes 131072 | tf_op jit(solution)/shard_map/all_to_all | solution.py:528
  194.6 5.0 %shard_map.36 = (f32[3,44,16,256]{3,2,1,0:T(8,128)S(1)}, f32[3,32,16,256]{3,2,1,0:T(8,128)S(1)}, f32[128,128]{1,0:T(8,128)S(1)}) custom-call(f32[2]{0:T(128)S(1)} %get-tuple-element.126.refs_0_, f32[128,128]{1,0:T(8,128)S(1)} %bitcast.44, f32[3,44,16,256]{3,2,1,0:T(8,128)S(1)} %get-tuple-element.128.refs_2_, ...), custom_call_target="tpu_custom_call" | custom-call | tf_op jit(solution)/shard_map/pallas_call | solution.py:511
  199.6 13.9 %all_to_all.71 = f32[128,1,128]{2,1,0:T(1,128)S(1)} all-to-all(f32[128,1,128]{2,1,0:T(1,128)S(1)} %bitcast.52), channel_id=1, replica_groups=mesh['img_0'=4,'img_1'=4,'tile_0'=4,'tile_1'=2] {'img_0','img_1','tile_0..., dimensions={0} | all-to-all | bytes 131072 | tf_op jit(solution)/shard_map/all_to_all | solution.py:528
  214.1 2.1 copy.14
  (37 shorter events, 14.2 us)
Async XLA Ops:
  2.3 6.3 %copy-start = (f32[16,32,256]{2,1,0:T(8,128)S(1)}, f32[16,32,256]{2,1,0:T(8,128)}, u32[]{:S(2)}) copy-start(f32[16,32,256]{2,1,0:T(8,128)} %param.3) | copy-start | bytes 1572868
  2.4 20.4 %collective-permute-start.3 = (f32[3,12,16,256]{3,2,1,0:T(8,128)S(1)}, f32[3,12,16,256]{3,2,1,0:T(8,128)S(1)}, u32[]{:S(2)}, u32[]{:S(2)}) collective-permute-start(f32[3,12,16,256]{3,2,1,0:T(8,128)S(1)} %pad_maximum_fusion.refs_0_), channel_id=1, source_target_pairs={{8,0},{16,8},{24,16},{32,24},{40,32},{48,40},{56,48},{64,56},{72,6... | collective-permute-start | bytes 1769480 | tf_op jit(solution)/shard_map/ppermute | solution.py:524
  3.9 18.9 %collective-permute-start.2 = (f32[3,12,16,256]{3,2,1,0:T(8,128)S(1)}, f32[3,12,16,256]{3,2,1,0:T(8,128)S(1)}, u32[]{:S(2)}, u32[]{:S(2)}) collective-permute-start(f32[3,12,16,256]{3,2,1,0:T(8,128)S(1)} %pad_maximum_fusion.refs_0_), channel_id=1, source_target_pairs={{0,8},{8,16},{16,24},{24,32},{32,40},{40,48},{48,56},{56,64},{64,7... | collective-permute-start | bytes 1769480 | tf_op jit(solution)/shard_map/ppermute | solution.py:524
  9.0 9.1 %collective-permute-start.4 = (f32[4,6,16,256]{3,2,1,0:T(8,128)S(1)}, f32[4,6,16,256]{3,2,1,0:T(8,128)S(1)}, u32[]{:S(2)}, u32[]{:S(2)}) collective-permute-start(f32[4,6,16,256]{3,2,1,0:T(8,128)S(1)} %pad_maximum_fusion.5), channel_id=1, source_target_pairs={{0,1},{1,2},{2,3},{3,4},{4,5},{5,6},{6,7},{8,9},{9,10},{10,11},{11... | collective-permute-start | bytes 1179656 | tf_op jit(solution)/shard_map/ppermute | solution.py:524
  13.4 9.4 %collective-permute-start.5 = (f32[4,6,16,256]{3,2,1,0:T(8,128)S(1)}, f32[4,6,16,256]{3,2,1,0:T(8,128)S(1)}, u32[]{:S(2)}, u32[]{:S(2)}) collective-permute-start(f32[4,6,16,256]{3,2,1,0:T(8,128)S(1)} %pad_maximum_fusion.6), channel_id=1, source_target_pairs={{1,0},{2,1},{3,2},{4,3},{5,4},{6,5},{7,6},{9,8},{10,9},{11,10},{12... | collective-permute-start | bytes 1179656 | tf_op jit(solution)/shard_map/ppermute | solution.py:524
  15.4 25.7 %collective-permute-start.1 = (f32[3,20,16,256]{3,2,1,0:T(8,128)S(1)}, f32[3,20,16,256]{3,2,1,0:T(8,128)S(1)}, u32[]{:S(2)}, u32[]{:S(2)}) collective-permute-start(f32[3,20,16,256]{3,2,1,0:T(8,128)S(1)} %slice.68.refs_0_), channel_id=1, source_target_pairs={{8,0},{16,8},{24,16},{32,24},{40,32},{48,40},{56,48},{64,56},{72,6... | collective-permute-start | bytes 2949128 | tf_op jit(solution)/shard_map/ppermute | solution.py:524
  18.1 24.8 %collective-permute-start = (f32[3,20,16,256]{3,2,1,0:T(8,128)S(1)}, f32[3,20,16,256]{3,2,1,0:T(8,128)S(1)}, u32[]{:S(2)}, u32[]{:S(2)}) collective-permute-start(f32[3,20,16,256]{3,2,1,0:T(8,128)S(1)} %slice.68.refs_0_), channel_id=1, source_target_pairs={{0,8},{8,16},{16,24},{24,32},{32,40},{40,48},{48,56},{56,64},{64,7... | collective-permute-start | bytes 2949128 | tf_op jit(solution)/shard_map/ppermute | solution.py:524
  22.9 10.0 %collective-permute-start.6 = (f32[6,6,16,256]{3,2,1,0:T(8,128)S(1)}, f32[6,6,16,256]{3,2,1,0:T(8,128)S(1)}, u32[]{:S(2)}, u32[]{:S(2)}) collective-permute-start(f32[6,6,16,256]{3,2,1,0:T(8,128)S(1)} %pad_maximum_fusion.1), channel_id=1, source_target_pairs={{0,1},{1,2},{2,3},{3,4},{4,5},{5,6},{6,7},{8,9},{9,10},{10,11},{11... | collective-permute-start | bytes 1769480 | tf_op jit(solution)/shard_map/ppermute | solution.py:524
  26.2 11.5 %collective-permute-start.7 = (f32[6,6,16,256]{3,2,1,0:T(8,128)S(1)}, f32[6,6,16,256]{3,2,1,0:T(8,128)S(1)}, u32[]{:S(2)}, u32[]{:S(2)}) collective-permute-start(f32[6,6,16,256]{3,2,1,0:T(8,128)S(1)} %pad_maximum_fusion.2), channel_id=1, source_target_pairs={{1,0},{2,1},{3,2},{4,3},{5,4},{6,5},{7,6},{9,8},{10,9},{11,10},{12... | collective-permute-start | bytes 1769480 | tf_op jit(solution)/shard_map/ppermute | solution.py:524
  111.4 16.5 %collective-permute-start.11 = (f32[3,12,16,256]{3,2,1,0:T(8,128)S(1)}, f32[3,12,16,256]{3,2,1,0:T(8,128)S(1)}, u32[]{:S(2)}, u32[]{:S(2)}) collective-permute-start(f32[3,12,16,256]{3,2,1,0:T(8,128)S(1)} %get-tuple-element.105.refs_0_), channel_id=1, source_target_pairs={{8,0},{16,8},{24,16},{32,24},{40,32},{48,40},{56,48},{64,56},{72,6... | collective-permute-start | bytes 1769480 | tf_op jit(solution)/shard_map/ppermute | solution.py:524
  112.7 15.6 %collective-permute-start.10 = (f32[3,12,16,256]{3,2,1,0:T(8,128)S(1)}, f32[3,12,16,256]{3,2,1,0:T(8,128)S(1)}, u32[]{:S(2)}, u32[]{:S(2)}) collective-permute-start(f32[3,12,16,256]{3,2,1,0:T(8,128)S(1)} %get-tuple-element.105.refs_0_), channel_id=1, source_target_pairs={{0,8},{8,16},{16,24},{24,32},{32,40},{40,48},{48,56},{56,64},{64,7... | collective-permute-start | bytes 1769480 | tf_op jit(solution)/shard_map/ppermute | solution.py:524
  116.8 8.3 %collective-permute-start.13 = (f32[3,6,16,256]{3,2,1,0:T(8,128)S(1)}, f32[3,6,16,256]{3,2,1,0:T(8,128)S(1)}, u32[]{:S(2)}, u32[]{:S(2)}) collective-permute-start(f32[3,6,16,256]{3,2,1,0:T(8,128)S(1)} %get-tuple-element.147), channel_id=1, source_target_pairs={{1,0},{2,1},{3,2},{4,3},{5,4},{6,5},{7,6},{9,8},{10,9},{11,10},{12... | collective-permute-start | bytes 884744 | tf_op jit(solution)/shard_map/ppermute | solution.py:524
  120.0 7.9 %collective-permute-start.12 = (f32[3,6,16,256]{3,2,1,0:T(8,128)S(1)}, f32[3,6,16,256]{3,2,1,0:T(8,128)S(1)}, u32[]{:S(2)}, u32[]{:S(2)}) collective-permute-start(f32[3,6,16,256]{3,2,1,0:T(8,128)S(1)} %get-tuple-element.148), channel_id=1, source_target_pairs={{0,1},{1,2},{2,3},{3,4},{4,5},{5,6},{6,7},{8,9},{9,10},{10,11},{11... | collective-permute-start | bytes 884744 | tf_op jit(solution)/shard_map/ppermute | solution.py:524
  122.4 26.5 %collective-permute-start.9 = (f32[3,20,16,256]{3,2,1,0:T(8,128)S(1)}, f32[3,20,16,256]{3,2,1,0:T(8,128)S(1)}, u32[]{:S(2)}, u32[]{:S(2)}) collective-permute-start(f32[3,20,16,256]{3,2,1,0:T(8,128)S(1)} %get-tuple-element.104.refs_0_), channel_id=1, source_target_pairs={{8,0},{16,8},{24,16},{32,24},{40,32},{48,40},{56,48},{64,56},{72,6... | collective-permute-start | bytes 2949128 | tf_op jit(solution)/shard_map/ppermute | solution.py:524
  125.1 24.4 %collective-permute-start.8 = (f32[3,20,16,256]{3,2,1,0:T(8,128)S(1)}, f32[3,20,16,256]{3,2,1,0:T(8,128)S(1)}, u32[]{:S(2)}, u32[]{:S(2)}) collective-permute-start(f32[3,20,16,256]{3,2,1,0:T(8,128)S(1)} %get-tuple-element.104.refs_0_), channel_id=1, source_target_pairs={{0,8},{8,16},{16,24},{24,32},{32,40},{40,48},{48,56},{56,64},{64,7... | collective-permute-start | bytes 2949128 | tf_op jit(solution)/shard_map/ppermute | solution.py:524
  128.4 12.3 %collective-permute-start.14 = (f32[6,6,16,256]{3,2,1,0:T(8,128)S(1)}, f32[6,6,16,256]{3,2,1,0:T(8,128)S(1)}, u32[]{:S(2)}, u32[]{:S(2)}) collective-permute-start(f32[6,6,16,256]{3,2,1,0:T(8,128)S(1)} %pad_maximum_fusion.3), channel_id=1, source_target_pairs={{0,1},{1,2},{2,3},{3,4},{4,5},{5,6},{6,7},{8,9},{9,10},{10,11},{11... | collective-permute-start | bytes 1769480 | tf_op jit(solution)/shard_map/ppermute | solution.py:524
  133.9 11.5 %collective-permute-start.15 = (f32[6,6,16,256]{3,2,1,0:T(8,128)S(1)}, f32[6,6,16,256]{3,2,1,0:T(8,128)S(1)}, u32[]{:S(2)}, u32[]{:S(2)}) collective-permute-start(f32[6,6,16,256]{3,2,1,0:T(8,128)S(1)} %pad_maximum_fusion.4), channel_id=1, source_target_pairs={{1,0},{2,1},{3,2},{4,3},{5,4},{6,5},{7,6},{9,8},{10,9},{11,10},{12... | collective-permute-start | bytes 1769480 | tf_op jit(solution)/shard_map/ppermute | solution.py:524

commit v9 on v8

--- a/solution.py
+++ b/solution.py
@@ -403,8 +403,8 @@
     live = interior(where)
     step = step * live
     inv = 1.0 / tau
-    scal_ref[0] = tau
-    scal_ref[1] = pull
+    first = lax.broadcasted_iota(jnp.int32, scal_ref.shape, 0) == 0
+    scal_ref[...] = jnp.where(first, tau, pull)
     from_p, from_m, from_n = -4.0 * step * inv, step * (inv + pull), step * (inv - pull)
     bend = step * tau
     regions = (
@@ -455,7 +455,8 @@
     own = rows - 2 * HALO
     tile, last_tile = where[1], where[2] - 1
     live = interior(where)
-    tau, pull = scal_ref[0], scal_ref[1]
+    kept = scal_ref[...]
+    tau, pull = kept[0, 0], kept[1, 0]
     step = step_of(all_ref, cells) * live
     advance(
         h_ref, -step, (p_ref, m0_ref, n0_ref, lm0_ref, ln0_ref), 0,
@@ -505,14 +506,13 @@
     return (*found, lax.axis_size(TILE), lax.axis_size(IMG))
 
 
-def call(kernel, operands, outs, scratch, scalars=0, small_out=()):
-    smem = pl.BlockSpec(memory_space=pltpu.SMEM)
+def call(kernel, operands, outs, scratch):
     vmem = pl.BlockSpec(memory_space=pltpu.VMEM)
     return pl.pallas_call(
         lambda *refs: kernel(position(), *refs),
         out_shape=outs,
-        in_specs=[smem if i < scalars else vmem for i in range(len(operands))],
-        out_specs=[smem if i in small_out else vmem for i in range(len(outs))],
+        in_specs=[vmem] * len(operands),
+        out_specs=[vmem] * len(outs),
         scratch_shapes=[pltpu.VMEM(shape, jnp.float32) for shape in scratch],
         compiler_params=pltpu.CompilerParams(vmem_limit_bytes=VMEM_LIMIT),
     )(*operands)
@@ -582,16 +582,14 @@
         phi, m, n, lm, ln, g, scal, sums = call(
             lambda *refs: second_kernel(tiles, cells, *refs),
             [from_everyone(sums), *far, *near, coef_ext],
-            [whole] * 6 + [f32(2), table],
+            [whole] * 6 + [f32(8, 128), table],
             [ext, *scratch(rows)],
-            small_out=(6,),
         )
         phi, g, sums = call(
             lambda *refs: third_kernel(cells, *refs),
             [scal, from_everyone(sums), phi, m, n, lm, ln, g, coef_ext],
             [whole, f32(3, own, depth, width), table],
             [ext, ext, *scratch(rows)],
-            scalars=1,
         )
         edge, mid = call(
             lambda *refs: last_kernel(cells, *refs),

time: 217 us -> 215 us (level)
  Pallas kernels: 40.8 us -> 38.5 us
    pallas_call x10, Pallas kernels: 40.8 us -> 38.5 us  [call(): pl.pallas_call(lambda *refs: kernel(position(), *refs), out_shape=outs, i...]
where the time goes in v9:
time: 215 us; the launch traced here: 214 us
  blocking collectives  99 us (46%)
  starting transfers between devices  44.6 us (21%)
  Pallas kernels  38.5 us (18%)
  waiting for transfers between devices  25.9 us (12%)
  local copies, waits for them, and re-layouts  5.11 us (2%)
    all_to_all x6, blocking collectives, from_everyone(): return lax.all_to_all(rows, IMG_TILE, 0, 0, tiled=True)  99 us
    ppermute x16, starting transfers between devices, beside(): return lax.ppermute(cells, axis, pairs)  44.6 us
    pallas_call x10, Pallas kernels, call(): pl.pallas_call(lambda *refs: kernel(position(), *refs), out_shape=outs, i...  38.5 us
    ppermute x16, waiting for transfers between devices, beside(): return lax.ppermute(cells, axis, pairs)  25.9 us
  transfers between devices with their start and end apart: 16, of which 10 were waited for; matrix products, arithmetic and copies ran while one was open for 0% of the time, Pallas kernels for 3%

profile of v9, /device:TPU:1, one launch (start us, length us, event | category | flops | bytes accessed | tf_op | source)
XLA Modules:
  0.0 213.9 jit_solution(14876392743120596781)
XLA Ops:
  0.0 2.3 %copy.17 = f32[1,3,16,32,256]{4,2,3,1,0:T(8,128)S(1)} copy(f32[1,3,16,32,256]{4,3,2,1,0:T(8,128)} %param.2) | data formatting | bytes 3145728 | tf_op args[0]
  3.9 4.7 %collective-permute-start.2 = (f32[3,12,16,256]{3,2,1,0:T(8,128)S(1)}, f32[3,12,16,256]{3,2,1,0:T(8,128)S(1)}, u32[]{:S(2)}, u32[]{:S(2)}) collective-permute-start(f32[3,12,16,256]{3,2,1,0:T(8,128)S(1)} %pad_maximum_fusion.refs_0_), channel_id=1, source_target_pairs={{0,8},{8,16},{16,24},{24,32},{32,40},{40,48},{48,56},{56,64},{64,7... | collective-permute-start | bytes 1769480 | tf_op jit(solution)/shard_map/ppermute | solution.py:524
  9.0 4.4 %collective-permute-start.4 = (f32[4,6,16,256]{3,2,1,0:T(8,128)S(1)}, f32[4,6,16,256]{3,2,1,0:T(8,128)S(1)}, u32[]{:S(2)}, u32[]{:S(2)}) collective-permute-start(f32[4,6,16,256]{3,2,1,0:T(8,128)S(1)} %pad_maximum_fusion.5), channel_id=1, source_target_pairs={{0,1},{1,2},{2,3},{3,4},{4,5},{5,6},{6,7},{8,9},{9,10},{10,11},{11... | collective-permute-start | bytes 1179656 | tf_op jit(solution)/shard_map/ppermute | solution.py:524
  13.4 1.9 collective-permute-start.5
  18.1 3.2 %collective-permute-start = (f32[3,20,16,256]{3,2,1,0:T(8,128)S(1)}, f32[3,20,16,256]{3,2,1,0:T(8,128)S(1)}, u32[]{:S(2)}, u32[]{:S(2)}) collective-permute-start(f32[3,20,16,256]{3,2,1,0:T(8,128)S(1)} %slice.68.refs_0_), channel_id=1, source_target_pairs={{0,8},{8,16},{16,24},{24,32},{32,40},{40,48},{48,56},{56,64},{64,7... | collective-permute-start | bytes 2949128 | tf_op jit(solution)/shard_map/ppermute | solution.py:524
  22.9 3.2 %collective-permute-start.6 = (f32[6,6,16,256]{3,2,1,0:T(8,128)S(1)}, f32[6,6,16,256]{3,2,1,0:T(8,128)S(1)}, u32[]{:S(2)}, u32[]{:S(2)}) collective-permute-start(f32[6,6,16,256]{3,2,1,0:T(8,128)S(1)} %pad_maximum_fusion.1), channel_id=1, source_target_pairs={{0,1},{1,2},{2,3},{3,4},{4,5},{5,6},{6,7},{8,9},{9,10},{10,11},{11... | collective-permute-start | bytes 1769480 | tf_op jit(solution)/shard_map/ppermute | solution.py:524
  26.2 1.9 collective-permute-start.7
  28.1 4.8 %collective-permute-done.6.refs_5_ = f32[6,6,16,256]{3,2,1,0:T(8,128)S(1)} collective-permute-done((f32[6,6,16,256]{3,2,1,0:T(8,128)S(1)}, f32[6,6,16,256]{3,2,1,0:T(8,128)S(1)}, u32[]{:S(2)}, u32[]{:S(2)}) %collective-permute-start.6) | collective-permute-done | bytes 589856 | tf_op jit(solution)/shard_map/ppermute | solution.py:524
  33.0 4.7 %collective-permute-done.7.refs_6_ = f32[6,6,16,256]{3,2,1,0:T(8,128)S(1)} collective-permute-done((f32[6,6,16,256]{3,2,1,0:T(8,128)S(1)}, f32[6,6,16,256]{3,2,1,0:T(8,128)S(1)}, u32[]{:S(2)}, u32[]{:S(2)}) %collective-permute-start.7) | collective-permute-done | bytes 589856 | tf_op jit(solution)/shard_map/ppermute | solution.py:524
  37.7 3.4 %shard_map.28 = (f32[3,24,16,256]{3,2,1,0:T(8,128)S(1)}, f32[3,24,16,256]{3,2,1,0:T(8,128)S(1)}, f32[3,24,16,256]{3,2,1,0:T(8,128)S(1)}, f32[3,24,16,256]{3,2,1,...) custom-call(f32[3,12,16,256]{3,2,1,0:T(8,128)S(1)} %pad_maximum_fusi, ...), custom_call_target="tpu_custom_call" | custom-call | tf_op jit(solution)/shard_map/pallas_call | solution.py:511
  42.8 5.1 %shard_map.29 = (f32[3,28,16,256]{3,2,1,0:T(8,128)S(1)}, f32[3,28,16,256]{3,2,1,0:T(8,128)S(1)}, f32[3,28,16,256]{3,2,1,0:T(8,128)S(1)}, f32[3,28,16,256]{3,2,1,...) custom-call(f32[3,20,16,256]{3,2,1,0:T(8,128)S(1)} %slice.68.refs_0_, ...), custom_call_target="tpu_custom_call" | custom-call | tf_op jit(solution)/shard_map/pallas_call | solution.py:511
  47.9 23.8 %all_to_all.66 = f32[128,1,128]{2,1,0:T(1,128)S(1)} all-to-all(f32[128,1,128]{2,1,0:T(1,128)S(1)} %bitcast.50), channel_id=1, replica_groups=mesh['img_0'=4,'img_1'=4,'tile_0'=4,'tile_1'=2] {'img_0','img_1','tile_0..., dimensions={0} | all-to-all | bytes 131072 | tf_op jit(solution)/shard_map/all_to_all | solution.py:528
  71.7 5.9 %shard_map.30 = (f32[3,44,16,256]{3,2,1,0:T(8,128)S(1)}, f32[3,44,16,256]{3,2,1,0:T(8,128)S(1)}, f32[3,44,16,256]{3,2,1,0:T(8,128)S(1)}, f32[3,44,16,256]{3,2,1,...) custom-call(f32[128,128]{1,0:T(8,128)S(1)} %bitcast.42, ...), custom_call_target="tpu_custom_call" | custom-call | tf_op jit(solution)/shard_map/pallas_call | solution.py:511
  77.6 13.9 %all_to_all.67 = f32[128,1,128]{2,1,0:T(1,128)S(1)} all-to-all(f32[128,1,128]{2,1,0:T(1,128)S(1)} %bitcast.48), channel_id=1, replica_groups=mesh['img_0'=4,'img_1'=4,'tile_0'=4,'tile_1'=2] {'img_0','img_1','tile_0..., dimensions={0} | all-to-all | bytes 131072 | tf_op jit(solution)/shard_map/all_to_all | solution.py:528
  91.5 4.4 %shard_map.31 = (f32[3,44,16,256]{3,2,1,0:T(8,128)S(1)}, f32[3,32,16,256]{3,2,1,0:T(8,128)S(1)}, f32[128,128]{1,0:T(8,128)S(1)}) custom-call(f32[8,128]{1,0:T(8,128)S(1)} %get-tuple-element.93.refs_0_, f32[128,128]{1,0:T(8,128)S(1)} %bitcast.45, f32[3,44,16,256]{3,2,1,0:T(8,128)S(1)} %get-tuple-element.95.refs_2_, ...), custom_call_target="tpu_custom_call" | custom-call | tf_op jit(solution)/shard_map/pallas_call | solution.py:511
  96.0 13.9 %all_to_all.68 = f32[128,1,128]{2,1,0:T(1,128)S(1)} all-to-all(f32[128,1,128]{2,1,0:T(1,128)S(1)} %bitcast.53), channel_id=1, replica_groups=mesh['img_0'=4,'img_1'=4,'tile_0'=4,'tile_1'=2] {'img_0','img_1','tile_0..., dimensions={0} | all-to-all | bytes 131072 | tf_op jit(solution)/shard_map/all_to_all | solution.py:528
  111.6 4.0 %collective-permute-start.10 = (f32[3,12,16,256]{3,2,1,0:T(8,128)S(1)}, f32[3,12,16,256]{3,2,1,0:T(8,128)S(1)}, u32[]{:S(2)}, u32[]{:S(2)}) collective-permute-start(f32[3,12,16,256]{3,2,1,0:T(8,128)S(1)} %get-tuple-element.105.refs_0_), channel_id=1, source_target_pairs={{0,8},{8,16},{16,24},{24,32},{32,40},{40,48},{48,56},{56,64},{64,7... | collective-permute-start | bytes 1769480 | tf_op jit(solution)/shard_map/ppermute | solution.py:524
  115.7 3.2 %collective-permute-start.13 = (f32[3,6,16,256]{3,2,1,0:T(8,128)S(1)}, f32[3,6,16,256]{3,2,1,0:T(8,128)S(1)}, u32[]{:S(2)}, u32[]{:S(2)}) collective-permute-start(f32[3,6,16,256]{3,2,1,0:T(8,128)S(1)} %get-tuple-element.147), channel_id=1, source_target_pairs={{1,0},{2,1},{3,2},{4,3},{5,4},{6,5},{7,6},{9,8},{10,9},{11,10},{12... | collective-permute-start | bytes 884744 | tf_op jit(solution)/shard_map/ppermute | solution.py:524
  118.9 2.3 %collective-permute-start.12 = (f32[3,6,16,256]{3,2,1,0:T(8,128)S(1)}, f32[3,6,16,256]{3,2,1,0:T(8,128)S(1)}, u32[]{:S(2)}, u32[]{:S(2)}) collective-permute-start(f32[3,6,16,256]{3,2,1,0:T(8,128)S(1)} %get-tuple-element.148), channel_id=1, source_target_pairs={{0,1},{1,2},{2,3},{3,4},{4,5},{5,6},{6,7},{8,9},{9,10},{10,11},{11... | collective-permute-start | bytes 884744 | tf_op jit(solution)/shard_map/ppermute | solution.py:524
  124.0 2.8 %collective-permute-start.8 = (f32[3,20,16,256]{3,2,1,0:T(8,128)S(1)}, f32[3,20,16,256]{3,2,1,0:T(8,128)S(1)}, u32[]{:S(2)}, u32[]{:S(2)}) collective-permute-start(f32[3,20,16,256]{3,2,1,0:T(8,128)S(1)} %get-tuple-element.104.refs_0_), channel_id=1, source_target_pairs={{0,8},{8,16},{16,24},{24,32},{32,40},{40,48},{48,56},{56,64},{64,7... | collective-permute-start | bytes 2949128 | tf_op jit(solution)/shard_map/ppermute | solution.py:524
  127.3 5.5 %collective-permute-start.14 = (f32[6,6,16,256]{3,2,1,0:T(8,128)S(1)}, f32[6,6,16,256]{3,2,1,0:T(8,128)S(1)}, u32[]{:S(2)}, u32[]{:S(2)}) collective-permute-start(f32[6,6,16,256]{3,2,1,0:T(8,128)S(1)} %pad_maximum_fusion.3), channel_id=1, source_target_pairs={{0,1},{1,2},{2,3},{3,4},{4,5},{5,6},{6,7},{8,9},{9,10},{10,11},{11... | collective-permute-start | bytes 1769480 | tf_op jit(solution)/shard_map/ppermute | solution.py:524
  132.8 1.9 collective-permute-start.15
  134.8 4.8 %collective-permute-done.14.refs_5_ = f32[6,6,16,256]{3,2,1,0:T(8,128)S(1)} collective-permute-done((f32[6,6,16,256]{3,2,1,0:T(8,128)S(1)}, f32[6,6,16,256]{3,2,1,0:T(8,128)S(1)}, u32[]{:S(2)}, u32[]{:S(2)}) %collective-permute-start.14) | collective-permute-done | bytes 589856 | tf_op jit(solution)/shard_map/ppermute | solution.py:524
  139.6 4.7 %collective-permute-done.15.refs_6_ = f32[6,6,16,256]{3,2,1,0:T(8,128)S(1)} collective-permute-done((f32[6,6,16,256]{3,2,1,0:T(8,128)S(1)}, f32[6,6,16,256]{3,2,1,0:T(8,128)S(1)}, u32[]{:S(2)}, u32[]{:S(2)}) %collective-permute-start.15) | collective-permute-done | bytes 589856 | tf_op jit(solution)/shard_map/ppermute | solution.py:524
  144.3 3.4 %shard_map.33 = (f32[3,24,16,256]{3,2,1,0:T(8,128)S(1)}, f32[3,24,16,256]{3,2,1,0:T(8,128)S(1)}, f32[3,24,16,256]{3,2,1,0:T(8,128)S(1)}, f32[3,24,16,256]{3,2,1,...) custom-call(f32[3,12,16,256]{3,2,1,0:T(8,128)S(1)} %get-tuple-elemen, ...), custom_call_target="tpu_custom_call" | custom-call | tf_op jit(solution)/shard_map/pallas_call | solution.py:511
  148.4 5.1 %shard_map.34 = (f32[3,28,16,256]{3,2,1,0:T(8,128)S(1)}, f32[3,28,16,256]{3,2,1,0:T(8,128)S(1)}, f32[3,28,16,256]{3,2,1,0:T(8,128)S(1)}, f32[3,28,16,256]{3,2,1,...) custom-call(f32[3,20,16,256]{3,2,1,0:T(8,128)S(1)} %get-tuple-elemen, ...), custom_call_target="tpu_custom_call" | custom-call | tf_op jit(solution)/shard_map/pallas_call | solution.py:511
  153.5 19.5 %all_to_all.69 = f32[128,1,128]{2,1,0:T(1,128)S(1)} all-to-all(f32[128,1,128]{2,1,0:T(1,128)S(1)} %bitcast.51), channel_id=1, replica_groups=mesh['img_0'=4,'img_1'=4,'tile_0'=4,'tile_1'=2] {'img_0','img_1','tile_0..., dimensions={0} | all-to-all | bytes 131072 | tf_op jit(solution)/shard_map/all_to_all | solution.py:528
  173.0 5.9 %shard_map.35 = (f32[3,44,16,256]{3,2,1,0:T(8,128)S(1)}, f32[3,44,16,256]{3,2,1,0:T(8,128)S(1)}, f32[3,44,16,256]{3,2,1,0:T(8,128)S(1)}, f32[3,44,16,256]{3,2,1,...) custom-call(f32[128,128]{1,0:T(8,128)S(1)} %bitcast.43, ...), custom_call_target="tpu_custom_call" | custom-call | tf_op jit(solution)/shard_map/pallas_call | solution.py:511
  178.9 13.9 %all_to_all.70 = f32[128,1,128]{2,1,0:T(1,128)S(1)} all-to-all(f32[128,1,128]{2,1,0:T(1,128)S(1)} %bitcast.49), channel_id=1, replica_groups=mesh['img_0'=4,'img_1'=4,'tile_0'=4,'tile_1'=2] {'img_0','img_1','tile_0..., dimensions={0} | all-to-all | bytes 131072 | tf_op jit(solution)/shard_map/all_to_all | solution.py:528
  192.9 4.4 %shard_map.36 = (f32[3,44,16,256]{3,2,1,0:T(8,128)S(1)}, f32[3,32,16,256]{3,2,1,0:T(8,128)S(1)}, f32[128,128]{1,0:T(8,128)S(1)}) custom-call(f32[8,128]{1,0:T(8,128)S(1)} %get-tuple-element.126.refs_0_, f32[128,128]{1,0:T(8,128)S(1)} %bitcast.44, f32[3,44,16,256]{3,2,1,0:T(8,128)S(1)} %get-tuple-element.128.refs_2_, ...), custom_call_target="tpu_custom_call" | custom-call | tf_op jit(solution)/shard_map/pallas_call | solution.py:511
  197.3 13.9 %all_to_all.71 = f32[128,1,128]{2,1,0:T(1,128)S(1)} all-to-all(f32[128,1,128]{2,1,0:T(1,128)S(1)} %bitcast.52), channel_id=1, replica_groups=mesh['img_0'=4,'img_1'=4,'tile_0'=4,'tile_1'=2] {'img_0','img_1','tile_0..., dimensions={0} | all-to-all | bytes 131072 | tf_op jit(solution)/shard_map/all_to_all | solution.py:528
  211.8 2.1 copy.14
  (37 shorter events, 14.2 us)
Async XLA Ops:
  2.3 6.3 %copy-start = (f32[16,32,256]{2,1,0:T(8,128)S(1)}, f32[16,32,256]{2,1,0:T(8,128)}, u32[]{:S(2)}) copy-start(f32[16,32,256]{2,1,0:T(8,128)} %param.3) | copy-start | bytes 1572868
  2.4 20.4 %collective-permute-start.3 = (f32[3,12,16,256]{3,2,1,0:T(8,128)S(1)}, f32[3,12,16,256]{3,2,1,0:T(8,128)S(1)}, u32[]{:S(2)}, u32[]{:S(2)}) collective-permute-start(f32[3,12,16,256]{3,2,1,0:T(8,128)S(1)} %pad_maximum_fusion.refs_0_), channel_id=1, source_target_pairs={{8,0},{16,8},{24,16},{32,24},{40,32},{48,40},{56,48},{64,56},{72,6... | collective-permute-start | bytes 1769480 | tf_op jit(solution)/shard_map/ppermute | solution.py:524
  3.9 18.9 %collective-permute-start.2 = (f32[3,12,16,256]{3,2,1,0:T(8,128)S(1)}, f32[3,12,16,256]{3,2,1,0:T(8,128)S(1)}, u32[]{:S(2)}, u32[]{:S(2)}) collective-permute-start(f32[3,12,16,256]{3,2,1,0:T(8,128)S(1)} %pad_maximum_fusion.refs_0_), channel_id=1, source_target_pairs={{0,8},{8,16},{16,24},{24,32},{32,40},{40,48},{48,56},{56,64},{64,7... | collective-permute-start | bytes 1769480 | tf_op jit(solution)/shard_map/ppermute | solution.py:524
  9.0 9.1 %collective-permute-start.4 = (f32[4,6,16,256]{3,2,1,0:T(8,128)S(1)}, f32[4,6,16,256]{3,2,1,0:T(8,128)S(1)}, u32[]{:S(2)}, u32[]{:S(2)}) collective-permute-start(f32[4,6,16,256]{3,2,1,0:T(8,128)S(1)} %pad_maximum_fusion.5), channel_id=1, source_target_pairs={{0,1},{1,2},{2,3},{3,4},{4,5},{5,6},{6,7},{8,9},{9,10},{10,11},{11... | collective-permute-start | bytes 1179656 | tf_op jit(solution)/shard_map/ppermute | solution.py:524
  13.4 9.4 %collective-permute-start.5 = (f32[4,6,16,256]{3,2,1,0:T(8,128)S(1)}, f32[4,6,16,256]{3,2,1,0:T(8,128)S(1)}, u32[]{:S(2)}, u32[]{:S(2)}) collective-permute-start(f32[4,6,16,256]{3,2,1,0:T(8,128)S(1)} %pad_maximum_fusion.6), channel_id=1, source_target_pairs={{1,0},{2,1},{3,2},{4,3},{5,4},{6,5},{7,6},{9,8},{10,9},{11,10},{12... | collective-permute-start | bytes 1179656 | tf_op jit(solution)/shard_map/ppermute | solution.py:524
  15.4 25.7 %collective-permute-start.1 = (f32[3,20,16,256]{3,2,1,0:T(8,128)S(1)}, f32[3,20,16,256]{3,2,1,0:T(8,128)S(1)}, u32[]{:S(2)}, u32[]{:S(2)}) collective-permute-start(f32[3,20,16,256]{3,2,1,0:T(8,128)S(1)} %slice.68.refs_0_), channel_id=1, source_target_pairs={{8,0},{16,8},{24,16},{32,24},{40,32},{48,40},{56,48},{64,56},{72,6... | collective-permute-start | bytes 2949128 | tf_op jit(solution)/shard_map/ppermute | solution.py:524
  18.1 24.8 %collective-permute-start = (f32[3,20,16,256]{3,2,1,0:T(8,128)S(1)}, f32[3,20,16,256]{3,2,1,0:T(8,128)S(1)}, u32[]{:S(2)}, u32[]{:S(2)}) collective-permute-start(f32[3,20,16,256]{3,2,1,0:T(8,128)S(1)} %slice.68.refs_0_), channel_id=1, source_target_pairs={{0,8},{8,16},{16,24},{24,32},{32,40},{40,48},{48,56},{56,64},{64,7... | collective-permute-start | bytes 2949128 | tf_op jit(solution)/shard_map/ppermute | solution.py:524
  22.9 10.0 %collective-permute-start.6 = (f32[6,6,16,256]{3,2,1,0:T(8,128)S(1)}, f32[6,6,16,256]{3,2,1,0:T(8,128)S(1)}, u32[]{:S(2)}, u32[]{:S(2)}) collective-permute-start(f32[6,6,16,256]{3,2,1,0:T(8,128)S(1)} %pad_maximum_fusion.1), channel_id=1, source_target_pairs={{0,1},{1,2},{2,3},{3,4},{4,5},{5,6},{6,7},{8,9},{9,10},{10,11},{11... | collective-permute-start | bytes 1769480 | tf_op jit(solution)/shard_map/ppermute | solution.py:524
  26.2 11.5 %collective-permute-start.7 = (f32[6,6,16,256]{3,2,1,0:T(8,128)S(1)}, f32[6,6,16,256]{3,2,1,0:T(8,128)S(1)}, u32[]{:S(2)}, u32[]{:S(2)}) collective-permute-start(f32[6,6,16,256]{3,2,1,0:T(8,128)S(1)} %pad_maximum_fusion.2), channel_id=1, source_target_pairs={{1,0},{2,1},{3,2},{4,3},{5,4},{6,5},{7,6},{9,8},{10,9},{11,10},{12... | collective-permute-start | bytes 1769480 | tf_op jit(solution)/shard_map/ppermute | solution.py:524
  110.3 16.5 %collective-permute-start.11 = (f32[3,12,16,256]{3,2,1,0:T(8,128)S(1)}, f32[3,12,16,256]{3,2,1,0:T(8,128)S(1)}, u32[]{:S(2)}, u32[]{:S(2)}) collective-permute-start(f32[3,12,16,256]{3,2,1,0:T(8,128)S(1)} %get-tuple-element.105.refs_0_), channel_id=1, source_target_pairs={{8,0},{16,8},{24,16},{32,24},{40,32},{48,40},{56,48},{64,56},{72,6... | collective-permute-start | bytes 1769480 | tf_op jit(solution)/shard_map/ppermute | solution.py:524
  111.6 15.6 %collective-permute-start.10 = (f32[3,12,16,256]{3,2,1,0:T(8,128)S(1)}, f32[3,12,16,256]{3,2,1,0:T(8,128)S(1)}, u32[]{:S(2)}, u32[]{:S(2)}) collective-permute-start(f32[3,12,16,256]{3,2,1,0:T(8,128)S(1)} %get-tuple-element.105.refs_0_), channel_id=1, source_target_pairs={{0,8},{8,16},{16,24},{24,32},{32,40},{40,48},{48,56},{56,64},{64,7... | collective-permute-start | bytes 1769480 | tf_op jit(solution)/shard_map/ppermute | solution.py:524
  115.7 8.3 %collective-permute-start.13 = (f32[3,6,16,256]{3,2,1,0:T(8,128)S(1)}, f32[3,6,16,256]{3,2,1,0:T(8,128)S(1)}, u32[]{:S(2)}, u32[]{:S(2)}) collective-permute-start(f32[3,6,16,256]{3,2,1,0:T(8,128)S(1)} %get-tuple-element.147), channel_id=1, source_target_pairs={{1,0},{2,1},{3,2},{4,3},{5,4},{6,5},{7,6},{9,8},{10,9},{11,10},{12... | collective-permute-start | bytes 884744 | tf_op jit(solution)/shard_map/ppermute | solution.py:524
  118.9 7.9 %collective-permute-start.12 = (f32[3,6,16,256]{3,2,1,0:T(8,128)S(1)}, f32[3,6,16,256]{3,2,1,0:T(8,128)S(1)}, u32[]{:S(2)}, u32[]{:S(2)}) collective-permute-start(f32[3,6,16,256]{3,2,1,0:T(8,128)S(1)} %get-tuple-element.148), channel_id=1, source_target_pairs={{0,1},{1,2},{2,3},{3,4},{4,5},{5,6},{6,7},{8,9},{9,10},{10,11},{11... | collective-permute-start | bytes 884744 | tf_op jit(solution)/shard_map/ppermute | solution.py:524
  121.2 26.5 %collective-permute-start.9 = (f32[3,20,16,256]{3,2,1,0:T(8,128)S(1)}, f32[3,20,16,256]{3,2,1,0:T(8,128)S(1)}, u32[]{:S(2)}, u32[]{:S(2)}) collective-permute-start(f32[3,20,16,256]{3,2,1,0:T(8,128)S(1)} %get-tuple-element.104.refs_0_), channel_id=1, source_target_pairs={{8,0},{16,8},{24,16},{32,24},{40,32},{48,40},{56,48},{64,56},{72,6... | collective-permute-start | bytes 2949128 | tf_op jit(solution)/shard_map/ppermute | solution.py:524
  124.0 24.4 %collective-permute-start.8 = (f32[3,20,16,256]{3,2,1,0:T(8,128)S(1)}, f32[3,20,16,256]{3,2,1,0:T(8,128)S(1)}, u32[]{:S(2)}, u32[]{:S(2)}) collective-permute-start(f32[3,20,16,256]{3,2,1,0:T(8,128)S(1)} %get-tuple-element.104.refs_0_), channel_id=1, source_target_pairs={{0,8},{8,16},{16,24},{24,32},{32,40},{40,48},{48,56},{56,64},{64,7... | collective-permute-start | bytes 2949128 | tf_op jit(solution)/shard_map/ppermute | solution.py:524
  127.3 12.3 %collective-permute-start.14 = (f32[6,6,16,256]{3,2,1,0:T(8,128)S(1)}, f32[6,6,16,256]{3,2,1,0:T(8,128)S(1)}, u32[]{:S(2)}, u32[]{:S(2)}) collective-permute-start(f32[6,6,16,256]{3,2,1,0:T(8,128)S(1)} %pad_maximum_fusion.3), channel_id=1, source_target_pairs={{0,1},{1,2},{2,3},{3,4},{4,5},{5,6},{6,7},{8,9},{9,10},{10,11},{11... | collective-permute-start | bytes 1769480 | tf_op jit(solution)/shard_map/ppermute | solution.py:524
  132.8 11.5 %collective-permute-start.15 = (f32[6,6,16,256]{3,2,1,0:T(8,128)S(1)}, f32[6,6,16,256]{3,2,1,0:T(8,128)S(1)}, u32[]{:S(2)}, u32[]{:S(2)}) collective-permute-start(f32[6,6,16,256]{3,2,1,0:T(8,128)S(1)} %pad_maximum_fusion.4), channel_id=1, source_target_pairs={{1,0},{2,1},{3,2},{4,3},{5,4},{6,5},{7,6},{9,8},{10,9},{11,10},{12... | collective-permute-start | bytes 1769480 | tf_op jit(solution)/shard_map/ppermute | solution.py:524

commit v10 on v9

--- a/solution.py
+++ b/solution.py
@@ -64,7 +64,7 @@
 def laplace(ref, comp, at):
     cells = [tile_of(ref, comp, at, place) for place in TILES]
     total = [
-        (tile_of(ref, comp, at - 1, place) + tile_of(ref, comp, at + 1, place)) - 6.0 * cells[place]
+        tile_of(ref, comp, at - 1, place) + tile_of(ref, comp, at + 1, place)
         for place in TILES
     ]
     for z in range(SUBLANES):
@@ -83,12 +83,15 @@
 
 
 def stiffness(square, coefs):
-    plain = 0.5 - 0.125 * square
+    plain = (0.5 - 6.0) - square
     return [plain, plain, plain + coefs]
 
 
 def loop(low, high, body, carry=0):
-    return lax.fori_loop(low, high, body, carry, unroll=4)
+    count = high - low
+    exact = [u for u in (8, 7, 6, 5, 4) if count and count % u == 0]
+    unroll = exact[0] if exact else (8 if count >= 20 else 4)
+    return lax.fori_loop(low, high, body, carry, unroll=unroll)
 
 
 def clear_outside(tile, last_tile, refs, own):
@@ -117,7 +120,7 @@
             stiff = []
             for place in TILES:
                 cells = vector(ref, at, place)
-                square = dot(cells, cells)
+                square = 0.125 * dot(cells, cells)
                 put_flat(squares, at, place, square)
                 stiff.append(stiffness(square, flat_of(coef_ref, at + offset, place)))
             for comp in range(3):
@@ -143,9 +146,9 @@
             coefs = flat_of(coef_ref, at + offset, place)
             stiff_m, stiff_n = stiffness(square_m, coefs), stiffness(square_n, coefs)
             turn_m, turn_n = 0.25 * dot(m, fa), 0.25 * dot(n, fb)
-            gap = 0.125 * (square_m - square_n)
-            rise_m = 0.25 * dot(m, phi) - 0.125 * square_m
-            rise_n = 0.125 * square_n - 0.25 * dot(n, phi)
+            gap = square_m - square_n
+            rise_m = 0.25 * dot(m, phi) - square_m
+            rise_n = square_n - 0.25 * dot(n, phi)
             flat, bent = [], []
             for c in range(3):
                 flat.append(phi[c] * gap + m[c] * rise_m + n[c] * rise_n)
@@ -320,12 +323,12 @@
             square_m, square_n = flat_of(sm_ref, at, place), flat_of(sn_ref, at, place)
             coefs = flat_of(coef_ref, at, place)
             stiff_m, stiff_n = stiffness(square_m, coefs), stiffness(square_n, coefs)
-            gap = 0.125 * (square_m - square_n) + 4.0 * inv
+            gap = (square_m - square_n) + 4.0 * inv
             lean_m = (
-                0.25 * (dot(m, phi) - turned * dot(m, fa)) - 0.125 * square_m - (pull + inv)
+                0.25 * (dot(m, phi) - turned * dot(m, fa)) - square_m - (pull + inv)
             )
             lean_n = (
-                0.125 * square_n - 0.25 * (dot(n, phi) + turned * dot(n, fb)) + (pull - inv)
+                square_n - 0.25 * (dot(n, phi) + turned * dot(n, fb)) + (pull - inv)
             )
             cells = [
                 phi[c] * gap
@@ -373,7 +376,7 @@
         ):
             for place in TILES:
                 cells = [tile_of(ref, comp, was, place) + moves[comp][place] for comp in range(3)]
-                square = dot(cells, cells)
+                square = 0.125 * dot(cells, cells)
                 put_flat(squares, at, place, square)
                 stiff = stiffness(square, flat_of(coef_ref, at, place))
                 for comp in range(3):

time: 215 us -> 212 us (0.986)
  Pallas kernels: 38.5 us -> 35.7 us
    pallas_call x10, Pallas kernels: 38.5 us -> 35.7 us  [call(): pl.pallas_call(lambda *refs: kernel(position(), *refs), out_shape=outs, i...]
  transfers between devices with their start and end apart: 16 -> 16, of which waited for: 10 -> 11; matrix products, arithmetic and copies ran while one was open for 0% -> 0% of each run, Pallas kernels for 3% -> 3%
where the time goes in v10:
time: 212 us
  blocking collectives  99 us (47%)
  starting transfers between devices  44.4 us (21%)
  Pallas kernels  35.7 us (17%)
  waiting for transfers between devices  26.7 us (13%)
  local copies, waits for them, and re-layouts  5.11 us (2%)
    all_to_all x6, blocking collectives, from_everyone(): return lax.all_to_all(rows, IMG_TILE, 0, 0, tiled=True)  99 us
    ppermute x16, starting transfers between devices, beside(): return lax.ppermute(cells, axis, pairs)  44.4 us
    pallas_call x10, Pallas kernels, call(): pl.pallas_call(lambda *refs: kernel(position(), *refs), out_shape=outs, i...  35.7 us
    ppermute x16, waiting for transfers between devices, beside(): return lax.ppermute(cells, axis, pairs)  26.7 us
  transfers between devices with their start and end apart: 16, of which 11 were waited for; matrix products, arithmetic and copies ran while one was open for 0% of the time, Pallas kernels for 3%

profile of v10, /device:TPU:1, one launch (start us, length us, event | category | flops | bytes accessed | tf_op | source)
XLA Modules:
  0.0 211.6 jit_solution(11082228548985270472)
XLA Ops:
  0.0 2.3 %copy.17 = f32[1,3,16,32,256]{4,2,3,1,0:T(8,128)S(1)} copy(f32[1,3,16,32,256]{4,3,2,1,0:T(8,128)} %param.2) | data formatting | bytes 3145728 | tf_op args[0]
  3.9 4.7 %collective-permute-start.2 = (f32[3,12,16,256]{3,2,1,0:T(8,128)S(1)}, f32[3,12,16,256]{3,2,1,0:T(8,128)S(1)}, u32[]{:S(2)}, u32[]{:S(2)}) collective-permute-start(f32[3,12,16,256]{3,2,1,0:T(8,128)S(1)} %pad_maximum_fusion.refs_0_), channel_id=1, source_target_pairs={{0,8},{8,16},{16,24},{24,32},{32,40},{40,48},{48,56},{56,64},{64,7... | collective-permute-start | bytes 1769480 | tf_op jit(solution)/shard_map/ppermute | solution.py:527
  9.0 4.4 %collective-permute-start.4 = (f32[4,6,16,256]{3,2,1,0:T(8,128)S(1)}, f32[4,6,16,256]{3,2,1,0:T(8,128)S(1)}, u32[]{:S(2)}, u32[]{:S(2)}) collective-permute-start(f32[4,6,16,256]{3,2,1,0:T(8,128)S(1)} %pad_maximum_fusion.5), channel_id=1, source_target_pairs={{0,1},{1,2},{2,3},{3,4},{4,5},{5,6},{6,7},{8,9},{9,10},{10,11},{11... | collective-permute-start | bytes 1179656 | tf_op jit(solution)/shard_map/ppermute | solution.py:527
  13.4 1.9 collective-permute-start.5
  18.1 3.2 %collective-permute-start = (f32[3,20,16,256]{3,2,1,0:T(8,128)S(1)}, f32[3,20,16,256]{3,2,1,0:T(8,128)S(1)}, u32[]{:S(2)}, u32[]{:S(2)}) collective-permute-start(f32[3,20,16,256]{3,2,1,0:T(8,128)S(1)} %slice.68.refs_0_), channel_id=1, source_target_pairs={{0,8},{8,16},{16,24},{24,32},{32,40},{40,48},{48,56},{56,64},{64,7... | collective-permute-start | bytes 2949128 | tf_op jit(solution)/shard_map/ppermute | solution.py:527
  22.9 3.2 %collective-permute-start.6 = (f32[6,6,16,256]{3,2,1,0:T(8,128)S(1)}, f32[6,6,16,256]{3,2,1,0:T(8,128)S(1)}, u32[]{:S(2)}, u32[]{:S(2)}) collective-permute-start(f32[6,6,16,256]{3,2,1,0:T(8,128)S(1)} %pad_maximum_fusion.1), channel_id=1, source_target_pairs={{0,1},{1,2},{2,3},{3,4},{4,5},{5,6},{6,7},{8,9},{9,10},{10,11},{11... | collective-permute-start | bytes 1769480 | tf_op jit(solution)/shard_map/ppermute | solution.py:527
  26.2 1.9 collective-permute-start.7
  28.1 4.8 %collective-permute-done.6.refs_5_ = f32[6,6,16,256]{3,2,1,0:T(8,128)S(1)} collective-permute-done((f32[6,6,16,256]{3,2,1,0:T(8,128)S(1)}, f32[6,6,16,256]{3,2,1,0:T(8,128)S(1)}, u32[]{:S(2)}, u32[]{:S(2)}) %collective-permute-start.6) | collective-permute-done | bytes 589856 | tf_op jit(solution)/shard_map/ppermute | solution.py:527
  33.0 4.7 %collective-permute-done.7.refs_6_ = f32[6,6,16,256]{3,2,1,0:T(8,128)S(1)} collective-permute-done((f32[6,6,16,256]{3,2,1,0:T(8,128)S(1)}, f32[6,6,16,256]{3,2,1,0:T(8,128)S(1)}, u32[]{:S(2)}, u32[]{:S(2)}) %collective-permute-start.7) | collective-permute-done | bytes 589856 | tf_op jit(solution)/shard_map/ppermute | solution.py:527
  37.7 3.1 %shard_map.28 = (f32[3,24,16,256]{3,2,1,0:T(8,128)S(1)}, f32[3,24,16,256]{3,2,1,0:T(8,128)S(1)}, f32[3,24,16,256]{3,2,1,0:T(8,128)S(1)}, f32[3,24,16,256]{3,2,1,...) custom-call(f32[3,12,16,256]{3,2,1,0:T(8,128)S(1)} %pad_maximum_fusi, ...), custom_call_target="tpu_custom_call" | custom-call | tf_op jit(solution)/shard_map/pallas_call | solution.py:514
  42.8 4.8 %shard_map.29 = (f32[3,28,16,256]{3,2,1,0:T(8,128)S(1)}, f32[3,28,16,256]{3,2,1,0:T(8,128)S(1)}, f32[3,28,16,256]{3,2,1,0:T(8,128)S(1)}, f32[3,28,16,256]{3,2,1,...) custom-call(f32[3,20,16,256]{3,2,1,0:T(8,128)S(1)} %slice.68.refs_0_, ...), custom_call_target="tpu_custom_call" | custom-call | tf_op jit(solution)/shard_map/pallas_call | solution.py:514
  47.6 23.8 %all_to_all.66 = f32[128,1,128]{2,1,0:T(1,128)S(1)} all-to-all(f32[128,1,128]{2,1,0:T(1,128)S(1)} %bitcast.50), channel_id=1, replica_groups=mesh['img_0'=4,'img_1'=4,'tile_0'=4,'tile_1'=2] {'img_0','img_1','tile_0..., dimensions={0} | all-to-all | bytes 131072 | tf_op jit(solution)/shard_map/all_to_all | solution.py:531
  71.4 5.3 %shard_map.30 = (f32[3,44,16,256]{3,2,1,0:T(8,128)S(1)}, f32[3,44,16,256]{3,2,1,0:T(8,128)S(1)}, f32[3,44,16,256]{3,2,1,0:T(8,128)S(1)}, f32[3,44,16,256]{3,2,1,...) custom-call(f32[128,128]{1,0:T(8,128)S(1)} %bitcast.42, ...), custom_call_target="tpu_custom_call" | custom-call | tf_op jit(solution)/shard_map/pallas_call | solution.py:514
  76.7 13.9 %all_to_all.67 = f32[128,1,128]{2,1,0:T(1,128)S(1)} all-to-all(f32[128,1,128]{2,1,0:T(1,128)S(1)} %bitcast.48), channel_id=1, replica_groups=mesh['img_0'=4,'img_1'=4,'tile_0'=4,'tile_1'=2] {'img_0','img_1','tile_0..., dimensions={0} | all-to-all | bytes 131072 | tf_op jit(solution)/shard_map/all_to_all | solution.py:531
  90.6 4.3 %shard_map.31 = (f32[3,44,16,256]{3,2,1,0:T(8,128)S(1)}, f32[3,32,16,256]{3,2,1,0:T(8,128)S(1)}, f32[128,128]{1,0:T(8,128)S(1)}) custom-call(f32[8,128]{1,0:T(8,128)S(1)} %get-tuple-element.93.refs_0_, f32[128,128]{1,0:T(8,128)S(1)} %bitcast.45, f32[3,44,16,256]{3,2,1,0:T(8,128)S(1)} %get-tuple-element.95.refs_2_, ...), custom_call_target="tpu_custom_call" | custom-call | tf_op jit(solution)/shard_map/pallas_call | solution.py:514
  94.9 13.9 %all_to_all.68 = f32[128,1,128]{2,1,0:T(1,128)S(1)} all-to-all(f32[128,1,128]{2,1,0:T(1,128)S(1)} %bitcast.53), channel_id=1, replica_groups=mesh['img_0'=4,'img_1'=4,'tile_0'=4,'tile_1'=2] {'img_0','img_1','tile_0..., dimensions={0} | all-to-all | bytes 131072 | tf_op jit(solution)/shard_map/all_to_all | solution.py:531
  110.5 4.0 %collective-permute-start.10 = (f32[3,12,16,256]{3,2,1,0:T(8,128)S(1)}, f32[3,12,16,256]{3,2,1,0:T(8,128)S(1)}, u32[]{:S(2)}, u32[]{:S(2)}) collective-permute-start(f32[3,12,16,256]{3,2,1,0:T(8,128)S(1)} %get-tuple-element.105.refs_0_), channel_id=1, source_target_pairs={{0,8},{8,16},{16,24},{24,32},{32,40},{40,48},{48,56},{56,64},{64,7... | collective-permute-start | bytes 1769480 | tf_op jit(solution)/shard_map/ppermute | solution.py:527
  114.6 3.2 %collective-permute-start.13 = (f32[3,6,16,256]{3,2,1,0:T(8,128)S(1)}, f32[3,6,16,256]{3,2,1,0:T(8,128)S(1)}, u32[]{:S(2)}, u32[]{:S(2)}) collective-permute-start(f32[3,6,16,256]{3,2,1,0:T(8,128)S(1)} %get-tuple-element.147), channel_id=1, source_target_pairs={{1,0},{2,1},{3,2},{4,3},{5,4},{6,5},{7,6},{9,8},{10,9},{11,10},{12... | collective-permute-start | bytes 884744 | tf_op jit(solution)/shard_map/ppermute | solution.py:527
  117.9 2.3 %collective-permute-start.12 = (f32[3,6,16,256]{3,2,1,0:T(8,128)S(1)}, f32[3,6,16,256]{3,2,1,0:T(8,128)S(1)}, u32[]{:S(2)}, u32[]{:S(2)}) collective-permute-start(f32[3,6,16,256]{3,2,1,0:T(8,128)S(1)} %get-tuple-element.148), channel_id=1, source_target_pairs={{0,1},{1,2},{2,3},{3,4},{4,5},{5,6},{6,7},{8,9},{9,10},{10,11},{11... | collective-permute-start | bytes 884744 | tf_op jit(solution)/shard_map/ppermute | solution.py:527
  123.0 2.6 %collective-permute-start.8 = (f32[3,20,16,256]{3,2,1,0:T(8,128)S(1)}, f32[3,20,16,256]{3,2,1,0:T(8,128)S(1)}, u32[]{:S(2)}, u32[]{:S(2)}) collective-permute-start(f32[3,20,16,256]{3,2,1,0:T(8,128)S(1)} %get-tuple-element.104.refs_0_), channel_id=1, source_target_pairs={{0,8},{8,16},{16,24},{24,32},{32,40},{40,48},{48,56},{56,64},{64,7... | collective-permute-start | bytes 2949128 | tf_op jit(solution)/shard_map/ppermute | solution.py:527
  126.3 5.6 %collective-permute-start.14 = (f32[6,6,16,256]{3,2,1,0:T(8,128)S(1)}, f32[6,6,16,256]{3,2,1,0:T(8,128)S(1)}, u32[]{:S(2)}, u32[]{:S(2)}) collective-permute-start(f32[6,6,16,256]{3,2,1,0:T(8,128)S(1)} %pad_maximum_fusion.3), channel_id=1, source_target_pairs={{0,1},{1,2},{2,3},{3,4},{4,5},{5,6},{6,7},{8,9},{9,10},{10,11},{11... | collective-permute-start | bytes 1769480 | tf_op jit(solution)/shard_map/ppermute | solution.py:527
  131.9 1.9 collective-permute-start.15
  133.9 4.8 %collective-permute-done.14.refs_5_ = f32[6,6,16,256]{3,2,1,0:T(8,128)S(1)} collective-permute-done((f32[6,6,16,256]{3,2,1,0:T(8,128)S(1)}, f32[6,6,16,256]{3,2,1,0:T(8,128)S(1)}, u32[]{:S(2)}, u32[]{:S(2)}) %collective-permute-start.14) | collective-permute-done | bytes 589856 | tf_op jit(solution)/shard_map/ppermute | solution.py:527
  138.7 4.7 %collective-permute-done.15.refs_6_ = f32[6,6,16,256]{3,2,1,0:T(8,128)S(1)} collective-permute-done((f32[6,6,16,256]{3,2,1,0:T(8,128)S(1)}, f32[6,6,16,256]{3,2,1,0:T(8,128)S(1)}, u32[]{:S(2)}, u32[]{:S(2)}) %collective-permute-start.15) | collective-permute-done | bytes 589856 | tf_op jit(solution)/shard_map/ppermute | solution.py:527
  143.4 3.0 %shard_map.33 = (f32[3,24,16,256]{3,2,1,0:T(8,128)S(1)}, f32[3,24,16,256]{3,2,1,0:T(8,128)S(1)}, f32[3,24,16,256]{3,2,1,0:T(8,128)S(1)}, f32[3,24,16,256]{3,2,1,...) custom-call(f32[3,12,16,256]{3,2,1,0:T(8,128)S(1)} %get-tuple-elemen, ...), custom_call_target="tpu_custom_call" | custom-call | tf_op jit(solution)/shard_map/pallas_call | solution.py:514
  147.2 4.9 %shard_map.34 = (f32[3,28,16,256]{3,2,1,0:T(8,128)S(1)}, f32[3,28,16,256]{3,2,1,0:T(8,128)S(1)}, f32[3,28,16,256]{3,2,1,0:T(8,128)S(1)}, f32[3,28,16,256]{3,2,1,...) custom-call(f32[3,20,16,256]{3,2,1,0:T(8,128)S(1)} %get-tuple-elemen, ...), custom_call_target="tpu_custom_call" | custom-call | tf_op jit(solution)/shard_map/pallas_call | solution.py:514
  152.0 19.5 %all_to_all.69 = f32[128,1,128]{2,1,0:T(1,128)S(1)} all-to-all(f32[128,1,128]{2,1,0:T(1,128)S(1)} %bitcast.51), channel_id=1, replica_groups=mesh['img_0'=4,'img_1'=4,'tile_0'=4,'tile_1'=2] {'img_0','img_1','tile_0..., dimensions={0} | all-to-all | bytes 131072 | tf_op jit(solution)/shard_map/all_to_all | solution.py:531
  171.5 5.4 %shard_map.35 = (f32[3,44,16,256]{3,2,1,0:T(8,128)S(1)}, f32[3,44,16,256]{3,2,1,0:T(8,128)S(1)}, f32[3,44,16,256]{3,2,1,0:T(8,128)S(1)}, f32[3,44,16,256]{3,2,1,...) custom-call(f32[128,128]{1,0:T(8,128)S(1)} %bitcast.43, ...), custom_call_target="tpu_custom_call" | custom-call | tf_op jit(solution)/shard_map/pallas_call | solution.py:514
  176.9 13.9 %all_to_all.70 = f32[128,1,128]{2,1,0:T(1,128)S(1)} all-to-all(f32[128,1,128]{2,1,0:T(1,128)S(1)} %bitcast.49), channel_id=1, replica_groups=mesh['img_0'=4,'img_1'=4,'tile_0'=4,'tile_1'=2] {'img_0','img_1','tile_0..., dimensions={0} | all-to-all | bytes 131072 | tf_op jit(solution)/shard_map/all_to_all | solution.py:531
  190.9 4.2 %shard_map.36 = (f32[3,44,16,256]{3,2,1,0:T(8,128)S(1)}, f32[3,32,16,256]{3,2,1,0:T(8,128)S(1)}, f32[128,128]{1,0:T(8,128)S(1)}) custom-call(f32[8,128]{1,0:T(8,128)S(1)} %get-tuple-element.126.refs_0_, f32[128,128]{1,0:T(8,128)S(1)} %bitcast.44, f32[3,44,16,256]{3,2,1,0:T(8,128)S(1)} %get-tuple-element.128.refs_2_, ...), custom_call_target="tpu_custom_call" | custom-call | tf_op jit(solution)/shard_map/pallas_call | solution.py:514
  195.0 13.9 %all_to_all.71 = f32[128,1,128]{2,1,0:T(1,128)S(1)} all-to-all(f32[128,1,128]{2,1,0:T(1,128)S(1)} %bitcast.52), channel_id=1, replica_groups=mesh['img_0'=4,'img_1'=4,'tile_0'=4,'tile_1'=2] {'img_0','img_1','tile_0..., dimensions={0} | all-to-all | bytes 131072 | tf_op jit(solution)/shard_map/all_to_all | solution.py:531
  209.5 2.1 copy.14
  (37 shorter events, 14.7 us)
Async XLA Ops:
  2.3 6.3 %copy-start = (f32[16,32,256]{2,1,0:T(8,128)S(1)}, f32[16,32,256]{2,1,0:T(8,128)}, u32[]{:S(2)}) copy-start(f32[16,32,256]{2,1,0:T(8,128)} %param.3) | copy-start | bytes 1572868
  2.4 20.4 %collective-permute-start.3 = (f32[3,12,16,256]{3,2,1,0:T(8,128)S(1)}, f32[3,12,16,256]{3,2,1,0:T(8,128)S(1)}, u32[]{:S(2)}, u32[]{:S(2)}) collective-permute-start(f32[3,12,16,256]{3,2,1,0:T(8,128)S(1)} %pad_maximum_fusion.refs_0_), channel_id=1, source_target_pairs={{8,0},{16,8},{24,16},{32,24},{40,32},{48,40},{56,48},{64,56},{72,6... | collective-permute-start | bytes 1769480 | tf_op jit(solution)/shard_map/ppermute | solution.py:527
  3.9 18.9 %collective-permute-start.2 = (f32[3,12,16,256]{3,2,1,0:T(8,128)S(1)}, f32[3,12,16,256]{3,2,1,0:T(8,128)S(1)}, u32[]{:S(2)}, u32[]{:S(2)}) collective-permute-start(f32[3,12,16,256]{3,2,1,0:T(8,128)S(1)} %pad_maximum_fusion.refs_0_), channel_id=1, source_target_pairs={{0,8},{8,16},{16,24},{24,32},{32,40},{40,48},{48,56},{56,64},{64,7... | collective-permute-start | bytes 1769480 | tf_op jit(solution)/shard_map/ppermute | solution.py:527
  9.0 9.1 %collective-permute-start.4 = (f32[4,6,16,256]{3,2,1,0:T(8,128)S(1)}, f32[4,6,16,256]{3,2,1,0:T(8,128)S(1)}, u32[]{:S(2)}, u32[]{:S(2)}) collective-permute-start(f32[4,6,16,256]{3,2,1,0:T(8,128)S(1)} %pad_maximum_fusion.5), channel_id=1, source_target_pairs={{0,1},{1,2},{2,3},{3,4},{4,5},{5,6},{6,7},{8,9},{9,10},{10,11},{11... | collective-permute-start | bytes 1179656 | tf_op jit(solution)/shard_map/ppermute | solution.py:527
  13.4 9.4 %collective-permute-start.5 = (f32[4,6,16,256]{3,2,1,0:T(8,128)S(1)}, f32[4,6,16,256]{3,2,1,0:T(8,128)S(1)}, u32[]{:S(2)}, u32[]{:S(2)}) collective-permute-start(f32[4,6,16,256]{3,2,1,0:T(8,128)S(1)} %pad_maximum_fusion.6), channel_id=1, source_target_pairs={{1,0},{2,1},{3,2},{4,3},{5,4},{6,5},{7,6},{9,8},{10,9},{11,10},{12... | collective-permute-start | bytes 1179656 | tf_op jit(solution)/shard_map/ppermute | solution.py:527
  15.4 25.7 %collective-permute-start.1 = (f32[3,20,16,256]{3,2,1,0:T(8,128)S(1)}, f32[3,20,16,256]{3,2,1,0:T(8,128)S(1)}, u32[]{:S(2)}, u32[]{:S(2)}) collective-permute-start(f32[3,20,16,256]{3,2,1,0:T(8,128)S(1)} %slice.68.refs_0_), channel_id=1, source_target_pairs={{8,0},{16,8},{24,16},{32,24},{40,32},{48,40},{56,48},{64,56},{72,6... | collective-permute-start | bytes 2949128 | tf_op jit(solution)/shard_map/ppermute | solution.py:527
  18.1 24.8 %collective-permute-start = (f32[3,20,16,256]{3,2,1,0:T(8,128)S(1)}, f32[3,20,16,256]{3,2,1,0:T(8,128)S(1)}, u32[]{:S(2)}, u32[]{:S(2)}) collective-permute-start(f32[3,20,16,256]{3,2,1,0:T(8,128)S(1)} %slice.68.refs_0_), channel_id=1, source_target_pairs={{0,8},{8,16},{16,24},{24,32},{32,40},{40,48},{48,56},{56,64},{64,7... | collective-permute-start | bytes 2949128 | tf_op jit(solution)/shard_map/ppermute | solution.py:527
  22.9 10.0 %collective-permute-start.6 = (f32[6,6,16,256]{3,2,1,0:T(8,128)S(1)}, f32[6,6,16,256]{3,2,1,0:T(8,128)S(1)}, u32[]{:S(2)}, u32[]{:S(2)}) collective-permute-start(f32[6,6,16,256]{3,2,1,0:T(8,128)S(1)} %pad_maximum_fusion.1), channel_id=1, source_target_pairs={{0,1},{1,2},{2,3},{3,4},{4,5},{5,6},{6,7},{8,9},{9,10},{10,11},{11... | collective-permute-start | bytes 1769480 | tf_op jit(solution)/shard_map/ppermute | solution.py:527
  26.2 11.5 %collective-permute-start.7 = (f32[6,6,16,256]{3,2,1,0:T(8,128)S(1)}, f32[6,6,16,256]{3,2,1,0:T(8,128)S(1)}, u32[]{:S(2)}, u32[]{:S(2)}) collective-permute-start(f32[6,6,16,256]{3,2,1,0:T(8,128)S(1)} %pad_maximum_fusion.2), channel_id=1, source_target_pairs={{1,0},{2,1},{3,2},{4,3},{5,4},{6,5},{7,6},{9,8},{10,9},{11,10},{12... | collective-permute-start | bytes 1769480 | tf_op jit(solution)/shard_map/ppermute | solution.py:527
  109.2 16.4 %collective-permute-start.11 = (f32[3,12,16,256]{3,2,1,0:T(8,128)S(1)}, f32[3,12,16,256]{3,2,1,0:T(8,128)S(1)}, u32[]{:S(2)}, u32[]{:S(2)}) collective-permute-start(f32[3,12,16,256]{3,2,1,0:T(8,128)S(1)} %get-tuple-element.105.refs_0_), channel_id=1, source_target_pairs={{8,0},{16,8},{24,16},{32,24},{40,32},{48,40},{56,48},{64,56},{72,6... | collective-permute-start | bytes 1769480 | tf_op jit(solution)/shard_map/ppermute | solution.py:527
  110.5 15.6 %collective-permute-start.10 = (f32[3,12,16,256]{3,2,1,0:T(8,128)S(1)}, f32[3,12,16,256]{3,2,1,0:T(8,128)S(1)}, u32[]{:S(2)}, u32[]{:S(2)}) collective-permute-start(f32[3,12,16,256]{3,2,1,0:T(8,128)S(1)} %get-tuple-element.105.refs_0_), channel_id=1, source_target_pairs={{0,8},{8,16},{16,24},{24,32},{32,40},{40,48},{48,56},{56,64},{64,7... | collective-permute-start | bytes 1769480 | tf_op jit(solution)/shard_map/ppermute | solution.py:527
  114.6 8.3 %collective-permute-start.13 = (f32[3,6,16,256]{3,2,1,0:T(8,128)S(1)}, f32[3,6,16,256]{3,2,1,0:T(8,128)S(1)}, u32[]{:S(2)}, u32[]{:S(2)}) collective-permute-start(f32[3,6,16,256]{3,2,1,0:T(8,128)S(1)} %get-tuple-element.147), channel_id=1, source_target_pairs={{1,0},{2,1},{3,2},{4,3},{5,4},{6,5},{7,6},{9,8},{10,9},{11,10},{12... | collective-permute-start | bytes 884744 | tf_op jit(solution)/shard_map/ppermute | solution.py:527
  117.9 7.7 %collective-permute-start.12 = (f32[3,6,16,256]{3,2,1,0:T(8,128)S(1)}, f32[3,6,16,256]{3,2,1,0:T(8,128)S(1)}, u32[]{:S(2)}, u32[]{:S(2)}) collective-permute-start(f32[3,6,16,256]{3,2,1,0:T(8,128)S(1)} %get-tuple-element.148), channel_id=1, source_target_pairs={{0,1},{1,2},{2,3},{3,4},{4,5},{5,6},{6,7},{8,9},{9,10},{10,11},{11... | collective-permute-start | bytes 884744 | tf_op jit(solution)/shard_map/ppermute | solution.py:527
  120.2 26.3 %collective-permute-start.9 = (f32[3,20,16,256]{3,2,1,0:T(8,128)S(1)}, f32[3,20,16,256]{3,2,1,0:T(8,128)S(1)}, u32[]{:S(2)}, u32[]{:S(2)}) collective-permute-start(f32[3,20,16,256]{3,2,1,0:T(8,128)S(1)} %get-tuple-element.104.refs_0_), channel_id=1, source_target_pairs={{8,0},{16,8},{24,16},{32,24},{40,32},{48,40},{56,48},{64,56},{72,6... | collective-permute-start | bytes 2949128 | tf_op jit(solution)/shard_map/ppermute | solution.py:527
  123.0 24.2 %collective-permute-start.8 = (f32[3,20,16,256]{3,2,1,0:T(8,128)S(1)}, f32[3,20,16,256]{3,2,1,0:T(8,128)S(1)}, u32[]{:S(2)}, u32[]{:S(2)}) collective-permute-start(f32[3,20,16,256]{3,2,1,0:T(8,128)S(1)} %get-tuple-element.104.refs_0_), channel_id=1, source_target_pairs={{0,8},{8,16},{16,24},{24,32},{32,40},{40,48},{48,56},{56,64},{64,7... | collective-permute-start | bytes 2949128 | tf_op jit(solution)/shard_map/ppermute | solution.py:527
  126.3 12.4 %collective-permute-start.14 = (f32[6,6,16,256]{3,2,1,0:T(8,128)S(1)}, f32[6,6,16,256]{3,2,1,0:T(8,128)S(1)}, u32[]{:S(2)}, u32[]{:S(2)}) collective-permute-start(f32[6,6,16,256]{3,2,1,0:T(8,128)S(1)} %pad_maximum_fusion.3), channel_id=1, source_target_pairs={{0,1},{1,2},{2,3},{3,4},{4,5},{5,6},{6,7},{8,9},{9,10},{10,11},{11... | collective-permute-start | bytes 1769480 | tf_op jit(solution)/shard_map/ppermute | solution.py:527
  131.9 11.5 %collective-permute-start.15 = (f32[6,6,16,256]{3,2,1,0:T(8,128)S(1)}, f32[6,6,16,256]{3,2,1,0:T(8,128)S(1)}, u32[]{:S(2)}, u32[]{:S(2)}) collective-permute-start(f32[6,6,16,256]{3,2,1,0:T(8,128)S(1)} %pad_maximum_fusion.4), channel_id=1, source_target_pairs={{1,0},{2,1},{3,2},{4,3},{5,4},{6,5},{7,6},{9,8},{10,9},{11,10},{12... | collective-permute-start | bytes 1769480 | tf_op jit(solution)/shard_map/ppermute | solution.py:527

commit v11 on v10

--- a/solution.py
+++ b/solution.py
@@ -108,34 +108,31 @@
             ref[:, HALO + own :] = jnp.zeros((3, rows - HALO - own) + ref.shape[2:], jnp.float32)
 
 
-def block(phi_ref, m_ref, n_ref, lm_ref, ln_ref, q_ref, r_ref, coef_ref, offset, scratch, cuts, clear, sums):
+def residual(ref, lap_ref, out, squares, coef_ref, offset, other_ref=None, sum_ref=None):
+    def body(at, carry):
+        stiff = []
+        for place in TILES:
+            cells = vector(ref, at, place)
+            square = 0.125 * dot(cells, cells)
+            put_flat(squares, at, place, square)
+            stiff.append(stiffness(square, flat_of(coef_ref, at + offset, place)))
+        for comp in range(3):
+            cells, bent = laplace(ref, comp, at)
+            for place in TILES:
+                put(lap_ref, comp, at, place, bent[place])
+                total = bent[place] + stiff[place][comp] * cells[place]
+                put(out, comp, at, place, total)
+                if sum_ref is not None:
+                    total = total + tile_of(other_ref, comp, at, place)
+                    put(sum_ref, comp, at, place, total)
+        return carry
+
+    loop(1, ref.shape[1] - 1, body)
+
+
+def block(phi_ref, m_ref, n_ref, q_ref, r_ref, coef_ref, offset, scratch, cuts, clear, sums):
     fa_ref, fb_ref, fs_ref, sm_ref, sn_ref = scratch
     rows = phi_ref.shape[1]
-
-    def drive(at, carry):
-        for ref, lap_ref, out, squares, before in (
-            (m_ref, lm_ref, fa_ref, sm_ref, None),
-            (n_ref, ln_ref, fb_ref, sn_ref, (fa_ref, fs_ref)),
-        ):
-            stiff = []
-            for place in TILES:
-                cells = vector(ref, at, place)
-                square = 0.125 * dot(cells, cells)
-                put_flat(squares, at, place, square)
-                stiff.append(stiffness(square, flat_of(coef_ref, at + offset, place)))
-            for comp in range(3):
-                cells, bent = laplace(ref, comp, at)
-                for place in TILES:
-                    put(lap_ref, comp, at, place, bent[place])
-                    total = bent[place] + stiff[place][comp] * cells[place]
-                    put(out, comp, at, place, total)
-                    if before is not None:
-                        total = total + tile_of(fa_ref, comp, at, place)
-                        put(fs_ref, comp, at, place, total)
-        return carry
-
-    loop(1, rows - 1, drive)
-    clear((fa_ref, fb_ref, fs_ref))
 
     def fields(at, sums):
         adjoint = [laplace(fs_ref, comp, at)[1] for comp in range(3)]
@@ -184,17 +181,15 @@
     return sums
 
 
-def join(pieces, outs, low, high, shift):
-    own_ref, a_ref, b_ref = pieces
-    phi_ref, m_ref, n_ref = outs
-
+def join(own_ref, beside_refs, phi_ref, sum_refs, low, high, shift):
     def one(at, carry):
         for comp in range(3):
             for place in TILES:
                 phi = tile_of(own_ref, comp, at, place)
-                put(phi_ref, comp, at + shift, place, phi)
-                put(m_ref, comp, at + shift, place, phi + tile_of(a_ref, comp, at, place))
-                put(n_ref, comp, at + shift, place, phi + tile_of(b_ref, comp, at, place))
+                if phi_ref is not None:
+                    put(phi_ref, comp, at + shift, place, phi)
+                for ref, sum_ref in zip(beside_refs, sum_refs):
+                    put(sum_ref, comp, at + shift, place, phi + tile_of(ref, comp, at, place))
         return carry
 
     loop(low, high, one)
@@ -226,16 +221,17 @@
         (first, ref.at[0:3], ref.at[3:6])
         for first, ref in ((up_own, up_ref), (down_own, down_ref))
     ]
-    edges = (own_edge, a_edge, b_edge)
     sums = [jnp.zeros((8, 128), jnp.float32)] * PRODUCTS
     for top in (True, False):
         first = 0 if top else span
         here = [ref.at[:, first : first + span] for ref in fields]
-        join(halos[0 if top else 1], here[:3], 0, HALO, 0 if top else HALO)
+        phi, m, n, lm, ln, q, r = here
+        halo = halos[0 if top else 1]
+        join(halo[0], halo[1:], phi, (m, n), 0, HALO, 0 if top else HALO)
         if top:
-            join(edges, here[:3], 0, HALO, HALO)
+            join(own_edge, (a_edge, b_edge), phi, (m, n), 0, HALO, HALO)
         else:
-            join(edges, here[:3], HALO, span, -HALO)
+            join(own_edge, (a_edge, b_edge), phi, (m, n), HALO, span, -HALO)
 
         def clear(refs, top=top):
             outside = slice(0, HALO) if top else slice(HALO, span)
@@ -247,25 +243,41 @@
 
         cuts = (HALO, span - 2) if top else (2, HALO)
         offset = 0 if top else coef_ref.shape[0] - span
-        sums = block(*here, coef_ref, offset, scratch, cuts, clear, sums)
+        residual(m, lm, fa_ref, sm_ref, coef_ref, offset)
+        residual(n, ln, fb_ref, sn_ref, coef_ref, offset, fa_ref, fs_ref)
+        clear((fa_ref, fb_ref, fs_ref))
+        sums = block(phi, m, n, q, r, coef_ref, offset, scratch, cuts, clear, sums)
     for which in range(PRODUCTS):
         sums_ref[which] = sums[which]
 
 
+def ends_into(ref, end, span):
+    rows = ref.shape[1]
+    ref[:, 0:4] = end[:, span - 4 : span]
+    ref[:, rows - 4 :] = end[:, span : span + 4]
+
+
+def ahead_kernel(
+    where, own_mid, b_mid, phi_end, n_end, coef_ref, phi_ref, n_ref, ln_ref, fb_ref, sn_ref
+):
+    span = 2 * HALO
+    ends_into(phi_ref, phi_end, span)
+    ends_into(n_ref, n_end, span)
+    join(own_mid, (b_mid,), phi_ref, (n_ref,), 0, phi_ref.shape[1] - 8, 4)
+    residual(n_ref, ln_ref, fb_ref, sn_ref, coef_ref, span - 4)
+
+
 def middle_kernel(
-    where, own_mid, a_mid, b_mid, phi_end, m_end, n_end, part_ref, coef_ref,
-    phi_ref, m_ref, n_ref, lm_ref, ln_ref, q_ref, r_ref, sums_ref,
-    fa_ref, fb_ref, fs_ref, sm_ref, sn_ref
+    where, own_mid, a_mid, m_end, phi_ref, n_ref, fb_ref, sn_ref, part_ref, coef_ref,
+    m_ref, lm_ref, q_ref, r_ref, sums_ref, fa_ref, fs_ref, sm_ref
 ):
     span = 2 * HALO
     rows = phi_ref.shape[1]
-    outs = (phi_ref, m_ref, n_ref)
-    for end, ref in zip((phi_end, m_end, n_end), outs):
-        ref[:, 0:4] = end[:, span - 4 : span]
-        ref[:, rows - 4 :] = end[:, span : span + 4]
-    join((own_mid, a_mid, b_mid), outs, 0, rows - 8, 4)
+    ends_into(m_ref, m_end, span)
+    join(own_mid, (a_mid,), None, (m_ref,), 0, rows - 8, 4)
+    residual(m_ref, lm_ref, fa_ref, sm_ref, coef_ref, span - 4, fb_ref, fs_ref)
     sums = block(
-        *outs, lm_ref, ln_ref, q_ref, r_ref, coef_ref, span - 4,
+        phi_ref, m_ref, n_ref, q_ref, r_ref, coef_ref, span - 4,
         (fa_ref, fb_ref, fs_ref, sm_ref, sn_ref), (2, rows - 2), lambda refs: None,
         [part_ref[which] for which in range(PRODUCTS)],
     )
@@ -576,12 +588,19 @@
                 shapes,
                 scratch(2 * HALO),
             )
-        *near, sums = call(
+        phi, n, ln, fb, sn = call(
+            ahead_kernel,
+            [mid, b_mid, far[0], far[2], coef_ext],
+            [f32(*middle)] * 4 + [f32(*middle[1:])],
+            [],
+        )
+        m, lm, q, r, sums = call(
             middle_kernel,
-            [mid, a_mid, b_mid, *far[:3], part, coef_ext],
-            [f32(*middle)] * 7 + [table],
-            scratch(own - 4),
+            [mid, a_mid, far[1], phi, n, fb, sn, part, coef_ext],
+            [f32(*middle)] * 4 + [table],
+            [middle, middle, middle[1:]],
         )
+        near = phi, m, n, lm, ln, q, r
         phi, m, n, lm, ln, g, scal, sums = call(
             lambda *refs: second_kernel(tiles, cells, *refs),
             [from_everyone(sums), *far, *near, coef_ext],

time: 212 us -> 211 us (level)
  waiting for transfers between devices: 26.7 us -> 24.4 us
    ppermute x16, waiting for transfers between devices: 26.7 us -> 24.4 us  [beside(): return lax.ppermute(cells, axis, pairs)]
    pallas_call x10 -> x12, Pallas kernels: 35.7 us -> 37.8 us  [call(): pl.pallas_call(lambda *refs: kernel(position(), *refs), out_shape=outs, i...]
  transfers between devices with their start and end apart: 16 -> 16, of which waited for: 11 -> 9; matrix products, arithmetic and copies ran while one was open for 0% -> 0% of each run, Pallas kernels for 3% -> 4%
where the time goes in v11:
time: 211 us; the launch traced here: 210 us
  blocking collectives  98.1 us (46%)
  starting transfers between devices  44.4 us (21%)
  Pallas kernels  37.8 us (18%)
  waiting for transfers between devices  24.4 us (12%)
  local copies, waits for them, and re-layouts  5.08 us (2%)
    all_to_all x6, blocking collectives, from_everyone(): return lax.all_to_all(rows, IMG_TILE, 0, 0, tiled=True)  98.1 us
    ppermute x16, starting transfers between devices, beside(): return lax.ppermute(cells, axis, pairs)  44.4 us
    pallas_call x12, Pallas kernels, call(): pl.pallas_call(lambda *refs: kernel(position(), *refs), out_shape=outs, i...  37.8 us
    ppermute x16, waiting for transfers between devices, beside(): return lax.ppermute(cells, axis, pairs)  24.4 us
  transfers between devices with their start and end apart: 16, of which 9 were waited for; matrix products, arithmetic and copies ran while one was open for 0% of the time, Pallas kernels for 4%

profile of v11, /device:TPU:1, one launch (start us, length us, event | category | flops | bytes accessed | tf_op | source)
XLA Modules:
  0.0 210.5 jit_solution(14761863365776059002)
XLA Ops:
  0.0 2.3 %copy.17 = f32[1,3,16,32,256]{4,2,3,1,0:T(8,128)S(1)} copy(f32[1,3,16,32,256]{4,3,2,1,0:T(8,128)} %param.2) | data formatting | bytes 3145728 | tf_op args[0]
  3.9 4.7 %collective-permute-start.1 = (f32[3,12,16,256]{3,2,1,0:T(8,128)S(1)}, f32[3,12,16,256]{3,2,1,0:T(8,128)S(1)}, u32[]{:S(2)}, u32[]{:S(2)}) collective-permute-start(f32[3,12,16,256]{3,2,1,0:T(8,128)S(1)} %pad_maximum_fusion.refs_0_), channel_id=1, source_target_pairs={{0,8},{8,16},{16,24},{24,32},{32,40},{40,48},{48,56},{56,64},{64,7... | collective-permute-start | bytes 1769480 | tf_op jit(solution)/shard_map/ppermute | solution.py:539
  9.0 4.4 %collective-permute-start.3 = (f32[4,6,16,256]{3,2,1,0:T(8,128)S(1)}, f32[4,6,16,256]{3,2,1,0:T(8,128)S(1)}, u32[]{:S(2)}, u32[]{:S(2)}) collective-permute-start(f32[4,6,16,256]{3,2,1,0:T(8,128)S(1)} %pad_maximum_fusion.5), channel_id=1, source_target_pairs={{0,1},{1,2},{2,3},{3,4},{4,5},{5,6},{6,7},{8,9},{9,10},{10,11},{11... | collective-permute-start | bytes 1179656 | tf_op jit(solution)/shard_map/ppermute | solution.py:539
  13.4 1.9 collective-permute-start.4
  18.1 3.2 %collective-permute-start = (f32[3,20,16,256]{3,2,1,0:T(8,128)S(1)}, f32[3,20,16,256]{3,2,1,0:T(8,128)S(1)}, u32[]{:S(2)}, u32[]{:S(2)}) collective-permute-start(f32[3,20,16,256]{3,2,1,0:T(8,128)S(1)} %slice.68.refs_0_), channel_id=1, source_target_pairs={{0,8},{8,16},{16,24},{24,32},{32,40},{40,48},{48,56},{56,64},{64,7... | collective-permute-start | bytes 2949128 | tf_op jit(solution)/shard_map/ppermute | solution.py:539
  22.9 3.2 %collective-permute-start.5 = (f32[6,6,16,256]{3,2,1,0:T(8,128)S(1)}, f32[6,6,16,256]{3,2,1,0:T(8,128)S(1)}, u32[]{:S(2)}, u32[]{:S(2)}) collective-permute-start(f32[6,6,16,256]{3,2,1,0:T(8,128)S(1)} %pad_maximum_fusion.1), channel_id=1, source_target_pairs={{0,1},{1,2},{2,3},{3,4},{4,5},{5,6},{6,7},{8,9},{9,10},{10,11},{11... | collective-permute-start | bytes 1769480 | tf_op jit(solution)/shard_map/ppermute | solution.py:539
  26.2 1.9 collective-permute-start.6
  28.1 4.8 %collective-permute-done.5.refs_5_ = f32[6,6,16,256]{3,2,1,0:T(8,128)S(1)} collective-permute-done((f32[6,6,16,256]{3,2,1,0:T(8,128)S(1)}, f32[6,6,16,256]{3,2,1,0:T(8,128)S(1)}, u32[]{:S(2)}, u32[]{:S(2)}) %collective-permute-start.5) | collective-permute-done | bytes 589856 | tf_op jit(solution)/shard_map/ppermute | solution.py:539
  33.0 4.7 %collective-permute-done.6.refs_6_ = f32[6,6,16,256]{3,2,1,0:T(8,128)S(1)} collective-permute-done((f32[6,6,16,256]{3,2,1,0:T(8,128)S(1)}, f32[6,6,16,256]{3,2,1,0:T(8,128)S(1)}, u32[]{:S(2)}, u32[]{:S(2)}) %collective-permute-start.6) | collective-permute-done | bytes 589856 | tf_op jit(solution)/shard_map/ppermute | solution.py:539
  37.7 3.5 %shard_map.28 = (f32[3,24,16,256]{3,2,1,0:T(8,128)S(1)}, f32[3,24,16,256]{3,2,1,0:T(8,128)S(1)}, f32[3,24,16,256]{3,2,1,0:T(8,128)S(1)}, f32[3,24,16,256]{3,2,1,...) custom-call(f32[3,12,16,256]{3,2,1,0:T(8,128)S(1)} %pad_maximum_fusi, ...), custom_call_target="tpu_custom_call" | custom-call | tf_op jit(solution)/shard_map/pallas_call | solution.py:526
  42.8 4.1 %shard_map.30 = (f32[3,28,16,256]{3,2,1,0:T(8,128)S(1)}, f32[3,28,16,256]{3,2,1,0:T(8,128)S(1)}, f32[3,28,16,256]{3,2,1,0:T(8,128)S(1)}, f32[3,28,16,256]{3,2,1,0:T(8,128)S(1)}, f32[128,128]{1,0:T(8,128)S(1)}) custom-call(f32[3,20,16,256]{3,2,1,0:T(8,128)S(1)} %slice.68.refs_0_, f32[3,20,16,256]{3,2,1,0:T(8,128)S(1)} %collective-permute-done.refs_1_, ...), custom_call_target="tpu_custom_call" | custom-call | tf_op jit(solution)/shard_map/pallas_call | solution.py:526
  46.9 23.8 %all_to_all.66 = f32[128,1,128]{2,1,0:T(1,128)S(1)} all-to-all(f32[128,1,128]{2,1,0:T(1,128)S(1)} %bitcast.52), channel_id=1, replica_groups=mesh['img_0'=4,'img_1'=4,'tile_0'=4,'tile_1'=2] {'img_0','img_1','tile_0..., dimensions={0} | all-to-all | bytes 131072 | tf_op jit(solution)/shard_map/all_to_all | solution.py:543
  70.7 5.5 %shard_map.31 = (f32[3,44,16,256]{3,2,1,0:T(8,128)S(1)}, f32[3,44,16,256]{3,2,1,0:T(8,128)S(1)}, f32[3,44,16,256]{3,2,1,0:T(8,128)S(1)}, f32[3,44,16,256]{3,2,1,...) custom-call(f32[128,128]{1,0:T(8,128)S(1)} %bitcast.42, ...), custom_call_target="tpu_custom_call" | custom-call | tf_op jit(solution)/shard_map/pallas_call | solution.py:526
  76.2 13.9 %all_to_all.67 = f32[128,1,128]{2,1,0:T(1,128)S(1)} all-to-all(f32[128,1,128]{2,1,0:T(1,128)S(1)} %bitcast.48), channel_id=1, replica_groups=mesh['img_0'=4,'img_1'=4,'tile_0'=4,'tile_1'=2] {'img_0','img_1','tile_0..., dimensions={0} | all-to-all | bytes 131072 | tf_op jit(solution)/shard_map/all_to_all | solution.py:543
  90.2 4.3 %shard_map.32 = (f32[3,44,16,256]{3,2,1,0:T(8,128)S(1)}, f32[3,32,16,256]{3,2,1,0:T(8,128)S(1)}, f32[128,128]{1,0:T(8,128)S(1)}) custom-call(f32[8,128]{1,0:T(8,128)S(1)} %get-tuple-element.99.refs_0_, f32[128,128]{1,0:T(8,128)S(1)} %bitcast.45, f32[3,44,16,256]{3,2,1,0:T(8,128)S(1)} %get-tuple-element.101.refs_2_, ...), custom_call_target="tpu_custom_call" | custom-call | tf_op jit(solution)/shard_map/pallas_call | solution.py:526
  94.5 13.9 %all_to_all.68 = f32[128,1,128]{2,1,0:T(1,128)S(1)} all-to-all(f32[128,1,128]{2,1,0:T(1,128)S(1)} %bitcast.51), channel_id=1, replica_groups=mesh['img_0'=4,'img_1'=4,'tile_0'=4,'tile_1'=2] {'img_0','img_1','tile_0..., dimensions={0} | all-to-all | bytes 131072 | tf_op jit(solution)/shard_map/all_to_all | solution.py:543
  110.1 4.0 %collective-permute-start.9 = (f32[3,12,16,256]{3,2,1,0:T(8,128)S(1)}, f32[3,12,16,256]{3,2,1,0:T(8,128)S(1)}, u32[]{:S(2)}, u32[]{:S(2)}) collective-permute-start(f32[3,12,16,256]{3,2,1,0:T(8,128)S(1)} %get-tuple-element.111.refs_0_), channel_id=1, source_target_pairs={{0,8},{8,16},{16,24},{24,32},{32,40},{40,48},{48,56},{56,64},{64,7... | collective-permute-start | bytes 1769480 | tf_op jit(solution)/shard_map/ppermute | solution.py:539
  114.2 3.2 %collective-permute-start.12 = (f32[3,6,16,256]{3,2,1,0:T(8,128)S(1)}, f32[3,6,16,256]{3,2,1,0:T(8,128)S(1)}, u32[]{:S(2)}, u32[]{:S(2)}) collective-permute-start(f32[3,6,16,256]{3,2,1,0:T(8,128)S(1)} %get-tuple-element.155), channel_id=1, source_target_pairs={{1,0},{2,1},{3,2},{4,3},{5,4},{6,5},{7,6},{9,8},{10,9},{11,10},{12... | collective-permute-start | bytes 884744 | tf_op jit(solution)/shard_map/ppermute | solution.py:539
  117.4 2.3 %collective-permute-start.11 = (f32[3,6,16,256]{3,2,1,0:T(8,128)S(1)}, f32[3,6,16,256]{3,2,1,0:T(8,128)S(1)}, u32[]{:S(2)}, u32[]{:S(2)}) collective-permute-start(f32[3,6,16,256]{3,2,1,0:T(8,128)S(1)} %get-tuple-element.156), channel_id=1, source_target_pairs={{0,1},{1,2},{2,3},{3,4},{4,5},{5,6},{6,7},{8,9},{9,10},{10,11},{11... | collective-permute-start | bytes 884744 | tf_op jit(solution)/shard_map/ppermute | solution.py:539
  122.5 2.6 %collective-permute-start.8 = (f32[3,20,16,256]{3,2,1,0:T(8,128)S(1)}, f32[3,20,16,256]{3,2,1,0:T(8,128)S(1)}, u32[]{:S(2)}, u32[]{:S(2)}) collective-permute-start(f32[3,20,16,256]{3,2,1,0:T(8,128)S(1)} %get-tuple-element.110.refs_0_), channel_id=1, source_target_pairs={{0,8},{8,16},{16,24},{24,32},{32,40},{40,48},{48,56},{56,64},{64,7... | collective-permute-start | bytes 2949128 | tf_op jit(solution)/shard_map/ppermute | solution.py:539
  125.8 5.6 %collective-permute-start.13 = (f32[6,6,16,256]{3,2,1,0:T(8,128)S(1)}, f32[6,6,16,256]{3,2,1,0:T(8,128)S(1)}, u32[]{:S(2)}, u32[]{:S(2)}) collective-permute-start(f32[6,6,16,256]{3,2,1,0:T(8,128)S(1)} %pad_maximum_fusion.3), channel_id=1, source_target_pairs={{0,1},{1,2},{2,3},{3,4},{4,5},{5,6},{6,7},{8,9},{9,10},{10,11},{11... | collective-permute-start | bytes 1769480 | tf_op jit(solution)/shard_map/ppermute | solution.py:539
  131.5 1.9 collective-permute-start.14
  133.4 4.8 %collective-permute-done.13.refs_5_ = f32[6,6,16,256]{3,2,1,0:T(8,128)S(1)} collective-permute-done((f32[6,6,16,256]{3,2,1,0:T(8,128)S(1)}, f32[6,6,16,256]{3,2,1,0:T(8,128)S(1)}, u32[]{:S(2)}, u32[]{:S(2)}) %collective-permute-start.13) | collective-permute-done | bytes 589856 | tf_op jit(solution)/shard_map/ppermute | solution.py:539
  138.2 4.7 %collective-permute-done.14.refs_6_ = f32[6,6,16,256]{3,2,1,0:T(8,128)S(1)} collective-permute-done((f32[6,6,16,256]{3,2,1,0:T(8,128)S(1)}, f32[6,6,16,256]{3,2,1,0:T(8,128)S(1)}, u32[]{:S(2)}, u32[]{:S(2)}) %collective-permute-start.14) | collective-permute-done | bytes 589856 | tf_op jit(solution)/shard_map/ppermute | solution.py:539
  143.0 3.3 %shard_map.34 = (f32[3,24,16,256]{3,2,1,0:T(8,128)S(1)}, f32[3,24,16,256]{3,2,1,0:T(8,128)S(1)}, f32[3,24,16,256]{3,2,1,0:T(8,128)S(1)}, f32[3,24,16,256]{3,2,1,...) custom-call(f32[3,12,16,256]{3,2,1,0:T(8,128)S(1)} %get-tuple-elemen, ...), custom_call_target="tpu_custom_call" | custom-call | tf_op jit(solution)/shard_map/pallas_call | solution.py:526
  147.6 4.0 %shard_map.36 = (f32[3,28,16,256]{3,2,1,0:T(8,128)S(1)}, f32[3,28,16,256]{3,2,1,0:T(8,128)S(1)}, f32[3,28,16,256]{3,2,1,0:T(8,128)S(1)}, f32[3,28,16,256]{3,2,1,0:T(8,128)S(1)}, f32[128,128]{1,0:T(8,128)S(1)}) custom-call(f32[3,20,16,256]{3,2,1,0:T(8,128)S(1)} %get-tuple-element.110.refs_0_, f32[3,20,16,256]{3,2,1,0:T(8,128)S(1)} %collective-permute-done.8.refs_1_, ...), custom_call_target="tpu_custom_call" | custom-call | tf_op jit(solution)/shard_map/pallas_call | solution.py:526
  151.6 18.6 %all_to_all.69 = f32[128,1,128]{2,1,0:T(1,128)S(1)} all-to-all(f32[128,1,128]{2,1,0:T(1,128)S(1)} %bitcast.53), channel_id=1, replica_groups=mesh['img_0'=4,'img_1'=4,'tile_0'=4,'tile_1'=2] {'img_0','img_1','tile_0..., dimensions={0} | all-to-all | bytes 131072 | tf_op jit(solution)/shard_map/all_to_all | solution.py:543
  170.2 5.4 %shard_map.37 = (f32[3,44,16,256]{3,2,1,0:T(8,128)S(1)}, f32[3,44,16,256]{3,2,1,0:T(8,128)S(1)}, f32[3,44,16,256]{3,2,1,0:T(8,128)S(1)}, f32[3,44,16,256]{3,2,1,...) custom-call(f32[128,128]{1,0:T(8,128)S(1)} %bitcast.43, ...), custom_call_target="tpu_custom_call" | custom-call | tf_op jit(solution)/shard_map/pallas_call | solution.py:526
  175.7 13.9 %all_to_all.70 = f32[128,1,128]{2,1,0:T(1,128)S(1)} all-to-all(f32[128,1,128]{2,1,0:T(1,128)S(1)} %bitcast.49), channel_id=1, replica_groups=mesh['img_0'=4,'img_1'=4,'tile_0'=4,'tile_1'=2] {'img_0','img_1','tile_0..., dimensions={0} | all-to-all | bytes 131072 | tf_op jit(solution)/shard_map/all_to_all | solution.py:543
  189.6 4.4 %shard_map.38 = (f32[3,44,16,256]{3,2,1,0:T(8,128)S(1)}, f32[3,32,16,256]{3,2,1,0:T(8,128)S(1)}, f32[128,128]{1,0:T(8,128)S(1)}) custom-call(f32[8,128]{1,0:T(8,128)S(1)} %get-tuple-element.134.refs_0_, f32[128,128]{1,0:T(8,128)S(1)} %bitcast.44, f32[3,44,16,256]{3,2,1,0:T(8,128)S(1)} %get-tuple-element.136.refs_2_, ...), custom_call_target="tpu_custom_call" | custom-call | tf_op jit(solution)/shard_map/pallas_call | solution.py:526
  194.0 13.9 %all_to_all.71 = f32[128,1,128]{2,1,0:T(1,128)S(1)} all-to-all(f32[128,1,128]{2,1,0:T(1,128)S(1)} %bitcast.50), channel_id=1, replica_groups=mesh['img_0'=4,'img_1'=4,'tile_0'=4,'tile_1'=2] {'img_0','img_1','tile_0..., dimensions={0} | all-to-all | bytes 131072 | tf_op jit(solution)/shard_map/all_to_all | solution.py:543
  208.4 2.1 copy.14
  (39 shorter events, 14.8 us)
Async XLA Ops:
  2.3 6.3 %copy-start = (f32[16,32,256]{2,1,0:T(8,128)S(1)}, f32[16,32,256]{2,1,0:T(8,128)}, u32[]{:S(2)}) copy-start(f32[16,32,256]{2,1,0:T(8,128)} %param.3) | copy-start | bytes 1572868
  2.4 20.4 %collective-permute-start.2 = (f32[3,12,16,256]{3,2,1,0:T(8,128)S(1)}, f32[3,12,16,256]{3,2,1,0:T(8,128)S(1)}, u32[]{:S(2)}, u32[]{:S(2)}) collective-permute-start(f32[3,12,16,256]{3,2,1,0:T(8,128)S(1)} %pad_maximum_fusion.refs_0_), channel_id=1, source_target_pairs={{8,0},{16,8},{24,16},{32,24},{40,32},{48,40},{56,48},{64,56},{72,6... | collective-permute-start | bytes 1769480 | tf_op jit(solution)/shard_map/ppermute | solution.py:539
  3.9 18.9 %collective-permute-start.1 = (f32[3,12,16,256]{3,2,1,0:T(8,128)S(1)}, f32[3,12,16,256]{3,2,1,0:T(8,128)S(1)}, u32[]{:S(2)}, u32[]{:S(2)}) collective-permute-start(f32[3,12,16,256]{3,2,1,0:T(8,128)S(1)} %pad_maximum_fusion.refs_0_), channel_id=1, source_target_pairs={{0,8},{8,16},{16,24},{24,32},{32,40},{40,48},{48,56},{56,64},{64,7... | collective-permute-start | bytes 1769480 | tf_op jit(solution)/shard_map/ppermute | solution.py:539
  9.0 9.1 %collective-permute-start.3 = (f32[4,6,16,256]{3,2,1,0:T(8,128)S(1)}, f32[4,6,16,256]{3,2,1,0:T(8,128)S(1)}, u32[]{:S(2)}, u32[]{:S(2)}) collective-permute-start(f32[4,6,16,256]{3,2,1,0:T(8,128)S(1)} %pad_maximum_fusion.5), channel_id=1, source_target_pairs={{0,1},{1,2},{2,3},{3,4},{4,5},{5,6},{6,7},{8,9},{9,10},{10,11},{11... | collective-permute-start | bytes 1179656 | tf_op jit(solution)/shard_map/ppermute | solution.py:539
  13.4 9.4 %collective-permute-start.4 = (f32[4,6,16,256]{3,2,1,0:T(8,128)S(1)}, f32[4,6,16,256]{3,2,1,0:T(8,128)S(1)}, u32[]{:S(2)}, u32[]{:S(2)}) collective-permute-start(f32[4,6,16,256]{3,2,1,0:T(8,128)S(1)} %pad_maximum_fusion.6), channel_id=1, source_target_pairs={{1,0},{2,1},{3,2},{4,3},{5,4},{6,5},{7,6},{9,8},{10,9},{11,10},{12... | collective-permute-start | bytes 1179656 | tf_op jit(solution)/shard_map/ppermute | solution.py:539
  15.4 25.8 %collective-permute-start.7 = (f32[3,20,16,256]{3,2,1,0:T(8,128)S(1)}, f32[3,20,16,256]{3,2,1,0:T(8,128)S(1)}, u32[]{:S(2)}, u32[]{:S(2)}) collective-permute-start(f32[3,20,16,256]{3,2,1,0:T(8,128)S(1)} %slice.68.refs_0_), channel_id=1, source_target_pairs={{8,0},{16,8},{24,16},{32,24},{40,32},{48,40},{56,48},{64,56},{72,6... | collective-permute-start | bytes 2949128 | tf_op jit(solution)/shard_map/ppermute | solution.py:539
  18.1 24.8 %collective-permute-start = (f32[3,20,16,256]{3,2,1,0:T(8,128)S(1)}, f32[3,20,16,256]{3,2,1,0:T(8,128)S(1)}, u32[]{:S(2)}, u32[]{:S(2)}) collective-permute-start(f32[3,20,16,256]{3,2,1,0:T(8,128)S(1)} %slice.68.refs_0_), channel_id=1, source_target_pairs={{0,8},{8,16},{16,24},{24,32},{32,40},{40,48},{48,56},{56,64},{64,7... | collective-permute-start | bytes 2949128 | tf_op jit(solution)/shard_map/ppermute | solution.py:539
  22.9 10.0 %collective-permute-start.5 = (f32[6,6,16,256]{3,2,1,0:T(8,128)S(1)}, f32[6,6,16,256]{3,2,1,0:T(8,128)S(1)}, u32[]{:S(2)}, u32[]{:S(2)}) collective-permute-start(f32[6,6,16,256]{3,2,1,0:T(8,128)S(1)} %pad_maximum_fusion.1), channel_id=1, source_target_pairs={{0,1},{1,2},{2,3},{3,4},{4,5},{5,6},{6,7},{8,9},{9,10},{10,11},{11... | collective-permute-start | bytes 1769480 | tf_op jit(solution)/shard_map/ppermute | solution.py:539
  26.2 11.5 %collective-permute-start.6 = (f32[6,6,16,256]{3,2,1,0:T(8,128)S(1)}, f32[6,6,16,256]{3,2,1,0:T(8,128)S(1)}, u32[]{:S(2)}, u32[]{:S(2)}) collective-permute-start(f32[6,6,16,256]{3,2,1,0:T(8,128)S(1)} %pad_maximum_fusion.2), channel_id=1, source_target_pairs={{1,0},{2,1},{3,2},{4,3},{5,4},{6,5},{7,6},{9,8},{10,9},{11,10},{12... | collective-permute-start | bytes 1769480 | tf_op jit(solution)/shard_map/ppermute | solution.py:539
  108.8 16.4 %collective-permute-start.10 = (f32[3,12,16,256]{3,2,1,0:T(8,128)S(1)}, f32[3,12,16,256]{3,2,1,0:T(8,128)S(1)}, u32[]{:S(2)}, u32[]{:S(2)}) collective-permute-start(f32[3,12,16,256]{3,2,1,0:T(8,128)S(1)} %get-tuple-element.111.refs_0_), channel_id=1, source_target_pairs={{8,0},{16,8},{24,16},{32,24},{40,32},{48,40},{56,48},{64,56},{72,6... | collective-permute-start | bytes 1769480 | tf_op jit(solution)/shard_map/ppermute | solution.py:539
  110.1 15.6 %collective-permute-start.9 = (f32[3,12,16,256]{3,2,1,0:T(8,128)S(1)}, f32[3,12,16,256]{3,2,1,0:T(8,128)S(1)}, u32[]{:S(2)}, u32[]{:S(2)}) collective-permute-start(f32[3,12,16,256]{3,2,1,0:T(8,128)S(1)} %get-tuple-element.111.refs_0_), channel_id=1, source_target_pairs={{0,8},{8,16},{16,24},{24,32},{32,40},{40,48},{48,56},{56,64},{64,7... | collective-permute-start | bytes 1769480 | tf_op jit(solution)/shard_map/ppermute | solution.py:539
  114.2 8.3 %collective-permute-start.12 = (f32[3,6,16,256]{3,2,1,0:T(8,128)S(1)}, f32[3,6,16,256]{3,2,1,0:T(8,128)S(1)}, u32[]{:S(2)}, u32[]{:S(2)}) collective-permute-start(f32[3,6,16,256]{3,2,1,0:T(8,128)S(1)} %get-tuple-element.155), channel_id=1, source_target_pairs={{1,0},{2,1},{3,2},{4,3},{5,4},{6,5},{7,6},{9,8},{10,9},{11,10},{12... | collective-permute-start | bytes 884744 | tf_op jit(solution)/shard_map/ppermute | solution.py:539
  117.4 7.7 %collective-permute-start.11 = (f32[3,6,16,256]{3,2,1,0:T(8,128)S(1)}, f32[3,6,16,256]{3,2,1,0:T(8,128)S(1)}, u32[]{:S(2)}, u32[]{:S(2)}) collective-permute-start(f32[3,6,16,256]{3,2,1,0:T(8,128)S(1)} %get-tuple-element.156), channel_id=1, source_target_pairs={{0,1},{1,2},{2,3},{3,4},{4,5},{5,6},{6,7},{8,9},{9,10},{10,11},{11... | collective-permute-start | bytes 884744 | tf_op jit(solution)/shard_map/ppermute | solution.py:539
  119.8 26.6 %collective-permute-start.15 = (f32[3,20,16,256]{3,2,1,0:T(8,128)S(1)}, f32[3,20,16,256]{3,2,1,0:T(8,128)S(1)}, u32[]{:S(2)}, u32[]{:S(2)}) collective-permute-start(f32[3,20,16,256]{3,2,1,0:T(8,128)S(1)} %get-tuple-element.110.refs_0_), channel_id=1, source_target_pairs={{8,0},{16,8},{24,16},{32,24},{40,32},{48,40},{56,48},{64,56},{72,6... | collective-permute-start | bytes 2949128 | tf_op jit(solution)/shard_map/ppermute | solution.py:539
  122.5 25.0 %collective-permute-start.8 = (f32[3,20,16,256]{3,2,1,0:T(8,128)S(1)}, f32[3,20,16,256]{3,2,1,0:T(8,128)S(1)}, u32[]{:S(2)}, u32[]{:S(2)}) collective-permute-start(f32[3,20,16,256]{3,2,1,0:T(8,128)S(1)} %get-tuple-element.110.refs_0_), channel_id=1, source_target_pairs={{0,8},{8,16},{16,24},{24,32},{32,40},{40,48},{48,56},{56,64},{64,7... | collective-permute-start | bytes 2949128 | tf_op jit(solution)/shard_map/ppermute | solution.py:539
  125.8 12.4 %collective-permute-start.13 = (f32[6,6,16,256]{3,2,1,0:T(8,128)S(1)}, f32[6,6,16,256]{3,2,1,0:T(8,128)S(1)}, u32[]{:S(2)}, u32[]{:S(2)}) collective-permute-start(f32[6,6,16,256]{3,2,1,0:T(8,128)S(1)} %pad_maximum_fusion.3), channel_id=1, source_target_pairs={{0,1},{1,2},{2,3},{3,4},{4,5},{5,6},{6,7},{8,9},{9,10},{10,11},{11... | collective-permute-start | bytes 1769480 | tf_op jit(solution)/shard_map/ppermute | solution.py:539
  131.5 11.5 %collective-permute-start.14 = (f32[6,6,16,256]{3,2,1,0:T(8,128)S(1)}, f32[6,6,16,256]{3,2,1,0:T(8,128)S(1)}, u32[]{:S(2)}, u32[]{:S(2)}) collective-permute-start(f32[6,6,16,256]{3,2,1,0:T(8,128)S(1)} %pad_maximum_fusion.4), channel_id=1, source_target_pairs={{1,0},{2,1},{3,2},{4,3},{5,4},{6,5},{7,6},{9,8},{10,9},{11,10},{12... | collective-permute-start | bytes 1769480 | tf_op jit(solution)/shard_map/ppermute | solution.py:539

commit v12 on v11

--- a/solution.py
+++ b/solution.py
@@ -507,6 +507,39 @@
         loop(low, high, move)
 
 
+def blocks(shape):
+    depth, own, width = shape
+    return [
+        (z, x, slice(z, z + 8), slice(x, x + 8), slice(y, y + 128))
+        for z in range(0, depth, 8)
+        for x in range(0, own, 8)
+        for y in range(0, width, 128)
+    ]
+
+
+def prep_kernel(where, raw_ref, edge_ref, mid_ref):
+    own = raw_ref.shape[2]
+    for comp in range(3):
+        for _, x, zs, xs, ys in blocks(raw_ref.shape[1:]):
+            cells = jnp.swapaxes(raw_ref[comp, zs, xs, ys], 0, 1)
+            for i in range(8):
+                ref, at = edge_ref, x + i
+                if HALO <= at < own - HALO:
+                    ref, at = mid_ref, at - HALO
+                elif at >= own - HALO:
+                    at = at - (own - 2 * HALO)
+                ref[comp, at, zs, ys] = cells[i]
+
+
+def final_kernel(cells, where, all_ref, p_ref, g_ref, out_ref):
+    step = step_of(all_ref, cells) * interior(where)
+    for comp in range(3):
+        for _, x, zs, xs, ys in blocks(out_ref.shape[1:]):
+            old = p_ref[comp, HALO + x : HALO + x + 8, zs, ys]
+            new = old - step * g_ref[comp, xs, zs, ys]
+            out_ref[comp, zs, xs, ys] = jnp.swapaxes(new, 0, 1)
+
+
 def f32(*shape):
     return jax.ShapeDtypeStruct(shape, jnp.float32)
 
@@ -549,10 +582,13 @@
     devices = images * tiles
     cells = float(images * comps * depth * own * tiles * width)
     rows = own + 2 * HALO
-    start = jnp.swapaxes(spins[0], 1, 2)
     coefs = jnp.swapaxes(aniso, 0, 1)
-    edge = jnp.concatenate([start[:, :HALO], start[:, own - HALO :]], axis=1)
-    mid = start[:, HALO : own - HALO]
+    edge, mid = call(
+        prep_kernel,
+        [spins[0]],
+        [f32(3, 2 * HALO, depth, width), f32(3, own - 2 * HALO, depth, width)],
+        [],
+    )
     ext = (3, rows, depth, width)
     ends, middle = (3, 4 * HALO, depth, width), (3, own - 4, depth, width)
     whole = f32(*ext)
@@ -562,7 +598,7 @@
     def scratch(count):
         return [(3, count, depth, width)] * 3 + [(count, depth, width)] * 2
 
-    for _ in range(OUTER):
+    for outer in range(OUTER):
         a_edge, b_edge = beside(edge, IMG, True), beside(edge, IMG, False)
         a_mid, b_mid = beside(mid, IMG, True), beside(mid, IMG, False)
         bottom, top = edge[:, HALO:], edge[:, :HALO]
@@ -613,14 +649,18 @@
             [whole, f32(3, own, depth, width), table],
             [ext, ext, *scratch(rows)],
         )
+        sums = from_everyone(sums)
+        if outer == OUTER - 1:
+            (path,) = call(
+                lambda *refs: final_kernel(cells, *refs), [sums, phi, g], [f32(*spins.shape[1:])], []
+            )
+            return path[None]
         edge, mid = call(
             lambda *refs: last_kernel(cells, *refs),
-            [from_everyone(sums), phi, g],
+            [sums, phi, g],
             [f32(3, 2 * HALO, depth, width), f32(3, own - 2 * HALO, depth, width)],
             [],
         )
-    final = jnp.concatenate([edge[:, :HALO], mid, edge[:, HALO:]], axis=1)
-    return jnp.swapaxes(final, 1, 2)[None]
 
 
 def solution(mesh):

time: 211 us -> 209 us (level)
  local copies, waits for them, and re-layouts: 5.08 us -> 1.99 us
    pallas_call x12 -> x13, Pallas kernels: 37.8 us -> 39 us  [call(): pl.pallas_call(lambda *refs: kernel(position(), *refs), out_shape=outs, i...]
where the time goes in v12:
time: 209 us; the launch traced here: 208 us
  blocking collectives  98.1 us (47%)
  starting transfers between devices  44.2 us (21%)
  Pallas kernels  39 us (19%)
  waiting for transfers between devices  24.3 us (12%)
    all_to_all x6, blocking collectives, from_everyone(): return lax.all_to_all(rows, IMG_TILE, 0, 0, tiled=True)  98.1 us
    ppermute x16, starting transfers between devices, beside(): return lax.ppermute(cells, axis, pairs)  44.2 us
    pallas_call x13, Pallas kernels, call(): pl.pallas_call(lambda *refs: kernel(position(), *refs), out_shape=outs, i...  39 us
    ppermute x16, waiting for transfers between devices, beside(): return lax.ppermute(cells, axis, pairs)  24.3 us
  transfers between devices with their start and end apart: 16, of which 9 were waited for; matrix products, arithmetic and copies ran while one was open for 0% of the time, Pallas kernels for 4%

profile of v12, /device:TPU:1, one launch (start us, length us, event | category | flops | bytes accessed | tf_op | source)
XLA Modules:
  0.0 208.3 jit_solution(9428502381113119927)
XLA Ops:
  3.0 4.7 %collective-permute-start.1 = (f32[3,12,16,256]{3,2,1,0:T(8,128)S(1)}, f32[3,12,16,256]{3,2,1,0:T(8,128)S(1)}, u32[]{:S(2)}, u32[]{:S(2)}) collective-permute-start(f32[3,12,16,256]{3,2,1,0:T(8,128)S(1)} %get-tuple-element.77.refs_0_), channel_id=1, source_target_pairs={{0,8},{8,16},{16,24},{24,32},{32,40},{40,48},{48,56},{56,64},{64,7... | collective-permute-start | bytes 1769480 | tf_op jit(solution)/shard_map/ppermute | solution.py:572
  8.1 4.4 %collective-permute-start.3 = (f32[4,6,16,256]{3,2,1,0:T(8,128)S(1)}, f32[4,6,16,256]{3,2,1,0:T(8,128)S(1)}, u32[]{:S(2)}, u32[]{:S(2)}) collective-permute-start(f32[4,6,16,256]{3,2,1,0:T(8,128)S(1)} %pad_maximum_fusion.4), channel_id=1, source_target_pairs={{0,1},{1,2},{2,3},{3,4},{4,5},{5,6},{6,7},{8,9},{9,10},{10,11},{11... | collective-permute-start | bytes 1179656 | tf_op jit(solution)/shard_map/ppermute | solution.py:572
  12.6 1.9 collective-permute-start.4
  17.2 3.2 %collective-permute-start = (f32[3,20,16,256]{3,2,1,0:T(8,128)S(1)}, f32[3,20,16,256]{3,2,1,0:T(8,128)S(1)}, u32[]{:S(2)}, u32[]{:S(2)}) collective-permute-start(f32[3,20,16,256]{3,2,1,0:T(8,128)S(1)} %get-tuple-element.76.refs_0_), channel_id=1, source_target_pairs={{0,8},{8,16},{16,24},{24,32},{32,40},{40,48},{48,56},{56,64},{64,7... | collective-permute-start | bytes 2949128 | tf_op jit(solution)/shard_map/ppermute | solution.py:572
  20.5 1.5 collective-permute-done.4.refs_4_
  22.1 3.2 %collective-permute-start.5 = (f32[6,6,16,256]{3,2,1,0:T(8,128)S(1)}, f32[6,6,16,256]{3,2,1,0:T(8,128)S(1)}, u32[]{:S(2)}, u32[]{:S(2)}) collective-permute-start(f32[6,6,16,256]{3,2,1,0:T(8,128)S(1)} %pad_maximum_fusion), channel_id=1, source_target_pairs={{0,1},{1,2},{2,3},{3,4},{4,5},{5,6},{6,7},{8,9},{9,10},{10,11},{11... | collective-permute-start | bytes 1769480 | tf_op jit(solution)/shard_map/ppermute | solution.py:572
  25.4 1.9 collective-permute-start.6
  27.3 4.8 %collective-permute-done.5.refs_5_ = f32[6,6,16,256]{3,2,1,0:T(8,128)S(1)} collective-permute-done((f32[6,6,16,256]{3,2,1,0:T(8,128)S(1)}, f32[6,6,16,256]{3,2,1,0:T(8,128)S(1)}, u32[]{:S(2)}, u32[]{:S(2)}) %collective-permute-start.5) | collective-permute-done | bytes 589856 | tf_op jit(solution)/shard_map/ppermute | solution.py:572
  32.1 4.7 %collective-permute-done.6.refs_6_ = f32[6,6,16,256]{3,2,1,0:T(8,128)S(1)} collective-permute-done((f32[6,6,16,256]{3,2,1,0:T(8,128)S(1)}, f32[6,6,16,256]{3,2,1,0:T(8,128)S(1)}, u32[]{:S(2)}, u32[]{:S(2)}) %collective-permute-start.6) | collective-permute-done | bytes 589856 | tf_op jit(solution)/shard_map/ppermute | solution.py:572
  36.9 3.5 %shard_map.29 = (f32[3,24,16,256]{3,2,1,0:T(8,128)S(1)}, f32[3,24,16,256]{3,2,1,0:T(8,128)S(1)}, f32[3,24,16,256]{3,2,1,0:T(8,128)S(1)}, f32[3,24,16,256]{3,2,1,...) custom-call(f32[3,12,16,256]{3,2,1,0:T(8,128)S(1)} %get-tuple-elemen, ...), custom_call_target="tpu_custom_call" | custom-call | tf_op jit(solution)/shard_map/pallas_call | solution.py:559
  41.9 4.1 %shard_map.31 = (f32[3,28,16,256]{3,2,1,0:T(8,128)S(1)}, f32[3,28,16,256]{3,2,1,0:T(8,128)S(1)}, f32[3,28,16,256]{3,2,1,0:T(8,128)S(1)}, f32[3,28,16,256]{3,2,1,0:T(8,128)S(1)}, f32[128,128]{1,0:T(8,128)S(1)}) custom-call(f32[3,20,16,256]{3,2,1,0:T(8,128)S(1)} %get-tuple-element.76.refs_0_, f32[3,20,16,256]{3,2,1,0:T(8,128)S(1)} %collective-permute-done.refs_1_, ...), custom_call_target="tpu_custom_call" | custom-call | tf_op jit(solution)/shard_map/pallas_call | solution.py:559
  46.0 23.8 %all_to_all.66 = f32[128,1,128]{2,1,0:T(1,128)S(1)} all-to-all(f32[128,1,128]{2,1,0:T(1,128)S(1)} %bitcast.46), channel_id=1, replica_groups=mesh['img_0'=4,'img_1'=4,'tile_0'=4,'tile_1'=2] {'img_0','img_1','tile_0..., dimensions={0} | all-to-all | bytes 131072 | tf_op jit(solution)/shard_map/all_to_all | solution.py:576
  69.8 5.5 %shard_map.32 = (f32[3,44,16,256]{3,2,1,0:T(8,128)S(1)}, f32[3,44,16,256]{3,2,1,0:T(8,128)S(1)}, f32[3,44,16,256]{3,2,1,0:T(8,128)S(1)}, f32[3,44,16,256]{3,2,1,...) custom-call(f32[128,128]{1,0:T(8,128)S(1)} %bitcast.36, ...), custom_call_target="tpu_custom_call" | custom-call | tf_op jit(solution)/shard_map/pallas_call | solution.py:559
  75.3 13.9 %all_to_all.67 = f32[128,1,128]{2,1,0:T(1,128)S(1)} all-to-all(f32[128,1,128]{2,1,0:T(1,128)S(1)} %bitcast.42), channel_id=1, replica_groups=mesh['img_0'=4,'img_1'=4,'tile_0'=4,'tile_1'=2] {'img_0','img_1','tile_0..., dimensions={0} | all-to-all | bytes 131072 | tf_op jit(solution)/shard_map/all_to_all | solution.py:576
  89.3 4.2 %shard_map.33 = (f32[3,44,16,256]{3,2,1,0:T(8,128)S(1)}, f32[3,32,16,256]{3,2,1,0:T(8,128)S(1)}, f32[128,128]{1,0:T(8,128)S(1)}) custom-call(f32[8,128]{1,0:T(8,128)S(1)} %get-tuple-element.101.refs_0_, f32[128,128]{1,0:T(8,128)S(1)} %bitcast.39, f32[3,44,16,256]{3,2,1,0:T(8,128)S(1)} %get-tuple-element.103.refs_2_, ...), custom_call_target="tpu_custom_call" | custom-call | tf_op jit(solution)/shard_map/pallas_call | solution.py:559
  93.4 13.9 %all_to_all.68 = f32[128,1,128]{2,1,0:T(1,128)S(1)} all-to-all(f32[128,1,128]{2,1,0:T(1,128)S(1)} %bitcast.45), channel_id=1, replica_groups=mesh['img_0'=4,'img_1'=4,'tile_0'=4,'tile_1'=2] {'img_0','img_1','tile_0..., dimensions={0} | all-to-all | bytes 131072 | tf_op jit(solution)/shard_map/all_to_all | solution.py:576
  109.0 4.0 %collective-permute-start.9 = (f32[3,12,16,256]{3,2,1,0:T(8,128)S(1)}, f32[3,12,16,256]{3,2,1,0:T(8,128)S(1)}, u32[]{:S(2)}, u32[]{:S(2)}) collective-permute-start(f32[3,12,16,256]{3,2,1,0:T(8,128)S(1)} %get-tuple-element.113.refs_0_), channel_id=1, source_target_pairs={{0,8},{8,16},{16,24},{24,32},{32,40},{40,48},{48,56},{56,64},{64,7... | collective-permute-start | bytes 1769480 | tf_op jit(solution)/shard_map/ppermute | solution.py:572
  113.1 3.2 %collective-permute-start.12 = (f32[3,6,16,256]{3,2,1,0:T(8,128)S(1)}, f32[3,6,16,256]{3,2,1,0:T(8,128)S(1)}, u32[]{:S(2)}, u32[]{:S(2)}) collective-permute-start(f32[3,6,16,256]{3,2,1,0:T(8,128)S(1)} %get-tuple-element.151), channel_id=1, source_target_pairs={{1,0},{2,1},{3,2},{4,3},{5,4},{6,5},{7,6},{9,8},{10,9},{11,10},{12... | collective-permute-start | bytes 884744 | tf_op jit(solution)/shard_map/ppermute | solution.py:572
  116.3 2.3 %collective-permute-start.11 = (f32[3,6,16,256]{3,2,1,0:T(8,128)S(1)}, f32[3,6,16,256]{3,2,1,0:T(8,128)S(1)}, u32[]{:S(2)}, u32[]{:S(2)}) collective-permute-start(f32[3,6,16,256]{3,2,1,0:T(8,128)S(1)} %get-tuple-element.152), channel_id=1, source_target_pairs={{0,1},{1,2},{2,3},{3,4},{4,5},{5,6},{6,7},{8,9},{9,10},{10,11},{11... | collective-permute-start | bytes 884744 | tf_op jit(solution)/shard_map/ppermute | solution.py:572
  121.4 2.6 %collective-permute-start.8 = (f32[3,20,16,256]{3,2,1,0:T(8,128)S(1)}, f32[3,20,16,256]{3,2,1,0:T(8,128)S(1)}, u32[]{:S(2)}, u32[]{:S(2)}) collective-permute-start(f32[3,20,16,256]{3,2,1,0:T(8,128)S(1)} %get-tuple-element.112.refs_0_), channel_id=1, source_target_pairs={{0,8},{8,16},{16,24},{24,32},{32,40},{40,48},{48,56},{56,64},{64,7... | collective-permute-start | bytes 2949128 | tf_op jit(solution)/shard_map/ppermute | solution.py:572
  124.7 5.6 %collective-permute-start.13 = (f32[6,6,16,256]{3,2,1,0:T(8,128)S(1)}, f32[6,6,16,256]{3,2,1,0:T(8,128)S(1)}, u32[]{:S(2)}, u32[]{:S(2)}) collective-permute-start(f32[6,6,16,256]{3,2,1,0:T(8,128)S(1)} %pad_maximum_fusion.2), channel_id=1, source_target_pairs={{0,1},{1,2},{2,3},{3,4},{4,5},{5,6},{6,7},{8,9},{9,10},{10,11},{11... | collective-permute-start | bytes 1769480 | tf_op jit(solution)/shard_map/ppermute | solution.py:572
  130.4 1.9 collective-permute-start.14
  132.3 4.8 %collective-permute-done.13.refs_5_ = f32[6,6,16,256]{3,2,1,0:T(8,128)S(1)} collective-permute-done((f32[6,6,16,256]{3,2,1,0:T(8,128)S(1)}, f32[6,6,16,256]{3,2,1,0:T(8,128)S(1)}, u32[]{:S(2)}, u32[]{:S(2)}) %collective-permute-start.13) | collective-permute-done | bytes 589856 | tf_op jit(solution)/shard_map/ppermute | solution.py:572
  137.1 4.7 %collective-permute-done.14.refs_6_ = f32[6,6,16,256]{3,2,1,0:T(8,128)S(1)} collective-permute-done((f32[6,6,16,256]{3,2,1,0:T(8,128)S(1)}, f32[6,6,16,256]{3,2,1,0:T(8,128)S(1)}, u32[]{:S(2)}, u32[]{:S(2)}) %collective-permute-start.14) | collective-permute-done | bytes 589856 | tf_op jit(solution)/shard_map/ppermute | solution.py:572
  141.9 3.3 %shard_map.35 = (f32[3,24,16,256]{3,2,1,0:T(8,128)S(1)}, f32[3,24,16,256]{3,2,1,0:T(8,128)S(1)}, f32[3,24,16,256]{3,2,1,0:T(8,128)S(1)}, f32[3,24,16,256]{3,2,1,...) custom-call(f32[3,12,16,256]{3,2,1,0:T(8,128)S(1)} %get-tuple-elemen, ...), custom_call_target="tpu_custom_call" | custom-call | tf_op jit(solution)/shard_map/pallas_call | solution.py:559
  146.5 4.0 %shard_map.37 = (f32[3,28,16,256]{3,2,1,0:T(8,128)S(1)}, f32[3,28,16,256]{3,2,1,0:T(8,128)S(1)}, f32[3,28,16,256]{3,2,1,0:T(8,128)S(1)}, f32[3,28,16,256]{3,2,1,0:T(8,128)S(1)}, f32[128,128]{1,0:T(8,128)S(1)}) custom-call(f32[3,20,16,256]{3,2,1,0:T(8,128)S(1)} %get-tuple-element.112.refs_0_, f32[3,20,16,256]{3,2,1,0:T(8,128)S(1)} %collective-permute-done.8.refs_1_, ...), custom_call_target="tpu_custom_call" | custom-call | tf_op jit(solution)/shard_map/pallas_call | solution.py:559
  150.5 18.6 %all_to_all.69 = f32[128,1,128]{2,1,0:T(1,128)S(1)} all-to-all(f32[128,1,128]{2,1,0:T(1,128)S(1)} %bitcast.47), channel_id=1, replica_groups=mesh['img_0'=4,'img_1'=4,'tile_0'=4,'tile_1'=2] {'img_0','img_1','tile_0..., dimensions={0} | all-to-all | bytes 131072 | tf_op jit(solution)/shard_map/all_to_all | solution.py:576
  169.1 5.4 %shard_map.38 = (f32[3,44,16,256]{3,2,1,0:T(8,128)S(1)}, f32[3,44,16,256]{3,2,1,0:T(8,128)S(1)}, f32[3,44,16,256]{3,2,1,0:T(8,128)S(1)}, f32[3,44,16,256]{3,2,1,...) custom-call(f32[128,128]{1,0:T(8,128)S(1)} %bitcast.37, ...), custom_call_target="tpu_custom_call" | custom-call | tf_op jit(solution)/shard_map/pallas_call | solution.py:559
  174.6 13.9 %all_to_all.70 = f32[128,1,128]{2,1,0:T(1,128)S(1)} all-to-all(f32[128,1,128]{2,1,0:T(1,128)S(1)} %bitcast.43), channel_id=1, replica_groups=mesh['img_0'=4,'img_1'=4,'tile_0'=4,'tile_1'=2] {'img_0','img_1','tile_0..., dimensions={0} | all-to-all | bytes 131072 | tf_op jit(solution)/shard_map/all_to_all | solution.py:576
  188.5 4.2 %shard_map.39 = (f32[3,44,16,256]{3,2,1,0:T(8,128)S(1)}, f32[3,32,16,256]{3,2,1,0:T(8,128)S(1)}, f32[128,128]{1,0:T(8,128)S(1)}) custom-call(f32[8,128]{1,0:T(8,128)S(1)} %get-tuple-element.136.refs_0_, f32[128,128]{1,0:T(8,128)S(1)} %bitcast.38, f32[3,44,16,256]{3,2,1,0:T(8,128)S(1)} %get-tuple-element.138.refs_2_, ...), custom_call_target="tpu_custom_call" | custom-call | tf_op jit(solution)/shard_map/pallas_call | solution.py:559
  192.6 13.9 %all_to_all.71 = f32[128,1,128]{2,1,0:T(1,128)S(1)} all-to-all(f32[128,1,128]{2,1,0:T(1,128)S(1)} %bitcast.44), channel_id=1, replica_groups=mesh['img_0'=4,'img_1'=4,'tile_0'=4,'tile_1'=2] {'img_0','img_1','tile_0..., dimensions={0} | all-to-all | bytes 131072 | tf_op jit(solution)/shard_map/all_to_all | solution.py:576
  206.6 1.7 shard_map.40
  (36 shorter events, 14.2 us)
Async XLA Ops:
  0.0 1.4 copy-start
  1.4 6.3 %copy-start.1 = (f32[16,32,256]{2,1,0:T(8,128)S(1)}, f32[16,32,256]{2,1,0:T(8,128)}, u32[]{:S(2)}) copy-start(f32[16,32,256]{2,1,0:T(8,128)} %param.3) | copy-start | bytes 1572868
  1.7 20.3 %collective-permute-start.2 = (f32[3,12,16,256]{3,2,1,0:T(8,128)S(1)}, f32[3,12,16,256]{3,2,1,0:T(8,128)S(1)}, u32[]{:S(2)}, u32[]{:S(2)}) collective-permute-start(f32[3,12,16,256]{3,2,1,0:T(8,128)S(1)} %get-tuple-element.77.refs_0_), channel_id=1, source_target_pairs={{8,0},{16,8},{24,16},{32,24},{40,32},{48,40},{56,48},{64,56},{72,6... | collective-permute-start | bytes 1769480 | tf_op jit(solution)/shard_map/ppermute | solution.py:572
  3.0 19.0 %collective-permute-start.1 = (f32[3,12,16,256]{3,2,1,0:T(8,128)S(1)}, f32[3,12,16,256]{3,2,1,0:T(8,128)S(1)}, u32[]{:S(2)}, u32[]{:S(2)}) collective-permute-start(f32[3,12,16,256]{3,2,1,0:T(8,128)S(1)} %get-tuple-element.77.refs_0_), channel_id=1, source_target_pairs={{0,8},{8,16},{16,24},{24,32},{32,40},{40,48},{48,56},{56,64},{64,7... | collective-permute-start | bytes 1769480 | tf_op jit(solution)/shard_map/ppermute | solution.py:572
  8.1 9.1 %collective-permute-start.3 = (f32[4,6,16,256]{3,2,1,0:T(8,128)S(1)}, f32[4,6,16,256]{3,2,1,0:T(8,128)S(1)}, u32[]{:S(2)}, u32[]{:S(2)}) collective-permute-start(f32[4,6,16,256]{3,2,1,0:T(8,128)S(1)} %pad_maximum_fusion.4), channel_id=1, source_target_pairs={{0,1},{1,2},{2,3},{3,4},{4,5},{5,6},{6,7},{8,9},{9,10},{10,11},{11... | collective-permute-start | bytes 1179656 | tf_op jit(solution)/shard_map/ppermute | solution.py:572
  12.6 9.4 %collective-permute-start.4 = (f32[4,6,16,256]{3,2,1,0:T(8,128)S(1)}, f32[4,6,16,256]{3,2,1,0:T(8,128)S(1)}, u32[]{:S(2)}, u32[]{:S(2)}) collective-permute-start(f32[4,6,16,256]{3,2,1,0:T(8,128)S(1)} %pad_maximum_fusion.5), channel_id=1, source_target_pairs={{1,0},{2,1},{3,2},{4,3},{5,4},{6,5},{7,6},{9,8},{10,9},{11,10},{12... | collective-permute-start | bytes 1179656 | tf_op jit(solution)/shard_map/ppermute | solution.py:572
  14.5 25.9 %collective-permute-start.7 = (f32[3,20,16,256]{3,2,1,0:T(8,128)S(1)}, f32[3,20,16,256]{3,2,1,0:T(8,128)S(1)}, u32[]{:S(2)}, u32[]{:S(2)}) collective-permute-start(f32[3,20,16,256]{3,2,1,0:T(8,128)S(1)} %get-tuple-element.76.refs_0_), channel_id=1, source_target_pairs={{8,0},{16,8},{24,16},{32,24},{40,32},{48,40},{56,48},{64,56},{72,6... | collective-permute-start | bytes 2949128 | tf_op jit(solution)/shard_map/ppermute | solution.py:572
  17.2 24.7 %collective-permute-start = (f32[3,20,16,256]{3,2,1,0:T(8,128)S(1)}, f32[3,20,16,256]{3,2,1,0:T(8,128)S(1)}, u32[]{:S(2)}, u32[]{:S(2)}) collective-permute-start(f32[3,20,16,256]{3,2,1,0:T(8,128)S(1)} %get-tuple-element.76.refs_0_), channel_id=1, source_target_pairs={{0,8},{8,16},{16,24},{24,32},{32,40},{40,48},{48,56},{56,64},{64,7... | collective-permute-start | bytes 2949128 | tf_op jit(solution)/shard_map/ppermute | solution.py:572
  22.1 10.0 %collective-permute-start.5 = (f32[6,6,16,256]{3,2,1,0:T(8,128)S(1)}, f32[6,6,16,256]{3,2,1,0:T(8,128)S(1)}, u32[]{:S(2)}, u32[]{:S(2)}) collective-permute-start(f32[6,6,16,256]{3,2,1,0:T(8,128)S(1)} %pad_maximum_fusion), channel_id=1, source_target_pairs={{0,1},{1,2},{2,3},{3,4},{4,5},{5,6},{6,7},{8,9},{9,10},{10,11},{11... | collective-permute-start | bytes 1769480 | tf_op jit(solution)/shard_map/ppermute | solution.py:572
  25.4 11.5 %collective-permute-start.6 = (f32[6,6,16,256]{3,2,1,0:T(8,128)S(1)}, f32[6,6,16,256]{3,2,1,0:T(8,128)S(1)}, u32[]{:S(2)}, u32[]{:S(2)}) collective-permute-start(f32[6,6,16,256]{3,2,1,0:T(8,128)S(1)} %pad_maximum_fusion.1), channel_id=1, source_target_pairs={{1,0},{2,1},{3,2},{4,3},{5,4},{6,5},{7,6},{9,8},{10,9},{11,10},{12... | collective-permute-start | bytes 1769480 | tf_op jit(solution)/shard_map/ppermute | solution.py:572
  107.7 16.4 %collective-permute-start.10 = (f32[3,12,16,256]{3,2,1,0:T(8,128)S(1)}, f32[3,12,16,256]{3,2,1,0:T(8,128)S(1)}, u32[]{:S(2)}, u32[]{:S(2)}) collective-permute-start(f32[3,12,16,256]{3,2,1,0:T(8,128)S(1)} %get-tuple-element.113.refs_0_), channel_id=1, source_target_pairs={{8,0},{16,8},{24,16},{32,24},{40,32},{48,40},{56,48},{64,56},{72,6... | collective-permute-start | bytes 1769480 | tf_op jit(solution)/shard_map/ppermute | solution.py:572
  109.0 15.6 %collective-permute-start.9 = (f32[3,12,16,256]{3,2,1,0:T(8,128)S(1)}, f32[3,12,16,256]{3,2,1,0:T(8,128)S(1)}, u32[]{:S(2)}, u32[]{:S(2)}) collective-permute-start(f32[3,12,16,256]{3,2,1,0:T(8,128)S(1)} %get-tuple-element.113.refs_0_), channel_id=1, source_target_pairs={{0,8},{8,16},{16,24},{24,32},{32,40},{40,48},{48,56},{56,64},{64,7... | collective-permute-start | bytes 1769480 | tf_op jit(solution)/shard_map/ppermute | solution.py:572
  113.1 8.3 %collective-permute-start.12 = (f32[3,6,16,256]{3,2,1,0:T(8,128)S(1)}, f32[3,6,16,256]{3,2,1,0:T(8,128)S(1)}, u32[]{:S(2)}, u32[]{:S(2)}) collective-permute-start(f32[3,6,16,256]{3,2,1,0:T(8,128)S(1)} %get-tuple-element.151), channel_id=1, source_target_pairs={{1,0},{2,1},{3,2},{4,3},{5,4},{6,5},{7,6},{9,8},{10,9},{11,10},{12... | collective-permute-start | bytes 884744 | tf_op jit(solution)/shard_map/ppermute | solution.py:572
  116.3 7.7 %collective-permute-start.11 = (f32[3,6,16,256]{3,2,1,0:T(8,128)S(1)}, f32[3,6,16,256]{3,2,1,0:T(8,128)S(1)}, u32[]{:S(2)}, u32[]{:S(2)}) collective-permute-start(f32[3,6,16,256]{3,2,1,0:T(8,128)S(1)} %get-tuple-element.152), channel_id=1, source_target_pairs={{0,1},{1,2},{2,3},{3,4},{4,5},{5,6},{6,7},{8,9},{9,10},{10,11},{11... | collective-permute-start | bytes 884744 | tf_op jit(solution)/shard_map/ppermute | solution.py:572
  118.7 26.6 %collective-permute-start.15 = (f32[3,20,16,256]{3,2,1,0:T(8,128)S(1)}, f32[3,20,16,256]{3,2,1,0:T(8,128)S(1)}, u32[]{:S(2)}, u32[]{:S(2)}) collective-permute-start(f32[3,20,16,256]{3,2,1,0:T(8,128)S(1)} %get-tuple-element.112.refs_0_), channel_id=1, source_target_pairs={{8,0},{16,8},{24,16},{32,24},{40,32},{48,40},{56,48},{64,56},{72,6... | collective-permute-start | bytes 2949128 | tf_op jit(solution)/shard_map/ppermute | solution.py:572
  121.4 25.0 %collective-permute-start.8 = (f32[3,20,16,256]{3,2,1,0:T(8,128)S(1)}, f32[3,20,16,256]{3,2,1,0:T(8,128)S(1)}, u32[]{:S(2)}, u32[]{:S(2)}) collective-permute-start(f32[3,20,16,256]{3,2,1,0:T(8,128)S(1)} %get-tuple-element.112.refs_0_), channel_id=1, source_target_pairs={{0,8},{8,16},{16,24},{24,32},{32,40},{40,48},{48,56},{56,64},{64,7... | collective-permute-start | bytes 2949128 | tf_op jit(solution)/shard_map/ppermute | solution.py:572
  124.7 12.4 %collective-permute-start.13 = (f32[6,6,16,256]{3,2,1,0:T(8,128)S(1)}, f32[6,6,16,256]{3,2,1,0:T(8,128)S(1)}, u32[]{:S(2)}, u32[]{:S(2)}) collective-permute-start(f32[6,6,16,256]{3,2,1,0:T(8,128)S(1)} %pad_maximum_fusion.2), channel_id=1, source_target_pairs={{0,1},{1,2},{2,3},{3,4},{4,5},{5,6},{6,7},{8,9},{9,10},{10,11},{11... | collective-permute-start | bytes 1769480 | tf_op jit(solution)/shard_map/ppermute | solution.py:572
  130.4 11.5 %collective-permute-start.14 = (f32[6,6,16,256]{3,2,1,0:T(8,128)S(1)}, f32[6,6,16,256]{3,2,1,0:T(8,128)S(1)}, u32[]{:S(2)}, u32[]{:S(2)}) collective-permute-start(f32[6,6,16,256]{3,2,1,0:T(8,128)S(1)} %pad_maximum_fusion.3), channel_id=1, source_target_pairs={{1,0},{2,1},{3,2},{4,3},{5,4},{6,5},{7,6},{9,8},{10,9},{11,10},{12... | collective-permute-start | bytes 1769480 | tf_op jit(solution)/shard_map/ppermute | solution.py:572

commit v13 on v12

--- a/solution.py
+++ b/solution.py
@@ -517,6 +517,17 @@
     ]
 
 
+def slabs(source, target, sems):
+    found = {}
+    for comp in range(3):
+        for z in range(0, source.shape[1], 8):
+            part = comp, pl.ds(z, 8)
+            found[comp, z] = pltpu.make_async_copy(
+                source.at[part], target.at[part], sems.at[comp, z // 8]
+            )
+    return found
+
+
 def prep_kernel(where, raw_ref, edge_ref, mid_ref):
     own = raw_ref.shape[2]
     for comp in range(3):
@@ -531,13 +542,19 @@
                 ref[comp, at, zs, ys] = cells[i]
 
 
-def final_kernel(cells, where, all_ref, p_ref, g_ref, out_ref):
+def final_kernel(cells, where, all_ref, p_ref, g_ref, output_ref, out_ref, sems):
     step = step_of(all_ref, cells) * interior(where)
+    copies = slabs(out_ref, output_ref, sems)
+    own, width = out_ref.shape[2:]
     for comp in range(3):
-        for _, x, zs, xs, ys in blocks(out_ref.shape[1:]):
+        for z, x, zs, xs, ys in blocks(out_ref.shape[1:]):
             old = p_ref[comp, HALO + x : HALO + x + 8, zs, ys]
             new = old - step * g_ref[comp, xs, zs, ys]
             out_ref[comp, zs, xs, ys] = jnp.swapaxes(new, 0, 1)
+            if x == own - 8 and ys.stop == width:
+                copies[comp, z].start()
+    for copy in copies.values():
+        copy.wait()
 
 
 def f32(*shape):
@@ -554,14 +571,17 @@
     return (*found, lax.axis_size(TILE), lax.axis_size(IMG))
 
 
-def call(kernel, operands, outs, scratch):
-    vmem = pl.BlockSpec(memory_space=pltpu.VMEM)
+def call(kernel, operands, outs, scratch, hbm_out=False):
+    vmem, hbm = pl.BlockSpec(memory_space=pltpu.VMEM), pl.BlockSpec(memory_space=pltpu.HBM)
     return pl.pallas_call(
         lambda *refs: kernel(position(), *refs),
         out_shape=outs,
         in_specs=[vmem] * len(operands),
-        out_specs=[vmem] * len(outs),
-        scratch_shapes=[pltpu.VMEM(shape, jnp.float32) for shape in scratch],
+        out_specs=[hbm if hbm_out else vmem] * len(outs),
+        scratch_shapes=[
+            pltpu.VMEM(shape, jnp.float32) if isinstance(shape, tuple) else shape
+            for shape in scratch
+        ],
         compiler_params=pltpu.CompilerParams(vmem_limit_bytes=VMEM_LIMIT),
     )(*operands)
 
@@ -583,6 +603,7 @@
     cells = float(images * comps * depth * own * tiles * width)
     rows = own + 2 * HALO
     coefs = jnp.swapaxes(aniso, 0, 1)
+    moved = [spins.shape[1:], pltpu.SemaphoreType.DMA((3, depth // 8))]
     edge, mid = call(
         prep_kernel,
         [spins[0]],
@@ -652,7 +673,11 @@
         sums = from_everyone(sums)
         if outer == OUTER - 1:
             (path,) = call(
-                lambda *refs: final_kernel(cells, *refs), [sums, phi, g], [f32(*spins.shape[1:])], []
+                lambda *refs: final_kernel(cells, *refs),
+                [sums, phi, g],
+                [f32(*spins.shape[1:])],
+                moved,
+                hbm_out=True,
             )
             return path[None]
         edge, mid = call(

time: 209 us -> 209 us (level)
  no operation moved by 1% of the time
where the time goes in v13:
time: 209 us; the launch traced here: 208 us
  blocking collectives  98.1 us (47%)
  starting transfers between devices  44.2 us (21%)
  Pallas kernels  38.8 us (19%)
  waiting for transfers between devices  24.3 us (12%)
    all_to_all x6, blocking collectives, from_everyone(): return lax.all_to_all(rows, IMG_TILE, 0, 0, tiled=True)  98.1 us
    ppermute x16, starting transfers between devices, beside(): return lax.ppermute(cells, axis, pairs)  44.2 us
    pallas_call x13, Pallas kernels, call(): pl.pallas_call(lambda *refs: kernel(position(), *refs), out_shape=outs, i...  38.8 us
    ppermute x16, waiting for transfers between devices, beside(): return lax.ppermute(cells, axis, pairs)  24.3 us
  transfers between devices with their start and end apart: 16, of which 9 were waited for; matrix products, arithmetic and copies ran while one was open for 0% of the time, Pallas kernels for 4%

profile of v13, /device:TPU:1, one launch (start us, length us, event | category | flops | bytes accessed | tf_op | source)
XLA Modules:
  0.0 208.2 jit_solution(2033937617481817679)
XLA Ops:
  3.0 4.7 %collective-permute-start.1 = (f32[3,12,16,256]{3,2,1,0:T(8,128)S(1)}, f32[3,12,16,256]{3,2,1,0:T(8,128)S(1)}, u32[]{:S(2)}, u32[]{:S(2)}) collective-permute-start(f32[3,12,16,256]{3,2,1,0:T(8,128)S(1)} %get-tuple-element.77.refs_0_), channel_id=1, source_target_pairs={{0,8},{8,16},{16,24},{24,32},{32,40},{40,48},{48,56},{56,64},{64,7... | collective-permute-start | bytes 1769480 | tf_op jit(solution)/shard_map/ppermute | solution.py:592
  8.1 4.4 %collective-permute-start.3 = (f32[4,6,16,256]{3,2,1,0:T(8,128)S(1)}, f32[4,6,16,256]{3,2,1,0:T(8,128)S(1)}, u32[]{:S(2)}, u32[]{:S(2)}) collective-permute-start(f32[4,6,16,256]{3,2,1,0:T(8,128)S(1)} %pad_maximum_fusion.4), channel_id=1, source_target_pairs={{0,1},{1,2},{2,3},{3,4},{4,5},{5,6},{6,7},{8,9},{9,10},{10,11},{11... | collective-permute-start | bytes 1179656 | tf_op jit(solution)/shard_map/ppermute | solution.py:592
  12.6 1.9 collective-permute-start.4
  17.2 3.2 %collective-permute-start = (f32[3,20,16,256]{3,2,1,0:T(8,128)S(1)}, f32[3,20,16,256]{3,2,1,0:T(8,128)S(1)}, u32[]{:S(2)}, u32[]{:S(2)}) collective-permute-start(f32[3,20,16,256]{3,2,1,0:T(8,128)S(1)} %get-tuple-element.76.refs_0_), channel_id=1, source_target_pairs={{0,8},{8,16},{16,24},{24,32},{32,40},{40,48},{48,56},{56,64},{64,7... | collective-permute-start | bytes 2949128 | tf_op jit(solution)/shard_map/ppermute | solution.py:592
  20.5 1.5 collective-permute-done.4.refs_4_
  22.1 3.2 %collective-permute-start.5 = (f32[6,6,16,256]{3,2,1,0:T(8,128)S(1)}, f32[6,6,16,256]{3,2,1,0:T(8,128)S(1)}, u32[]{:S(2)}, u32[]{:S(2)}) collective-permute-start(f32[6,6,16,256]{3,2,1,0:T(8,128)S(1)} %pad_maximum_fusion), channel_id=1, source_target_pairs={{0,1},{1,2},{2,3},{3,4},{4,5},{5,6},{6,7},{8,9},{9,10},{10,11},{11... | collective-permute-start | bytes 1769480 | tf_op jit(solution)/shard_map/ppermute | solution.py:592
  25.4 1.9 collective-permute-start.6
  27.3 4.8 %collective-permute-done.5.refs_5_ = f32[6,6,16,256]{3,2,1,0:T(8,128)S(1)} collective-permute-done((f32[6,6,16,256]{3,2,1,0:T(8,128)S(1)}, f32[6,6,16,256]{3,2,1,0:T(8,128)S(1)}, u32[]{:S(2)}, u32[]{:S(2)}) %collective-permute-start.5) | collective-permute-done | bytes 589856 | tf_op jit(solution)/shard_map/ppermute | solution.py:592
  32.1 4.7 %collective-permute-done.6.refs_6_ = f32[6,6,16,256]{3,2,1,0:T(8,128)S(1)} collective-permute-done((f32[6,6,16,256]{3,2,1,0:T(8,128)S(1)}, f32[6,6,16,256]{3,2,1,0:T(8,128)S(1)}, u32[]{:S(2)}, u32[]{:S(2)}) %collective-permute-start.6) | collective-permute-done | bytes 589856 | tf_op jit(solution)/shard_map/ppermute | solution.py:592
  36.9 3.5 %shard_map.29 = (f32[3,24,16,256]{3,2,1,0:T(8,128)S(1)}, f32[3,24,16,256]{3,2,1,0:T(8,128)S(1)}, f32[3,24,16,256]{3,2,1,0:T(8,128)S(1)}, f32[3,24,16,256]{3,2,1,...) custom-call(f32[3,12,16,256]{3,2,1,0:T(8,128)S(1)} %get-tuple-elemen, ...), custom_call_target="tpu_custom_call" | custom-call | tf_op jit(solution)/shard_map/pallas_call | solution.py:576
  41.9 4.1 %shard_map.31 = (f32[3,28,16,256]{3,2,1,0:T(8,128)S(1)}, f32[3,28,16,256]{3,2,1,0:T(8,128)S(1)}, f32[3,28,16,256]{3,2,1,0:T(8,128)S(1)}, f32[3,28,16,256]{3,2,1,0:T(8,128)S(1)}, f32[128,128]{1,0:T(8,128)S(1)}) custom-call(f32[3,20,16,256]{3,2,1,0:T(8,128)S(1)} %get-tuple-element.76.refs_0_, f32[3,20,16,256]{3,2,1,0:T(8,128)S(1)} %collective-permute-done.refs_1_, ...), custom_call_target="tpu_custom_call" | custom-call | tf_op jit(solution)/shard_map/pallas_call | solution.py:576
  46.0 23.8 %all_to_all.66 = f32[128,1,128]{2,1,0:T(1,128)S(1)} all-to-all(f32[128,1,128]{2,1,0:T(1,128)S(1)} %bitcast.46), channel_id=1, replica_groups=mesh['img_0'=4,'img_1'=4,'tile_0'=4,'tile_1'=2] {'img_0','img_1','tile_0..., dimensions={0} | all-to-all | bytes 131072 | tf_op jit(solution)/shard_map/all_to_all | solution.py:596
  69.8 5.5 %shard_map.32 = (f32[3,44,16,256]{3,2,1,0:T(8,128)S(1)}, f32[3,44,16,256]{3,2,1,0:T(8,128)S(1)}, f32[3,44,16,256]{3,2,1,0:T(8,128)S(1)}, f32[3,44,16,256]{3,2,1,...) custom-call(f32[128,128]{1,0:T(8,128)S(1)} %bitcast.36, ...), custom_call_target="tpu_custom_call" | custom-call | tf_op jit(solution)/shard_map/pallas_call | solution.py:576
  75.3 13.9 %all_to_all.67 = f32[128,1,128]{2,1,0:T(1,128)S(1)} all-to-all(f32[128,1,128]{2,1,0:T(1,128)S(1)} %bitcast.42), channel_id=1, replica_groups=mesh['img_0'=4,'img_1'=4,'tile_0'=4,'tile_1'=2] {'img_0','img_1','tile_0..., dimensions={0} | all-to-all | bytes 131072 | tf_op jit(solution)/shard_map/all_to_all | solution.py:596
  89.3 4.2 %shard_map.33 = (f32[3,44,16,256]{3,2,1,0:T(8,128)S(1)}, f32[3,32,16,256]{3,2,1,0:T(8,128)S(1)}, f32[128,128]{1,0:T(8,128)S(1)}) custom-call(f32[8,128]{1,0:T(8,128)S(1)} %get-tuple-element.101.refs_0_, f32[128,128]{1,0:T(8,128)S(1)} %bitcast.39, f32[3,44,16,256]{3,2,1,0:T(8,128)S(1)} %get-tuple-element.103.refs_2_, ...), custom_call_target="tpu_custom_call" | custom-call | tf_op jit(solution)/shard_map/pallas_call | solution.py:576
  93.4 13.9 %all_to_all.68 = f32[128,1,128]{2,1,0:T(1,128)S(1)} all-to-all(f32[128,1,128]{2,1,0:T(1,128)S(1)} %bitcast.45), channel_id=1, replica_groups=mesh['img_0'=4,'img_1'=4,'tile_0'=4,'tile_1'=2] {'img_0','img_1','tile_0..., dimensions={0} | all-to-all | bytes 131072 | tf_op jit(solution)/shard_map/all_to_all | solution.py:596
  109.0 4.0 %collective-permute-start.9 = (f32[3,12,16,256]{3,2,1,0:T(8,128)S(1)}, f32[3,12,16,256]{3,2,1,0:T(8,128)S(1)}, u32[]{:S(2)}, u32[]{:S(2)}) collective-permute-start(f32[3,12,16,256]{3,2,1,0:T(8,128)S(1)} %get-tuple-element.113.refs_0_), channel_id=1, source_target_pairs={{0,8},{8,16},{16,24},{24,32},{32,40},{40,48},{48,56},{56,64},{64,7... | collective-permute-start | bytes 1769480 | tf_op jit(solution)/shard_map/ppermute | solution.py:592
  113.1 3.2 %collective-permute-start.12 = (f32[3,6,16,256]{3,2,1,0:T(8,128)S(1)}, f32[3,6,16,256]{3,2,1,0:T(8,128)S(1)}, u32[]{:S(2)}, u32[]{:S(2)}) collective-permute-start(f32[3,6,16,256]{3,2,1,0:T(8,128)S(1)} %get-tuple-element.151), channel_id=1, source_target_pairs={{1,0},{2,1},{3,2},{4,3},{5,4},{6,5},{7,6},{9,8},{10,9},{11,10},{12... | collective-permute-start | bytes 884744 | tf_op jit(solution)/shard_map/ppermute | solution.py:592
  116.3 2.3 %collective-permute-start.11 = (f32[3,6,16,256]{3,2,1,0:T(8,128)S(1)}, f32[3,6,16,256]{3,2,1,0:T(8,128)S(1)}, u32[]{:S(2)}, u32[]{:S(2)}) collective-permute-start(f32[3,6,16,256]{3,2,1,0:T(8,128)S(1)} %get-tuple-element.152), channel_id=1, source_target_pairs={{0,1},{1,2},{2,3},{3,4},{4,5},{5,6},{6,7},{8,9},{9,10},{10,11},{11... | collective-permute-start | bytes 884744 | tf_op jit(solution)/shard_map/ppermute | solution.py:592
  121.4 2.6 %collective-permute-start.8 = (f32[3,20,16,256]{3,2,1,0:T(8,128)S(1)}, f32[3,20,16,256]{3,2,1,0:T(8,128)S(1)}, u32[]{:S(2)}, u32[]{:S(2)}) collective-permute-start(f32[3,20,16,256]{3,2,1,0:T(8,128)S(1)} %get-tuple-element.112.refs_0_), channel_id=1, source_target_pairs={{0,8},{8,16},{16,24},{24,32},{32,40},{40,48},{48,56},{56,64},{64,7... | collective-permute-start | bytes 2949128 | tf_op jit(solution)/shard_map/ppermute | solution.py:592
  124.7 5.6 %collective-permute-start.13 = (f32[6,6,16,256]{3,2,1,0:T(8,128)S(1)}, f32[6,6,16,256]{3,2,1,0:T(8,128)S(1)}, u32[]{:S(2)}, u32[]{:S(2)}) collective-permute-start(f32[6,6,16,256]{3,2,1,0:T(8,128)S(1)} %pad_maximum_fusion.2), channel_id=1, source_target_pairs={{0,1},{1,2},{2,3},{3,4},{4,5},{5,6},{6,7},{8,9},{9,10},{10,11},{11... | collective-permute-start | bytes 1769480 | tf_op jit(solution)/shard_map/ppermute | solution.py:592
  130.4 1.9 collective-permute-start.14
  132.3 4.8 %collective-permute-done.13.refs_5_ = f32[6,6,16,256]{3,2,1,0:T(8,128)S(1)} collective-permute-done((f32[6,6,16,256]{3,2,1,0:T(8,128)S(1)}, f32[6,6,16,256]{3,2,1,0:T(8,128)S(1)}, u32[]{:S(2)}, u32[]{:S(2)}) %collective-permute-start.13) | collective-permute-done | bytes 589856 | tf_op jit(solution)/shard_map/ppermute | solution.py:592
  137.1 4.7 %collective-permute-done.14.refs_6_ = f32[6,6,16,256]{3,2,1,0:T(8,128)S(1)} collective-permute-done((f32[6,6,16,256]{3,2,1,0:T(8,128)S(1)}, f32[6,6,16,256]{3,2,1,0:T(8,128)S(1)}, u32[]{:S(2)}, u32[]{:S(2)}) %collective-permute-start.14) | collective-permute-done | bytes 589856 | tf_op jit(solution)/shard_map/ppermute | solution.py:592
  141.9 3.3 %shard_map.35 = (f32[3,24,16,256]{3,2,1,0:T(8,128)S(1)}, f32[3,24,16,256]{3,2,1,0:T(8,128)S(1)}, f32[3,24,16,256]{3,2,1,0:T(8,128)S(1)}, f32[3,24,16,256]{3,2,1,...) custom-call(f32[3,12,16,256]{3,2,1,0:T(8,128)S(1)} %get-tuple-elemen, ...), custom_call_target="tpu_custom_call" | custom-call | tf_op jit(solution)/shard_map/pallas_call | solution.py:576
  146.5 4.0 %shard_map.37 = (f32[3,28,16,256]{3,2,1,0:T(8,128)S(1)}, f32[3,28,16,256]{3,2,1,0:T(8,128)S(1)}, f32[3,28,16,256]{3,2,1,0:T(8,128)S(1)}, f32[3,28,16,256]{3,2,1,0:T(8,128)S(1)}, f32[128,128]{1,0:T(8,128)S(1)}) custom-call(f32[3,20,16,256]{3,2,1,0:T(8,128)S(1)} %get-tuple-element.112.refs_0_, f32[3,20,16,256]{3,2,1,0:T(8,128)S(1)} %collective-permute-done.8.refs_1_, ...), custom_call_target="tpu_custom_call" | custom-call | tf_op jit(solution)/shard_map/pallas_call | solution.py:576
  150.5 18.6 %all_to_all.69 = f32[128,1,128]{2,1,0:T(1,128)S(1)} all-to-all(f32[128,1,128]{2,1,0:T(1,128)S(1)} %bitcast.47), channel_id=1, replica_groups=mesh['img_0'=4,'img_1'=4,'tile_0'=4,'tile_1'=2] {'img_0','img_1','tile_0..., dimensions={0} | all-to-all | bytes 131072 | tf_op jit(solution)/shard_map/all_to_all | solution.py:596
  169.1 5.4 %shard_map.38 = (f32[3,44,16,256]{3,2,1,0:T(8,128)S(1)}, f32[3,44,16,256]{3,2,1,0:T(8,128)S(1)}, f32[3,44,16,256]{3,2,1,0:T(8,128)S(1)}, f32[3,44,16,256]{3,2,1,...) custom-call(f32[128,128]{1,0:T(8,128)S(1)} %bitcast.37, ...), custom_call_target="tpu_custom_call" | custom-call | tf_op jit(solution)/shard_map/pallas_call | solution.py:576
  174.6 13.9 %all_to_all.70 = f32[128,1,128]{2,1,0:T(1,128)S(1)} all-to-all(f32[128,1,128]{2,1,0:T(1,128)S(1)} %bitcast.43), channel_id=1, replica_groups=mesh['img_0'=4,'img_1'=4,'tile_0'=4,'tile_1'=2] {'img_0','img_1','tile_0..., dimensions={0} | all-to-all | bytes 131072 | tf_op jit(solution)/shard_map/all_to_all | solution.py:596
  188.5 4.2 %shard_map.39 = (f32[3,44,16,256]{3,2,1,0:T(8,128)S(1)}, f32[3,32,16,256]{3,2,1,0:T(8,128)S(1)}, f32[128,128]{1,0:T(8,128)S(1)}) custom-call(f32[8,128]{1,0:T(8,128)S(1)} %get-tuple-element.136.refs_0_, f32[128,128]{1,0:T(8,128)S(1)} %bitcast.38, f32[3,44,16,256]{3,2,1,0:T(8,128)S(1)} %get-tuple-element.138.refs_2_, ...), custom_call_target="tpu_custom_call" | custom-call | tf_op jit(solution)/shard_map/pallas_call | solution.py:576
  192.6 13.9 %all_to_all.71 = f32[128,1,128]{2,1,0:T(1,128)S(1)} all-to-all(f32[128,1,128]{2,1,0:T(1,128)S(1)} %bitcast.44), channel_id=1, replica_groups=mesh['img_0'=4,'img_1'=4,'tile_0'=4,'tile_1'=2] {'img_0','img_1','tile_0..., dimensions={0} | all-to-all | bytes 131072 | tf_op jit(solution)/shard_map/all_to_all | solution.py:596
  206.6 1.5 shard_map.40
  (36 shorter events, 14.2 us)
Async XLA Ops:
  0.0 1.4 copy-start
  1.4 6.3 %copy-start.1 = (f32[16,32,256]{2,1,0:T(8,128)S(1)}, f32[16,32,256]{2,1,0:T(8,128)}, u32[]{:S(2)}) copy-start(f32[16,32,256]{2,1,0:T(8,128)} %param.3) | copy-start | bytes 1572868
  1.7 20.3 %collective-permute-start.2 = (f32[3,12,16,256]{3,2,1,0:T(8,128)S(1)}, f32[3,12,16,256]{3,2,1,0:T(8,128)S(1)}, u32[]{:S(2)}, u32[]{:S(2)}) collective-permute-start(f32[3,12,16,256]{3,2,1,0:T(8,128)S(1)} %get-tuple-element.77.refs_0_), channel_id=1, source_target_pairs={{8,0},{16,8},{24,16},{32,24},{40,32},{48,40},{56,48},{64,56},{72,6... | collective-permute-start | bytes 1769480 | tf_op jit(solution)/shard_map/ppermute | solution.py:592
  3.0 19.0 %collective-permute-start.1 = (f32[3,12,16,256]{3,2,1,0:T(8,128)S(1)}, f32[3,12,16,256]{3,2,1,0:T(8,128)S(1)}, u32[]{:S(2)}, u32[]{:S(2)}) collective-permute-start(f32[3,12,16,256]{3,2,1,0:T(8,128)S(1)} %get-tuple-element.77.refs_0_), channel_id=1, source_target_pairs={{0,8},{8,16},{16,24},{24,32},{32,40},{40,48},{48,56},{56,64},{64,7... | collective-permute-start | bytes 1769480 | tf_op jit(solution)/shard_map/ppermute | solution.py:592
  8.1 9.1 %collective-permute-start.3 = (f32[4,6,16,256]{3,2,1,0:T(8,128)S(1)}, f32[4,6,16,256]{3,2,1,0:T(8,128)S(1)}, u32[]{:S(2)}, u32[]{:S(2)}) collective-permute-start(f32[4,6,16,256]{3,2,1,0:T(8,128)S(1)} %pad_maximum_fusion.4), channel_id=1, source_target_pairs={{0,1},{1,2},{2,3},{3,4},{4,5},{5,6},{6,7},{8,9},{9,10},{10,11},{11... | collective-permute-start | bytes 1179656 | tf_op jit(solution)/shard_map/ppermute | solution.py:592
  12.6 9.4 %collective-permute-start.4 = (f32[4,6,16,256]{3,2,1,0:T(8,128)S(1)}, f32[4,6,16,256]{3,2,1,0:T(8,128)S(1)}, u32[]{:S(2)}, u32[]{:S(2)}) collective-permute-start(f32[4,6,16,256]{3,2,1,0:T(8,128)S(1)} %pad_maximum_fusion.5), channel_id=1, source_target_pairs={{1,0},{2,1},{3,2},{4,3},{5,4},{6,5},{7,6},{9,8},{10,9},{11,10},{12... | collective-permute-start | bytes 1179656 | tf_op jit(solution)/shard_map/ppermute | solution.py:592
  14.5 25.9 %collective-permute-start.7 = (f32[3,20,16,256]{3,2,1,0:T(8,128)S(1)}, f32[3,20,16,256]{3,2,1,0:T(8,128)S(1)}, u32[]{:S(2)}, u32[]{:S(2)}) collective-permute-start(f32[3,20,16,256]{3,2,1,0:T(8,128)S(1)} %get-tuple-element.76.refs_0_), channel_id=1, source_target_pairs={{8,0},{16,8},{24,16},{32,24},{40,32},{48,40},{56,48},{64,56},{72,6... | collective-permute-start | bytes 2949128 | tf_op jit(solution)/shard_map/ppermute | solution.py:592
  17.2 24.7 %collective-permute-start = (f32[3,20,16,256]{3,2,1,0:T(8,128)S(1)}, f32[3,20,16,256]{3,2,1,0:T(8,128)S(1)}, u32[]{:S(2)}, u32[]{:S(2)}) collective-permute-start(f32[3,20,16,256]{3,2,1,0:T(8,128)S(1)} %get-tuple-element.76.refs_0_), channel_id=1, source_target_pairs={{0,8},{8,16},{16,24},{24,32},{32,40},{40,48},{48,56},{56,64},{64,7... | collective-permute-start | bytes 2949128 | tf_op jit(solution)/shard_map/ppermute | solution.py:592
  22.1 10.0 %collective-permute-start.5 = (f32[6,6,16,256]{3,2,1,0:T(8,128)S(1)}, f32[6,6,16,256]{3,2,1,0:T(8,128)S(1)}, u32[]{:S(2)}, u32[]{:S(2)}) collective-permute-start(f32[6,6,16,256]{3,2,1,0:T(8,128)S(1)} %pad_maximum_fusion), channel_id=1, source_target_pairs={{0,1},{1,2},{2,3},{3,4},{4,5},{5,6},{6,7},{8,9},{9,10},{10,11},{11... | collective-permute-start | bytes 1769480 | tf_op jit(solution)/shard_map/ppermute | solution.py:592
  25.4 11.5 %collective-permute-start.6 = (f32[6,6,16,256]{3,2,1,0:T(8,128)S(1)}, f32[6,6,16,256]{3,2,1,0:T(8,128)S(1)}, u32[]{:S(2)}, u32[]{:S(2)}) collective-permute-start(f32[6,6,16,256]{3,2,1,0:T(8,128)S(1)} %pad_maximum_fusion.1), channel_id=1, source_target_pairs={{1,0},{2,1},{3,2},{4,3},{5,4},{6,5},{7,6},{9,8},{10,9},{11,10},{12... | collective-permute-start | bytes 1769480 | tf_op jit(solution)/shard_map/ppermute | solution.py:592
  107.7 16.4 %collective-permute-start.10 = (f32[3,12,16,256]{3,2,1,0:T(8,128)S(1)}, f32[3,12,16,256]{3,2,1,0:T(8,128)S(1)}, u32[]{:S(2)}, u32[]{:S(2)}) collective-permute-start(f32[3,12,16,256]{3,2,1,0:T(8,128)S(1)} %get-tuple-element.113.refs_0_), channel_id=1, source_target_pairs={{8,0},{16,8},{24,16},{32,24},{40,32},{48,40},{56,48},{64,56},{72,6... | collective-permute-start | bytes 1769480 | tf_op jit(solution)/shard_map/ppermute | solution.py:592
  109.0 15.6 %collective-permute-start.9 = (f32[3,12,16,256]{3,2,1,0:T(8,128)S(1)}, f32[3,12,16,256]{3,2,1,0:T(8,128)S(1)}, u32[]{:S(2)}, u32[]{:S(2)}) collective-permute-start(f32[3,12,16,256]{3,2,1,0:T(8,128)S(1)} %get-tuple-element.113.refs_0_), channel_id=1, source_target_pairs={{0,8},{8,16},{16,24},{24,32},{32,40},{40,48},{48,56},{56,64},{64,7... | collective-permute-start | bytes 1769480 | tf_op jit(solution)/shard_map/ppermute | solution.py:592
  113.1 8.3 %collective-permute-start.12 = (f32[3,6,16,256]{3,2,1,0:T(8,128)S(1)}, f32[3,6,16,256]{3,2,1,0:T(8,128)S(1)}, u32[]{:S(2)}, u32[]{:S(2)}) collective-permute-start(f32[3,6,16,256]{3,2,1,0:T(8,128)S(1)} %get-tuple-element.151), channel_id=1, source_target_pairs={{1,0},{2,1},{3,2},{4,3},{5,4},{6,5},{7,6},{9,8},{10,9},{11,10},{12... | collective-permute-start | bytes 884744 | tf_op jit(solution)/shard_map/ppermute | solution.py:592
  116.3 7.7 %collective-permute-start.11 = (f32[3,6,16,256]{3,2,1,0:T(8,128)S(1)}, f32[3,6,16,256]{3,2,1,0:T(8,128)S(1)}, u32[]{:S(2)}, u32[]{:S(2)}) collective-permute-start(f32[3,6,16,256]{3,2,1,0:T(8,128)S(1)} %get-tuple-element.152), channel_id=1, source_target_pairs={{0,1},{1,2},{2,3},{3,4},{4,5},{5,6},{6,7},{8,9},{9,10},{10,11},{11... | collective-permute-start | bytes 884744 | tf_op jit(solution)/shard_map/ppermute | solution.py:592
  118.7 26.6 %collective-permute-start.15 = (f32[3,20,16,256]{3,2,1,0:T(8,128)S(1)}, f32[3,20,16,256]{3,2,1,0:T(8,128)S(1)}, u32[]{:S(2)}, u32[]{:S(2)}) collective-permute-start(f32[3,20,16,256]{3,2,1,0:T(8,128)S(1)} %get-tuple-element.112.refs_0_), channel_id=1, source_target_pairs={{8,0},{16,8},{24,16},{32,24},{40,32},{48,40},{56,48},{64,56},{72,6... | collective-permute-start | bytes 2949128 | tf_op jit(solution)/shard_map/ppermute | solution.py:592
  121.4 25.0 %collective-permute-start.8 = (f32[3,20,16,256]{3,2,1,0:T(8,128)S(1)}, f32[3,20,16,256]{3,2,1,0:T(8,128)S(1)}, u32[]{:S(2)}, u32[]{:S(2)}) collective-permute-start(f32[3,20,16,256]{3,2,1,0:T(8,128)S(1)} %get-tuple-element.112.refs_0_), channel_id=1, source_target_pairs={{0,8},{8,16},{16,24},{24,32},{32,40},{40,48},{48,56},{56,64},{64,7... | collective-permute-start | bytes 2949128 | tf_op jit(solution)/shard_map/ppermute | solution.py:592
  124.7 12.4 %collective-permute-start.13 = (f32[6,6,16,256]{3,2,1,0:T(8,128)S(1)}, f32[6,6,16,256]{3,2,1,0:T(8,128)S(1)}, u32[]{:S(2)}, u32[]{:S(2)}) collective-permute-start(f32[6,6,16,256]{3,2,1,0:T(8,128)S(1)} %pad_maximum_fusion.2), channel_id=1, source_target_pairs={{0,1},{1,2},{2,3},{3,4},{4,5},{5,6},{6,7},{8,9},{9,10},{10,11},{11... | collective-permute-start | bytes 1769480 | tf_op jit(solution)/shard_map/ppermute | solution.py:592
  130.4 11.5 %collective-permute-start.14 = (f32[6,6,16,256]{3,2,1,0:T(8,128)S(1)}, f32[6,6,16,256]{3,2,1,0:T(8,128)S(1)}, u32[]{:S(2)}, u32[]{:S(2)}) collective-permute-start(f32[6,6,16,256]{3,2,1,0:T(8,128)S(1)} %pad_maximum_fusion.3), channel_id=1, source_target_pairs={{1,0},{2,1},{3,2},{4,3},{5,4},{6,5},{7,6},{9,8},{10,9},{11,10},{12... | collective-permute-start | bytes 1769480 | tf_op jit(solution)/shard_map/ppermute | solution.py:592

commit v14 on v12

--- a/solution.py
+++ b/solution.py
@@ -108,26 +108,27 @@
             ref[:, HALO + own :] = jnp.zeros((3, rows - HALO - own) + ref.shape[2:], jnp.float32)
 
 
-def residual(ref, lap_ref, out, squares, coef_ref, offset, other_ref=None, sum_ref=None):
+def residual(sides, coef_ref, offset):
     def body(at, carry):
-        stiff = []
-        for place in TILES:
-            cells = vector(ref, at, place)
-            square = 0.125 * dot(cells, cells)
-            put_flat(squares, at, place, square)
-            stiff.append(stiffness(square, flat_of(coef_ref, at + offset, place)))
-        for comp in range(3):
-            cells, bent = laplace(ref, comp, at)
+        for ref, lap_ref, out, squares, other_ref, sum_ref in sides:
+            stiff = []
             for place in TILES:
-                put(lap_ref, comp, at, place, bent[place])
-                total = bent[place] + stiff[place][comp] * cells[place]
-                put(out, comp, at, place, total)
-                if sum_ref is not None:
-                    total = total + tile_of(other_ref, comp, at, place)
-                    put(sum_ref, comp, at, place, total)
+                cells = vector(ref, at, place)
+                square = 0.125 * dot(cells, cells)
+                put_flat(squares, at, place, square)
+                stiff.append(stiffness(square, flat_of(coef_ref, at + offset, place)))
+            for comp in range(3):
+                cells, bent = laplace(ref, comp, at)
+                for place in TILES:
+                    put(lap_ref, comp, at, place, bent[place])
+                    total = bent[place] + stiff[place][comp] * cells[place]
+                    put(out, comp, at, place, total)
+                    if sum_ref is not None:
+                        total = total + tile_of(other_ref, comp, at, place)
+                        put(sum_ref, comp, at, place, total)
         return carry
 
-    loop(1, ref.shape[1] - 1, body)
+    loop(1, sides[0][0].shape[1] - 1, body)
 
 
 def block(phi_ref, m_ref, n_ref, q_ref, r_ref, coef_ref, offset, scratch, cuts, clear, sums):
@@ -243,8 +244,14 @@
 
         cuts = (HALO, span - 2) if top else (2, HALO)
         offset = 0 if top else coef_ref.shape[0] - span
-        residual(m, lm, fa_ref, sm_ref, coef_ref, offset)
-        residual(n, ln, fb_ref, sn_ref, coef_ref, offset, fa_ref, fs_ref)
+        residual(
+            [
+                (m, lm, fa_ref, sm_ref, None, None),
+                (n, ln, fb_ref, sn_ref, fa_ref, fs_ref),
+            ],
+            coef_ref,
+            offset,
+        )
         clear((fa_ref, fb_ref, fs_ref))
         sums = block(phi, m, n, q, r, coef_ref, offset, scratch, cuts, clear, sums)
     for which in range(PRODUCTS):
@@ -264,7 +271,7 @@
     ends_into(phi_ref, phi_end, span)
     ends_into(n_ref, n_end, span)
     join(own_mid, (b_mid,), phi_ref, (n_ref,), 0, phi_ref.shape[1] - 8, 4)
-    residual(n_ref, ln_ref, fb_ref, sn_ref, coef_ref, span - 4)
+    residual([(n_ref, ln_ref, fb_ref, sn_ref, None, None)], coef_ref, span - 4)
 
 
 def middle_kernel(
@@ -275,7 +282,7 @@
     rows = phi_ref.shape[1]
     ends_into(m_ref, m_end, span)
     join(own_mid, (a_mid,), None, (m_ref,), 0, rows - 8, 4)
-    residual(m_ref, lm_ref, fa_ref, sm_ref, coef_ref, span - 4, fb_ref, fs_ref)
+    residual([(m_ref, lm_ref, fa_ref, sm_ref, fb_ref, fs_ref)], coef_ref, span - 4)
     sums = block(
         phi_ref, m_ref, n_ref, q_ref, r_ref, coef_ref, span - 4,
         (fa_ref, fb_ref, fs_ref, sm_ref, sn_ref), (2, rows - 2), lambda refs: None,

time: 209 us -> 209 us (level)
  transfers between devices with their start and end apart: 16 -> 16, of which waited for: 9 -> 10; matrix products, arithmetic and copies ran while one was open for 0% -> 0% of each run, Pallas kernels for 4% -> 4%
where the time goes in v14:
time: 209 us; the launch traced here: 208 us
  blocking collectives  98.4 us (47%)
  starting transfers between devices  44.2 us (21%)
  Pallas kernels  38.4 us (18%)
  waiting for transfers between devices  24.7 us (12%)
    all_to_all x6, blocking collectives, from_everyone(): return lax.all_to_all(rows, IMG_TILE, 0, 0, tiled=True)  98.4 us
    ppermute x16, starting transfers between devices, beside(): return lax.ppermute(cells, axis, pairs)  44.2 us
    pallas_call x13, Pallas kernels, call(): pl.pallas_call(lambda *refs: kernel(position(), *refs), out_shape=outs, i...  38.4 us
    ppermute x16, waiting for transfers between devices, beside(): return lax.ppermute(cells, axis, pairs)  24.7 us
  transfers between devices with their start and end apart: 16, of which 10 were waited for; matrix products, arithmetic and copies ran while one was open for 0% of the time, Pallas kernels for 4%

profile of v14, /device:TPU:1, one launch (start us, length us, event | category | flops | bytes accessed | tf_op | source)
XLA Modules:
  0.0 208.3 jit_solution(262087417031872445)
XLA Ops:
  3.0 4.7 %collective-permute-start.1 = (f32[3,12,16,256]{3,2,1,0:T(8,128)S(1)}, f32[3,12,16,256]{3,2,1,0:T(8,128)S(1)}, u32[]{:S(2)}, u32[]{:S(2)}) collective-permute-start(f32[3,12,16,256]{3,2,1,0:T(8,128)S(1)} %get-tuple-element.77.refs_0_), channel_id=1, source_target_pairs={{0,8},{8,16},{16,24},{24,32},{32,40},{40,48},{48,56},{56,64},{64,7... | collective-permute-start | bytes 1769480 | tf_op jit(solution)/shard_map/ppermute | solution.py:579
  8.1 4.4 %collective-permute-start.3 = (f32[4,6,16,256]{3,2,1,0:T(8,128)S(1)}, f32[4,6,16,256]{3,2,1,0:T(8,128)S(1)}, u32[]{:S(2)}, u32[]{:S(2)}) collective-permute-start(f32[4,6,16,256]{3,2,1,0:T(8,128)S(1)} %pad_maximum_fusion.4), channel_id=1, source_target_pairs={{0,1},{1,2},{2,3},{3,4},{4,5},{5,6},{6,7},{8,9},{9,10},{10,11},{11... | collective-permute-start | bytes 1179656 | tf_op jit(solution)/shard_map/ppermute | solution.py:579
  12.6 1.9 collective-permute-start.4
  17.2 3.2 %collective-permute-start = (f32[3,20,16,256]{3,2,1,0:T(8,128)S(1)}, f32[3,20,16,256]{3,2,1,0:T(8,128)S(1)}, u32[]{:S(2)}, u32[]{:S(2)}) collective-permute-start(f32[3,20,16,256]{3,2,1,0:T(8,128)S(1)} %get-tuple-element.76.refs_0_), channel_id=1, source_target_pairs={{0,8},{8,16},{16,24},{24,32},{32,40},{40,48},{48,56},{56,64},{64,7... | collective-permute-start | bytes 2949128 | tf_op jit(solution)/shard_map/ppermute | solution.py:579
  20.5 1.5 collective-permute-done.4.refs_4_
  22.1 3.2 %collective-permute-start.5 = (f32[6,6,16,256]{3,2,1,0:T(8,128)S(1)}, f32[6,6,16,256]{3,2,1,0:T(8,128)S(1)}, u32[]{:S(2)}, u32[]{:S(2)}) collective-permute-start(f32[6,6,16,256]{3,2,1,0:T(8,128)S(1)} %pad_maximum_fusion), channel_id=1, source_target_pairs={{0,1},{1,2},{2,3},{3,4},{4,5},{5,6},{6,7},{8,9},{9,10},{10,11},{11... | collective-permute-start | bytes 1769480 | tf_op jit(solution)/shard_map/ppermute | solution.py:579
  25.4 1.9 collective-permute-start.6
  27.3 4.8 %collective-permute-done.5.refs_5_ = f32[6,6,16,256]{3,2,1,0:T(8,128)S(1)} collective-permute-done((f32[6,6,16,256]{3,2,1,0:T(8,128)S(1)}, f32[6,6,16,256]{3,2,1,0:T(8,128)S(1)}, u32[]{:S(2)}, u32[]{:S(2)}) %collective-permute-start.5) | collective-permute-done | bytes 589856 | tf_op jit(solution)/shard_map/ppermute | solution.py:579
  32.1 4.7 %collective-permute-done.6.refs_6_ = f32[6,6,16,256]{3,2,1,0:T(8,128)S(1)} collective-permute-done((f32[6,6,16,256]{3,2,1,0:T(8,128)S(1)}, f32[6,6,16,256]{3,2,1,0:T(8,128)S(1)}, u32[]{:S(2)}, u32[]{:S(2)}) %collective-permute-start.6) | collective-permute-done | bytes 589856 | tf_op jit(solution)/shard_map/ppermute | solution.py:579
  36.9 3.2 %shard_map.29 = (f32[3,24,16,256]{3,2,1,0:T(8,128)S(1)}, f32[3,24,16,256]{3,2,1,0:T(8,128)S(1)}, f32[3,24,16,256]{3,2,1,0:T(8,128)S(1)}, f32[3,24,16,256]{3,2,1,...) custom-call(f32[3,12,16,256]{3,2,1,0:T(8,128)S(1)} %get-tuple-elemen, ...), custom_call_target="tpu_custom_call" | custom-call | tf_op jit(solution)/shard_map/pallas_call | solution.py:566
  41.9 4.1 %shard_map.31 = (f32[3,28,16,256]{3,2,1,0:T(8,128)S(1)}, f32[3,28,16,256]{3,2,1,0:T(8,128)S(1)}, f32[3,28,16,256]{3,2,1,0:T(8,128)S(1)}, f32[3,28,16,256]{3,2,1,0:T(8,128)S(1)}, f32[128,128]{1,0:T(8,128)S(1)}) custom-call(f32[3,20,16,256]{3,2,1,0:T(8,128)S(1)} %get-tuple-element.76.refs_0_, f32[3,20,16,256]{3,2,1,0:T(8,128)S(1)} %collective-permute-done.refs_1_, ...), custom_call_target="tpu_custom_call" | custom-call | tf_op jit(solution)/shard_map/pallas_call | solution.py:566
  46.0 23.8 %all_to_all.66 = f32[128,1,128]{2,1,0:T(1,128)S(1)} all-to-all(f32[128,1,128]{2,1,0:T(1,128)S(1)} %bitcast.46), channel_id=1, replica_groups=mesh['img_0'=4,'img_1'=4,'tile_0'=4,'tile_1'=2] {'img_0','img_1','tile_0..., dimensions={0} | all-to-all | bytes 131072 | tf_op jit(solution)/shard_map/all_to_all | solution.py:583
  69.8 5.5 %shard_map.32 = (f32[3,44,16,256]{3,2,1,0:T(8,128)S(1)}, f32[3,44,16,256]{3,2,1,0:T(8,128)S(1)}, f32[3,44,16,256]{3,2,1,0:T(8,128)S(1)}, f32[3,44,16,256]{3,2,1,...) custom-call(f32[128,128]{1,0:T(8,128)S(1)} %bitcast.36, ...), custom_call_target="tpu_custom_call" | custom-call | tf_op jit(solution)/shard_map/pallas_call | solution.py:566
  75.3 13.9 %all_to_all.67 = f32[128,1,128]{2,1,0:T(1,128)S(1)} all-to-all(f32[128,1,128]{2,1,0:T(1,128)S(1)} %bitcast.42), channel_id=1, replica_groups=mesh['img_0'=4,'img_1'=4,'tile_0'=4,'tile_1'=2] {'img_0','img_1','tile_0..., dimensions={0} | all-to-all | bytes 131072 | tf_op jit(solution)/shard_map/all_to_all | solution.py:583
  89.3 4.2 %shard_map.33 = (f32[3,44,16,256]{3,2,1,0:T(8,128)S(1)}, f32[3,32,16,256]{3,2,1,0:T(8,128)S(1)}, f32[128,128]{1,0:T(8,128)S(1)}) custom-call(f32[8,128]{1,0:T(8,128)S(1)} %get-tuple-element.101.refs_0_, f32[128,128]{1,0:T(8,128)S(1)} %bitcast.39, f32[3,44,16,256]{3,2,1,0:T(8,128)S(1)} %get-tuple-element.103.refs_2_, ...), custom_call_target="tpu_custom_call" | custom-call | tf_op jit(solution)/shard_map/pallas_call | solution.py:566
  93.4 13.9 %all_to_all.68 = f32[128,1,128]{2,1,0:T(1,128)S(1)} all-to-all(f32[128,1,128]{2,1,0:T(1,128)S(1)} %bitcast.45), channel_id=1, replica_groups=mesh['img_0'=4,'img_1'=4,'tile_0'=4,'tile_1'=2] {'img_0','img_1','tile_0..., dimensions={0} | all-to-all | bytes 131072 | tf_op jit(solution)/shard_map/all_to_all | solution.py:583
  109.0 4.0 %collective-permute-start.9 = (f32[3,12,16,256]{3,2,1,0:T(8,128)S(1)}, f32[3,12,16,256]{3,2,1,0:T(8,128)S(1)}, u32[]{:S(2)}, u32[]{:S(2)}) collective-permute-start(f32[3,12,16,256]{3,2,1,0:T(8,128)S(1)} %get-tuple-element.113.refs_0_), channel_id=1, source_target_pairs={{0,8},{8,16},{16,24},{24,32},{32,40},{40,48},{48,56},{56,64},{64,7... | collective-permute-start | bytes 1769480 | tf_op jit(solution)/shard_map/ppermute | solution.py:579
  113.1 3.2 %collective-permute-start.12 = (f32[3,6,16,256]{3,2,1,0:T(8,128)S(1)}, f32[3,6,16,256]{3,2,1,0:T(8,128)S(1)}, u32[]{:S(2)}, u32[]{:S(2)}) collective-permute-start(f32[3,6,16,256]{3,2,1,0:T(8,128)S(1)} %get-tuple-element.151), channel_id=1, source_target_pairs={{1,0},{2,1},{3,2},{4,3},{5,4},{6,5},{7,6},{9,8},{10,9},{11,10},{12... | collective-permute-start | bytes 884744 | tf_op jit(solution)/shard_map/ppermute | solution.py:579
  116.3 2.3 %collective-permute-start.11 = (f32[3,6,16,256]{3,2,1,0:T(8,128)S(1)}, f32[3,6,16,256]{3,2,1,0:T(8,128)S(1)}, u32[]{:S(2)}, u32[]{:S(2)}) collective-permute-start(f32[3,6,16,256]{3,2,1,0:T(8,128)S(1)} %get-tuple-element.152), channel_id=1, source_target_pairs={{0,1},{1,2},{2,3},{3,4},{4,5},{5,6},{6,7},{8,9},{9,10},{10,11},{11... | collective-permute-start | bytes 884744 | tf_op jit(solution)/shard_map/ppermute | solution.py:579
  121.4 2.6 %collective-permute-start.8 = (f32[3,20,16,256]{3,2,1,0:T(8,128)S(1)}, f32[3,20,16,256]{3,2,1,0:T(8,128)S(1)}, u32[]{:S(2)}, u32[]{:S(2)}) collective-permute-start(f32[3,20,16,256]{3,2,1,0:T(8,128)S(1)} %get-tuple-element.112.refs_0_), channel_id=1, source_target_pairs={{0,8},{8,16},{16,24},{24,32},{32,40},{40,48},{48,56},{56,64},{64,7... | collective-permute-start | bytes 2949128 | tf_op jit(solution)/shard_map/ppermute | solution.py:579
  124.7 5.6 %collective-permute-start.13 = (f32[6,6,16,256]{3,2,1,0:T(8,128)S(1)}, f32[6,6,16,256]{3,2,1,0:T(8,128)S(1)}, u32[]{:S(2)}, u32[]{:S(2)}) collective-permute-start(f32[6,6,16,256]{3,2,1,0:T(8,128)S(1)} %pad_maximum_fusion.2), channel_id=1, source_target_pairs={{0,1},{1,2},{2,3},{3,4},{4,5},{5,6},{6,7},{8,9},{9,10},{10,11},{11... | collective-permute-start | bytes 1769480 | tf_op jit(solution)/shard_map/ppermute | solution.py:579
  130.4 1.9 collective-permute-start.14
  132.3 4.8 %collective-permute-done.13.refs_5_ = f32[6,6,16,256]{3,2,1,0:T(8,128)S(1)} collective-permute-done((f32[6,6,16,256]{3,2,1,0:T(8,128)S(1)}, f32[6,6,16,256]{3,2,1,0:T(8,128)S(1)}, u32[]{:S(2)}, u32[]{:S(2)}) %collective-permute-start.13) | collective-permute-done | bytes 589856 | tf_op jit(solution)/shard_map/ppermute | solution.py:579
  137.1 4.7 %collective-permute-done.14.refs_6_ = f32[6,6,16,256]{3,2,1,0:T(8,128)S(1)} collective-permute-done((f32[6,6,16,256]{3,2,1,0:T(8,128)S(1)}, f32[6,6,16,256]{3,2,1,0:T(8,128)S(1)}, u32[]{:S(2)}, u32[]{:S(2)}) %collective-permute-start.14) | collective-permute-done | bytes 589856 | tf_op jit(solution)/shard_map/ppermute | solution.py:579
  141.9 3.0 %shard_map.35 = (f32[3,24,16,256]{3,2,1,0:T(8,128)S(1)}, f32[3,24,16,256]{3,2,1,0:T(8,128)S(1)}, f32[3,24,16,256]{3,2,1,0:T(8,128)S(1)}, f32[3,24,16,256]{3,2,1,...) custom-call(f32[3,12,16,256]{3,2,1,0:T(8,128)S(1)} %get-tuple-elemen, ...), custom_call_target="tpu_custom_call" | custom-call | tf_op jit(solution)/shard_map/pallas_call | solution.py:566
  146.2 4.0 %shard_map.37 = (f32[3,28,16,256]{3,2,1,0:T(8,128)S(1)}, f32[3,28,16,256]{3,2,1,0:T(8,128)S(1)}, f32[3,28,16,256]{3,2,1,0:T(8,128)S(1)}, f32[3,28,16,256]{3,2,1,0:T(8,128)S(1)}, f32[128,128]{1,0:T(8,128)S(1)}) custom-call(f32[3,20,16,256]{3,2,1,0:T(8,128)S(1)} %get-tuple-element.112.refs_0_, f32[3,20,16,256]{3,2,1,0:T(8,128)S(1)} %collective-permute-done.8.refs_1_, ...), custom_call_target="tpu_custom_call" | custom-call | tf_op jit(solution)/shard_map/pallas_call | solution.py:566
  150.2 19.0 %all_to_all.69 = f32[128,1,128]{2,1,0:T(1,128)S(1)} all-to-all(f32[128,1,128]{2,1,0:T(1,128)S(1)} %bitcast.47), channel_id=1, replica_groups=mesh['img_0'=4,'img_1'=4,'tile_0'=4,'tile_1'=2] {'img_0','img_1','tile_0..., dimensions={0} | all-to-all | bytes 131072 | tf_op jit(solution)/shard_map/all_to_all | solution.py:583
  169.1 5.4 %shard_map.38 = (f32[3,44,16,256]{3,2,1,0:T(8,128)S(1)}, f32[3,44,16,256]{3,2,1,0:T(8,128)S(1)}, f32[3,44,16,256]{3,2,1,0:T(8,128)S(1)}, f32[3,44,16,256]{3,2,1,...) custom-call(f32[128,128]{1,0:T(8,128)S(1)} %bitcast.37, ...), custom_call_target="tpu_custom_call" | custom-call | tf_op jit(solution)/shard_map/pallas_call | solution.py:566
  174.6 13.9 %all_to_all.70 = f32[128,1,128]{2,1,0:T(1,128)S(1)} all-to-all(f32[128,1,128]{2,1,0:T(1,128)S(1)} %bitcast.43), channel_id=1, replica_groups=mesh['img_0'=4,'img_1'=4,'tile_0'=4,'tile_1'=2] {'img_0','img_1','tile_0..., dimensions={0} | all-to-all | bytes 131072 | tf_op jit(solution)/shard_map/all_to_all | solution.py:583
  188.5 4.2 %shard_map.39 = (f32[3,44,16,256]{3,2,1,0:T(8,128)S(1)}, f32[3,32,16,256]{3,2,1,0:T(8,128)S(1)}, f32[128,128]{1,0:T(8,128)S(1)}) custom-call(f32[8,128]{1,0:T(8,128)S(1)} %get-tuple-element.136.refs_0_, f32[128,128]{1,0:T(8,128)S(1)} %bitcast.38, f32[3,44,16,256]{3,2,1,0:T(8,128)S(1)} %get-tuple-element.138.refs_2_, ...), custom_call_target="tpu_custom_call" | custom-call | tf_op jit(solution)/shard_map/pallas_call | solution.py:566
  192.6 13.9 %all_to_all.71 = f32[128,1,128]{2,1,0:T(1,128)S(1)} all-to-all(f32[128,1,128]{2,1,0:T(1,128)S(1)} %bitcast.44), channel_id=1, replica_groups=mesh['img_0'=4,'img_1'=4,'tile_0'=4,'tile_1'=2] {'img_0','img_1','tile_0..., dimensions={0} | all-to-all | bytes 131072 | tf_op jit(solution)/shard_map/all_to_all | solution.py:583
  206.6 1.7 shard_map.40
  (36 shorter events, 14.5 us)
Async XLA Ops:
  0.0 1.4 copy-start
  1.4 6.3 %copy-start.1 = (f32[16,32,256]{2,1,0:T(8,128)S(1)}, f32[16,32,256]{2,1,0:T(8,128)}, u32[]{:S(2)}) copy-start(f32[16,32,256]{2,1,0:T(8,128)} %param.3) | copy-start | bytes 1572868
  1.7 20.3 %collective-permute-start.2 = (f32[3,12,16,256]{3,2,1,0:T(8,128)S(1)}, f32[3,12,16,256]{3,2,1,0:T(8,128)S(1)}, u32[]{:S(2)}, u32[]{:S(2)}) collective-permute-start(f32[3,12,16,256]{3,2,1,0:T(8,128)S(1)} %get-tuple-element.77.refs_0_), channel_id=1, source_target_pairs={{8,0},{16,8},{24,16},{32,24},{40,32},{48,40},{56,48},{64,56},{72,6... | collective-permute-start | bytes 1769480 | tf_op jit(solution)/shard_map/ppermute | solution.py:579
  3.0 19.0 %collective-permute-start.1 = (f32[3,12,16,256]{3,2,1,0:T(8,128)S(1)}, f32[3,12,16,256]{3,2,1,0:T(8,128)S(1)}, u32[]{:S(2)}, u32[]{:S(2)}) collective-permute-start(f32[3,12,16,256]{3,2,1,0:T(8,128)S(1)} %get-tuple-element.77.refs_0_), channel_id=1, source_target_pairs={{0,8},{8,16},{16,24},{24,32},{32,40},{40,48},{48,56},{56,64},{64,7... | collective-permute-start | bytes 1769480 | tf_op jit(solution)/shard_map/ppermute | solution.py:579
  8.1 9.1 %collective-permute-start.3 = (f32[4,6,16,256]{3,2,1,0:T(8,128)S(1)}, f32[4,6,16,256]{3,2,1,0:T(8,128)S(1)}, u32[]{:S(2)}, u32[]{:S(2)}) collective-permute-start(f32[4,6,16,256]{3,2,1,0:T(8,128)S(1)} %pad_maximum_fusion.4), channel_id=1, source_target_pairs={{0,1},{1,2},{2,3},{3,4},{4,5},{5,6},{6,7},{8,9},{9,10},{10,11},{11... | collective-permute-start | bytes 1179656 | tf_op jit(solution)/shard_map/ppermute | solution.py:579
  12.6 9.4 %collective-permute-start.4 = (f32[4,6,16,256]{3,2,1,0:T(8,128)S(1)}, f32[4,6,16,256]{3,2,1,0:T(8,128)S(1)}, u32[]{:S(2)}, u32[]{:S(2)}) collective-permute-start(f32[4,6,16,256]{3,2,1,0:T(8,128)S(1)} %pad_maximum_fusion.5), channel_id=1, source_target_pairs={{1,0},{2,1},{3,2},{4,3},{5,4},{6,5},{7,6},{9,8},{10,9},{11,10},{12... | collective-permute-start | bytes 1179656 | tf_op jit(solution)/shard_map/ppermute | solution.py:579
  14.5 25.7 %collective-permute-start.7 = (f32[3,20,16,256]{3,2,1,0:T(8,128)S(1)}, f32[3,20,16,256]{3,2,1,0:T(8,128)S(1)}, u32[]{:S(2)}, u32[]{:S(2)}) collective-permute-start(f32[3,20,16,256]{3,2,1,0:T(8,128)S(1)} %get-tuple-element.76.refs_0_), channel_id=1, source_target_pairs={{8,0},{16,8},{24,16},{32,24},{40,32},{48,40},{56,48},{64,56},{72,6... | collective-permute-start | bytes 2949128 | tf_op jit(solution)/shard_map/ppermute | solution.py:579
  17.2 24.7 %collective-permute-start = (f32[3,20,16,256]{3,2,1,0:T(8,128)S(1)}, f32[3,20,16,256]{3,2,1,0:T(8,128)S(1)}, u32[]{:S(2)}, u32[]{:S(2)}) collective-permute-start(f32[3,20,16,256]{3,2,1,0:T(8,128)S(1)} %get-tuple-element.76.refs_0_), channel_id=1, source_target_pairs={{0,8},{8,16},{16,24},{24,32},{32,40},{40,48},{48,56},{56,64},{64,7... | collective-permute-start | bytes 2949128 | tf_op jit(solution)/shard_map/ppermute | solution.py:579
  22.1 10.0 %collective-permute-start.5 = (f32[6,6,16,256]{3,2,1,0:T(8,128)S(1)}, f32[6,6,16,256]{3,2,1,0:T(8,128)S(1)}, u32[]{:S(2)}, u32[]{:S(2)}) collective-permute-start(f32[6,6,16,256]{3,2,1,0:T(8,128)S(1)} %pad_maximum_fusion), channel_id=1, source_target_pairs={{0,1},{1,2},{2,3},{3,4},{4,5},{5,6},{6,7},{8,9},{9,10},{10,11},{11... | collective-permute-start | bytes 1769480 | tf_op jit(solution)/shard_map/ppermute | solution.py:579
  25.4 11.5 %collective-permute-start.6 = (f32[6,6,16,256]{3,2,1,0:T(8,128)S(1)}, f32[6,6,16,256]{3,2,1,0:T(8,128)S(1)}, u32[]{:S(2)}, u32[]{:S(2)}) collective-permute-start(f32[6,6,16,256]{3,2,1,0:T(8,128)S(1)} %pad_maximum_fusion.1), channel_id=1, source_target_pairs={{1,0},{2,1},{3,2},{4,3},{5,4},{6,5},{7,6},{9,8},{10,9},{11,10},{12... | collective-permute-start | bytes 1769480 | tf_op jit(solution)/shard_map/ppermute | solution.py:579
  107.7 16.4 %collective-permute-start.10 = (f32[3,12,16,256]{3,2,1,0:T(8,128)S(1)}, f32[3,12,16,256]{3,2,1,0:T(8,128)S(1)}, u32[]{:S(2)}, u32[]{:S(2)}) collective-permute-start(f32[3,12,16,256]{3,2,1,0:T(8,128)S(1)} %get-tuple-element.113.refs_0_), channel_id=1, source_target_pairs={{8,0},{16,8},{24,16},{32,24},{40,32},{48,40},{56,48},{64,56},{72,6... | collective-permute-start | bytes 1769480 | tf_op jit(solution)/shard_map/ppermute | solution.py:579
  109.0 15.6 %collective-permute-start.9 = (f32[3,12,16,256]{3,2,1,0:T(8,128)S(1)}, f32[3,12,16,256]{3,2,1,0:T(8,128)S(1)}, u32[]{:S(2)}, u32[]{:S(2)}) collective-permute-start(f32[3,12,16,256]{3,2,1,0:T(8,128)S(1)} %get-tuple-element.113.refs_0_), channel_id=1, source_target_pairs={{0,8},{8,16},{16,24},{24,32},{32,40},{40,48},{48,56},{56,64},{64,7... | collective-permute-start | bytes 1769480 | tf_op jit(solution)/shard_map/ppermute | solution.py:579
  113.1 8.3 %collective-permute-start.12 = (f32[3,6,16,256]{3,2,1,0:T(8,128)S(1)}, f32[3,6,16,256]{3,2,1,0:T(8,128)S(1)}, u32[]{:S(2)}, u32[]{:S(2)}) collective-permute-start(f32[3,6,16,256]{3,2,1,0:T(8,128)S(1)} %get-tuple-element.151), channel_id=1, source_target_pairs={{1,0},{2,1},{3,2},{4,3},{5,4},{6,5},{7,6},{9,8},{10,9},{11,10},{12... | collective-permute-start | bytes 884744 | tf_op jit(solution)/shard_map/ppermute | solution.py:579
  116.3 7.7 %collective-permute-start.11 = (f32[3,6,16,256]{3,2,1,0:T(8,128)S(1)}, f32[3,6,16,256]{3,2,1,0:T(8,128)S(1)}, u32[]{:S(2)}, u32[]{:S(2)}) collective-permute-start(f32[3,6,16,256]{3,2,1,0:T(8,128)S(1)} %get-tuple-element.152), channel_id=1, source_target_pairs={{0,1},{1,2},{2,3},{3,4},{4,5},{5,6},{6,7},{8,9},{9,10},{10,11},{11... | collective-permute-start | bytes 884744 | tf_op jit(solution)/shard_map/ppermute | solution.py:579
  118.7 26.3 %collective-permute-start.15 = (f32[3,20,16,256]{3,2,1,0:T(8,128)S(1)}, f32[3,20,16,256]{3,2,1,0:T(8,128)S(1)}, u32[]{:S(2)}, u32[]{:S(2)}) collective-permute-start(f32[3,20,16,256]{3,2,1,0:T(8,128)S(1)} %get-tuple-element.112.refs_0_), channel_id=1, source_target_pairs={{8,0},{16,8},{24,16},{32,24},{40,32},{48,40},{56,48},{64,56},{72,6... | collective-permute-start | bytes 2949128 | tf_op jit(solution)/shard_map/ppermute | solution.py:579
  121.4 24.7 %collective-permute-start.8 = (f32[3,20,16,256]{3,2,1,0:T(8,128)S(1)}, f32[3,20,16,256]{3,2,1,0:T(8,128)S(1)}, u32[]{:S(2)}, u32[]{:S(2)}) collective-permute-start(f32[3,20,16,256]{3,2,1,0:T(8,128)S(1)} %get-tuple-element.112.refs_0_), channel_id=1, source_target_pairs={{0,8},{8,16},{16,24},{24,32},{32,40},{40,48},{48,56},{56,64},{64,7... | collective-permute-start | bytes 2949128 | tf_op jit(solution)/shard_map/ppermute | solution.py:579
  124.7 12.4 %collective-permute-start.13 = (f32[6,6,16,256]{3,2,1,0:T(8,128)S(1)}, f32[6,6,16,256]{3,2,1,0:T(8,128)S(1)}, u32[]{:S(2)}, u32[]{:S(2)}) collective-permute-start(f32[6,6,16,256]{3,2,1,0:T(8,128)S(1)} %pad_maximum_fusion.2), channel_id=1, source_target_pairs={{0,1},{1,2},{2,3},{3,4},{4,5},{5,6},{6,7},{8,9},{9,10},{10,11},{11... | collective-permute-start | bytes 1769480 | tf_op jit(solution)/shard_map/ppermute | solution.py:579
  130.4 11.5 %collective-permute-start.14 = (f32[6,6,16,256]{3,2,1,0:T(8,128)S(1)}, f32[6,6,16,256]{3,2,1,0:T(8,128)S(1)}, u32[]{:S(2)}, u32[]{:S(2)}) collective-permute-start(f32[6,6,16,256]{3,2,1,0:T(8,128)S(1)} %pad_maximum_fusion.3), channel_id=1, source_target_pairs={{1,0},{2,1},{3,2},{4,3},{5,4},{6,5},{7,6},{9,8},{10,9},{11,10},{12... | collective-permute-start | bytes 1769480 | tf_op jit(solution)/shard_map/ppermute | solution.py:579

commit v15 on v14

--- a/solution.py
+++ b/solution.py
@@ -524,6 +524,17 @@
     ]
 
 
+def slabs(source, target, sems):
+    found = {}
+    for comp in range(3):
+        for z in range(0, source.shape[1], 8):
+            part = comp, pl.ds(z, 8)
+            found[comp, z] = pltpu.make_async_copy(
+                source.at[part], target.at[part], sems.at[comp, z // 8]
+            )
+    return found
+
+
 def prep_kernel(where, raw_ref, edge_ref, mid_ref):
     own = raw_ref.shape[2]
     for comp in range(3):
@@ -538,13 +549,19 @@
                 ref[comp, at, zs, ys] = cells[i]
 
 
-def final_kernel(cells, where, all_ref, p_ref, g_ref, out_ref):
+def final_kernel(cells, where, all_ref, p_ref, g_ref, output_ref, out_ref, sems):
     step = step_of(all_ref, cells) * interior(where)
+    copies = slabs(out_ref, output_ref, sems)
+    own, width = out_ref.shape[2:]
     for comp in range(3):
-        for _, x, zs, xs, ys in blocks(out_ref.shape[1:]):
+        for z, x, zs, xs, ys in blocks(out_ref.shape[1:]):
             old = p_ref[comp, HALO + x : HALO + x + 8, zs, ys]
             new = old - step * g_ref[comp, xs, zs, ys]
             out_ref[comp, zs, xs, ys] = jnp.swapaxes(new, 0, 1)
+            if x == own - 8 and ys.stop == width:
+                copies[comp, z].start()
+    for copy in copies.values():
+        copy.wait()
 
 
 def f32(*shape):
@@ -561,14 +578,17 @@
     return (*found, lax.axis_size(TILE), lax.axis_size(IMG))
 
 
-def call(kernel, operands, outs, scratch):
-    vmem = pl.BlockSpec(memory_space=pltpu.VMEM)
+def call(kernel, operands, outs, scratch, hbm_out=False):
+    vmem, hbm = pl.BlockSpec(memory_space=pltpu.VMEM), pl.BlockSpec(memory_space=pltpu.HBM)
     return pl.pallas_call(
         lambda *refs: kernel(position(), *refs),
         out_shape=outs,
         in_specs=[vmem] * len(operands),
-        out_specs=[vmem] * len(outs),
-        scratch_shapes=[pltpu.VMEM(shape, jnp.float32) for shape in scratch],
+        out_specs=[hbm if hbm_out else vmem] * len(outs),
+        scratch_shapes=[
+            pltpu.VMEM(shape, jnp.float32) if isinstance(shape, tuple) else shape
+            for shape in scratch
+        ],
         compiler_params=pltpu.CompilerParams(vmem_limit_bytes=VMEM_LIMIT),
     )(*operands)
 
@@ -590,6 +610,7 @@
     cells = float(images * comps * depth * own * tiles * width)
     rows = own + 2 * HALO
     coefs = jnp.swapaxes(aniso, 0, 1)
+    moved = [spins.shape[1:], pltpu.SemaphoreType.DMA((3, depth // 8))]
     edge, mid = call(
         prep_kernel,
         [spins[0]],
@@ -659,7 +680,11 @@
         sums = from_everyone(sums)
         if outer == OUTER - 1:
             (path,) = call(
-                lambda *refs: final_kernel(cells, *refs), [sums, phi, g], [f32(*spins.shape[1:])], []
+                lambda *refs: final_kernel(cells, *refs),
+                [sums, phi, g],
+                [f32(*spins.shape[1:])],
+                moved,
+                hbm_out=True,
             )
             return path[None]
         edge, mid = call(

time: 209 us -> 209 us (level)
  no operation moved by 1% of the time
where the time goes in v15:
time: 209 us; the launch traced here: 208 us
  blocking collectives  98.4 us (47%)
  starting transfers between devices  44.2 us (21%)
  Pallas kernels  38.1 us (18%)
  waiting for transfers between devices  24.7 us (12%)
    all_to_all x6, blocking collectives, from_everyone(): return lax.all_to_all(rows, IMG_TILE, 0, 0, tiled=True)  98.4 us
    ppermute x16, starting transfers between devices, beside(): return lax.ppermute(cells, axis, pairs)  44.2 us
    pallas_call x13, Pallas kernels, call(): pl.pallas_call(lambda *refs: kernel(position(), *refs), out_shape=outs, i...  38.1 us
    ppermute x16, waiting for transfers between devices, beside(): return lax.ppermute(cells, axis, pairs)  24.7 us
  transfers between devices with their start and end apart: 16, of which 10 were waited for; matrix products, arithmetic and copies ran while one was open for 0% of the time, Pallas kernels for 4%

profile of v15, /device:TPU:1, one launch (start us, length us, event | category | flops | bytes accessed | tf_op | source)
XLA Modules:
  0.0 208.2 jit_solution(2426325963262898306)
XLA Ops:
  3.0 4.7 %collective-permute-start.1 = (f32[3,12,16,256]{3,2,1,0:T(8,128)S(1)}, f32[3,12,16,256]{3,2,1,0:T(8,128)S(1)}, u32[]{:S(2)}, u32[]{:S(2)}) collective-permute-start(f32[3,12,16,256]{3,2,1,0:T(8,128)S(1)} %get-tuple-element.77.refs_0_), channel_id=1, source_target_pairs={{0,8},{8,16},{16,24},{24,32},{32,40},{40,48},{48,56},{56,64},{64,7... | collective-permute-start | bytes 1769480 | tf_op jit(solution)/shard_map/ppermute | solution.py:599
  8.1 4.4 %collective-permute-start.3 = (f32[4,6,16,256]{3,2,1,0:T(8,128)S(1)}, f32[4,6,16,256]{3,2,1,0:T(8,128)S(1)}, u32[]{:S(2)}, u32[]{:S(2)}) collective-permute-start(f32[4,6,16,256]{3,2,1,0:T(8,128)S(1)} %pad_maximum_fusion.4), channel_id=1, source_target_pairs={{0,1},{1,2},{2,3},{3,4},{4,5},{5,6},{6,7},{8,9},{9,10},{10,11},{11... | collective-permute-start | bytes 1179656 | tf_op jit(solution)/shard_map/ppermute | solution.py:599
  12.6 1.9 collective-permute-start.4
  17.2 3.2 %collective-permute-start = (f32[3,20,16,256]{3,2,1,0:T(8,128)S(1)}, f32[3,20,16,256]{3,2,1,0:T(8,128)S(1)}, u32[]{:S(2)}, u32[]{:S(2)}) collective-permute-start(f32[3,20,16,256]{3,2,1,0:T(8,128)S(1)} %get-tuple-element.76.refs_0_), channel_id=1, source_target_pairs={{0,8},{8,16},{16,24},{24,32},{32,40},{40,48},{48,56},{56,64},{64,7... | collective-permute-start | bytes 2949128 | tf_op jit(solution)/shard_map/ppermute | solution.py:599
  20.5 1.5 collective-permute-done.4.refs_4_
  22.1 3.2 %collective-permute-start.5 = (f32[6,6,16,256]{3,2,1,0:T(8,128)S(1)}, f32[6,6,16,256]{3,2,1,0:T(8,128)S(1)}, u32[]{:S(2)}, u32[]{:S(2)}) collective-permute-start(f32[6,6,16,256]{3,2,1,0:T(8,128)S(1)} %pad_maximum_fusion), channel_id=1, source_target_pairs={{0,1},{1,2},{2,3},{3,4},{4,5},{5,6},{6,7},{8,9},{9,10},{10,11},{11... | collective-permute-start | bytes 1769480 | tf_op jit(solution)/shard_map/ppermute | solution.py:599
  25.4 1.9 collective-permute-start.6
  27.3 4.8 %collective-permute-done.5.refs_5_ = f32[6,6,16,256]{3,2,1,0:T(8,128)S(1)} collective-permute-done((f32[6,6,16,256]{3,2,1,0:T(8,128)S(1)}, f32[6,6,16,256]{3,2,1,0:T(8,128)S(1)}, u32[]{:S(2)}, u32[]{:S(2)}) %collective-permute-start.5) | collective-permute-done | bytes 589856 | tf_op jit(solution)/shard_map/ppermute | solution.py:599
  32.1 4.7 %collective-permute-done.6.refs_6_ = f32[6,6,16,256]{3,2,1,0:T(8,128)S(1)} collective-permute-done((f32[6,6,16,256]{3,2,1,0:T(8,128)S(1)}, f32[6,6,16,256]{3,2,1,0:T(8,128)S(1)}, u32[]{:S(2)}, u32[]{:S(2)}) %collective-permute-start.6) | collective-permute-done | bytes 589856 | tf_op jit(solution)/shard_map/ppermute | solution.py:599
  36.9 3.2 %shard_map.29 = (f32[3,24,16,256]{3,2,1,0:T(8,128)S(1)}, f32[3,24,16,256]{3,2,1,0:T(8,128)S(1)}, f32[3,24,16,256]{3,2,1,0:T(8,128)S(1)}, f32[3,24,16,256]{3,2,1,...) custom-call(f32[3,12,16,256]{3,2,1,0:T(8,128)S(1)} %get-tuple-elemen, ...), custom_call_target="tpu_custom_call" | custom-call | tf_op jit(solution)/shard_map/pallas_call | solution.py:583
  41.9 4.1 %shard_map.31 = (f32[3,28,16,256]{3,2,1,0:T(8,128)S(1)}, f32[3,28,16,256]{3,2,1,0:T(8,128)S(1)}, f32[3,28,16,256]{3,2,1,0:T(8,128)S(1)}, f32[3,28,16,256]{3,2,1,0:T(8,128)S(1)}, f32[128,128]{1,0:T(8,128)S(1)}) custom-call(f32[3,20,16,256]{3,2,1,0:T(8,128)S(1)} %get-tuple-element.76.refs_0_, f32[3,20,16,256]{3,2,1,0:T(8,128)S(1)} %collective-permute-done.refs_1_, ...), custom_call_target="tpu_custom_call" | custom-call | tf_op jit(solution)/shard_map/pallas_call | solution.py:583
  46.0 23.8 %all_to_all.66 = f32[128,1,128]{2,1,0:T(1,128)S(1)} all-to-all(f32[128,1,128]{2,1,0:T(1,128)S(1)} %bitcast.46), channel_id=1, replica_groups=mesh['img_0'=4,'img_1'=4,'tile_0'=4,'tile_1'=2] {'img_0','img_1','tile_0..., dimensions={0} | all-to-all | bytes 131072 | tf_op jit(solution)/shard_map/all_to_all | solution.py:603
  69.8 5.5 %shard_map.32 = (f32[3,44,16,256]{3,2,1,0:T(8,128)S(1)}, f32[3,44,16,256]{3,2,1,0:T(8,128)S(1)}, f32[3,44,16,256]{3,2,1,0:T(8,128)S(1)}, f32[3,44,16,256]{3,2,1,...) custom-call(f32[128,128]{1,0:T(8,128)S(1)} %bitcast.36, ...), custom_call_target="tpu_custom_call" | custom-call | tf_op jit(solution)/shard_map/pallas_call | solution.py:583
  75.3 13.9 %all_to_all.67 = f32[128,1,128]{2,1,0:T(1,128)S(1)} all-to-all(f32[128,1,128]{2,1,0:T(1,128)S(1)} %bitcast.42), channel_id=1, replica_groups=mesh['img_0'=4,'img_1'=4,'tile_0'=4,'tile_1'=2] {'img_0','img_1','tile_0..., dimensions={0} | all-to-all | bytes 131072 | tf_op jit(solution)/shard_map/all_to_all | solution.py:603
  89.3 4.2 %shard_map.33 = (f32[3,44,16,256]{3,2,1,0:T(8,128)S(1)}, f32[3,32,16,256]{3,2,1,0:T(8,128)S(1)}, f32[128,128]{1,0:T(8,128)S(1)}) custom-call(f32[8,128]{1,0:T(8,128)S(1)} %get-tuple-element.101.refs_0_, f32[128,128]{1,0:T(8,128)S(1)} %bitcast.39, f32[3,44,16,256]{3,2,1,0:T(8,128)S(1)} %get-tuple-element.103.refs_2_, ...), custom_call_target="tpu_custom_call" | custom-call | tf_op jit(solution)/shard_map/pallas_call | solution.py:583
  93.4 13.9 %all_to_all.68 = f32[128,1,128]{2,1,0:T(1,128)S(1)} all-to-all(f32[128,1,128]{2,1,0:T(1,128)S(1)} %bitcast.45), channel_id=1, replica_groups=mesh['img_0'=4,'img_1'=4,'tile_0'=4,'tile_1'=2] {'img_0','img_1','tile_0..., dimensions={0} | all-to-all | bytes 131072 | tf_op jit(solution)/shard_map/all_to_all | solution.py:603
  109.0 4.0 %collective-permute-start.9 = (f32[3,12,16,256]{3,2,1,0:T(8,128)S(1)}, f32[3,12,16,256]{3,2,1,0:T(8,128)S(1)}, u32[]{:S(2)}, u32[]{:S(2)}) collective-permute-start(f32[3,12,16,256]{3,2,1,0:T(8,128)S(1)} %get-tuple-element.113.refs_0_), channel_id=1, source_target_pairs={{0,8},{8,16},{16,24},{24,32},{32,40},{40,48},{48,56},{56,64},{64,7... | collective-permute-start | bytes 1769480 | tf_op jit(solution)/shard_map/ppermute | solution.py:599
  113.1 3.2 %collective-permute-start.12 = (f32[3,6,16,256]{3,2,1,0:T(8,128)S(1)}, f32[3,6,16,256]{3,2,1,0:T(8,128)S(1)}, u32[]{:S(2)}, u32[]{:S(2)}) collective-permute-start(f32[3,6,16,256]{3,2,1,0:T(8,128)S(1)} %get-tuple-element.151), channel_id=1, source_target_pairs={{1,0},{2,1},{3,2},{4,3},{5,4},{6,5},{7,6},{9,8},{10,9},{11,10},{12... | collective-permute-start | bytes 884744 | tf_op jit(solution)/shard_map/ppermute | solution.py:599
  116.3 2.3 %collective-permute-start.11 = (f32[3,6,16,256]{3,2,1,0:T(8,128)S(1)}, f32[3,6,16,256]{3,2,1,0:T(8,128)S(1)}, u32[]{:S(2)}, u32[]{:S(2)}) collective-permute-start(f32[3,6,16,256]{3,2,1,0:T(8,128)S(1)} %get-tuple-element.152), channel_id=1, source_target_pairs={{0,1},{1,2},{2,3},{3,4},{4,5},{5,6},{6,7},{8,9},{9,10},{10,11},{11... | collective-permute-start | bytes 884744 | tf_op jit(solution)/shard_map/ppermute | solution.py:599
  121.4 2.6 %collective-permute-start.8 = (f32[3,20,16,256]{3,2,1,0:T(8,128)S(1)}, f32[3,20,16,256]{3,2,1,0:T(8,128)S(1)}, u32[]{:S(2)}, u32[]{:S(2)}) collective-permute-start(f32[3,20,16,256]{3,2,1,0:T(8,128)S(1)} %get-tuple-element.112.refs_0_), channel_id=1, source_target_pairs={{0,8},{8,16},{16,24},{24,32},{32,40},{40,48},{48,56},{56,64},{64,7... | collective-permute-start | bytes 2949128 | tf_op jit(solution)/shard_map/ppermute | solution.py:599
  124.7 5.6 %collective-permute-start.13 = (f32[6,6,16,256]{3,2,1,0:T(8,128)S(1)}, f32[6,6,16,256]{3,2,1,0:T(8,128)S(1)}, u32[]{:S(2)}, u32[]{:S(2)}) collective-permute-start(f32[6,6,16,256]{3,2,1,0:T(8,128)S(1)} %pad_maximum_fusion.2), channel_id=1, source_target_pairs={{0,1},{1,2},{2,3},{3,4},{4,5},{5,6},{6,7},{8,9},{9,10},{10,11},{11... | collective-permute-start | bytes 1769480 | tf_op jit(solution)/shard_map/ppermute | solution.py:599
  130.4 1.9 collective-permute-start.14
  132.3 4.8 %collective-permute-done.13.refs_5_ = f32[6,6,16,256]{3,2,1,0:T(8,128)S(1)} collective-permute-done((f32[6,6,16,256]{3,2,1,0:T(8,128)S(1)}, f32[6,6,16,256]{3,2,1,0:T(8,128)S(1)}, u32[]{:S(2)}, u32[]{:S(2)}) %collective-permute-start.13) | collective-permute-done | bytes 589856 | tf_op jit(solution)/shard_map/ppermute | solution.py:599
  137.1 4.7 %collective-permute-done.14.refs_6_ = f32[6,6,16,256]{3,2,1,0:T(8,128)S(1)} collective-permute-done((f32[6,6,16,256]{3,2,1,0:T(8,128)S(1)}, f32[6,6,16,256]{3,2,1,0:T(8,128)S(1)}, u32[]{:S(2)}, u32[]{:S(2)}) %collective-permute-start.14) | collective-permute-done | bytes 589856 | tf_op jit(solution)/shard_map/ppermute | solution.py:599
  141.9 3.0 %shard_map.35 = (f32[3,24,16,256]{3,2,1,0:T(8,128)S(1)}, f32[3,24,16,256]{3,2,1,0:T(8,128)S(1)}, f32[3,24,16,256]{3,2,1,0:T(8,128)S(1)}, f32[3,24,16,256]{3,2,1,...) custom-call(f32[3,12,16,256]{3,2,1,0:T(8,128)S(1)} %get-tuple-elemen, ...), custom_call_target="tpu_custom_call" | custom-call | tf_op jit(solution)/shard_map/pallas_call | solution.py:583
  146.2 4.0 %shard_map.37 = (f32[3,28,16,256]{3,2,1,0:T(8,128)S(1)}, f32[3,28,16,256]{3,2,1,0:T(8,128)S(1)}, f32[3,28,16,256]{3,2,1,0:T(8,128)S(1)}, f32[3,28,16,256]{3,2,1,0:T(8,128)S(1)}, f32[128,128]{1,0:T(8,128)S(1)}) custom-call(f32[3,20,16,256]{3,2,1,0:T(8,128)S(1)} %get-tuple-element.112.refs_0_, f32[3,20,16,256]{3,2,1,0:T(8,128)S(1)} %collective-permute-done.8.refs_1_, ...), custom_call_target="tpu_custom_call" | custom-call | tf_op jit(solution)/shard_map/pallas_call | solution.py:583
  150.2 19.0 %all_to_all.69 = f32[128,1,128]{2,1,0:T(1,128)S(1)} all-to-all(f32[128,1,128]{2,1,0:T(1,128)S(1)} %bitcast.47), channel_id=1, replica_groups=mesh['img_0'=4,'img_1'=4,'tile_0'=4,'tile_1'=2] {'img_0','img_1','tile_0..., dimensions={0} | all-to-all | bytes 131072 | tf_op jit(solution)/shard_map/all_to_all | solution.py:603
  169.1 5.4 %shard_map.38 = (f32[3,44,16,256]{3,2,1,0:T(8,128)S(1)}, f32[3,44,16,256]{3,2,1,0:T(8,128)S(1)}, f32[3,44,16,256]{3,2,1,0:T(8,128)S(1)}, f32[3,44,16,256]{3,2,1,...) custom-call(f32[128,128]{1,0:T(8,128)S(1)} %bitcast.37, ...), custom_call_target="tpu_custom_call" | custom-call | tf_op jit(solution)/shard_map/pallas_call | solution.py:583
  174.6 13.9 %all_to_all.70 = f32[128,1,128]{2,1,0:T(1,128)S(1)} all-to-all(f32[128,1,128]{2,1,0:T(1,128)S(1)} %bitcast.43), channel_id=1, replica_groups=mesh['img_0'=4,'img_1'=4,'tile_0'=4,'tile_1'=2] {'img_0','img_1','tile_0..., dimensions={0} | all-to-all | bytes 131072 | tf_op jit(solution)/shard_map/all_to_all | solution.py:603
  188.5 4.2 %shard_map.39 = (f32[3,44,16,256]{3,2,1,0:T(8,128)S(1)}, f32[3,32,16,256]{3,2,1,0:T(8,128)S(1)}, f32[128,128]{1,0:T(8,128)S(1)}) custom-call(f32[8,128]{1,0:T(8,128)S(1)} %get-tuple-element.136.refs_0_, f32[128,128]{1,0:T(8,128)S(1)} %bitcast.38, f32[3,44,16,256]{3,2,1,0:T(8,128)S(1)} %get-tuple-element.138.refs_2_, ...), custom_call_target="tpu_custom_call" | custom-call | tf_op jit(solution)/shard_map/pallas_call | solution.py:583
  192.6 13.9 %all_to_all.71 = f32[128,1,128]{2,1,0:T(1,128)S(1)} all-to-all(f32[128,1,128]{2,1,0:T(1,128)S(1)} %bitcast.44), channel_id=1, replica_groups=mesh['img_0'=4,'img_1'=4,'tile_0'=4,'tile_1'=2] {'img_0','img_1','tile_0..., dimensions={0} | all-to-all | bytes 131072 | tf_op jit(solution)/shard_map/all_to_all | solution.py:603
  206.6 1.5 shard_map.40
  (36 shorter events, 14.5 us)
Async XLA Ops:
  0.0 1.4 copy-start
  1.4 6.3 %copy-start.1 = (f32[16,32,256]{2,1,0:T(8,128)S(1)}, f32[16,32,256]{2,1,0:T(8,128)}, u32[]{:S(2)}) copy-start(f32[16,32,256]{2,1,0:T(8,128)} %param.3) | copy-start | bytes 1572868
  1.7 20.3 %collective-permute-start.2 = (f32[3,12,16,256]{3,2,1,0:T(8,128)S(1)}, f32[3,12,16,256]{3,2,1,0:T(8,128)S(1)}, u32[]{:S(2)}, u32[]{:S(2)}) collective-permute-start(f32[3,12,16,256]{3,2,1,0:T(8,128)S(1)} %get-tuple-element.77.refs_0_), channel_id=1, source_target_pairs={{8,0},{16,8},{24,16},{32,24},{40,32},{48,40},{56,48},{64,56},{72,6... | collective-permute-start | bytes 1769480 | tf_op jit(solution)/shard_map/ppermute | solution.py:599
  3.0 19.0 %collective-permute-start.1 = (f32[3,12,16,256]{3,2,1,0:T(8,128)S(1)}, f32[3,12,16,256]{3,2,1,0:T(8,128)S(1)}, u32[]{:S(2)}, u32[]{:S(2)}) collective-permute-start(f32[3,12,16,256]{3,2,1,0:T(8,128)S(1)} %get-tuple-element.77.refs_0_), channel_id=1, source_target_pairs={{0,8},{8,16},{16,24},{24,32},{32,40},{40,48},{48,56},{56,64},{64,7... | collective-permute-start | bytes 1769480 | tf_op jit(solution)/shard_map/ppermute | solution.py:599
  8.1 9.1 %collective-permute-start.3 = (f32[4,6,16,256]{3,2,1,0:T(8,128)S(1)}, f32[4,6,16,256]{3,2,1,0:T(8,128)S(1)}, u32[]{:S(2)}, u32[]{:S(2)}) collective-permute-start(f32[4,6,16,256]{3,2,1,0:T(8,128)S(1)} %pad_maximum_fusion.4), channel_id=1, source_target_pairs={{0,1},{1,2},{2,3},{3,4},{4,5},{5,6},{6,7},{8,9},{9,10},{10,11},{11... | collective-permute-start | bytes 1179656 | tf_op jit(solution)/shard_map/ppermute | solution.py:599
  12.6 9.4 %collective-permute-start.4 = (f32[4,6,16,256]{3,2,1,0:T(8,128)S(1)}, f32[4,6,16,256]{3,2,1,0:T(8,128)S(1)}, u32[]{:S(2)}, u32[]{:S(2)}) collective-permute-start(f32[4,6,16,256]{3,2,1,0:T(8,128)S(1)} %pad_maximum_fusion.5), channel_id=1, source_target_pairs={{1,0},{2,1},{3,2},{4,3},{5,4},{6,5},{7,6},{9,8},{10,9},{11,10},{12... | collective-permute-start | bytes 1179656 | tf_op jit(solution)/shard_map/ppermute | solution.py:599
  14.5 25.7 %collective-permute-start.7 = (f32[3,20,16,256]{3,2,1,0:T(8,128)S(1)}, f32[3,20,16,256]{3,2,1,0:T(8,128)S(1)}, u32[]{:S(2)}, u32[]{:S(2)}) collective-permute-start(f32[3,20,16,256]{3,2,1,0:T(8,128)S(1)} %get-tuple-element.76.refs_0_), channel_id=1, source_target_pairs={{8,0},{16,8},{24,16},{32,24},{40,32},{48,40},{56,48},{64,56},{72,6... | collective-permute-start | bytes 2949128 | tf_op jit(solution)/shard_map/ppermute | solution.py:599
  17.2 24.7 %collective-permute-start = (f32[3,20,16,256]{3,2,1,0:T(8,128)S(1)}, f32[3,20,16,256]{3,2,1,0:T(8,128)S(1)}, u32[]{:S(2)}, u32[]{:S(2)}) collective-permute-start(f32[3,20,16,256]{3,2,1,0:T(8,128)S(1)} %get-tuple-element.76.refs_0_), channel_id=1, source_target_pairs={{0,8},{8,16},{16,24},{24,32},{32,40},{40,48},{48,56},{56,64},{64,7... | collective-permute-start | bytes 2949128 | tf_op jit(solution)/shard_map/ppermute | solution.py:599
  22.1 10.0 %collective-permute-start.5 = (f32[6,6,16,256]{3,2,1,0:T(8,128)S(1)}, f32[6,6,16,256]{3,2,1,0:T(8,128)S(1)}, u32[]{:S(2)}, u32[]{:S(2)}) collective-permute-start(f32[6,6,16,256]{3,2,1,0:T(8,128)S(1)} %pad_maximum_fusion), channel_id=1, source_target_pairs={{0,1},{1,2},{2,3},{3,4},{4,5},{5,6},{6,7},{8,9},{9,10},{10,11},{11... | collective-permute-start | bytes 1769480 | tf_op jit(solution)/shard_map/ppermute | solution.py:599
  25.4 11.5 %collective-permute-start.6 = (f32[6,6,16,256]{3,2,1,0:T(8,128)S(1)}, f32[6,6,16,256]{3,2,1,0:T(8,128)S(1)}, u32[]{:S(2)}, u32[]{:S(2)}) collective-permute-start(f32[6,6,16,256]{3,2,1,0:T(8,128)S(1)} %pad_maximum_fusion.1), channel_id=1, source_target_pairs={{1,0},{2,1},{3,2},{4,3},{5,4},{6,5},{7,6},{9,8},{10,9},{11,10},{12... | collective-permute-start | bytes 1769480 | tf_op jit(solution)/shard_map/ppermute | solution.py:599
  107.7 16.4 %collective-permute-start.10 = (f32[3,12,16,256]{3,2,1,0:T(8,128)S(1)}, f32[3,12,16,256]{3,2,1,0:T(8,128)S(1)}, u32[]{:S(2)}, u32[]{:S(2)}) collective-permute-start(f32[3,12,16,256]{3,2,1,0:T(8,128)S(1)} %get-tuple-element.113.refs_0_), channel_id=1, source_target_pairs={{8,0},{16,8},{24,16},{32,24},{40,32},{48,40},{56,48},{64,56},{72,6... | collective-permute-start | bytes 1769480 | tf_op jit(solution)/shard_map/ppermute | solution.py:599
  109.0 15.6 %collective-permute-start.9 = (f32[3,12,16,256]{3,2,1,0:T(8,128)S(1)}, f32[3,12,16,256]{3,2,1,0:T(8,128)S(1)}, u32[]{:S(2)}, u32[]{:S(2)}) collective-permute-start(f32[3,12,16,256]{3,2,1,0:T(8,128)S(1)} %get-tuple-element.113.refs_0_), channel_id=1, source_target_pairs={{0,8},{8,16},{16,24},{24,32},{32,40},{40,48},{48,56},{56,64},{64,7... | collective-permute-start | bytes 1769480 | tf_op jit(solution)/shard_map/ppermute | solution.py:599
  113.1 8.3 %collective-permute-start.12 = (f32[3,6,16,256]{3,2,1,0:T(8,128)S(1)}, f32[3,6,16,256]{3,2,1,0:T(8,128)S(1)}, u32[]{:S(2)}, u32[]{:S(2)}) collective-permute-start(f32[3,6,16,256]{3,2,1,0:T(8,128)S(1)} %get-tuple-element.151), channel_id=1, source_target_pairs={{1,0},{2,1},{3,2},{4,3},{5,4},{6,5},{7,6},{9,8},{10,9},{11,10},{12... | collective-permute-start | bytes 884744 | tf_op jit(solution)/shard_map/ppermute | solution.py:599
  116.3 7.7 %collective-permute-start.11 = (f32[3,6,16,256]{3,2,1,0:T(8,128)S(1)}, f32[3,6,16,256]{3,2,1,0:T(8,128)S(1)}, u32[]{:S(2)}, u32[]{:S(2)}) collective-permute-start(f32[3,6,16,256]{3,2,1,0:T(8,128)S(1)} %get-tuple-element.152), channel_id=1, source_target_pairs={{0,1},{1,2},{2,3},{3,4},{4,5},{5,6},{6,7},{8,9},{9,10},{10,11},{11... | collective-permute-start | bytes 884744 | tf_op jit(solution)/shard_map/ppermute | solution.py:599
  118.7 26.3 %collective-permute-start.15 = (f32[3,20,16,256]{3,2,1,0:T(8,128)S(1)}, f32[3,20,16,256]{3,2,1,0:T(8,128)S(1)}, u32[]{:S(2)}, u32[]{:S(2)}) collective-permute-start(f32[3,20,16,256]{3,2,1,0:T(8,128)S(1)} %get-tuple-element.112.refs_0_), channel_id=1, source_target_pairs={{8,0},{16,8},{24,16},{32,24},{40,32},{48,40},{56,48},{64,56},{72,6... | collective-permute-start | bytes 2949128 | tf_op jit(solution)/shard_map/ppermute | solution.py:599
  121.4 24.7 %collective-permute-start.8 = (f32[3,20,16,256]{3,2,1,0:T(8,128)S(1)}, f32[3,20,16,256]{3,2,1,0:T(8,128)S(1)}, u32[]{:S(2)}, u32[]{:S(2)}) collective-permute-start(f32[3,20,16,256]{3,2,1,0:T(8,128)S(1)} %get-tuple-element.112.refs_0_), channel_id=1, source_target_pairs={{0,8},{8,16},{16,24},{24,32},{32,40},{40,48},{48,56},{56,64},{64,7... | collective-permute-start | bytes 2949128 | tf_op jit(solution)/shard_map/ppermute | solution.py:599
  124.7 12.4 %collective-permute-start.13 = (f32[6,6,16,256]{3,2,1,0:T(8,128)S(1)}, f32[6,6,16,256]{3,2,1,0:T(8,128)S(1)}, u32[]{:S(2)}, u32[]{:S(2)}) collective-permute-start(f32[6,6,16,256]{3,2,1,0:T(8,128)S(1)} %pad_maximum_fusion.2), channel_id=1, source_target_pairs={{0,1},{1,2},{2,3},{3,4},{4,5},{5,6},{6,7},{8,9},{9,10},{10,11},{11... | collective-permute-start | bytes 1769480 | tf_op jit(solution)/shard_map/ppermute | solution.py:599
  130.4 11.5 %collective-permute-start.14 = (f32[6,6,16,256]{3,2,1,0:T(8,128)S(1)}, f32[6,6,16,256]{3,2,1,0:T(8,128)S(1)}, u32[]{:S(2)}, u32[]{:S(2)}) collective-permute-start(f32[6,6,16,256]{3,2,1,0:T(8,128)S(1)} %pad_maximum_fusion.3), channel_id=1, source_target_pairs={{1,0},{2,1},{3,2},{4,3},{5,4},{6,5},{7,6},{9,8},{10,9},{11,10},{12... | collective-permute-start | bytes 1769480 | tf_op jit(solution)/shard_map/ppermute | solution.py:599
